TPU v7x, 32 devices: a whole 2x2x4 slice. The times are simulated.
32 devices in a mesh: dp: 8 (over y, x, core), expert: 4 (over z).
Axes of the slice: x: 2, y: 2, z: 4, core: 2. Of those that a mesh axis runs over, the one named last changes fastest.
Arguments:
- tokens: bfloat16 [4096, 2048], P(('dp', 'expert')), may hold values from -6 to 6
- lengths: int32 [64], replicated, may hold values from 32 to 96, as said below
- permutation: int32 [64], replicated, may hold values from 0 to 63, as said below
- routes: int32 [4096, 8], P(('dp', 'expert')), may hold values from 0 to 15, all different within a row; in each aligned block of 128 rows (0 to 127, 128 to 255, ...) at most 80 rows name the same one
- norm_gains: bfloat16 [2048, 4], P(('dp', 'expert')), may hold values from 0.25 to 1.75
- w_qkv: bfloat16 [2048, 6144], P(('dp', 'expert')), may hold values from -0.125 to 0.125
- w_out: bfloat16 [2048, 2048], P(('dp', 'expert')), may hold values from -0.75 to 0.75
- router: bfloat16 [2048, 16], P(('dp', 'expert')), may hold values from -0.0625 to 0.0625
- w_gate_up: bfloat16 [2048, 16, 2048], P('dp', 'expert'), may hold values from -0.125 to 0.125
- w_down: bfloat16 [2048, 16, 1024], P('dp', 'expert'), may hold values from -0.75 to 0.75
- cotangent: bfloat16 [4096, 2048], P(('dp', 'expert')), may hold values from -6 to 6
Outputs:
- output: float32 [4096, 2048], P(('dp', 'expert'))
- grad_tokens: float32 [4096, 2048], P(('dp', 'expert'))
- grad_gains: float32 [2048, 4], P(('dp', 'expert'))
- grad_w_qkv: float32 [2048, 6144], P(('dp', 'expert'))
- grad_w_out: float32 [2048, 2048], P(('dp', 'expert'))
- grad_router: float32 [2048, 16], P(('dp', 'expert'))
- grad_w_gate_up: float32 [2048, 16, 2048], P('dp', 'expert')
- grad_w_down: float32 [2048, 16, 1024], P('dp', 'expert')
Inputs may be any that keep to these rules, and one draw needn't show every extreme that they name: `lengths`: the 2 sequences dealt to one block fill its 128 rows; some sequence has exactly 96 tokens. A permutation of the sequence numbers. `routes`: each row names 8 different experts; among the 32 aligned blocks of 128 rows (the rows of one device), no expert is named in more than 80 rows of a block, and some expert reaches 80.
All inputs are finite; a program needn't handle non-finite values.
Results may differ from a plain program's by a relative error of at most 0.017.
Values may be sent and summed in bfloat16 or wider, within the bound.
No kernel may reach another device: no remote copies, remote signals or barrier semaphores. Data moves between devices by JAX's collectives and lax.ppermute only.
A program may use at most 384 MiB of HBM per device.

v0:
```python
import jax
import jax.numpy as jnp
from jax import lax
from jax.sharding import PartitionSpec as P

HEAD_DIM = 128
SEQ_DEV = 2
CAP = 80


EPSILON = 1e-06
ROPE_BASE = 50000.0


def rms_scale(values, gain_vec):
    return (
        values * lax.rsqrt(jnp.mean(values * values, axis=-1, keepdims=True) + EPSILON) * gain_vec
    )


def rotate(values, cos_table, sin_table):
    half_dim = values.shape[-1] // 2
    first_half = values[..., :half_dim]
    second_half = values[..., half_dim:]
    return jnp.concatenate(
        [
            first_half * cos_table - second_half * sin_table,
            second_half * cos_table + first_half * sin_table,
        ],
        axis=-1,
    )


def angles(position):
    half_dim = HEAD_DIM // 2
    inverse = ROPE_BASE ** (-2.0 * jnp.arange(half_dim, dtype=jnp.float32) / HEAD_DIM)
    turned = position.astype(jnp.float32)[..., None] * inverse
    return (jnp.cos(turned)[..., None, :], jnp.sin(turned)[..., None, :])


def on_device(
    tokens,
    lengths,
    permutation,
    routes,
    norm_gains,
    w_qkv,
    w_out,
    router,
    w_gate_up,
    w_down,
    cotangent,
):
    tok_rows, model_width = tokens.shape
    route_count = routes.shape[1]
    local_count = w_gate_up.shape[1]
    expert_count = local_count * lax.axis_size("expert")
    capacity = CAP
    ff_width = w_down.shape[2]
    attn_scale = HEAD_DIM ** (-0.5)
    device = lax.axis_index(("dp", "expert"))
    dealt_lens = jnp.take(lengths, lax.dynamic_slice_in_dim(permutation, device * SEQ_DEV, SEQ_DEV))
    seq_ends = jnp.cumsum(dealt_lens)
    places = jnp.arange(tok_rows, dtype=jnp.int32)
    segment = jnp.sum((places[:, None] >= seq_ends[None, :]).astype(jnp.int32), axis=1)
    starts = seq_ends - dealt_lens
    offset = jnp.sum(
        jnp.where(
            segment[:, None] == jnp.arange(SEQ_DEV, dtype=jnp.int32)[None, :], starts[None, :], 0
        ),
        axis=1,
    )
    cos_table, sin_table = angles(places - offset)
    full_gains, full_qkv, full_out, full_router = (
        lax.all_gather(norm_gains, ("dp", "expert"), axis=0, tiled=True),
        lax.all_gather(w_qkv, ("dp", "expert"), axis=0, tiled=True),
        lax.all_gather(w_out, ("dp", "expert"), axis=0, tiled=True),
        lax.all_gather(router, ("dp", "expert"), axis=0, tiled=True),
    )
    gain_full = full_gains.astype(jnp.float32)
    residual = tokens.astype(jnp.float32)
    normed_f, attn_norm_pull = jax.vjp(rms_scale, residual, gain_full[:, 0])
    normed = normed_f.astype(jnp.bfloat16)
    proj_qkv = jnp.dot(normed, full_qkv, preferred_element_type=jnp.float32)

    def front_local(query_part, keys_part, gain_query, gain_keys):
        query_n = rms_scale(query_part, gain_query).reshape(tok_rows, -1, HEAD_DIM)
        keys_n = rms_scale(keys_part, gain_keys).reshape(tok_rows, -1, HEAD_DIM)
        return (rotate(query_n, cos_table, sin_table), rotate(keys_n, cos_table, sin_table))

    rotated, front_pull = jax.vjp(
        front_local,
        proj_qkv[:, :model_width],
        proj_qkv[:, model_width : 2 * model_width],
        gain_full[:, 1],
        gain_full[:, 2],
    )
    query_rot = rotated[0].astype(jnp.bfloat16)
    keys_rot = rotated[1].astype(jnp.bfloat16)
    values_low = proj_qkv[:, 2 * model_width :].astype(jnp.bfloat16).reshape(tok_rows, -1, HEAD_DIM)
    scores = (
        jnp.einsum("thd,shd->hts", query_rot, keys_rot, preferred_element_type=jnp.float32)
        * attn_scale
    )
    same_seq = segment[:, None] == segment[None, :]
    scores = jnp.where(same_seq[None], scores, -1e30)
    row_peak = jnp.max(scores, axis=2, keepdims=True)
    exp_scores = jnp.exp(scores - row_peak)
    attn_probs = exp_scores / jnp.sum(exp_scores, axis=2, keepdims=True)
    probs_low = attn_probs.astype(jnp.bfloat16)
    mixed = (
        jnp.einsum("hts,shd->thd", probs_low, values_low, preferred_element_type=jnp.float32)
        .reshape(tok_rows, model_width)
        .astype(jnp.bfloat16)
    )
    hidden = residual + jnp.dot(mixed, full_out, preferred_element_type=jnp.float32)
    moe_f, ffn_norm_pull = jax.vjp(rms_scale, hidden, gain_full[:, 3])
    moe_in = moe_f.astype(jnp.bfloat16)
    logits = jnp.dot(moe_in, full_router, preferred_element_type=jnp.float32)
    picked = jnp.take_along_axis(logits, routes, axis=1)
    gate_prob, gate_pull = jax.vjp(lambda picked_in: jax.nn.softmax(picked_in, axis=1), picked)
    flat_routes = routes.reshape(-1)
    onehot = (flat_routes[:, None] == jnp.arange(expert_count, dtype=jnp.int32)[None, :]).astype(
        jnp.int32
    )
    before = jnp.cumsum(onehot, axis=0) - onehot
    slot_index = jnp.sum(before * onehot, axis=1)
    target = flat_routes * capacity + slot_index
    source = jnp.repeat(moe_in, route_count, axis=0)
    outgoing = (
        jnp.zeros((expert_count * capacity, model_width), jnp.bfloat16).at[target].set(source)
    )
    arrived = lax.all_to_all(
        outgoing.reshape(expert_count, capacity, model_width),
        "expert",
        split_axis=0,
        concat_axis=1,
        tiled=True,
    )
    expert_gate_up, expert_down = (
        lax.all_gather(w_gate_up, "dp", axis=0, tiled=True),
        lax.all_gather(w_down, "dp", axis=0, tiled=True),
    )
    gate_up_val = jnp.einsum(
        "erd,dek->erk", arrived, expert_gate_up, preferred_element_type=jnp.float32
    )
    gate_part = gate_up_val[..., :ff_width]
    up_part = gate_up_val[..., ff_width:]
    activation = (jax.nn.silu(gate_part) * up_part).astype(jnp.bfloat16)
    result = jnp.einsum(
        "erk,dek->erd", activation, expert_down, preferred_element_type=jnp.float32
    ).astype(jnp.bfloat16)
    returned = lax.all_to_all(result, "expert", split_axis=1, concat_axis=0, tiled=True)
    returned_rows = returned.reshape(expert_count * capacity, model_width)[target].reshape(
        tok_rows, route_count, model_width
    )
    output = hidden + jnp.sum(gate_prob[:, :, None] * returned_rows, axis=1)
    full_gains, full_qkv, full_out, full_router = (
        lax.all_gather(norm_gains, ("dp", "expert"), axis=0, tiled=True),
        lax.all_gather(w_qkv, ("dp", "expert"), axis=0, tiled=True),
        lax.all_gather(w_out, ("dp", "expert"), axis=0, tiled=True),
        lax.all_gather(router, ("dp", "expert"), axis=0, tiled=True),
    )
    expert_gate_up, expert_down = (
        lax.all_gather(w_gate_up, "dp", axis=0, tiled=True),
        lax.all_gather(w_down, "dp", axis=0, tiled=True),
    )
    grad_out = cotangent.astype(jnp.float32)
    to_experts = (
        (gate_prob[:, :, None] * grad_out[:, None, :])
        .astype(jnp.bfloat16)
        .reshape(tok_rows * route_count, model_width)
    )
    grad_gates = jnp.sum(grad_out[:, None, :] * returned_rows, axis=2)
    grad_picked = gate_pull(grad_gates)[0]
    grad_logits = jnp.sum(
        jnp.where(
            routes[:, :, None] == jnp.arange(expert_count, dtype=jnp.int32)[None, None, :],
            grad_picked[:, :, None],
            0.0,
        ),
        axis=1,
    ).astype(jnp.bfloat16)
    outgoing_grad = (
        jnp.zeros((expert_count * capacity, model_width), jnp.bfloat16).at[target].set(to_experts)
    )
    arrived_grad = lax.all_to_all(
        outgoing_grad.reshape(expert_count, capacity, model_width),
        "expert",
        split_axis=0,
        concat_axis=1,
        tiled=True,
    )
    grad_act = jnp.einsum(
        "erd,dek->erk", arrived_grad, expert_down, preferred_element_type=jnp.float32
    )
    sigmoid_gate = jax.nn.sigmoid(gate_part)
    grad_gate = grad_act * up_part * (sigmoid_gate * (1.0 + gate_part * (1.0 - sigmoid_gate)))
    grad_up = grad_act * (gate_part * sigmoid_gate)
    grad_both = jnp.concatenate([grad_gate, grad_up], axis=2).astype(jnp.bfloat16)
    grad_arrived = jnp.einsum(
        "erk,dek->erd", grad_both, expert_gate_up, preferred_element_type=jnp.float32
    ).astype(jnp.bfloat16)
    grad_back = lax.all_to_all(grad_arrived, "expert", split_axis=1, concat_axis=0, tiled=True)
    first_term = jnp.einsum("erd,erk->dek", arrived, grad_both, preferred_element_type=jnp.float32)
    second_term = jnp.einsum(
        "erd,erk->dek", arrived_grad, activation, preferred_element_type=jnp.float32
    )
    expert_grads = lax.psum_scatter(
        jnp.concatenate([first_term, second_term], axis=2).astype(jnp.bfloat16),
        "dp",
        scatter_dimension=0,
        tiled=True,
    ).astype(jnp.float32)
    copies = grad_back.reshape(expert_count * capacity, model_width)[target].reshape(
        tok_rows, route_count, model_width
    )
    grad_moe = jnp.einsum(
        "te,de->td", grad_logits, full_router, preferred_element_type=jnp.float32
    ) + jnp.sum(copies, axis=1, dtype=jnp.float32)
    router_partial = jnp.einsum(
        "td,te->de", moe_in, grad_logits, preferred_element_type=jnp.float32
    )
    grad_hidden_n, grad_gain_ffn = ffn_norm_pull(grad_moe)
    grad_hidden = grad_out + grad_hidden_n
    grad_hidden_low = grad_hidden.astype(jnp.bfloat16)
    grad_mixed = jnp.einsum(
        "tc,dc->td", grad_hidden_low, full_out, preferred_element_type=jnp.float32
    ).astype(jnp.bfloat16)
    grad_mixed_heads = grad_mixed.reshape(tok_rows, -1, HEAD_DIM)
    grad_probs = jnp.einsum(
        "thd,shd->hts", grad_mixed_heads, values_low, preferred_element_type=jnp.float32
    )
    grad_values = jnp.einsum(
        "hts,thd->shd", probs_low, grad_mixed_heads, preferred_element_type=jnp.float32
    )
    centre = jnp.sum(attn_probs * grad_probs, axis=2, keepdims=True)
    grad_scores = (attn_probs * (grad_probs - centre)).astype(jnp.bfloat16)
    grad_query_rot = (
        jnp.einsum("hts,shd->thd", grad_scores, keys_rot, preferred_element_type=jnp.float32)
        * attn_scale
    )
    grad_keys_rot = (
        jnp.einsum("hts,thd->shd", grad_scores, query_rot, preferred_element_type=jnp.float32)
        * attn_scale
    )
    grad_query, grad_keys, grad_gain_query, grad_gain_keys = front_pull(
        (grad_query_rot, grad_keys_rot)
    )
    grad_qkv = jnp.concatenate(
        [grad_query, grad_keys, grad_values.reshape(tok_rows, model_width)], axis=1
    ).astype(jnp.bfloat16)
    grad_normed = jnp.einsum("tc,dc->td", grad_qkv, full_qkv, preferred_element_type=jnp.float32)
    grad_residual_n, grad_gain_attn = attn_norm_pull(grad_normed)
    grad_tokens = grad_hidden + grad_residual_n
    first_term = jnp.einsum("tc,tk->ck", normed, grad_qkv, preferred_element_type=jnp.float32)
    second_term = jnp.einsum(
        "tc,tk->ck", mixed, grad_hidden_low, preferred_element_type=jnp.float32
    )
    attention_grads = lax.psum_scatter(
        jnp.concatenate([first_term, second_term], axis=1),
        ("dp", "expert"),
        scatter_dimension=0,
        tiled=True,
    )
    gain_partial = jnp.stack(
        [grad_gain_attn, grad_gain_query, grad_gain_keys, grad_gain_ffn], axis=1
    )
    grad_gains, grad_router = (
        lax.psum_scatter(gain_partial, ("dp", "expert"), scatter_dimension=0, tiled=True),
        lax.psum_scatter(router_partial, ("dp", "expert"), scatter_dimension=0, tiled=True),
    )
    return (
        output,
        grad_tokens,
        grad_gains,
        attention_grads[:, : 3 * model_width],
        attention_grads[:, 3 * model_width :],
        grad_router,
        expert_grads[..., : 2 * ff_width],
        expert_grads[..., 2 * ff_width :],
    )


def solution(mesh):
    return jax.shard_map(
        on_device,
        mesh=mesh,
        in_specs=(
            P(("dp", "expert"), None),
            P(),
            P(),
            P(("dp", "expert"), None),
            P(("dp", "expert"), None),
            P(("dp", "expert"), None),
            P(("dp", "expert"), None),
            P(("dp", "expert"), None),
            P("dp", "expert", None),
            P("dp", "expert", None),
            P(("dp", "expert"), None),
        ),
        out_specs=(
            P(("dp", "expert"), None),
            P(("dp", "expert"), None),
            P(("dp", "expert"), None),
            P(("dp", "expert"), None),
            P(("dp", "expert"), None),
            P(("dp", "expert"), None),
            P("dp", "expert", None),
            P("dp", "expert", None),
        ),
        check_vma=False,
    )
```

profile of v0, /device:TPU:4, one launch (start us, length us, event | category | flops | bytes accessed | tf_op | source)
XLA Modules:
  0.0 2866.3 jit_solution(11694385318177306290)
XLA Ops:
  17.6 68.0 %all-gather = bf16[32,64,4]{1,2,0:T(4,128)(2,1)S(1)} all-gather(bf16[1,64,4]{1,2,0:T(4,128)(2,1)S(1)} %bitcast.204), channel_id=1, replica_groups=mesh['dp'=8,'expert'=4] {'dp','expert'}, dimensions={0}, use_global_device_ids=true | all-gather | bytes 16896 | tf_op jit(solution)/shard_map/all_gather | solution.py:75
  92.1 67.6 %all-gather.1 = bf16[32,64,16]{1,2,0:T(8,128)(2,1)S(1)} all-gather(bf16[1,64,16]{1,2,0:T(8,128)(2,1)S(1)} %bitcast.203), channel_id=1, replica_groups=mesh['dp'=8,'expert'=4] {'dp','expert'}, dimensions={0}, use_global_device_ids=true | all-gather | bytes 67584 | tf_op jit(solution)/shard_map/all_gather | solution.py:78
  190.2 56.4 %all-gather.9.cloned.1.call-done = bf16[2048,2048]{1,0:T(8,128)(2,1)} async-done(((bf16[64,2048]{1,0:T(8,128)(2,1)}), bf16[2048,2048]{1,0:T(8,128)(2,1)}) %all-gather.9.cloned.1.call-update) | async-done | bytes 8388624 | tf_op jit(solution)/shard_map/all_gather | solution.py:77
  260.6 10.4 scatter_custom_fusion.1
  285.7 106.7 %all-to-all-done.2 = bf16[16,80,2048]{2,1,0:T(8,128)(2,1)} async-done(((bf16[16,80,2048]{2,1,0:T(8,128)(2,1)}), bf16[16,80,2048]{2,1,0:T(8,128)(2,1)}, u32[]{:S(2)}, u32[]{:S(2)}) %all-to-all-start.2) | async-done | bytes 5242912 | tf_op jit(solution)/shard_map/all_to_all | solution.py:187
  403.5 109.8 %all-to-all-done = bf16[16,80,2048]{2,1,0:T(8,128)(2,1)} async-done(((bf16[16,80,2048]{2,1,0:T(8,128)(2,1)}), bf16[16,80,2048]{2,1,0:T(8,128)(2,1)}, u32[]{:S(2)}, u32[]{:S(2)}) %all-to-all-start) | async-done | bytes 5242912 | tf_op jit(solution)/shard_map/all_to_all | solution.py:133
  519.0 20.9 fusion.81
  539.8 16.0 multiply_convert_fusion.1
  555.9 11.8 convolution_convert_fusion.1
  581.6 19.0 convolution_convert_fusion
  609.4 87.3 %all-to-all-done.1 = bf16[4,320,2048]{2,0,1:T(4,128)(2,1)} async-done(((bf16[4,320,2048]{2,0,1:T(4,128)(2,1)}), bf16[4,320,2048]{2,0,1:T(4,128)(2,1)}, u32[]{:S(2)}, u32[]{:S(2)}) %all-to-all-start.1) | async-done | bytes 5242912 | tf_op jit(solution)/shard_map/all_to_all | solution.py:153
  701.9 15.6 convert_bitcast_fusion.1
  717.5 24.5 convert_bitcast_fusion
  749.8 12.2 gather_fusion.1
  767.1 49.9 %all-to-all-done.3 = bf16[4,320,2048]{2,0,1:T(4,128)(2,1)} async-done(((bf16[4,320,2048]{2,0,1:T(4,128)(2,1)}), bf16[4,320,2048]{2,0,1:T(4,128)(2,1)}, u32[]{:S(2)}, u32[]{:S(2)}) %all-to-all-start.3) | async-done | bytes 5242912 | tf_op jit(solution)/shard_map/all_to_all | solution.py:204
  824.7 12.2 gather_fusion.2
  871.2 14.7 fusion.22
  888.9 46.0 %pad_maximum_fusion.1 = bf16[2048,4,3072]{0,2,1:T(8,128)(2,1)} fusion(bf16[2048,4,1024]{0,2,1:T(8,128)(2,1)} %convert_bitcast_fusion.1, bf16[2048,4,2048]{0,2,1:T(8,128)(2,1)} %convert_bitcast_fusion), kind=kLoop, calls=%fused_computation.8 | loop fusion | flops 100663296 | bytes 100663296 | tf_op jit(solution)/shard_map/concatenate | solution.py:210
  944.2 20.9 fusion.31
  965.1 43.9 %pad_maximum_fusion = f32[2048,8192]{1,0:T(8,128)} fusion(f32[2048,2048]{1,0:T(8,128)} %fusion.39, f32[2048,6144]{1,0:T(8,128)} %fusion.31), kind=kLoop, calls=%fused_computation.7 | loop fusion | flops 16777216 | bytes 134217728 | tf_op jit(solution)/shard_map/concatenate | solution.py:261
  1021.9 133.3 %reduce-scatter.15.cloned.1.call-done = f32[64,16]{1,0:T(8,128)} async-done(((f32[2048,16]{1,0:T(8,128)}), f32[64,16]{1,0:T(8,128)}) %reduce-scatter.15.cloned.1.call-update) | async-done | bytes 4112
  1156.6 285.5 %reduce-scatter.11.cloned.1.call-done = bf16[256,4,3072]{0,2,1:T(8,128)(2,1)} async-done(((bf16[2048,4,3072]{0,2,1:T(8,128)(2,1)}), bf16[256,4,3072]{0,2,1:T(8,128)(2,1)}) %reduce-scatter.11.cloned.1.call-update) | async-done | bytes 6291472 | tf_op jit(solution)/shard_map/reduce_scatter | solution.py:209
  1457.8 10.4 copy.259
  1468.2 1386.2 %reduce-scatter.9.cloned.1.call-done = f32[64,8192]{1,0:T(8,128)} async-done(((f32[2048,8192]{1,0:T(8,128)}), f32[64,8192]{1,0:T(8,128)}) %reduce-scatter.9.cloned.1.call-update) | async-done | bytes 2097168 | tf_op jit(solution)/shard_map/reduce_scatter | solution.py:260
  (271 shorter events, 221.4 us)
Async XLA Ops:
  7.2 78.4 %copy-start = (s32[64]{0:T(128)S(1)}, s32[64]{0:T(128)}, u32[]{:S(2)}) copy-start(s32[64]{0:T(128)} %param.12) | copy-start | bytes 772
  7.2 160.4 %all-gather.7.cloned.1.call-start = ((), (), s32[]{:S(2)}) async-start(), calls=%async_computation.8 | async-start | bytes 25952256 | tf_op jit(solution)/shard_map/all_gather | solution.py:76
  7.9 238.7 %all-gather.9.cloned.1.call-start = ((), (), s32[]{:S(2)}) async-start(), calls=%async_computation.9 | async-start | bytes 8650752 | tf_op jit(solution)/shard_map/all_gather | solution.py:77
  8.7 510.3 %all-gather.11.cloned.1.call-start = ((), (), s32[]{:S(2)}) async-start(), calls=%async_computation.10 | async-start | bytes 37748736 | tf_op jit(solution)/shard_map/all_gather | solution.py:141
  15.4 76.7 %copy-start.58 = (bf16[64,16]{0,1:T(8,128)(2,1)S(1)}, bf16[64,16]{0,1:T(8,128)(2,1)}, u32[]{:S(2)}) copy-start(bf16[64,16]{0,1:T(8,128)(2,1)} %param.18) | copy-start | bytes 6148
  15.4 144.5 %copy-start.16 = (bf16[128,2048]{1,0:T(8,128)(2,1)S(1)}, bf16[128,2048]{1,0:T(8,128)(2,1)}, u32[]{:S(2)}) copy-start(bf16[128,2048]{1,0:T(8,128)(2,1)} %param.21) | copy-start | bytes 1572868
  15.4 145.9 %copy-start.8 = (bf16[128,2048]{1,0:T(8,128)(2,1)S(1)}, bf16[128,2048]{1,0:T(8,128)(2,1)}, u32[]{:S(2)}) copy-start(bf16[128,2048]{1,0:T(8,128)(2,1)} %param.11) | copy-start | bytes 1572868
  15.4 524.4 %all-gather.13.cloned.1.call-start = ((), (), s32[]{:S(2)}) async-start(), calls=%async_computation.11 | async-start | bytes 18874368 | tf_op jit(solution)/shard_map/all_gather | solution.py:142
  159.9 92.9 %copy-start.31 = (bf16[2048,16]{0,1:T(8,128)(2,1)}, bf16[2048,16]{0,1:T(8,128)(2,1)S(1)}, u32[]{:S(2)}) copy-start(bf16[2048,16]{0,1:T(8,128)(2,1)S(1)} %reshape.467) | copy-start | bytes 196612
  162.1 24.7 copy-start.47
  162.4 18.3 copy-start.25
  162.5 18.3 copy-start.27
  162.5 89.2 %copy-start.35 = (f32[2048,1]{0,1:T(1,128)}, f32[2048,1]{0,1:T(1,128)S(1)}, u32[]{:S(2)}) copy-start(f32[2048,1]{0,1:T(1,128)S(1)} %get-tuple-element.97) | copy-start | bytes 24580
  186.8 64.9 %copy-start.50 = (f32[16,128]{1,0:T(8,128)}, f32[16,128]{1,0:T(8,128)S(1)}, u32[]{:S(2)}) copy-start(f32[16,128]{1,0:T(8,128)S(1)} %get-tuple-element.103) | copy-start | bytes 24580
  252.8 23.3 copy-start.11
  271.0 121.5 %all-to-all-start.2 = ((bf16[16,80,2048]{2,1,0:T(8,128)(2,1)}), bf16[16,80,2048]{2,1,0:T(8,128)(2,1)}, u32[]{:S(2)}, u32[]{:S(2)}) async-start(bf16[16,80,2048]{2,1,0:T(8,128)(2,1)} %bitcast.170), calls=%async_computation.2 | async-start | bytes 10485760 | tf_op jit(solution)/shard_map/all_to_all | solution.py:187
  392.4 120.8 %all-to-all-start = ((bf16[16,80,2048]{2,1,0:T(8,128)(2,1)}), bf16[16,80,2048]{2,1,0:T(8,128)(2,1)}, u32[]{:S(2)}, u32[]{:S(2)}) async-start(bf16[16,80,2048]{2,1,0:T(8,128)(2,1)} %bitcast.169), calls=%async_computation | async-start | bytes 10485760 | tf_op jit(solution)/shard_map/all_to_all | solution.py:133
  576.6 120.2 %all-to-all-start.1 = ((bf16[4,320,2048]{2,0,1:T(4,128)(2,1)}), bf16[4,320,2048]{2,0,1:T(4,128)(2,1)}, u32[]{:S(2)}, u32[]{:S(2)}) async-start(bf16[4,320,2048]{2,0,1:T(4,128)(2,1)} %copy.237), calls=%async_computation.1 | async-start | bytes 10485760 | tf_op jit(solution)/shard_map/all_to_all | solution.py:153
  696.8 120.2 %all-to-all-start.3 = ((bf16[4,320,2048]{2,0,1:T(4,128)(2,1)}), bf16[4,320,2048]{2,0,1:T(4,128)(2,1)}, u32[]{:S(2)}, u32[]{:S(2)}) async-start(bf16[4,320,2048]{2,0,1:T(4,128)(2,1)} %copy.243), calls=%async_computation.3 | async-start | bytes 10485760 | tf_op jit(solution)/shard_map/all_to_all | solution.py:204
  701.8 318.6 %reduce-scatter.13.cloned.1.call-start = ((), (), s32[]{:S(2)}) async-start(), calls=%async_computation.14 | async-start | bytes 1081344
  887.4 267.8 %reduce-scatter.15.cloned.1.call-start = ((), (), s32[]{:S(2)}) async-start(), calls=%async_computation.15 | async-start | bytes 1081344
  888.8 553.3 %reduce-scatter.11.cloned.1.call-start = ((), (), s32[]{:S(2)}) async-start(), calls=%async_computation.13 | async-start | bytes 56623104 | tf_op jit(solution)/shard_map/reduce_scatter | solution.py:209
  934.9 1919.5 %reduce-scatter.9.cloned.1.call-start = ((), (), s32[]{:S(2)}) async-start(), calls=%async_computation.12 | async-start | bytes 69206016 | tf_op jit(solution)/shard_map/reduce_scatter | solution.py:260
  1457.8 1401.1 %copy-start.1 = (s32[64]{0:T(128)S(1)}, s32[64]{0:T(128)}, u32[]{:S(2)}) copy-start(s32[64]{0:T(128)} %param.12) | copy-start | bytes 772
  (57 other events, 327.8 us)
Sparse Core Ops, SparseCore 0:
  10.9 156.6 all-gather.6
  170.5 76.1 all-gather.8
  249.1 158.2 all-gather.10
  409.2 90.2 all-gather.12
  887.5 132.8 reduce-scatter.12
  1023.2 131.9 reduce-scatter.14
  1158.8 283.2 reduce-scatter.10
  1444.6 1409.7 reduce-scatter.8
where the time goes:
time: 2870 us
  waiting for transfers between devices  2230 us (78%)
  matrix products  191 us (7%)
  local copies, waits for them, and re-layouts  143 us (5%)
  blocking collectives  136 us (5%)
  other arithmetic  130 us (5%)
    reduce_scatter x1, waiting for transfers between devices, on_device(): lax.psum_scatter(jnp.concatenate([first_term, second_term], axis=1), ('dp...  1390 us
    reduce_scatter x1, waiting for transfers between devices, on_device(): lax.psum_scatter(jnp.concatenate([first_term, second_term], axis=2).astyp...  285 us
    unnamed x10, waiting for transfers between devices  144 us
    all_to_all x1, waiting for transfers between devices, on_device(): lax.all_to_all(outgoing.reshape(expert_count, capacity, model_width), 'ex...  110 us
    all_to_all x1, waiting for transfers between devices, on_device(): lax.all_to_all(outgoing_grad.reshape(expert_count, capacity, model_width)...  107 us
    all_to_all x1, waiting for transfers between devices, on_device(): lax.all_to_all(result, 'expert', split_axis=1, concat_axis=0, tiled=True)  87.3 us
    all_gather x1, blocking collectives, on_device(): lax.all_gather(norm_gains, ('dp', 'expert'), axis=0, tiled=True)  68 us
    all_gather x1, blocking collectives, on_device(): lax.all_gather(router, ('dp', 'expert'), axis=0, tiled=True)  67.6 us
  transfers between devices with their start and end apart: 12, of which 10 were waited for; matrix products, arithmetic and copies ran while one was open for 12% of the time, Pallas kernels for 0%

commit v1 on v0

v1 whole, which is shorter than its diff:
```python
import jax
import jax.numpy as jnp
from jax import lax
from jax.sharding import PartitionSpec as P

HEADS = 16
HEAD_DIM = 128
SEQ_DEV = 2
EPSILON = 1e-06
ROPE_BASE = 50000.0
EXTRA = 128

F32 = jnp.float32
BF16 = jnp.bfloat16


def dot(a, b, dims, out=F32):
    return lax.dot_general(a, b, (dims, ((), ())), preferred_element_type=F32).astype(out)


def nn(a, b, out=F32):
    return dot(a, b, ((1,), (0,)), out)


def nt(a, b, out=F32):
    return dot(a, b, ((1,), (1,)), out)


def tn(a, b, out=F32):
    return dot(a, b, ((0,), (0,)), out)


def flip(v, bit):
    return lax.ppermute(v, "dp", [(i, i ^ bit) for i in range(lax.axis_size("dp"))])


def shift(v, step):
    n = lax.axis_size("expert")
    return lax.ppermute(v, "expert", [(i, i + step) for i in range(n) if 0 <= i + step < n])


def gather_line(v):
    n = lax.axis_size("expert")
    rows = v.shape[0]
    below, above = [v], [v]
    for _ in range(n - 1):
        below.append(shift(below[-1], 1))
        above.append(shift(above[-1], -1))
    line = jnp.concatenate(below[:0:-1] + above, axis=0)
    start = (n - 1 - lax.axis_index("expert")) * rows
    return lax.dynamic_slice_in_dim(line, start, n * rows, axis=0)


def bits_of(low, high):
    out = []
    while low < high:
        out.append(low)
        low *= 2
    return out


def pick(v, index, axis):
    return lax.dynamic_index_in_dim(v, index, axis, keepdims=False)


def spread(w):
    rows, local, k = w.shape
    n = lax.axis_size("dp")
    me = lax.axis_index("dp")
    own = lax.rem(me, local)
    have = {(0, e): pick(w, own ^ e, 1) for e in range(local)}
    groups = []
    for bit in bits_of(1, local):
        keys = sorted(key for key in have if key[1] & bit)
        got = flip(jnp.stack([have.pop(key) for key in keys]), bit)
        for at, key in enumerate(keys):
            have[(key[0] ^ bit, key[1] ^ bit)] = got[at]
    rows_of = {key[0]: v for key, v in have.items()}
    for bit in bits_of(local, n):
        for half in (0, 1):
            keys = sorted(r for r in rows_of if r < bit and (r & (local // 2) > 0) == (half == 1))
            got = flip(jnp.stack([rows_of[r] for r in keys]), bit)
            for at, r in enumerate(keys):
                rows_of[r ^ bit] = got[at]
    full = jnp.zeros((n, rows, k), w.dtype)
    for r, v in rows_of.items():
        full = lax.dynamic_update_index_in_dim(full, v, me ^ r, 0)
    return full.reshape(n * rows, k)


def collect(g, local):
    n = lax.axis_size("dp")
    me = lax.axis_index("dp")
    own = lax.rem(me, local)
    rows, k = g.shape[0] // n, g.shape[1]
    g = g.reshape(n, rows, k)
    held = {r: pick(g, me ^ r, 0) for r in range(n)}
    for bit in reversed(bits_of(local, n)):
        keys = sorted(r for r in held if r & bit)
        got = flip(jnp.stack([held.pop(r) for r in keys]), bit)
        for at, r in enumerate(keys):
            held[r ^ bit] = (held[r ^ bit].astype(F32) + got[at].astype(F32)).astype(BF16)
    have = {(r, 0): v for r, v in held.items()}
    for bit in reversed(bits_of(1, local)):
        keys = sorted(key for key in have if key[0] & bit)
        got = flip(jnp.stack([have.pop(key) for key in keys]), bit)
        for at, key in enumerate(keys):
            have[(key[0] ^ bit, key[1] ^ bit)] = got[at]
    stacked = jnp.stack([have[(0, e)] for e in range(local)])
    return jnp.stack([pick(stacked, own ^ e, 0) for e in range(local)], axis=1).astype(F32)


def share(v, local):
    for bit in reversed(bits_of(1, local)):
        v = jnp.concatenate([v, flip(v, bit)], axis=0)
    return v


def unshare(v, local):
    for bit in bits_of(1, local):
        half = v.shape[0] // 2
        v = (v[:half].astype(F32) + flip(v[half:], bit).astype(F32)).astype(BF16)
    return v


def inv_rms(v):
    return lax.rsqrt(jnp.mean(v * v, axis=-1, keepdims=True) + EPSILON)


def rms_back(v, r, gain, c):
    gc = gain * c
    return r * gc - v * (r * r * r) * jnp.mean(v * gc, axis=-1, keepdims=True)


def rotate(v, cos, sin):
    half = v.shape[-1] // 2
    u, w = v[..., :half], v[..., half:]
    return jnp.concatenate([u * cos - w * sin, w * cos + u * sin], axis=-1)


def on_device(
    tokens,
    lengths,
    permutation,
    routes,
    norm_gains,
    w_qkv,
    w_out,
    router,
    w_gate_up,
    w_down,
    cotangent,
):
    rows, width = tokens.shape
    zs = lax.axis_size("expert")
    dps = lax.axis_size("dp")
    z = lax.axis_index("expert")
    dp = lax.axis_index("dp")
    local = w_gate_up.shape[1]
    ff = w_down.shape[2]
    experts = router.shape[1]
    own_rows = w_qkv.shape[0]
    cols = width // zs
    heads = HEADS // zs
    scale = HEAD_DIM ** (-0.5)
    expert = z * local + lax.rem(dp, local)

    extra = jnp.concatenate(
        [router, norm_gains, jnp.zeros((own_rows, EXTRA - experts - 4), BF16)], axis=1
    )
    parts = w_qkv.reshape(own_rows, 3, zs, cols)
    sent = jnp.stack(
        [
            jnp.concatenate([parts[:, i, e] for i in range(3)] + [extra], axis=1)
            for e in range(zs)
        ]
    )
    mine = lax.all_to_all(sent, "expert", split_axis=0, concat_axis=0, tiled=True)
    attn_w = lax.all_gather(
        mine.reshape(zs * own_rows, 3 * cols + EXTRA), "dp", axis=0, tiled=True
    )
    qkv_w = attn_w[:, : 3 * cols]
    router_full = attn_w[:, 3 * cols : 3 * cols + experts]
    gains = attn_w[:, 3 * cols + experts : 3 * cols + experts + 4].astype(F32).T
    moved = [(b, (b % dps) * zs + b // dps) for b in range(dps * zs)]
    out_w = lax.all_gather(
        lax.ppermute(w_out, ("dp", "expert"), moved), "dp", axis=0, tiled=True
    )

    x_all = gather_line(tokens)
    mask = jnp.sum(
        (routes[:, :, None] == jnp.arange(experts, dtype=jnp.int32)).astype(BF16), axis=1
    )
    mask_pad = jnp.concatenate([mask, jnp.zeros((rows, EXTRA - experts), BF16)], axis=1)
    g_line = gather_line(jnp.concatenate([cotangent, mask_pad], axis=1))
    w_gu = spread(w_gate_up)
    w_dn = spread(w_down)
    g_share = share(g_line, local)
    g_all = g_share[:, :width]
    mask_all = g_share[:, width : width + experts].astype(F32)

    dealt = lax.dynamic_slice_in_dim(permutation, dp * zs * SEQ_DEV, zs * SEQ_DEV)
    lens = jnp.take(lengths, dealt).reshape(zs, SEQ_DEV)
    ends = jnp.cumsum(lens, axis=1)
    places = jnp.arange(rows, dtype=jnp.int32)
    segment = jnp.sum((places[None, :, None] >= ends[:, None, :]).astype(jnp.int32), axis=2)
    starts = ends - lens
    offset = jnp.sum(
        jnp.where(
            segment[:, :, None] == jnp.arange(SEQ_DEV, dtype=jnp.int32), starts[:, None, :], 0
        ),
        axis=2,
    )
    half = HEAD_DIM // 2
    inverse = ROPE_BASE ** (-2.0 * jnp.arange(half, dtype=F32) / HEAD_DIM)
    turned = (places[None] - offset).astype(F32)[..., None] * inverse
    cos, sin = jnp.cos(turned)[:, :, None, :], jnp.sin(turned)[:, :, None, :]
    same = (segment[:, :, None] == segment[:, None, :])[:, None]

    xf = x_all.astype(F32)
    r_attn = inv_rms(xf)
    a_all = (xf * r_attn * gains[0]).astype(BF16)
    qkv = nn(a_all, qkv_w)
    q, k, v = qkv[:, :cols], qkv[:, cols : 2 * cols], qkv[:, 2 * cols :]
    squares = lax.psum(
        jnp.stack([jnp.sum(q * q, axis=1), jnp.sum(k * k, axis=1)]), "expert"
    )
    r_q = lax.rsqrt(squares[0] / width + EPSILON)[:, None]
    r_k = lax.rsqrt(squares[1] / width + EPSILON)[:, None]
    gain_q = lax.dynamic_slice_in_dim(gains[1], z * cols, cols)
    gain_k = lax.dynamic_slice_in_dim(gains[2], z * cols, cols)
    split = (zs, rows, heads, HEAD_DIM)
    qr = rotate((q * r_q * gain_q).reshape(split), cos, sin).astype(BF16)
    kr = rotate((k * r_k * gain_k).reshape(split), cos, sin).astype(BF16)
    vb = v.astype(BF16).reshape(split)
    s = jnp.einsum("bthd,bshd->bhts", qr, kr, preferred_element_type=F32) * scale
    s = jnp.where(same, s, -1e30)
    es = jnp.exp(s - jnp.max(s, axis=3, keepdims=True))
    p = es / jnp.sum(es, axis=3, keepdims=True)
    pb = p.astype(BF16)
    o = (
        jnp.einsum("bhts,bshd->bthd", pb, vb, preferred_element_type=F32)
        .reshape(zs * rows, cols)
        .astype(BF16)
    )
    added = lax.psum_scatter(
        nn(o, out_w, BF16), "expert", scatter_dimension=0, tiled=True
    ).astype(F32)
    hid = tokens.astype(F32) + added
    r_ffn = inv_rms(hid)
    m = (hid * r_ffn * gains[3]).astype(BF16)
    m_line = lax.all_gather(m, "expert", axis=0, tiled=True)
    m_all = share(m_line, local)

    def gates(rows_m, rows_mask):
        logits = jnp.where(rows_mask > 0, nn(rows_m, router_full), -1e30)
        e = jnp.where(
            rows_mask > 0, jnp.exp(logits - jnp.max(logits, axis=1, keepdims=True)), 0.0
        )
        return e / jnp.sum(e, axis=1, keepdims=True)

    mine_e = (jnp.arange(experts) == expert).astype(F32)
    gate = jnp.sum(gates(m_all, mask_all) * mine_e, axis=1, keepdims=True)
    gw = nn(g_all, w_dn)
    gu = nn(m_all, w_gu)
    g, u = gu[:, :ff], gu[:, ff:]
    sg = jax.nn.sigmoid(g)
    act = (g * sg * u).astype(BF16).astype(F32)
    gact = (gate * act).astype(BF16)
    dgate = jnp.sum(act * gw, axis=1, keepdims=True)
    dact = gate * gw
    dgu = jnp.concatenate(
        [dact * u * (sg * (1.0 + g * (1.0 - sg))), dact * (g * sg)], axis=1
    ).astype(BF16)
    dg_e = jnp.where(gate > 0, dgate, 0.0) * mine_e
    dg_hi = dg_e.astype(BF16)
    dg_lo = (dg_e - dg_hi.astype(F32)).astype(BF16)
    dg_pad = jnp.concatenate(
        [dg_hi, dg_lo, jnp.zeros((dg_e.shape[0], EXTRA - 2 * experts), BF16)], axis=1
    )
    dm_part = jnp.concatenate([nt(dgu, w_gu, BF16), dg_pad], axis=1)
    dm = lax.psum_scatter(
        unshare(dm_part, local), "expert", scatter_dimension=0, tiled=True
    ).astype(F32)
    y = lax.psum_scatter(
        unshare(nt(gact, w_dn, BF16), local), "expert", scatter_dimension=0, tiled=True
    ).astype(F32)
    output = hid + y
    grad_gu = collect(tn(m_all, dgu, BF16), local)
    grad_dn = collect(tn(g_all, gact, BF16), local)

    gate_own = gates(m, mask.astype(F32))
    dgates = dm[:, width : width + experts] + dm[:, width + experts : width + 2 * experts]
    dz = (
        gate_own * (dgates - jnp.sum(gate_own * dgates, axis=1, keepdims=True))
    ).astype(BF16)
    dmt = nt(dz, router_full) + dm[:, :width]
    router_part = tn(m, dz)
    grad_out = cotangent.astype(F32)
    dh = grad_out + rms_back(hid, r_ffn, gains[3], dmt)
    gain_ffn = jnp.sum(dmt * hid * r_ffn, axis=0)

    dhb = lax.all_gather(dh.astype(BF16), "expert", axis=0, tiled=True)
    do = nt(dhb, out_w, BF16).reshape(split)
    grad_out_w = lax.psum_scatter(
        tn(o, dhb, BF16), "dp", scatter_dimension=0, tiled=True
    )
    grad_w_out = lax.ppermute(
        grad_out_w, ("dp", "expert"), [(b, a) for a, b in moved]
    ).astype(F32)
    dp_ = jnp.einsum("bthd,bshd->bhts", do, vb, preferred_element_type=F32)
    dv = jnp.einsum("bhts,bthd->bshd", pb, do, preferred_element_type=F32)
    ds = (p * (dp_ - jnp.sum(p * dp_, axis=3, keepdims=True))).astype(BF16)
    dqr = jnp.einsum("bhts,bshd->bthd", ds, kr, preferred_element_type=F32) * scale
    dkr = jnp.einsum("bhts,bthd->bshd", ds, qr, preferred_element_type=F32) * scale
    dqn = rotate(dqr, cos, -sin).reshape(zs * rows, cols)
    dkn = rotate(dkr, cos, -sin).reshape(zs * rows, cols)
    means = lax.psum(
        jnp.stack(
            [jnp.sum(q * (gain_q * dqn), axis=1), jnp.sum(k * (gain_k * dkn), axis=1)]
        ),
        "expert",
    )
    dq = r_q * gain_q * dqn - q * (r_q * r_q * r_q) * (means[0] / width)[:, None]
    dk = r_k * gain_k * dkn - k * (r_k * r_k * r_k) * (means[1] / width)[:, None]
    dqkv = jnp.concatenate([dq, dk, dv.reshape(zs * rows, cols)], axis=1).astype(BF16)
    da_part = nt(dqkv, qkv_w)
    da = lax.psum_scatter(
        da_part.astype(BF16), "expert", scatter_dimension=0, tiled=True
    ).astype(F32)
    gain_attn = jnp.sum(da_part * (xf * r_attn), axis=0)
    at = z * cols
    zero = jnp.zeros((width,), F32)
    gain_query = lax.dynamic_update_slice_in_dim(zero, jnp.sum(dqn * q * r_q, axis=0), at, 0)
    gain_keys = lax.dynamic_update_slice_in_dim(zero, jnp.sum(dkn * k * r_k, axis=0), at, 0)
    gain_part = jnp.stack([gain_attn, gain_query, gain_keys, gain_ffn], axis=1)
    extra_part = jnp.concatenate(
        [router_part, gain_part, jnp.zeros((width, EXTRA - experts - 4), F32)], axis=1
    ).astype(BF16)
    qkv_part = jnp.concatenate([tn(a_all, dqkv, BF16), extra_part], axis=1)
    summed = lax.psum_scatter(qkv_part, "dp", scatter_dimension=0, tiled=True)
    back = lax.all_to_all(
        summed.reshape(zs, own_rows, 3 * cols + EXTRA),
        "expert",
        split_axis=0,
        concat_axis=0,
        tiled=True,
    ).astype(F32)
    grad_w_qkv = jnp.concatenate(
        [back[e, :, i * cols : (i + 1) * cols] for i in range(3) for e in range(zs)], axis=1
    )
    extra_sum = jnp.sum(back[:, :, 3 * cols :], axis=0)
    grad_router = extra_sum[:, :experts]
    grad_gains = extra_sum[:, experts : experts + 4]

    x_own = tokens.astype(F32)
    grad_tokens = dh + rms_back(x_own, inv_rms(x_own), gains[0], da)
    return (
        output,
        grad_tokens,
        grad_gains,
        grad_w_qkv,
        grad_w_out,
        grad_router,
        grad_gu,
        grad_dn,
    )


def solution(mesh):
    both = P(("dp", "expert"), None)
    experts = P("dp", "expert", None)
    return jax.shard_map(
        on_device,
        mesh=mesh,
        in_specs=(both, P(), P(), both, both, both, both, both, experts, experts, both),
        out_specs=(both, both, both, both, both, both, experts, experts),
        check_vma=False,
    )
```

time: 2870 us -> 1190 us (0.41)
  waiting for transfers between devices: 2230 us -> 610 us
  blocking collectives: 136 us -> 47.9 us
  other arithmetic: 130 us -> 69.8 us
  starting transfers between devices: 20.7 us -> 75.5 us
  local copies, waits for them, and re-layouts: 143 us -> 182 us
    reduce_scatter x2 -> x6, waiting for transfers between devices: 1670 us -> 57.2 us  [the longest x1 44.7 us: on_device(): lax.psum_scatter(unshare(dm_part, local), 'expert', scatter_dimension=0,...]
    ppermute x0 -> x36, waiting for transfers between devices: none -> 475 us  [the longest x22 423 us: flip(): lax.ppermute(v, 'dp', [(i, i ^ bit) for i in range(lax.axis_size('dp'))])]
    all_to_all x4 -> x1, waiting for transfers between devices: 354 us -> 5.82 us  [on_device(): lax.all_to_all(summed.reshape(zs, own_rows, 3 * cols + EXTRA), 'expert',...]
    unnamed x10, waiting for transfers between devices: 144 us -> 0.17 us
    all_gather x2 -> x0, blocking collectives: 136 us -> none  [the longest x1 68 us: on_device(): lax.all_gather(norm_gains, ('dp', 'expert'), axis=0, tiled=True)]
    concatenate x2 -> x5, other arithmetic: 89.9 us -> 6.53 us  [the longest x2 4.7 us: share(): v = jnp.concatenate([v, flip(v, bit)], axis=0)]
    ppermute x0 -> x36, starting transfers between devices: none -> 69.5 us  [the longest x12 47.5 us: shift(): lax.ppermute(v, 'expert', [(i, i + step) for i in range(n) if 0 <= i + st...]
    concatenate x0 -> x13, local copies, waits for them, and re-layouts: none -> 49.8 us  [the longest x1 30.6 us: on_device(): qkv_part = jnp.concatenate([tn(a_all, dqkv, BF16), extra_part], axis=1)]
  transfers between devices with their start and end apart: 12 -> 47, of which waited for: 10 -> 24; matrix products, arithmetic and copies ran while one was open for 12% -> 24% of each run, Pallas kernels for 0% -> 0%
where the time goes in v1:
time: 1190 us; the launch traced here: 1180 us
  waiting for transfers between devices  610 us (51%)
  local copies, waits for them, and re-layouts  182 us (15%)
  matrix products  180 us (15%)
  starting transfers between devices  75.5 us (6%)
  other arithmetic  69.8 us (6%)
  blocking collectives  47.9 us (4%)
  between operations  16.2 us (1%)
    ppermute x22, waiting for transfers between devices, flip(): lax.ppermute(v, 'dp', [(i, i ^ bit) for i in range(lax.axis_size('dp'))])  423 us
    dot_general x16, matrix products, dot(): lax.dot_general(a, b, (dims, ((), ())), preferred_element_type=F32)  171 us
    unnamed x212, local copies, waits for them, and re-layouts  54.1 us
    ppermute x12, starting transfers between devices, shift(): lax.ppermute(v, 'expert', [(i, i + step) for i in range(n) if 0 <= i + st...  47.5 us
    all_gather x1, waiting for transfers between devices, on_device(): dhb = lax.all_gather(dh.astype(BF16), 'expert', axis=0, tiled=True)  45.1 us
    reduce_scatter x1, waiting for transfers between devices, on_device(): lax.psum_scatter(unshare(dm_part, local), 'expert', scatter_dimension=0,...  44.7 us
    ppermute x12, waiting for transfers between devices, shift(): lax.ppermute(v, 'expert', [(i, i + step) for i in range(n) if 0 <= i + st...  43.8 us
    concatenate x1, local copies, waits for them, and re-layouts, on_device(): qkv_part = jnp.concatenate([tn(a_all, dqkv, BF16), extra_part], axis=1)  30.6 us
  transfers between devices with their start and end apart: 47, of which 24 were waited for; matrix products, arithmetic and copies ran while one was open for 24% of the time, Pallas kernels for 0%

profile of v1, /device:TPU:4, one launch (start us, length us, event | category | flops | bytes accessed | tf_op | source)
XLA Modules:
  0.0 1181.7 jit_solution(3023432941699135444)
XLA Ops:
  12.1 26.2 %all_to_all.10 = bf16[4,64,1664]{2,1,0:T(8,128)(2,1)S(1)} all-to-all(bf16[4,64,1664]{2,1,0:T(8,128)(2,1)S(1)} %pad_maximum_fusion.26), channel_id=1, replica_groups=mesh['dp'=8,'expert'=4] {'expert'}, dimensions={0} | all-to-all | bytes 1703936 | tf_op jit(solution)/shard_map/all_to_all | solution.py:178
  105.7 12.2 %psum.14 = f32[2,512]{1,0:T(2,128)S(1)} all-reduce(f32[2,512]{1,0:T(2,128)S(1)} %pad_maximum_fusion.39), channel_id=1, replica_groups=mesh['dp'=8,'expert'=4] {'expert'}, use_global_device_ids=true, to_apply=%region_5.6 | all-reduce | flops 1024 | bytes 8192 | tf_op jit(solution)/shard_map/psum | solution.py:225
  147.3 10.2 collective-permute-done.7
  242.0 25.7 %all-gather.9.cloned.1.call-done = bf16[512,2048]{1,0:T(8,128)(2,1)} async-done(((bf16[128,2048]{1,0:T(8,128)(2,1)}), bf16[512,2048]{1,0:T(8,128)(2,1)}) %all-gather.9.cloned.1.call-update) | async-done | bytes 2097168 | tf_op jit(solution)/shard_map/all_gather | solution.py:252
  272.9 32.7 %collective-permute-done.22 = bf16[2,256,1024]{2,1,0:T(8,128)(2,1)} collective-permute-done((bf16[2,256,1024]{2,1,0:T(8,128)(2,1)}, bf16[2,256,1024]{2,1,0:T(8,128)(2,1)}, u32[]{:S(2)}, u32[]{:S(2)}) %collective-permute-start.22) | collective-permute-done | bytes 1048608 | tf_op jit(solution)/shard_map/ppermute | solution.py:34
  317.9 32.5 %collective-permute-done.15 = bf16[512,2048]{1,0:T(8,128)(2,1)S(1)} collective-permute-done((bf16[512,2048]{1,0:T(8,128)(2,1)}, bf16[512,2048]{1,0:T(8,128)(2,1)S(1)}, u32[]{:S(2)}, u32[]{:S(2)}) %collective-permute-start.15) | collective-permute-done | bytes 2097184 | tf_op jit(solution)/shard_map/ppermute | solution.py:34
  354.6 39.8 %collective-permute-done.18 = bf16[2,256,2048]{2,1,0:T(8,128)(2,1)S(1)} collective-permute-done((bf16[2,256,2048]{2,1,0:T(8,128)(2,1)S(1)}, bf16[2,256,2048]{2,1,0:T(8,128)(2,1)S(1)}, u32[]{:S(2)}, u32[]{:S(2)}) %collective-permute-start.18) | collective-permute-done | bytes 2097184 | tf_op jit(solution)/shard_map/ppermute | solution.py:34
  400.5 40.7 %collective-permute-done.20 = bf16[2,256,2048]{2,1,0:T(8,128)(2,1)S(1)} collective-permute-done((bf16[2,256,2048]{2,1,0:T(8,128)(2,1)S(1)}, bf16[2,256,2048]{2,1,0:T(8,128)(2,1)S(1)}, u32[]{:S(2)}, u32[]{:S(2)}) %collective-permute-start.20) | collective-permute-done | bytes 2097184 | tf_op jit(solution)/shard_map/ppermute | solution.py:34
  446.2 24.5 %fusion.110 = f32[2048,2048]{0,1:T(8,128)} fusion(bf16[2048,2048]{1,0:T(8,128)(2,1)S(1)} %constant_dynamic-update-slice_fusion.14, bf16[2048,2048]{1,0:T(8,128)(2,1)} %bitcast.216), kind=kOutput, calls=%fused_computation.339 | convolution fusion | flops 17179869184 | bytes 33554432 | tf_op jit(solution)/shard_map/dot_general | solution.py:18
  474.0 29.8 %multiply_convert_fusion.1 = (bf16[2048,1024]{0,1:T(8,128)(2,1)}, bf16[2048,1024]{0,1:T(8,128)(2,1)}, f32[2048]{0:T(1024)S(1)}, bf16[2048,1024]{0,1:T(8,128)(2,1)}) fusion(f32[2048,2048]{0,1:T(8,128)} %fusion.110, f32[2048]{0:T(1024)S(1)} %multiply_reduce_fusion.6, bf16[2048,1024]{1,0:T(8,128)(2,1)} %bitcast.24, bf16[1024,2176]{0,1:T(8,128)(2,1)} %copy-done.25, ...), kind=kOutput, calls=%fused_computation.11 | convolution fusion | flops 8654944256 | bytes 42483712 | tf_op jit(solution)/shard_map/dot_general | solution.py:18
  504.4 23.7 %convolution_convert_fusion.2 = bf16[2048,2048]{1,0:T(8,128)(2,1)} fusion(bf16[2048,2048]{1,0:T(8,128)(2,1)} %bitcast.217, bf16[2048,1024]{0,1:T(8,128)(2,1)} %get-tuple-element.154, bf16[2048,1024]{0,1:T(8,128)(2,1)} %get-tuple-element.153), kind=kOutput, calls=%fused_computation.18 | convolution fusion | flops 17200840704 | bytes 25165824 | tf_op jit(solution)/shard_map/dot_general | solution.py:18
  528.2 14.2 %concatenate.88 = bf16[2048,2176]{1,0:T(8,128)(2,1)} concatenate(bf16[2048,2048]{1,0:T(8,128)(2,1)} %convolution_convert_fusion.2, bf16[2048,16]{1,0:T(8,128)(2,1)S(1)} %copy.814, bf16[2048,16]{1,0:T(8,128)(2,1)S(1)} %copy.815, bf16[2048,96]{1,0:T(8,128)(2,1)S(1)} %broadcast_in_dim.136), dimensions={1} | concatenate | bytes 17825792 | tf_op jit(solution)/shard_map/concatenate | solution.py:281
  558.0 49.1 %collective-permute-done.28 = bf16[512,2176]{1,0:T(8,128)(2,1)S(1)} collective-permute-done((bf16[512,2176]{1,0:T(8,128)(2,1)S(1)}, bf16[512,2176]{1,0:T(8,128)(2,1)S(1)}, u32[]{:S(2)}, u32[]{:S(2)}) %collective-permute-start.28) | collective-permute-done | bytes 2228256 | tf_op jit(solution)/shard_map/ppermute | solution.py:34
  610.6 44.7 %reduce-scatter.11.cloned.1.call-done = bf16[128,2176]{1,0:T(8,128)(2,1)} async-done(((bf16[512,2176]{1,0:T(8,128)(2,1)}), bf16[128,2176]{1,0:T(8,128)(2,1)}) %reduce-scatter.11.cloned.1.call-update) | async-done | bytes 557072 | tf_op jit(solution)/shard_map/reduce_scatter | solution.py:282
  661.4 45.1 %all-gather.11.cloned.1.call-done = bf16[512,2048]{1,0:T(8,128)(2,1)} async-done(((bf16[128,2048]{1,0:T(8,128)(2,1)}), bf16[512,2048]{1,0:T(8,128)(2,1)}) %all-gather.11.cloned.1.call-update) | async-done | bytes 2097168 | tf_op jit(solution)/shard_map/all_gather | solution.py:303
  758.8 30.6 %concatenate.92 = bf16[2048,1664]{0,1:T(8,128)(2,1)} concatenate(bf16[2048,1536]{0,1:T(8,128)(2,1)} %convolution_convert_fusion.1, bf16[2048,16]{0,1:T(8,128)(2,1)S(1)} %convolution_convert_fusion.7, bf16[2048,1]{0,1:T(2,128)(2,1)S(1)} %stack.180, bf16[2048,1]{0,1:T(2,128)(2,1)S(1)} %constant_dynamic-update-slice_fusion.18, ...), dimensions={1} | concatenate | bytes 13631488 | tf_op jit(solution)/shard_map/concatenate | solution.py:340
  789.7 23.0 %convolution_convert_fusion = bf16[2048,2048]{1,0:T(8,128)(2,1)S(1)} fusion(bf16[2048,2048]{1,0:T(8,128)(2,1)} %copy-done.5, bf16[2048,1024]{0,1:T(8,128)(2,1)} %get-tuple-element.154, bf16[2048,1024]{0,1:T(8,128)(2,1)} %get-tuple-element.153), kind=kOutput, calls=%fused_computation.16 | convolution fusion | flops 17200840704 | bytes 25165824 | tf_op jit(solution)/shard_map/dot_general | solution.py:18
  819.7 11.2 convolution_convert_fusion.3
  836.0 21.6 %convolution_convert_fusion.4 = bf16[2048,1024]{1,0:T(8,128)(2,1)S(1)} fusion(bf16[2048,1024]{0,1:T(8,128)(2,1)} %get-tuple-element.156, f32[2048]{0:T(1024)S(1)} %multiply_reduce_fusion.6, bf16[1024,2176]{0,1:T(8,128)(2,1)S(1)} %bitcast.219, bf16[512,2176]{0,1:T(8,128)(2,1)} %collective-permute-done.13, bf16[512,2176]{0,1:T(8,128)(2,1)S(1)} %copy-done.7), kind=kOutput, calls=%fused_computation.38 | convolution fusion | flops 8623489024 | bytes 17309696 | tf_op jit(solution)/shard_map/dot_general | solution.py:18
  859.0 116.2 %collective-permute-done.33 = bf16[4,256,1024]{2,1,0:T(8,128)(2,1)S(1)} collective-permute-done((bf16[4,256,1024]{2,1,0:T(8,128)(2,1)S(1)}, bf16[4,256,1024]{2,1,0:T(8,128)(2,1)S(1)}, u32[]{:S(2)}, u32[]{:S(2)}) %collective-permute-start.33) | collective-permute-done | bytes 2097184 | tf_op jit(solution)/shard_map/ppermute | solution.py:34
  991.6 61.4 %collective-permute-done.34 = bf16[2,256,1024]{2,1,0:T(8,128)(2,1)S(1)} collective-permute-done((bf16[2,256,1024]{2,1,0:T(8,128)(2,1)S(1)}, bf16[2,256,1024]{2,1,0:T(8,128)(2,1)S(1)}, u32[]{:S(2)}, u32[]{:S(2)}) %collective-permute-start.34) | collective-permute-done | bytes 1048608 | tf_op jit(solution)/shard_map/ppermute | solution.py:34
  1055.8 40.5 %collective-permute-done.26 = bf16[512,2048]{1,0:T(8,128)(2,1)S(1)} collective-permute-done((bf16[512,2048]{1,0:T(8,128)(2,1)S(1)}, bf16[512,2048]{1,0:T(8,128)(2,1)S(1)}, u32[]{:S(2)}, u32[]{:S(2)}) %collective-permute-start.26) | collective-permute-done | bytes 2097184 | tf_op jit(solution)/shard_map/ppermute | solution.py:34
  1126.8 12.3 %copy.832 = f32[256,4,2048]{2,1,0:T(4,128)} copy(f32[256,4,2048]{2,0,1:T(8,128)} %maximum_convert_fusion) | data formatting | bytes 16777216
  1149.7 12.5 %reduce-scatter.9.cloned.1.call-done = bf16[128,2048]{1,0:T(8,128)(2,1)} async-done(((bf16[512,2048]{1,0:T(8,128)(2,1)}), bf16[128,2048]{1,0:T(8,128)(2,1)}) %reduce-scatter.9.cloned.1.call-update) | async-done | bytes 524304 | tf_op jit(solution)/shard_map/reduce_scatter | solution.py:285
  (480 shorter events, 384.8 us)
Async XLA Ops:
  7.2 90.2 %all-gather.5.cloned.1.call-start = ((), (), s32[]{:S(2)}) async-start(), calls=%async_computation.8 | async-start | bytes 7667712 | tf_op jit(solution)/shard_map/all_gather | solution.py:179
  39.5 91.9 %all-gather.7.cloned.1.call-start = ((), (), s32[]{:S(2)}) async-start(), calls=%async_computation.9 | async-start | bytes 2359296 | tf_op jit(solution)/shard_map/all_gather | solution.py:186
  81.1 135.3 %reduce-scatter.7.cloned.1.call-start = ((), (), s32[]{:S(2)}) async-start(), calls=%async_computation.10 | async-start | bytes 2621440 | tf_op jit(solution)/shard_map/reduce_scatter | solution.py:246
  135.9 131.8 %all-gather.9.cloned.1.call-start = ((), (), s32[]{:S(2)}) async-start(), calls=%async_computation.11 | async-start | bytes 2621440 | tf_op jit(solution)/shard_map/all_gather | solution.py:252
  147.3 90.0 %collective-permute-start.21 = (bf16[2,256,1024]{2,1,0:T(8,128)(2,1)}, bf16[2,256,1024]{2,1,0:T(8,128)(2,1)}, u32[]{:S(2)}, u32[]{:S(2)}) collective-permute-start(bf16[2,256,1024]{2,1,0:T(8,128)(2,1)} %pad_maximum_fusion.19), channel_id=1, source_target_pairs={{0,4},{4,0},{8,12},{12,8},{16,20},{20,16},{24,28},{28,24},{1,5},{5... | collective-permute-start | bytes 3145736 | tf_op jit(solution)/shard_map/ppermute | solution.py:34
  199.8 69.4 %collective-permute-start.17 = (bf16[2,256,2048]{2,1,0:T(8,128)(2,1)}, bf16[2,256,2048]{2,1,0:T(8,128)(2,1)}, u32[]{:S(2)}, u32[]{:S(2)}) collective-permute-start(bf16[2,256,2048]{2,1,0:T(8,128)(2,1)} %pad_maximum_fusion.11), channel_id=1, source_target_pairs={{0,4},{4,0},{8,12},{12,8},{16,20},{20,16},{24,28},{28,24},{1,5},{5... | collective-permute-start | bytes 6291464 | tf_op jit(solution)/shard_map/ppermute | solution.py:34
  219.8 435.5 %reduce-scatter.11.cloned.1.call-start = ((), (), s32[]{:S(2)}) async-start(), calls=%async_computation.13 | async-start | bytes 2785280 | tf_op jit(solution)/shard_map/reduce_scatter | solution.py:282
  231.2 76.9 %collective-permute-start.13 = (bf16[512,2176]{0,1:T(8,128)(2,1)S(1)}, bf16[512,2176]{0,1:T(8,128)(2,1)}, u32[]{:S(2)}, u32[]{:S(2)}) collective-permute-start(bf16[512,2176]{0,1:T(8,128)(2,1)S(1)} %constant_dynamic-slice_fusion.16), channel_id=1, source_target_pairs={{0,8},{4,12},{8,0},{12,4},{16,24},{20,28},{24,16},{28,20},{1,9},{5... | collective-permute-start | bytes 6684680 | tf_op jit(solution)/shard_map/ppermute | solution.py:34
  241.8 70.7 %collective-permute-start.23 = (bf16[2,256,1024]{2,1,0:T(8,128)(2,1)}, bf16[2,256,1024]{2,1,0:T(8,128)(2,1)}, u32[]{:S(2)}, u32[]{:S(2)}) collective-permute-start(bf16[2,256,1024]{2,1,0:T(8,128)(2,1)} %pad_maximum_fusion.21), channel_id=1, source_target_pairs={{0,16},{4,20},{8,24},{12,28},{16,0},{20,4},{24,8},{28,12},{1,17},{... | collective-permute-start | bytes 3145736 | tf_op jit(solution)/shard_map/ppermute | solution.py:34
  267.7 82.7 %collective-permute-start.15 = (bf16[512,2048]{1,0:T(8,128)(2,1)}, bf16[512,2048]{1,0:T(8,128)(2,1)S(1)}, u32[]{:S(2)}, u32[]{:S(2)}) collective-permute-start(bf16[512,2048]{1,0:T(8,128)(2,1)} %all-gather.9.cloned.1.call-done), channel_id=1, source_target_pairs={{0,8},{4,12},{8,0},{12,4},{16,24},{20,28},{24,16},{28,20},{1,9},{5... | collective-permute-start | bytes 6291464 | tf_op jit(solution)/shard_map/ppermute | solution.py:34
  272.3 122.2 %collective-permute-start.18 = (bf16[2,256,2048]{2,1,0:T(8,128)(2,1)S(1)}, bf16[2,256,2048]{2,1,0:T(8,128)(2,1)S(1)}, u32[]{:S(2)}, u32[]{:S(2)}) collective-permute-start(bf16[2,256,2048]{2,1,0:T(8,128)(2,1)S(1)} %pad_maximum_fusion.12), channel_id=1, source_target_pairs={{0,8},{4,12},{8,0},{12,4},{16,24},{20,28},{24,16},{28,20},{1,9},{5... | collective-permute-start | bytes 6291464 | tf_op jit(solution)/shard_map/ppermute | solution.py:34
  310.5 132.9 %collective-permute-start.14 = (bf16[1024,2176]{0,1:T(8,128)(2,1)S(1)}, bf16[1024,2176]{0,1:T(8,128)(2,1)S(1)}, u32[]{:S(2)}, u32[]{:S(2)}) collective-permute-start(bf16[1024,2176]{0,1:T(8,128)(2,1)S(1)} %pad_maximum_fusion.5), channel_id=1, source_target_pairs={{0,4},{4,0},{8,12},{12,8},{16,20},{20,16},{24,28},{28,24},{1,5},{5... | collective-permute-start | bytes 13369352 | tf_op jit(solution)/shard_map/ppermute | solution.py:34
  312.5 85.9 %collective-permute-start.19 = (bf16[2,256,2048]{2,1,0:T(8,128)(2,1)S(1)}, bf16[2,256,2048]{2,1,0:T(8,128)(2,1)S(1)}, u32[]{:S(2)}, u32[]{:S(2)}) collective-permute-start(bf16[2,256,2048]{2,1,0:T(8,128)(2,1)S(1)} %pad_maximum_fusion.13), channel_id=1, source_target_pairs={{0,16},{4,20},{8,24},{12,28},{16,0},{20,4},{24,8},{28,12},{1,17},{... | collective-permute-start | bytes 6291464 | tf_op jit(solution)/shard_map/ppermute | solution.py:34
  352.7 93.1 %collective-permute-start.16 = (bf16[1024,2048]{1,0:T(8,128)(2,1)}, bf16[1024,2048]{1,0:T(8,128)(2,1)S(1)}, u32[]{:S(2)}, u32[]{:S(2)}) collective-permute-start(bf16[1024,2048]{1,0:T(8,128)(2,1)} %pad_maximum_fusion.6), channel_id=1, source_target_pairs={{0,4},{4,0},{8,12},{12,8},{16,20},{20,16},{24,28},{28,24},{1,5},{5... | collective-permute-start | bytes 12582920 | tf_op jit(solution)/shard_map/ppermute | solution.py:34
  608.9 97.6 %all-gather.11.cloned.1.call-start = ((), (), s32[]{:S(2)}) async-start(), calls=%async_computation.14 | async-start | bytes 2621440 | tf_op jit(solution)/shard_map/all_gather | solution.py:303
  661.1 450.6 %reduce-scatter.17.cloned.1.call-start = ((), (), s32[]{:S(2)}) async-start(), calls=%async_computation.17 | async-start | bytes 2359296 | tf_op jit(solution)/shard_map/reduce_scatter | solution.py:305
  717.1 397.8 %reduce-scatter.15.cloned.1.call-start = ((), (), s32[]{:S(2)}) async-start(), calls=%async_computation.16 | async-start | bytes 7667712 | tf_op jit(solution)/shard_map/reduce_scatter | solution.py:341
  789.4 359.0 %reduce-scatter.13.cloned.1.call-start = ((), (), s32[]{:S(2)}) async-start(), calls=%async_computation.15 | async-start | bytes 2621440 | tf_op jit(solution)/shard_map/reduce_scatter | solution.py:328
  818.4 158.0 %collective-permute-start.30 = (bf16[4,256,2048]{2,1,0:T(8,128)(2,1)}, bf16[4,256,2048]{2,1,0:T(8,128)(2,1)}, u32[]{:S(2)}, u32[]{:S(2)}) collective-permute-start(bf16[4,256,2048]{2,1,0:T(8,128)(2,1)} %pad_maximum_fusion.7), channel_id=1, source_target_pairs={{0,16},{4,20},{8,24},{12,28},{16,0},{20,4},{24,8},{28,12},{1,17},{... | collective-permute-start | bytes 12582920 | tf_op jit(solution)/shard_map/ppermute | solution.py:34
  836.0 148.2 %collective-permute-start.25 = (bf16[1024,2048]{1,0:T(8,128)(2,1)}, bf16[1024,2048]{1,0:T(8,128)(2,1)}, u32[]{:S(2)}, u32[]{:S(2)}) collective-permute-start(bf16[1024,2048]{1,0:T(8,128)(2,1)} %slice.438), channel_id=1, source_target_pairs={{0,4},{4,0},{8,12},{12,8},{16,20},{20,16},{24,28},{28,24},{1,5},{5... | collective-permute-start | bytes 12582920 | tf_op jit(solution)/shard_map/ppermute | solution.py:34
  858.1 117.1 %collective-permute-start.33 = (bf16[4,256,1024]{2,1,0:T(8,128)(2,1)S(1)}, bf16[4,256,1024]{2,1,0:T(8,128)(2,1)S(1)}, u32[]{:S(2)}, u32[]{:S(2)}) collective-permute-start(bf16[4,256,1024]{2,1,0:T(8,128)(2,1)S(1)} %pad_maximum_fusion.16), channel_id=1, source_target_pairs={{0,16},{4,20},{8,24},{12,28},{16,0},{20,4},{24,8},{28,12},{1,17},{... | collective-permute-start | bytes 6291464 | tf_op jit(solution)/shard_map/ppermute | solution.py:34
  976.2 186.0 %reduce-scatter.9.cloned.1.call-start = ((), (), s32[]{:S(2)}) async-start(), calls=%async_computation.12 | async-start | bytes 2621440 | tf_op jit(solution)/shard_map/reduce_scatter | solution.py:285
  981.9 72.1 %collective-permute-start.31 = (bf16[2,256,2048]{2,1,0:T(8,128)(2,1)S(1)}, bf16[2,256,2048]{2,1,0:T(8,128)(2,1)S(1)}, u32[]{:S(2)}, u32[]{:S(2)}) collective-permute-start(bf16[2,256,2048]{2,1,0:T(8,128)(2,1)S(1)} %pad_maximum_fusion.14), channel_id=1, source_target_pairs={{0,8},{4,12},{8,0},{12,4},{16,24},{20,28},{24,16},{28,20},{1,9},{5... | collective-permute-start | bytes 6291464 | tf_op jit(solution)/shard_map/ppermute | solution.py:34
  989.9 106.4 %collective-permute-start.26 = (bf16[512,2048]{1,0:T(8,128)(2,1)S(1)}, bf16[512,2048]{1,0:T(8,128)(2,1)S(1)}, u32[]{:S(2)}, u32[]{:S(2)}) collective-permute-start(bf16[512,2048]{1,0:T(8,128)(2,1)S(1)} %slice.440), channel_id=1, source_target_pairs={{0,8},{4,12},{8,0},{12,4},{16,24},{20,28},{24,16},{28,20},{1,9},{5... | collective-permute-start | bytes 6291464 | tf_op jit(solution)/shard_map/ppermute | solution.py:34
  (109 other events, 3710.1 us)
Sparse Core Ops, SparseCore 0:
  39.7 57.6 all-gather.4
  99.2 28.9 all-gather.6
  136.0 60.8 reduce-scatter.6
  219.9 47.7 all-gather.8
  609.1 46.2 reduce-scatter.10
  661.2 45.3 all-gather.10
  717.3 39.8 reduce-scatter.16
  789.5 85.3 reduce-scatter.14
  976.3 45.0 reduce-scatter.12
  1098.5 63.6 reduce-scatter.8

commit v2 on v1

v2 whole, which is shorter than its diff:
```python
import functools

import jax
import jax.numpy as jnp
from jax import lax
from jax.experimental import pallas as pl
from jax.experimental.pallas import tpu as pltpu
from jax.sharding import PartitionSpec as P

HEADS = 16
HEAD_DIM = 128
SEQ_DEV = 2
EPSILON = 1e-06
ROPE_BASE = 50000.0
CAP = 80
EXTRA = 128
VMEM = 56 * 2**20

F32 = jnp.float32
BF16 = jnp.bfloat16


def dot(a, b, dims, out=F32):
    return lax.dot_general(a, b, (dims, ((), ())), preferred_element_type=F32).astype(out)


def nn(a, b, out=F32):
    return dot(a, b, ((1,), (0,)), out)


def nt(a, b, out=F32):
    return dot(a, b, ((1,), (1,)), out)


def tn(a, b, out=F32):
    return dot(a, b, ((0,), (0,)), out)


def flip(v, bit):
    return lax.ppermute(v, "dp", [(i, i ^ bit) for i in range(lax.axis_size("dp"))])


def ring(n):
    return [*range(0, n, 2), *reversed(range(1, n, 2))]


def hop(v, back=False):
    order = ring(lax.axis_size("expert"))
    pairs = list(zip(order, order[1:] + order[:1], strict=True))
    return lax.ppermute(v, "expert", [(b, a) for a, b in pairs] if back else pairs)


def gather_ring(v):
    out = [v]
    for _ in range(lax.axis_size("expert") - 1):
        out.append(hop(out[-1]))
    return out


def places_in_ring():
    n = lax.axis_size("expert")
    at = [ring(n).index(i) for i in range(n)]
    at = jnp.asarray(at, jnp.int32)
    return lax.rem(at[lax.axis_index("expert")] - at + n, n)


def by_line(blocks):
    where = places_in_ring()
    stacked = jnp.stack(blocks)
    return jnp.concatenate([pick(stacked, where[i], 0) for i in range(len(blocks))], axis=0)


def bits_of(low, high):
    out = []
    while low < high:
        out.append(low)
        low *= 2
    return out


def pick(v, index, axis):
    return lax.dynamic_index_in_dim(v, index, axis, keepdims=False)


def tie(*values):
    return lax.optimization_barrier(values)


class Weights:
    def __init__(self, gate_up, down):
        self.rows, self.local, wide = gate_up.shape
        self.k = wide + down.shape[2]
        self.n = lax.axis_size("dp")
        self.me = lax.axis_index("dp")
        own = lax.rem(self.me, self.local)
        self.have = {
            (0, e): jnp.concatenate([pick(gate_up, own ^ e, 1), pick(down, own ^ e, 1)], axis=1)
            for e in range(self.local)
        }
        self.steps = self.plan()

    def plan(self):
        if self.local == 4 and self.n == 8:
            return [
                [([(0, 1), (0, 3)], 1), ([(0, 0)], 4)],
                [([(0, 2)], 2), ([(1, 0)], 4)],
                [([(1, 2)], 2), ([(2, 0)], 4)],
                [([(3, 0)], 4)],
            ]
        out, rows = [], [0]
        for bit in bits_of(1, self.local):
            left = [e for e in range(self.local) if e % bit == 0]
            out.append([([(r, e) for r in rows for e in left if e & bit], bit)])
            rows = rows + [r ^ bit for r in rows]
        for bit in bits_of(self.local, self.n):
            out.append([([(r, 0) for r in rows], bit)])
            rows = rows + [r ^ bit for r in rows]
        return out

    def step(self, at):
        if at >= len(self.steps):
            return
        for keys, bit in self.steps[at]:
            keep = keys[0][1] == 0
            v = [self.have[key] if keep else self.have.pop(key) for key in keys]
            got = flip(jnp.stack(v) if len(v) > 1 else v[0][None], bit)
            for i, (r, e) in enumerate(keys):
                self.have[(r ^ bit, e if keep else e ^ bit)] = got[i]

    def join(self, *values):
        keys = sorted(self.have)
        out = tie(*values, *[self.have[key] for key in keys])
        for key, v in zip(keys, out[len(values) :], strict=True):
            self.have[key] = v
        return out[: len(values)]

    def whole(self):
        for at in range(4, len(self.steps)):
            self.step(at)
        rows = [self.have[key] for key in sorted(self.have)]
        return jnp.concatenate(rows, axis=0)


class Tail:
    def __init__(self, held, local, n):
        self.local = local
        self.have = {(r, 0): v for r, v in held.items()}
        self.own = lax.rem(lax.axis_index("dp"), local)
        for bit in reversed(bits_of(local, n // 2)):
            for key in sorted(k for k in self.have if k[0] & bit):
                got = flip(self.have.pop(key), bit)
                to = (key[0] ^ bit, 0)
                self.have[to] = add(self.have[to], got)
        self.bits = list(reversed(bits_of(1, local)))

    def step(self, at):
        if at >= len(self.bits):
            return
        bit = self.bits[at]
        keys = sorted(key for key in self.have if key[0] & bit)
        got = flip(jnp.stack([self.have.pop(key) for key in keys]), bit)
        for i, (r, e) in enumerate(keys):
            self.have[(r ^ bit, e ^ bit)] = got[i]

    def join(self, *values):
        keys = sorted(self.have)
        out = tie(*values, *[self.have[key] for key in keys])
        for key, v in zip(keys, out[len(values) :], strict=True):
            self.have[key] = v
        return out[: len(values)]

    def done(self, ff):
        stacked = jnp.stack([self.have[(0, e)] for e in range(self.local)])
        blocks = [pick(stacked, self.own ^ e, 0) for e in range(self.local)]
        return (
            jnp.stack([b[:, : 2 * ff] for b in blocks], axis=1).astype(F32),
            jnp.stack([b[:, 2 * ff :] for b in blocks], axis=1).astype(F32),
        )


def fan(pieces, low):
    out = [list(pieces)]
    for bit in bits_of(1, low):
        out = out + [[flip(x, bit) for x in xs] for xs in out]
    return out


def add(a, b):
    return (a.astype(F32) + b.astype(F32)).astype(BF16)


def match(pieces, like):
    if len(pieces) == len(like):
        return pieces
    step = like[0].shape[0]
    return [x[i : i + step] for x in pieces for i in range(0, x.shape[0], step)]


def fold(parts):
    parts = list(parts)
    while len(parts) > 1:
        half = len(parts) // 2
        for i in range(half):
            got = match([flip(x, half) for x in reversed(parts[half + i])][::-1], parts[i])
            parts[i] = [add(a, b) for a, b in zip(parts[i], got, strict=True)]
        parts = parts[:half]
    return parts[0]


def scatter_dp(part, rows):
    n = lax.axis_size("dp")
    held = [part[r * rows : (r + 1) * rows] for r in range(n)]
    for bit in bits_of(1, n):
        odd = jnp.concatenate(held[1::2], axis=0) if len(held) > 2 else held[1]
        got = flip(odd, bit)
        held = [add(v, got[i * rows : (i + 1) * rows]) for i, v in enumerate(held[::2])]
    return held[0]


def blocks_of(parts, tok):
    return [(i, at) for i, p in enumerate(parts) for at in range(0, p.shape[0], tok)]


def onehot(pos_ref, b):
    slot = lax.broadcasted_iota(jnp.int32, (CAP, pos_ref.shape[1]), 0)
    return slot == pos_ref[b : b + 1, :]


def mm(a, b, dims):
    return lax.dot_general(a, b, (dims, ((), ())), preferred_element_type=F32)


def front_kernel(count, me, *refs):
    parts, (pos, wd, rows_out, gw) = refs[:count], refs[count:]
    tok = pos.shape[1]
    width = rows_out.shape[1]

    @pl.when(pl.program_id(0) == 0)
    def _():
        for b, (i, at) in enumerate(blocks_of(parts, tok)):
            part = parts[i][at : at + tok, :width]
            hot = onehot(pos, b).astype(BF16)
            found = mm(hot, part, ((1,), (0,))).astype(BF16)
            to_distance(rows_out, slice(b * CAP, (b + 1) * CAP), found, me[0])

    gw[...] = mm(rows_out[...], wd[...], ((1,), (0,)))


def front(parts, pos, weights, ff, me):
    count, width = len(parts), weights.shape[0]
    slots = pos.shape[0] * CAP
    tile = min(256, ff)
    first = (weights.shape[1] - ff) // tile
    whole = lambda x: pl.BlockSpec(x.shape, lambda n, me: (0, 0))
    return pl.pallas_call(
        functools.partial(front_kernel, count),
        grid_spec=pltpu.PrefetchScalarGridSpec(
            num_scalar_prefetch=1,
            grid=(ff // tile,),
            in_specs=[whole(x) for x in parts]
            + [whole(pos), pl.BlockSpec((width, tile), lambda n, me: (0, first + n))],
            out_specs=[
                pl.BlockSpec((slots, width), lambda n, me: (0, 0)),
                pl.BlockSpec((slots, tile), lambda n, me: (0, n)),
            ],
        ),
        out_shape=[
            jax.ShapeDtypeStruct((slots, width), BF16),
            jax.ShapeDtypeStruct((slots, ff), F32),
        ],
        compiler_params=pltpu.CompilerParams(vmem_limit_bytes=VMEM),
        cost_estimate=pl.CostEstimate(
            flops=2 * slots * width * ff,
            bytes_accessed=2 * width * ff + 6 * slots * width,
            transcendentals=0,
        ),
        name="front",
    )(me, *parts, pos, weights)


def to_distance(ref, rows, value, me):
    n = lax.axis_size("dp")
    wide = value.shape[1] // n
    for c in range(n):
        at = pl.multiple_of((me ^ c) * wide, wide)
        ref[rows, pl.ds(at, wide)] = value[:, c * wide : (c + 1) * wide]


def expert_kernel(count, expert, *refs):
    parts = refs[:count]
    pos, named, router, wg, wu, gw = refs[count : count + 6]
    backs = refs[count + 6 : 2 * count + 6]
    rows_out, dg_out, du_out, gact_out, acc, gate, dgate = refs[2 * count + 6 :]
    n = pl.program_id(0)
    tok = pos.shape[1]
    width = rows_out.shape[1]
    experts = router.shape[0]

    @pl.when(n == 0)
    def _():
        for b, (i, first) in enumerate(blocks_of(parts, tok)):
            at = slice(b * CAP, (b + 1) * CAP)
            part = parts[i][first : first + tok, :]
            hot = onehot(pos, b)
            found = mm(hot.astype(BF16), part, ((1,), (0,))).astype(BF16)
            to_distance(rows_out, at, found, expert[1])
            chosen = named[b] > 0
            logits = jnp.where(chosen, mm(router[...], part, ((1,), (1,))), -1e30)
            e = jnp.where(chosen, jnp.exp(logits - jnp.max(logits, axis=0, keepdims=True)), 0.0)
            gates = e / jnp.sum(e, axis=0, keepdims=True)
            mine = lax.broadcasted_iota(jnp.int32, gates.shape, 0) == expert[0]
            row = jnp.sum(jnp.where(mine, gates, 0.0), axis=0, keepdims=True)
            gate[at, :] = jnp.sum(jnp.where(hot, row, 0.0), axis=1, keepdims=True)
            dgate[at, :] = jnp.zeros((CAP, 1), F32)

    rows = rows_out[...]
    g = mm(rows, wg[...], ((1,), (0,)))
    u = mm(rows, wu[...], ((1,), (0,)))
    sg = 1.0 / (1.0 + jnp.exp(-g))
    silu = g * sg
    act = (silu * u).astype(BF16).astype(F32)
    gw_v = gw[...]
    dgate[...] += jnp.sum(act * gw_v, axis=1, keepdims=True)
    gate_v = gate[...]
    gact_out[...] = (gate_v * act).astype(BF16)
    dact = gate_v * gw_v
    dg = (dact * u * (sg * (1.0 + g * (1.0 - sg)))).astype(BF16)
    du = (dact * silu).astype(BF16)
    dg_out[...] = dg
    du_out[...] = du
    back = mm(dg, wg[...], ((1,), (1,))) + mm(du, wu[...], ((1,), (1,)))

    @pl.when(n == 0)
    def _():
        acc[...] = back

    @pl.when(n > 0)
    def _():
        acc[...] += back

    @pl.when(n == pl.num_programs(0) - 1)
    def _():
        lane = lax.broadcasted_iota(jnp.int32, (CAP, EXTRA), 1)
        for b, (i, first) in enumerate(blocks_of(parts, tok)):
            at = slice(b * CAP, (b + 1) * CAP)
            to = slice(first, first + tok)
            hot = onehot(pos, b).astype(BF16)
            out = backs[i]
            found = mm(hot, acc[at, :].astype(BF16), ((0,), (0,))).astype(BF16)
            to_distance(out, to, found, expert[1])
            d = dgate[at, :]
            hi = d.astype(BF16).astype(F32)
            beside = jnp.where(
                lane == expert[0], hi, jnp.where(lane == experts + expert[0], d - hi, 0.0)
            ).astype(BF16)
            out[to, width:] = mm(hot, beside, ((0,), (0,))).astype(BF16)


def run_expert(parts, pos, named, router, weights, gw, expert, ff):
    count, width = len(parts), weights.shape[0]
    slots = pos.shape[0] * CAP
    tile = min(256, ff)
    steps = ff // tile
    whole = lambda x: pl.BlockSpec(x.shape, lambda n, e: (0,) * x.ndim)
    column = pl.BlockSpec((slots, tile), lambda n, e: (0, n))
    backs = [jax.ShapeDtypeStruct((x.shape[0], width + EXTRA), BF16) for x in parts]
    thin = jax.ShapeDtypeStruct((slots, ff), BF16)
    outs = pl.pallas_call(
        functools.partial(expert_kernel, count),
        grid_spec=pltpu.PrefetchScalarGridSpec(
            num_scalar_prefetch=1,
            grid=(steps,),
            in_specs=[whole(x) for x in parts]
            + [
                whole(pos),
                whole(named),
                whole(router),
                pl.BlockSpec((width, tile), lambda n, e: (0, n)),
                pl.BlockSpec((width, tile), lambda n, e: (0, steps + n)),
                column,
            ],
            out_specs=[whole(x) for x in backs]
            + [pl.BlockSpec((slots, width), lambda n, e: (0, 0)), column, column, column],
            scratch_shapes=[
                pltpu.VMEM((slots, width), F32),
                pltpu.VMEM((slots, 1), F32),
                pltpu.VMEM((slots, 1), F32),
            ],
        ),
        out_shape=backs
        + [jax.ShapeDtypeStruct((slots, width), BF16), thin, thin, thin],
        compiler_params=pltpu.CompilerParams(vmem_limit_bytes=VMEM),
        cost_estimate=pl.CostEstimate(
            flops=8 * slots * width * ff,
            bytes_accessed=4 * width * ff + 12 * slots * width,
            transcendentals=slots * ff,
        ),
        name="expert",
    )(expert, *parts, pos, named, router, weights, weights, gw)
    return outs[:count], outs[count:]


def result_kernel(count, me, gact, wd, pos, *outs):
    tok = pos.shape[1]
    y = mm(gact[...], wd[...], ((1,), (1,))).astype(BF16)
    for b, (i, at) in enumerate(blocks_of(outs, tok)):
        hot = onehot(pos, b).astype(BF16)
        outs[i][at : at + tok, :] = mm(
            hot, y[b * CAP : (b + 1) * CAP, :], ((0,), (0,))
        ).astype(BF16)


def result(gact, pos, weights, count, me):
    slots, ff = gact.shape
    width = weights.shape[0]
    tile = width // lax.axis_size("dp")
    last = (weights.shape[1] - ff) // ff
    out = jax.ShapeDtypeStruct((pos.shape[0] // count * pos.shape[1], width), BF16)
    return pl.pallas_call(
        functools.partial(result_kernel, count),
        grid_spec=pltpu.PrefetchScalarGridSpec(
            num_scalar_prefetch=1,
            grid=(width // tile,),
            in_specs=[
                pl.BlockSpec((slots, ff), lambda n, me: (0, 0)),
                pl.BlockSpec((tile, ff), lambda n, me: (n, last)),
                pl.BlockSpec(pos.shape, lambda n, me: (0, 0)),
            ],
            out_specs=[pl.BlockSpec((out.shape[0], tile), lambda n, me: (0, me[0] ^ n))] * count,
        ),
        out_shape=[out] * count,
        compiler_params=pltpu.CompilerParams(vmem_limit_bytes=VMEM),
        cost_estimate=pl.CostEstimate(
            flops=2 * slots * width * ff,
            bytes_accessed=2 * width * ff + 2 * count * out.shape[0] * width,
            transcendentals=0,
        ),
        name="result",
    )(me, gact, weights, pos)


def grads_kernel(count, *refs):
    out = refs[-1]
    ff = refs[2].shape[1]
    gate = up = down = 0.0
    for c in range(count):
        rows, gs, dg, du, gact = refs[5 * c : 5 * c + 5]
        gate = gate + mm(rows[...], dg[...], ((0,), (0,)))
        up = up + mm(rows[...], du[...], ((0,), (0,)))
        down = down + mm(gs[...], gact[...], ((0,), (0,)))
    out[0, :, :ff] = gate.astype(BF16)
    out[0, :, ff : 2 * ff] = up.astype(BF16)
    out[0, :, 2 * ff :] = down.astype(BF16)


def grads(chunks, first, blocks, rows):
    ff = chunks[0][2].shape[1]
    specs, ins = [], []
    for chunk in chunks:
        slots = chunk[0].shape[0]
        tall = pl.BlockSpec((slots, rows), lambda i: (0, first + i))
        flat = pl.BlockSpec((slots, ff), lambda i: (0, 0))
        specs += [tall, tall, flat, flat, flat]
        ins += list(chunk)
    slots = sum(chunk[0].shape[0] for chunk in chunks)
    return pl.pallas_call(
        functools.partial(grads_kernel, len(chunks)),
        grid=(blocks,),
        in_specs=specs,
        out_specs=pl.BlockSpec((1, rows, 3 * ff), lambda i: (i, 0, 0)),
        out_shape=jax.ShapeDtypeStruct((blocks, rows, 3 * ff), BF16),
        compiler_params=pltpu.CompilerParams(vmem_limit_bytes=VMEM),
        cost_estimate=pl.CostEstimate(
            flops=6 * slots * blocks * rows * ff,
            bytes_accessed=6 * slots * ff + 6 * blocks * rows * ff,
            transcendentals=0,
        ),
        name="grads",
    )(*ins)


def attn_grads_kernel(me, a, d, *rest):
    k = d.shape[1]
    out = rest[-1]
    out[:, :k] = mm(a[...], d[...], ((0,), (0,))).astype(BF16)
    if len(rest) > 1:
        out[:, k:] = rest[0][...]


def attn_grads(a, d, extra, me, first, stride):
    rows, width = a.shape
    n = lax.axis_size("dp")
    tile = width // n
    count = n // stride
    at = lambda i, me: me[0] ^ (first + stride * i)
    k = d.shape[1] + sum(e.shape[1] for e in extra)
    return pl.pallas_call(
        attn_grads_kernel,
        grid_spec=pltpu.PrefetchScalarGridSpec(
            num_scalar_prefetch=1,
            grid=(count,),
            in_specs=[
                pl.BlockSpec((rows, tile), lambda i, me: (0, at(i, me))),
                pl.BlockSpec(d.shape, lambda i, me: (0, 0)),
            ]
            + [pl.BlockSpec((tile, e.shape[1]), lambda i, me: (at(i, me), 0)) for e in extra],
            out_specs=pl.BlockSpec((tile, k), lambda i, me: (i, 0)),
        ),
        out_shape=jax.ShapeDtypeStruct((count * tile, k), BF16),
        compiler_params=pltpu.CompilerParams(vmem_limit_bytes=VMEM),
        cost_estimate=pl.CostEstimate(
            flops=2 * rows * width * k // stride,
            bytes_accessed=2 * (rows * width + rows * k + width * k // stride),
            transcendentals=0,
        ),
        name="attn_grads",
    )(me, a, d, *extra)


def scatter_wide(odd, even, rows):
    n = lax.axis_size("dp")
    got = flip(odd, 1)
    held = add(even, got)
    wide = held.shape[1] // 256 * 128
    sides = []
    for left, right, order in (
        (0, wide, bits_of(2, n)),
        (wide, held.shape[1], bits_of(2, n)[::-1]),
    ):
        side = {2 * i: held[i * rows : (i + 1) * rows, left:right] for i in range(n // 2)}
        sides.append((side, order))
    for at in range(len(sides[0][1])):
        for side, order in sides:
            bit = order[at]
            keys = sorted(r for r in side if r & bit)
            v = [side.pop(r) for r in keys]
            got = flip(jnp.concatenate(v, axis=0) if len(v) > 1 else v[0], bit)
            for i, r in enumerate(keys):
                side[r ^ bit] = add(side[r ^ bit], got[i * rows : (i + 1) * rows])
    return jnp.concatenate([side[0] for side, _ in sides], axis=1)


def inv_rms(v):
    return lax.rsqrt(jnp.mean(v * v, axis=-1, keepdims=True) + EPSILON)


def rms_back(v, r, gain, c):
    gc = gain * c
    return r * gc - v * (r * r * r) * jnp.mean(v * gc, axis=-1, keepdims=True)


def rotate(v, cos, sin):
    half = v.shape[-1] // 2
    u, w = v[..., :half], v[..., half:]
    return jnp.concatenate([u * cos - w * sin, w * cos + u * sin], axis=-1)


def on_device(
    tokens,
    lengths,
    permutation,
    routes,
    norm_gains,
    w_qkv,
    w_out,
    router,
    w_gate_up,
    w_down,
    cotangent,
):
    rows, width = tokens.shape
    zs = lax.axis_size("expert")
    dps = lax.axis_size("dp")
    z = lax.axis_index("expert")
    dp = lax.axis_index("dp")
    local = w_gate_up.shape[1]
    ff = w_down.shape[2]
    experts = router.shape[1]
    own_rows = w_qkv.shape[0]
    cols = width // zs
    heads = HEADS // zs
    scale = HEAD_DIM ** (-0.5)
    expert = z * local + lax.rem(dp, local)

    extra = jnp.concatenate(
        [router, norm_gains, jnp.zeros((own_rows, EXTRA - experts - 4), BF16)], axis=1
    )
    sent = jnp.stack(
        [
            jnp.concatenate(
                [w_qkv[:, i * width + e * cols : i * width + (e + 1) * cols] for i in range(3)]
                + [extra],
                axis=1,
            )
            for e in range(zs)
        ]
    )
    mine = lax.all_to_all(sent, "expert", split_axis=0, concat_axis=0, tiled=True)
    moved = [(b, (b % dps) * zs + b // dps) for b in range(dps * zs)]
    held = Weights(w_gate_up, w_down)
    first = dict(held.have)
    held.step(0)
    keys = sorted(set(first) & set(held.have))
    out = tie(mine, tokens, w_out, *[first[key] for key in keys])
    mine, tokens_now, out_rows = out[:3]
    for key, v in zip(keys, out[3:], strict=True):
        held.have[key] = v
    x_all = by_line(gather_ring(tokens_now))
    out_rows = lax.ppermute(out_rows, ("dp", "expert"), moved)
    attn_w = lax.all_gather(
        mine.reshape(zs * own_rows, 3 * cols + EXTRA), "dp", axis=0, tiled=True
    )
    mask = jnp.sum(
        (routes[:, :, None] == jnp.arange(experts, dtype=jnp.int32)).astype(BF16), axis=1
    )
    mask_pad = jnp.concatenate([mask, jnp.zeros((rows, EXTRA - experts), BF16)], axis=1)
    g_own = jnp.concatenate([cotangent, mask_pad], axis=1)
    attn_w, x_all, out_rows, g_own = held.join(attn_w, x_all, out_rows, g_own)
    held.step(1)
    out_w = lax.all_gather(out_rows, "dp", axis=0, tiled=True)
    g_line = jnp.concatenate(gather_ring(g_own), axis=0)
    qkv_w = attn_w[:, : 3 * cols]
    router_full = attn_w[:, 3 * cols : 3 * cols + experts]
    gains = attn_w[:, 3 * cols + experts : 3 * cols + experts + 4].astype(F32).T

    dealt = lax.dynamic_slice_in_dim(permutation, dp * zs * SEQ_DEV, zs * SEQ_DEV)
    lens = jnp.take(lengths, dealt).reshape(zs, SEQ_DEV)
    ends = jnp.cumsum(lens, axis=1)
    places = jnp.arange(rows, dtype=jnp.int32)
    segment = jnp.sum((places[None, :, None] >= ends[:, None, :]).astype(jnp.int32), axis=2)
    starts = ends - lens
    offset = jnp.sum(
        jnp.where(
            segment[:, :, None] == jnp.arange(SEQ_DEV, dtype=jnp.int32), starts[:, None, :], 0
        ),
        axis=2,
    )
    half = HEAD_DIM // 2
    inverse = ROPE_BASE ** (-2.0 * jnp.arange(half, dtype=F32) / HEAD_DIM)
    turned = (places[None] - offset).astype(F32)[..., None] * inverse
    cos, sin = jnp.cos(turned)[:, :, None, :], jnp.sin(turned)[:, :, None, :]
    same = (segment[:, :, None] == segment[:, None, :])[:, None]

    xf = x_all.astype(F32)
    r_attn = inv_rms(xf)
    a_all = (xf * r_attn * gains[0]).astype(BF16)
    qkv = nn(a_all, qkv_w)
    q, k, v = qkv[:, :cols], qkv[:, cols : 2 * cols], qkv[:, 2 * cols :]
    squares = lax.psum(
        jnp.stack([jnp.sum(q * q, axis=1), jnp.sum(k * k, axis=1)]), "expert"
    )
    r_q = lax.rsqrt(squares[0] / width + EPSILON)[:, None]
    r_k = lax.rsqrt(squares[1] / width + EPSILON)[:, None]
    gain_q = lax.dynamic_slice_in_dim(gains[1], z * cols, cols)
    gain_k = lax.dynamic_slice_in_dim(gains[2], z * cols, cols)
    split = (zs, rows, heads, HEAD_DIM)
    qr = rotate((q * r_q * gain_q).reshape(split), cos, sin).astype(BF16)
    kr = rotate((k * r_k * gain_k).reshape(split), cos, sin).astype(BF16)
    vb = v.astype(BF16).reshape(split)
    s = jnp.einsum("bthd,bshd->bhts", qr, kr, preferred_element_type=F32) * scale
    s = jnp.where(same, s, -1e30)
    es = jnp.exp(s - jnp.max(s, axis=3, keepdims=True))
    p = es / jnp.sum(es, axis=3, keepdims=True)
    pb = p.astype(BF16)
    o = (
        jnp.einsum("bhts,bshd->bthd", pb, vb, preferred_element_type=F32)
        .reshape(zs * rows, cols)
        .astype(BF16)
    )
    top = local // 2
    added = nn(o, out_w, BF16)
    added, g_line = held.join(added, g_line)
    held.step(2)
    g_far = flip(g_line, top)
    added = lax.psum_scatter(added, "expert", scatter_dimension=0, tiled=True)
    (added,) = held.join(added)
    held.step(3)
    hid = tokens.astype(F32) + added.astype(F32)
    r_ffn = inv_rms(hid)
    m = (hid * r_ffn * gains[3]).astype(BF16)

    m_near, m_far = [m], [flip(m, top)]
    for _ in range(zs - 1):
        m_near.append(hop(m_near[-1]))
        m_far.append(flip(m_near[-1], top))
    weights = held.whole()
    mine_e = (jnp.arange(experts) == expert).astype(F32)
    me_at = jnp.reshape(dp, (1,)).astype(jnp.int32)
    expert_at = jnp.stack([expert, dp]).astype(jnp.int32)
    router_t = router_full.T

    def chunk_front(g_part):
        parts = [x for xs in fan([g_part], top) for x in xs]
        masks = jnp.concatenate([x[:, width : width + experts] for x in parts], axis=0)
        masks = masks.astype(F32).reshape(len(parts) * zs, rows, experts)
        on = jnp.sum(masks * mine_e, axis=2)
        pos = jnp.where(on > 0, jnp.cumsum(on, axis=1) - 1.0, -1.0).astype(jnp.int32)
        gs, gw = front(parts, pos, weights, ff, me_at)
        return pos, masks.transpose(0, 2, 1), gs, gw

    def chunk_expert(blocks, pieces, fronted):
        pos, named, gs, gw = fronted
        parts = [blocks] + fan(pieces, top)[1:]
        flat = [x for xs in parts for x in xs]
        backs, outs = run_expert(flat, pos, named, router_t, weights, gw, expert_at, ff)
        back = []
        for xs in parts:
            back.append(backs[: len(xs)])
            backs = backs[len(xs) :]
        return back, (outs[0], gs, outs[1], outs[2], outs[3])

    near = chunk_front(g_line)
    far = chunk_front(g_far)
    near_back, near_outs = chunk_expert(m_near, [jnp.concatenate(m_near, axis=0)], near)
    mid = zs // 2
    m_far = tie(*m_far, near_outs[4])[:zs]
    far_pieces = [jnp.concatenate(m_far[:mid], axis=0), jnp.concatenate(m_far[mid:], axis=0)]
    far_back, far_outs = chunk_expert(list(m_far), far_pieces, far)
    chunks = [near_outs, far_outs]
    e_rows = w_gate_up.shape[0]

    far_sum = fold(far_back)
    near_sum = fold(near_back)
    acc = None
    for i in reversed(range(zs)):
        here = near_sum[i].astype(F32) + flip(far_sum[i], top).astype(F32)
        acc = here if acc is None else here + hop(acc, back=True).astype(F32)
        acc = acc.astype(BF16)
    dm = acc
    send_high = grads(chunks, 3 * dps // 4, dps // 4, e_rows)
    got_high = flip(send_high, dps // 2)
    send_low = grads(chunks, dps // 2, dps // 4, e_rows)
    y_far = fold([[x] for x in result(far_outs[4], far[0], weights, top, me_at)])[0]
    y_near = fold([[x] for x in result(near_outs[4], near[0], weights, top, me_at)])[0]
    kept = grads(chunks, 0, dps // 2, e_rows)
    dm, got_high, send_low, y_far, y_near, kept = tie(
        dm, got_high, send_low, y_far, y_near, kept
    )
    dm = dm.astype(F32)
    y_far = flip(y_far, top)
    held_g = {}
    for i in range(dps // 4):
        held_g[dps // 4 + i] = add(kept[dps // 4 + i], got_high[i])
    got_low = flip(send_low, dps // 2)

    own_mask = mask.astype(F32)
    own_logits = jnp.where(own_mask > 0, nn(m, router_full), -1e30)
    own_e = jnp.where(
        own_mask > 0, jnp.exp(own_logits - jnp.max(own_logits, axis=1, keepdims=True)), 0.0
    )
    gate_own = own_e / jnp.sum(own_e, axis=1, keepdims=True)
    dgates = dm[:, width : width + experts] + dm[:, width + experts : width + 2 * experts]
    dz = (
        gate_own * (dgates - jnp.sum(gate_own * dgates, axis=1, keepdims=True))
    ).astype(BF16)
    dmt = nt(dz, router_full) + dm[:, :width]
    router_part = tn(m, dz)
    grad_out = cotangent.astype(F32)
    dh = grad_out + rms_back(hid, r_ffn, gains[3], dmt)
    gain_ffn = jnp.sum(dmt * hid * r_ffn, axis=0)

    dhb = lax.all_gather(dh.astype(BF16), "expert", axis=0, tiled=True)
    dhb, y_far = tie(dhb, y_far)
    y_own = add(y_near, y_far)
    y = lax.psum_scatter(
        by_line([y_own[i * rows : (i + 1) * rows] for i in range(zs)]),
        "expert",
        scatter_dimension=0,
        tiled=True,
    )
    do = nt(dhb, out_w, BF16).reshape(split)
    out_blocks = tn(o, dhb, BF16).reshape(dps, own_rows, width)
    grad_out_w = scatter_dp(
        jnp.concatenate([pick(out_blocks, dp ^ r, 0) for r in range(dps)], axis=0), own_rows
    )
    grad_w_out = lax.ppermute(
        grad_out_w, ("dp", "expert"), [(b, a) for a, b in moved]
    ).astype(F32)
    dp_ = jnp.einsum("bthd,bshd->bhts", do, vb, preferred_element_type=F32)
    dv = jnp.einsum("bhts,bthd->bshd", pb, do, preferred_element_type=F32)
    ds = (p * (dp_ - jnp.sum(p * dp_, axis=3, keepdims=True))).astype(BF16)
    dqr = jnp.einsum("bhts,bshd->bthd", ds, kr, preferred_element_type=F32) * scale
    dkr = jnp.einsum("bhts,bthd->bshd", ds, qr, preferred_element_type=F32) * scale
    dqn = rotate(dqr, cos, -sin).reshape(zs * rows, cols)
    dkn = rotate(dkr, cos, -sin).reshape(zs * rows, cols)
    means = lax.psum(
        jnp.stack(
            [jnp.sum(q * (gain_q * dqn), axis=1), jnp.sum(k * (gain_k * dkn), axis=1)]
        ),
        "expert",
    )
    dq = r_q * gain_q * dqn - q * (r_q * r_q * r_q) * (means[0] / width)[:, None]
    dk = r_k * gain_k * dkn - k * (r_k * r_k * r_k) * (means[1] / width)[:, None]
    dqkv = jnp.concatenate([dq, dk, dv.reshape(zs * rows, cols)], axis=1).astype(BF16)
    da_part = nt(dqkv, qkv_w)
    da = lax.psum_scatter(
        da_part.astype(BF16), "expert", scatter_dimension=0, tiled=True
    ).astype(F32)
    gain_attn = jnp.sum(da_part * (xf * r_attn), axis=0)
    at = z * cols
    zero = jnp.zeros((width,), F32)
    gain_query = lax.dynamic_update_slice_in_dim(zero, jnp.sum(dqn * q * r_q, axis=0), at, 0)
    gain_keys = lax.dynamic_update_slice_in_dim(zero, jnp.sum(dkn * k * r_k, axis=0), at, 0)
    gain_part = jnp.stack([gain_attn, gain_query, gain_keys, gain_ffn], axis=1)
    extra_part = jnp.concatenate(
        [router_part, gain_part, jnp.zeros((width, EXTRA - experts - 4), F32)], axis=1
    ).astype(BF16)
    dqkv, got_low = tie(dqkv, got_low)
    for i in range(dps // 4):
        held_g[i] = add(kept[i], got_low[i])
    tail = Tail(held_g, local, dps)
    summed = scatter_wide(
        attn_grads(a_all, dqkv, [extra_part], me_at, 1, 2),
        attn_grads(a_all, dqkv, [extra_part], me_at, 0, 2),
        zs * own_rows,
    )
    tail.step(0)
    tail.step(1)
    output = hid + y.astype(F32)
    grad_gu, grad_dn = tail.done(ff)
    back = lax.all_to_all(
        summed.reshape(zs, own_rows, 3 * cols + EXTRA),
        "expert",
        split_axis=0,
        concat_axis=0,
        tiled=True,
    ).astype(F32)
    grad_w_qkv = jnp.concatenate(
        [back[e, :, i * cols : (i + 1) * cols] for i in range(3) for e in range(zs)], axis=1
    )
    extra_sum = jnp.sum(back[:, :, 3 * cols :], axis=0)
    grad_router = extra_sum[:, :experts]
    grad_gains = extra_sum[:, experts : experts + 4]

    x_own = tokens.astype(F32)
    grad_tokens = dh + rms_back(x_own, inv_rms(x_own), gains[0], da)
    return (
        output,
        grad_tokens,
        grad_gains,
        grad_w_qkv,
        grad_w_out,
        grad_router,
        grad_gu,
        grad_dn,
    )


def solution(mesh):
    both = P(("dp", "expert"), None)
    experts = P("dp", "expert", None)
    return jax.shard_map(
        on_device,
        mesh=mesh,
        in_specs=(both, P(), P(), both, both, both, both, both, experts, experts, both),
        out_specs=(both, both, both, both, both, both, experts, experts),
        check_vma=False,
    )
```

time: 1190 us -> 842 us (0.71)
  waiting for transfers between devices: 610 us -> 309 us
  Pallas kernels: 0 us -> 138 us
  matrix products: 180 us -> 45.8 us
  local copies, waits for them, and re-layouts: 182 us -> 128 us
  other arithmetic: 69.8 us -> 103 us
  blocking collectives: 47.9 us -> 23.3 us
  starting transfers between devices: 75.5 us -> 57.8 us
    ppermute x22 -> x39, waiting for transfers between devices: 423 us -> 172 us  [flip(): lax.ppermute(v, 'dp', [(i, i ^ bit) for i in range(lax.axis_size('dp'))])]
    dot_general x16 -> x8, matrix products: 171 us -> 30.4 us  [dot(): lax.dot_general(a, b, (dims, ((), ())), preferred_element_type=F32)]
    pallas_call x0 -> x11, Pallas kernels: none -> 138 us  [the longest x2 51.8 us: run_expert(): pl.pallas_call(functools.partial(expert_kernel, count), grid_spec=pltpu.P...]
    reduce_scatter x5 -> x2, waiting for transfers between devices: 57.2 us -> 5.2 us  [the longest x1 5.18 us: on_device(): added = lax.psum_scatter(added, 'expert', scatter_dimension=0, tiled=True)]
    all_gather x1, waiting for transfers between devices: 45.1 us -> 0.01 us  [on_device(): dhb = lax.all_gather(dh.astype(BF16), 'expert', axis=0, tiled=True)]
    concatenate x10 -> x8, local copies, waits for them, and re-layouts: 46.5 us -> 6.46 us  [the longest x1 2.68 us: whole(): return jnp.concatenate(rows, axis=0)]
    ppermute x13, waiting for transfers between devices: 43.8 us -> 83.6 us  [the longest x12 63.3 us: hop(): lax.ppermute(v, 'expert', [(b, a) for a, b in pairs] if back else pairs)]
    ppermute x13, starting transfers between devices: 51.9 us -> 16 us  [the longest x12 13 us: hop(): lax.ppermute(v, 'expert', [(b, a) for a, b in pairs] if back else pairs)]
  transfers between devices with their start and end apart: 47 -> 61, of which waited for: 24 -> 25; matrix products, arithmetic and copies ran while one was open for 24% -> 27% of each run, Pallas kernels for 0% -> 17%
where the time goes in v2:
time: 842 us; the launch traced here: 828 us
  waiting for transfers between devices  309 us (37%)
  Pallas kernels  138 us (16%)
  local copies, waits for them, and re-layouts  128 us (15%)
  other arithmetic  103 us (12%)
  starting transfers between devices  57.8 us (7%)
  matrix products  45.8 us (5%)
  between operations  23.8 us (3%)
  blocking collectives  23.3 us (3%)
    ppermute x39, waiting for transfers between devices, flip(): lax.ppermute(v, 'dp', [(i, i ^ bit) for i in range(lax.axis_size('dp'))])  172 us
    ppermute x12, waiting for transfers between devices, hop(): lax.ppermute(v, 'expert', [(b, a) for a, b in pairs] if back else pairs)  63.3 us
    pallas_call x2, Pallas kernels, run_expert(): pl.pallas_call(functools.partial(expert_kernel, count), grid_spec=pltpu.P...  51.8 us
    unnamed x209, local copies, waits for them, and re-layouts  51.2 us
    pallas_call x3, Pallas kernels, grads(): pl.pallas_call(functools.partial(grads_kernel, len(chunks)), grid=(blocks...  36.5 us
    ppermute x1, waiting for transfers between devices, on_device(): lax.ppermute(grad_out_w, ('dp', 'expert'), [(b, a) for a, b in moved])  31.1 us
    dot_general x8, matrix products, dot(): lax.dot_general(a, b, (dims, ((), ())), preferred_element_type=F32)  30.4 us
    ppermute x39, starting transfers between devices, flip(): lax.ppermute(v, 'dp', [(i, i ^ bit) for i in range(lax.axis_size('dp'))])  30.3 us
  transfers between devices with their start and end apart: 61, of which 25 were waited for; matrix products, arithmetic and copies ran while one was open for 27% of the time, Pallas kernels for 17%

profile of v2, /device:TPU:4, one launch (start us, length us, event | category | flops | bytes accessed | tf_op | source)
XLA Modules:
  0.0 828.2 jit_solution(10628898084127098902)
XLA Ops:
  21.7 9.6 %constant_dynamic-slice_fusion.5 = (bf16[256,1,2048]{2,1,0:T(2,128)(2,1)S(1)}, bf16[256,1,2048]{2,1,0:T(2,128)(2,1)S(1)}, bf16[256,1,2048]{2,1,0:T(2,128)(2,1)S(1)}, bf16[256,1,2048]{2,1,0:T(2,128)(2,1)}) fusion(bf16[256,4,2048]{2,1,0:T(4,128)(2,1)S(1)} %copy-done.8, s32[]{:T(128)S(6)} %select_n.132, s32[]{:T(128)S(6)} %select_n.126, s32[]{:T(128)S(6)} %select_n.125, ...), kind=kLoop, calls=%fused_computation.262 | loop fusion | bytes 8388624 | tf_op jit(solution)/shard_map/jit(dynamic_index_in_dim)/dynamic_slice | solution.py:82
  49.0 12.0 %collective-permute-done = bf16[128,2048]{1,0:T(8,128)(2,1)S(1)} collective-permute-done((bf16[128,2048]{1,0:T(8,128)(2,1)S(1)}, bf16[128,2048]{1,0:T(8,128)(2,1)S(1)}, u32[]{:S(2)}, u32[]{:S(2)}) %collective-permute-start) | collective-permute-done | bytes 524320 | tf_op jit(solution)/shard_map/ppermute | solution.py:50
  63.0 11.4 %collective-permute-done.1 = bf16[128,2048]{1,0:T(8,128)(2,1)S(1)} collective-permute-done((bf16[128,2048]{1,0:T(8,128)(2,1)S(1)}, bf16[128,2048]{1,0:T(8,128)(2,1)S(1)}, u32[]{:S(2)}, u32[]{:S(2)}) %collective-permute-start.1) | collective-permute-done | bytes 524320 | tf_op jit(solution)/shard_map/ppermute | solution.py:50
  95.4 20.3 %collective-permute-done.3 = bf16[64,2048]{1,0:T(8,128)(2,1)} collective-permute-done((bf16[64,2048]{1,0:T(8,128)(2,1)}, bf16[64,2048]{1,0:T(8,128)(2,1)}, u32[]{:S(2)}, u32[]{:S(2)}) %collective-permute-start.3) | collective-permute-done | bytes 262176 | tf_op jit(solution)/shard_map/ppermute | solution.py:609
  125.6 12.1 %psum.14 = f32[2,512]{1,0:T(2,128)S(1)} all-reduce(f32[2,512]{1,0:T(2,128)S(1)} %pad_maximum_fusion.34), channel_id=1, replica_groups=mesh['dp'=8,'expert'=4] {'expert'}, use_global_device_ids=true, to_apply=%region_6.7 | all-reduce | flops 1024 | bytes 8192 | tf_op jit(solution)/shard_map/psum | solution.py:649
  150.7 9.9 %collective-permute-done.7 = bf16[128,2176]{1,0:T(8,128)(2,1)} collective-permute-done((bf16[128,2176]{1,0:T(8,128)(2,1)}, bf16[128,2176]{1,0:T(8,128)(2,1)}, u32[]{:S(2)}, u32[]{:S(2)}) %collective-permute-start.7) | collective-permute-done | bytes 557088 | tf_op jit(solution)/shard_map/ppermute | solution.py:50
  188.2 32.6 %collective-permute-done.11 = bf16[1,256,3072]{2,1,0:T(8,128)(2,1)} collective-permute-done((bf16[1,256,3072]{2,1,0:T(8,128)(2,1)}, bf16[1,256,3072]{2,1,0:T(8,128)(2,1)}, u32[]{:S(2)}, u32[]{:S(2)}) %collective-permute-start.11) | collective-permute-done | bytes 1572896 | tf_op jit(solution)/shard_map/ppermute | solution.py:40
  236.2 28.2 %collective-permute-done.26.refs_0_ = bf16[512,2176]{1,0:T(8,128)(2,1)} collective-permute-done((bf16[512,2176]{1,0:T(8,128)(2,1)}, bf16[512,2176]{1,0:T(8,128)(2,1)}, u32[]{:S(2)}, u32[]{:S(2)}) %collective-permute-start.26) | collective-permute-done | bytes 2228256 | tf_op jit(solution)/shard_map/ppermute | solution.py:40
  322.5 8.9 %front.2 = (bf16[640,2048]{1,0:T(8,128)(2,1)}, f32[640,1024]{1,0:T(8,128)}) custom-call(s32[1]{0:T(128)} %bitcast.50.me, bf16[512,2176]{1,0:T(8,128)(2,1)} %pad_maximum_fusion.4.refs_0_, bf16[512,2176]{1,0:T(8,128)(2,1)} %collective-permute-done.17.refs_1_, s32[8,128]{1,0:T(8,128)} %select_convert_fusion.1.refs_2_.refs_5_.pos, ...), custom_call_target="tpu_custom_call" | custom-call | flops 2684354560 | bytes 12058624 | tf_op jit(solution)/shard_map/front/pallas_call | solution.py:255
  331.5 25.8 %expert.2 = (bf16[128,2176]{1,0:T(8,128)(2,1)}, bf16[128,2176]{1,0:T(8,128)(2,1)}, bf16[128,2176]{1,0:T(8,128)(2,1)}, bf16[128,2176]{1,0:T(8,128)(2,1)}, bf16[51...) custom-call(s32[2]{0:T(128)} %pad_add_fusion.expert, ...), custom_call_target="tpu_custom_call" | custom-call | flops 10737418240 | bytes 24117248 | tf_op jit(solution)/shard_map/expert/pallas_call | solution.py:368
  377.5 10.4 %result.3 = (bf16[512,2048]{1,0:T(8,128)(2,1)}, bf16[512,2048]{1,0:T(8,128)(2,1)}) custom-call(s32[1]{0:T(128)} %bitcast.50.me, bf16[640,1024]{1,0:T(8,128)(2,1)} %get-tuple-element.112.refs_4_.gact, bf16[2048,3072]{1,0:T(8,128)(2,1)} %bitcast_dynamic-update-slice_fusion.refs_3_.refs_8_.refs_9_.refs_10_.wd, s32[8,128]{1,0:T(8,128)} %select_convert_fusion.1.refs_2_.refs_5_.pos), custom_call_target="tpu_custom_call" | custom-call | flops 2684354560 | bytes 8388608 | tf_op jit(solution)/shard_map/result/pallas_call | solution.py:419
  388.3 26.0 %expert.3 = (bf16[128,2176]{1,0:T(8,128)(2,1)}, bf16[128,2176]{1,0:T(8,128)(2,1)}, bf16[128,2176]{1,0:T(8,128)(2,1)}, bf16[128,2176]{1,0:T(8,128)(2,1)}, bf16[25...) custom-call(s32[2]{0:T(128)} %pad_add_fusion.expert, ...), custom_call_target="tpu_custom_call" | custom-call | flops 10737418240 | bytes 24117248 | tf_op jit(solution)/shard_map/expert/pallas_call | solution.py:368
  414.9 10.2 %grads.3 = bf16[2,256,3072]{2,1,0:T(8,128)(2,1)} custom-call(bf16[640,2048]{1,0:T(8,128)(2,1)} %get-tuple-element.127.refs_0_, bf16[640,2048]{1,0:T(8,128)(2,1)} %get-tuple-element.128.refs_1_, bf16[640,1024]{1,0:T(8,128)(2,1)} %get-tuple-element.129.refs_2_, bf16[640,1024]{1,0:T(8,128)(2,1)} %get-tuple-element.130.refs_3_, ...), custom_call_target="tpu_custom_call" | custom-call | flops 4026531840 | bytes 11010048 | tf_op jit(solution)/shard_map/grads/pallas_call | solution.py:466
  426.9 15.6 %grads.5 = bf16[4,256,3072]{2,1,0:T(8,128)(2,1)} custom-call(bf16[640,2048]{1,0:T(8,128)(2,1)} %get-tuple-element.127.refs_0_, bf16[640,2048]{1,0:T(8,128)(2,1)} %get-tuple-element.128.refs_1_, bf16[640,1024]{1,0:T(8,128)(2,1)} %get-tuple-element.129.refs_2_, bf16[640,1024]{1,0:T(8,128)(2,1)} %get-tuple-element.130.refs_3_, ...), custom_call_target="tpu_custom_call" | custom-call | flops 8053063680 | bytes 14155776 | tf_op jit(solution)/shard_map/grads/pallas_call | solution.py:466
  445.9 10.3 %result.2 = (bf16[512,2048]{1,0:T(8,128)(2,1)}, bf16[512,2048]{1,0:T(8,128)(2,1)}) custom-call(s32[1]{0:T(128)} %bitcast.50.me, bf16[640,1024]{1,0:T(8,128)(2,1)} %get-tuple-element.135.refs_9_.gact, bf16[2048,3072]{1,0:T(8,128)(2,1)} %bitcast_dynamic-update-slice_fusion.refs_3_.refs_8_.refs_9_.refs_10_.wd, s32[8,128]{1,0:T(8,128)} %select_convert_fusion.refs_2_.refs_6_.pos), custom_call_target="tpu_custom_call" | custom-call | flops 2684354560 | bytes 8388608 | tf_op jit(solution)/shard_map/result/pallas_call | solution.py:419
  456.2 10.7 %grads.4 = bf16[2,256,3072]{2,1,0:T(8,128)(2,1)} custom-call(bf16[640,2048]{1,0:T(8,128)(2,1)} %get-tuple-element.127.refs_0_, bf16[640,2048]{1,0:T(8,128)(2,1)} %get-tuple-element.128.refs_1_, bf16[640,1024]{1,0:T(8,128)(2,1)} %get-tuple-element.129.refs_2_, bf16[640,1024]{1,0:T(8,128)(2,1)} %get-tuple-element.130.refs_3_, ...), custom_call_target="tpu_custom_call" | custom-call | flops 4026531840 | bytes 11010048 | tf_op jit(solution)/shard_map/grads/pallas_call | solution.py:466
  472.7 9.4 %collective-permute-done.32 = bf16[128,2176]{1,0:T(8,128)(2,1)S(1)} collective-permute-done((bf16[128,2176]{1,0:T(8,128)(2,1)}, bf16[128,2176]{1,0:T(8,128)(2,1)S(1)}, u32[]{:S(2)}, u32[]{:S(2)}) %collective-permute-start.32) | collective-permute-done | bytes 557088 | tf_op jit(solution)/shard_map/ppermute | solution.py:40
  508.3 8.9 %collective-permute-done.36 = bf16[128,2176]{1,0:T(8,128)(2,1)S(1)} collective-permute-done((bf16[128,2176]{1,0:T(8,128)(2,1)S(1)}, bf16[128,2176]{1,0:T(8,128)(2,1)S(1)}, u32[]{:S(2)}, u32[]{:S(2)}) %collective-permute-start.36) | collective-permute-done | bytes 557088 | tf_op jit(solution)/shard_map/ppermute | solution.py:50
  527.9 41.3 %collective-permute-done.40 = bf16[512,2048]{1,0:T(8,128)(2,1)} collective-permute-done((bf16[512,2048]{1,0:T(8,128)(2,1)}, bf16[512,2048]{1,0:T(8,128)(2,1)}, u32[]{:S(2)}, u32[]{:S(2)}) %collective-permute-start.40) | collective-permute-done | bytes 2097184 | tf_op jit(solution)/shard_map/ppermute | solution.py:40
  597.0 11.2 %psum.15 = f32[2,512]{1,0:T(2,128)S(1)} all-reduce(f32[2,512]{1,0:T(2,128)S(1)} %pad_maximum_fusion.35), channel_id=1, replica_groups=mesh['dp'=8,'expert'=4] {'expert'}, use_global_device_ids=true, to_apply=%region_25.26 | all-reduce | flops 1024 | bytes 8192 | tf_op jit(solution)/shard_map/psum | solution.py:786
  676.7 31.1 %collective-permute-done.50 = bf16[64,2048]{1,0:T(8,128)(2,1)S(1)} collective-permute-done((bf16[64,2048]{1,0:T(8,128)(2,1)S(1)}, bf16[64,2048]{1,0:T(8,128)(2,1)S(1)}, u32[]{:S(2)}, u32[]{:S(2)}) %collective-permute-start.50) | collective-permute-done | bytes 262176 | tf_op jit(solution)/shard_map/ppermute | solution.py:776
  708.7 42.2 %collective-permute-done.43 = bf16[512,768]{1,0:T(8,128)(2,1)} collective-permute-done((bf16[512,768]{1,0:T(8,128)(2,1)}, bf16[512,768]{1,0:T(8,128)(2,1)}, u32[]{:S(2)}, u32[]{:S(2)}) %collective-permute-start.43) | collective-permute-done | bytes 786464 | tf_op jit(solution)/shard_map/ppermute | solution.py:40
  779.5 12.6 %all-to-all-done.1 = bf16[4,64,1664]{2,1,0:T(8,128)(2,1)} async-done(((bf16[4,64,1664]{2,1,0:T(8,128)(2,1)}), bf16[4,64,1664]{2,1,0:T(8,128)(2,1)}, u32[]{:S(2)}, u32[]{:S(2)}) %all-to-all-start.1) | async-done | bytes 852000 | tf_op jit(solution)/shard_map/all_to_all | solution.py:821
  803.9 12.2 %copy.325 = f32[256,4,2048]{2,1,0:T(4,128)} copy(f32[256,4,2048]{2,0,1:T(8,128)} %maximum_convert_fusion) | data formatting | bytes 16777216
  (516 shorter events, 381.5 us)
Async XLA Ops:
  16.3 100.6 %all-gather.4.cloned.1.call-start = ((), (), s32[]{:S(2)}) async-start(), calls=%async_computation.5 | async-start | bytes 7667712 | tf_op jit(solution)/shard_map/all_gather | solution.py:610
  40.2 138.5 %all-gather.6.cloned.1.call-start = ((), (), s32[]{:S(2)}) async-start(), calls=%async_computation.6 | async-start | bytes 2359296 | tf_op jit(solution)/shard_map/all_gather | solution.py:620
  45.7 45.3 %collective-permute-start.4 = (bf16[2,256,3072]{2,1,0:T(8,128)(2,1)}, bf16[2,256,3072]{2,1,0:T(8,128)(2,1)}, u32[]{:S(2)}, u32[]{:S(2)}) collective-permute-start(bf16[2,256,3072]{2,1,0:T(8,128)(2,1)} %pad_maximum_fusion.1), channel_id=1, source_target_pairs={{0,4},{4,0},{8,12},{12,8},{16,20},{20,16},{24,28},{28,24},{1,5},{5... | collective-permute-start | bytes 9437192 | tf_op jit(solution)/shard_map/ppermute | solution.py:40
  45.7 70.1 %collective-permute-start.5 = (bf16[1,256,3072]{2,1,0:T(8,128)(2,1)}, bf16[1,256,3072]{2,1,0:T(8,128)(2,1)}, u32[]{:S(2)}, u32[]{:S(2)}) collective-permute-start(bf16[1,256,3072]{2,1,0:T(8,128)(2,1)} %get-tuple-element.269), channel_id=1, source_target_pairs={{0,16},{4,20},{8,24},{12,28},{16,0},{20,4},{24,8},{28,12},{1,17},{... | collective-permute-start | bytes 4718600 | tf_op jit(solution)/shard_map/ppermute | solution.py:40
  117.4 108.5 %reduce-scatter.4.cloned.1.call-start = ((), (), s32[]{:S(2)}) async-start(), calls=%async_computation.7 | async-start | bytes 2621440 | tf_op jit(solution)/shard_map/reduce_scatter | solution.py:675
  183.0 386.3 %all-gather.8.cloned.1.call-start = ((), (), s32[]{:S(2)}) async-start(), calls=%async_computation.8 | async-start | bytes 2621440 | tf_op jit(solution)/shard_map/all_gather | solution.py:762
  185.1 79.4 %collective-permute-start.26 = (bf16[512,2176]{1,0:T(8,128)(2,1)}, bf16[512,2176]{1,0:T(8,128)(2,1)}, u32[]{:S(2)}, u32[]{:S(2)}) collective-permute-start(bf16[512,2176]{1,0:T(8,128)(2,1)} %pad_maximum_fusion.4.refs_0_), channel_id=1, source_target_pairs={{0,8},{4,12},{8,0},{12,4},{16,24},{20,28},{24,16},{28,20},{1,9},{5... | collective-permute-start | bytes 6684680 | tf_op jit(solution)/shard_map/ppermute | solution.py:40
  186.8 80.2 %collective-permute-start.17 = (bf16[512,2176]{1,0:T(8,128)(2,1)}, bf16[512,2176]{1,0:T(8,128)(2,1)}, u32[]{:S(2)}, u32[]{:S(2)}) collective-permute-start(bf16[512,2176]{1,0:T(8,128)(2,1)} %pad_maximum_fusion.4.refs_0_), channel_id=1, source_target_pairs={{0,4},{4,0},{8,12},{12,8},{16,20},{20,16},{24,28},{28,24},{1,5},{5... | collective-permute-start | bytes 6684680 | tf_op jit(solution)/shard_map/ppermute | solution.py:40
  230.1 40.5 %collective-permute-start.13 = (bf16[128,2048]{1,0:T(8,128)(2,1)}, bf16[128,2048]{1,0:T(8,128)(2,1)}, u32[]{:S(2)}, u32[]{:S(2)}) collective-permute-start(bf16[128,2048]{1,0:T(8,128)(2,1)} %multiply_convert_fusion.1.refs_0_), channel_id=1, source_target_pairs={{0,2},{2,3},{3,1},{1,0},{4,6},{6,7},{7,5},{5,4},{8,10},{10,11},{11... | collective-permute-start | bytes 1572872 | tf_op jit(solution)/shard_map/ppermute | solution.py:50
  269.6 39.9 %collective-permute-start.27 = (bf16[512,2176]{1,0:T(8,128)(2,1)}, bf16[512,2176]{1,0:T(8,128)(2,1)S(1)}, u32[]{:S(2)}, u32[]{:S(2)}) collective-permute-start(bf16[512,2176]{1,0:T(8,128)(2,1)} %collective-permute-done.26.refs_0_), channel_id=1, source_target_pairs={{0,4},{4,0},{8,12},{12,8},{16,20},{20,16},{24,28},{28,24},{1,5},{5... | collective-permute-start | bytes 6684680 | tf_op jit(solution)/shard_map/ppermute | solution.py:40
  270.3 87.0 %collective-permute-start.20 = (bf16[128,2048]{1,0:T(8,128)(2,1)}, bf16[128,2048]{1,0:T(8,128)(2,1)}, u32[]{:S(2)}, u32[]{:S(2)}) collective-permute-start(bf16[128,2048]{1,0:T(8,128)(2,1)} %multiply_convert_fusion.1.refs_0_), channel_id=1, source_target_pairs={{0,8},{4,12},{8,0},{12,4},{16,24},{20,28},{24,16},{28,20},{1,9},{5... | collective-permute-start | bytes 1572872 | tf_op jit(solution)/shard_map/ppermute | solution.py:40
  273.7 44.4 %collective-permute-start.18 = (bf16[1,256,3072]{2,1,0:T(8,128)(2,1)}, bf16[1,256,3072]{2,1,0:T(8,128)(2,1)}, u32[]{:S(2)}, u32[]{:S(2)}) collective-permute-start(bf16[1,256,3072]{2,1,0:T(8,128)(2,1)} %bitcast.55), channel_id=1, source_target_pairs={{0,16},{4,20},{8,24},{12,28},{16,0},{20,4},{24,8},{28,12},{1,17},{... | collective-permute-start | bytes 4718600 | tf_op jit(solution)/shard_map/ppermute | solution.py:40
  316.1 41.2 %collective-permute-start.21 = (bf16[128,2048]{1,0:T(8,128)(2,1)}, bf16[128,2048]{1,0:T(8,128)(2,1)S(1)}, u32[]{:S(2)}, u32[]{:S(2)}) collective-permute-start(bf16[128,2048]{1,0:T(8,128)(2,1)} %collective-permute-done.13.refs_1_), channel_id=1, source_target_pairs={{0,8},{4,12},{8,0},{12,4},{16,24},{20,28},{24,16},{28,20},{1,9},{5... | collective-permute-start | bytes 1572872 | tf_op jit(solution)/shard_map/ppermute | solution.py:40
  377.5 89.4 %collective-permute-start.19 = (bf16[512,2176]{1,0:T(8,128)(2,1)}, bf16[512,2176]{1,0:T(8,128)(2,1)}, u32[]{:S(2)}, u32[]{:S(2)}) collective-permute-start(bf16[512,2176]{1,0:T(8,128)(2,1)} %get-tuple-element.111), channel_id=1, source_target_pairs={{0,4},{4,0},{8,12},{12,8},{16,20},{20,16},{24,28},{28,24},{1,5},{5... | collective-permute-start | bytes 6684680 | tf_op jit(solution)/shard_map/ppermute | solution.py:40
  387.9 100.7 %collective-permute-start.39 = (bf16[512,2048]{1,0:T(8,128)(2,1)}, bf16[512,2048]{1,0:T(8,128)(2,1)}, u32[]{:S(2)}, u32[]{:S(2)}) collective-permute-start(bf16[512,2048]{1,0:T(8,128)(2,1)} %get-tuple-element.139), channel_id=1, source_target_pairs={{0,4},{4,0},{8,12},{12,8},{16,20},{20,16},{24,28},{28,24},{1,5},{5... | collective-permute-start | bytes 6291464 | tf_op jit(solution)/shard_map/ppermute | solution.py:40
  414.4 55.7 %collective-permute-start.28 = (bf16[256,2176]{1,0:T(8,128)(2,1)}, bf16[256,2176]{1,0:T(8,128)(2,1)S(1)}, u32[]{:S(2)}, u32[]{:S(2)}) collective-permute-start(bf16[256,2176]{1,0:T(8,128)(2,1)} %get-tuple-element.119), channel_id=1, source_target_pairs={{0,4},{4,0},{8,12},{12,8},{16,20},{20,16},{24,28},{28,24},{1,5},{5... | collective-permute-start | bytes 3342344 | tf_op jit(solution)/shard_map/ppermute | solution.py:40
  425.1 93.7 %collective-permute-start.37 = (bf16[2,256,3072]{2,1,0:T(8,128)(2,1)}, bf16[2,256,3072]{2,1,0:T(8,128)(2,1)S(1)}, u32[]{:S(2)}, u32[]{:S(2)}) collective-permute-start(bf16[2,256,3072]{2,1,0:T(8,128)(2,1)} %grads.3), channel_id=1, source_target_pairs={{0,16},{4,20},{8,24},{12,28},{16,0},{20,4},{24,8},{28,12},{1,17},{... | collective-permute-start | bytes 9437192 | tf_op jit(solution)/shard_map/ppermute | solution.py:40
  523.8 250.6 %reduce-scatter.8.cloned.1.call-start = ((), (), s32[]{:S(2)}) async-start(), calls=%async_computation.10 | async-start | bytes 2621440 | tf_op jit(solution)/shard_map/reduce_scatter | solution.py:796
  523.8 45.4 %collective-permute-start.40 = (bf16[512,2048]{1,0:T(8,128)(2,1)}, bf16[512,2048]{1,0:T(8,128)(2,1)}, u32[]{:S(2)}, u32[]{:S(2)}) collective-permute-start(bf16[512,2048]{1,0:T(8,128)(2,1)} %add_convert_fusion.3), channel_id=1, source_target_pairs={{0,8},{4,12},{8,0},{12,4},{16,24},{20,28},{24,16},{28,20},{1,9},{5... | collective-permute-start | bytes 6291464 | tf_op jit(solution)/shard_map/ppermute | solution.py:40
  524.4 100.4 %collective-permute-start.41 = (bf16[2,256,3072]{2,1,0:T(8,128)(2,1)}, bf16[2,256,3072]{2,1,0:T(8,128)(2,1)}, u32[]{:S(2)}, u32[]{:S(2)}) collective-permute-start(bf16[2,256,3072]{2,1,0:T(8,128)(2,1)} %grads.4), channel_id=1, source_target_pairs={{0,16},{4,20},{8,24},{12,28},{16,0},{20,4},{24,8},{28,12},{1,17},{... | collective-permute-start | bytes 9437192 | tf_op jit(solution)/shard_map/ppermute | solution.py:40
  618.7 157.1 %reduce-scatter.6.cloned.1.call-start = ((), (), s32[]{:S(2)}) async-start(), calls=%async_computation.9 | async-start | bytes 2621440 | tf_op jit(solution)/shard_map/reduce_scatter | solution.py:765
  649.0 105.8 %collective-permute-start.51 = (bf16[2,256,3072]{2,1,0:T(8,128)(2,1)}, bf16[2,256,3072]{2,1,0:T(8,128)(2,1)}, u32[]{:S(2)}, u32[]{:S(2)}) collective-permute-start(bf16[2,256,3072]{2,1,0:T(8,128)(2,1)} %pad_maximum_fusion.2), channel_id=1, source_target_pairs={{0,8},{4,12},{8,0},{12,4},{16,24},{20,28},{24,16},{28,20},{1,9},{5... | collective-permute-start | bytes 9437192 | tf_op jit(solution)/shard_map/ppermute | solution.py:40
  670.1 80.8 %collective-permute-start.43 = (bf16[512,768]{1,0:T(8,128)(2,1)}, bf16[512,768]{1,0:T(8,128)(2,1)}, u32[]{:S(2)}, u32[]{:S(2)}) collective-permute-start(bf16[512,768]{1,0:T(8,128)(2,1)} %pad_maximum_fusion.20), channel_id=1, source_target_pairs={{0,8},{4,12},{8,0},{12,4},{16,24},{20,28},{24,16},{28,20},{1,9},{5... | collective-permute-start | bytes 2359304 | tf_op jit(solution)/shard_map/ppermute | solution.py:40
  670.6 81.5 %collective-permute-start.45 = (bf16[512,896]{1,0:T(8,128)(2,1)S(1)}, bf16[512,896]{1,0:T(8,128)(2,1)S(1)}, u32[]{:S(2)}, u32[]{:S(2)}) collective-permute-start(bf16[512,896]{1,0:T(8,128)(2,1)S(1)} %concatenate.129), channel_id=1, source_target_pairs={{0,16},{4,20},{8,24},{12,28},{16,0},{20,4},{24,8},{28,12},{1,17},{... | collective-permute-start | bytes 2752520 | tf_op jit(solution)/shard_map/ppermute | solution.py:40
  (127 other events, 1508.8 us)
Sparse Core Ops, SparseCore 0:
  40.3 76.5 all-gather.3
  118.8 28.0 all-gather.5
  183.1 42.7 reduce-scatter.3
  523.9 45.1 all-gather.7
  618.8 40.8 reduce-scatter.7
  661.9 52.1 reduce-scatter.5

commit v3 on v2

v3 whole, which is shorter than its diff:
```python
import functools

import jax
import jax.numpy as jnp
from jax import lax
from jax.experimental import pallas as pl
from jax.experimental.pallas import tpu as pltpu
from jax.sharding import PartitionSpec as P

HEADS = 16
HEAD_DIM = 128
SEQ_DEV = 2
EPSILON = 1e-06
ROPE_BASE = 50000.0
CAP = 80
EXTRA = 128
VMEM = 56 * 2**20
COST = pl.CostEstimate(flops=10**6, bytes_accessed=10**5, transcendentals=0)

F32 = jnp.float32
BF16 = jnp.bfloat16


def dot(a, b, dims, out=F32):
    return lax.dot_general(a, b, (dims, ((), ())), preferred_element_type=F32).astype(out)


def nn(a, b, out=F32):
    return dot(a, b, ((1,), (0,)), out)


def nt(a, b, out=F32):
    return dot(a, b, ((1,), (1,)), out)


def tn(a, b, out=F32):
    return dot(a, b, ((0,), (0,)), out)


def flip(v, bit):
    return lax.ppermute(v, "dp", [(i, i ^ bit) for i in range(lax.axis_size("dp"))])


def ring(n):
    return [*range(0, n, 2), *reversed(range(1, n, 2))]


def hop(v, step=1):
    order = ring(lax.axis_size("expert"))
    n = len(order)
    pairs = [(order[i], order[(i + step) % n]) for i in range(n)]
    return lax.ppermute(v, "expert", pairs)


def gather_ring(v):
    return [v] + [hop(v, i) for i in range(1, lax.axis_size("expert"))]


def places_in_ring():
    n = lax.axis_size("expert")
    at = [ring(n).index(i) for i in range(n)]
    at = jnp.asarray(at, jnp.int32)
    return lax.rem(at[lax.axis_index("expert")] - at + n, n)


def by_line(blocks):
    where = places_in_ring()
    stacked = jnp.stack(blocks)
    return jnp.concatenate([pick(stacked, where[i], 0) for i in range(len(blocks))], axis=0)


def bits_of(low, high):
    out = []
    while low < high:
        out.append(low)
        low *= 2
    return out


def pick(v, index, axis):
    return lax.dynamic_index_in_dim(v, index, axis, keepdims=False)


def tie(*values):
    return lax.optimization_barrier(values)


class Flow:
    def __init__(self):
        self.of = {}

    def fence(self, *keys):
        out = tie(*[self.of[key] for key in keys])
        for key, v in zip(keys, out, strict=True):
            self.of[key] = v

    def __getitem__(self, key):
        return self.of[key]

    def __setitem__(self, key, value):
        self.of[key] = value

    def having(self, kind):
        return [key for key in self.of if isinstance(key, tuple) and key[0] == kind]


def fan(pieces, low):
    out = [list(pieces)]
    for bit in bits_of(1, low):
        out = out + [[flip(x, bit) for x in xs] for xs in out]
    return out


def add(a, b):
    return (a.astype(F32) + b.astype(F32)).astype(BF16)


def match(pieces, like):
    if len(pieces) == len(like):
        return pieces
    step = like[0].shape[0]
    return [x[i : i + step] for x in pieces for i in range(0, x.shape[0], step)]


def fold(parts):
    parts = list(parts)
    while len(parts) > 1:
        half = len(parts) // 2
        for i in range(half):
            got = match([flip(x, half) for x in reversed(parts[half + i])][::-1], parts[i])
            parts[i] = [add(a, b) for a, b in zip(parts[i], got, strict=True)]
        parts = parts[:half]
    return parts[0]


def scatter_dp(part, rows):
    n = lax.axis_size("dp")
    held = [part[r * rows : (r + 1) * rows] for r in range(n)]
    for bit in bits_of(1, n):
        odd = jnp.concatenate(held[1::2], axis=0) if len(held) > 2 else held[1]
        got = flip(odd, bit)
        held = [add(v, got[i * rows : (i + 1) * rows]) for i, v in enumerate(held[::2])]
    return held[0]


def blocks_of(parts, tok):
    return [(i, at) for i, p in enumerate(parts) for at in range(0, p.shape[0], tok)]


def onehot_back(pos_t, b):
    slot = lax.broadcasted_iota(jnp.int32, (pos_t.shape[0], CAP), 1)
    return (slot == pos_t[:, b : b + 1]).astype(BF16)


def onehot(pos_ref, b):
    slot = lax.broadcasted_iota(jnp.int32, (CAP, pos_ref.shape[1]), 0)
    return slot == pos_ref[b : b + 1, :]


def mm(a, b, dims):
    return lax.dot_general(a, b, (dims, ((), ())), preferred_element_type=F32)


def front_kernel(count, me, *refs):
    parts, (pos, wd, rows_out, gw) = refs[:count], refs[count:]
    tok = pos.shape[1]
    width = rows_out.shape[1]

    @pl.when(pl.program_id(0) == 0)
    def _():
        for b, (i, at) in enumerate(blocks_of(parts, tok)):
            part = parts[i][at : at + tok, :width]
            hot = onehot(pos, b).astype(BF16)
            found = mm(hot, part, ((1,), (0,))).astype(BF16)
            to_distance(rows_out, slice(b * CAP, (b + 1) * CAP), found, me[0])

    gw[...] = mm(rows_out[...], wd[...], ((1,), (0,)))


def front(parts, pos, weights, ff, me):
    count, width = len(parts), weights.shape[0]
    slots = pos.shape[0] * CAP
    tile = min(256, ff)
    first = (weights.shape[1] - ff) // tile
    whole = lambda x: pl.BlockSpec(x.shape, lambda n, me: (0, 0))
    return pl.pallas_call(
        functools.partial(front_kernel, count),
        grid_spec=pltpu.PrefetchScalarGridSpec(
            num_scalar_prefetch=1,
            grid=(ff // tile,),
            in_specs=[whole(x) for x in parts]
            + [whole(pos), pl.BlockSpec((width, tile), lambda n, me: (0, first + n))],
            out_specs=[
                pl.BlockSpec((slots, width), lambda n, me: (0, 0)),
                pl.BlockSpec((slots, tile), lambda n, me: (0, n)),
            ],
        ),
        out_shape=[
            jax.ShapeDtypeStruct((slots, width), BF16),
            jax.ShapeDtypeStruct((slots, ff), F32),
        ],
        compiler_params=pltpu.CompilerParams(vmem_limit_bytes=VMEM),
        cost_estimate=COST,
        name="front",
    )(me, *parts, pos, weights)


def to_distance(ref, rows, value, me):
    n = lax.axis_size("dp")
    wide = value.shape[1] // n
    for c in range(n):
        at = pl.multiple_of((me ^ c) * wide, wide)
        ref[rows, pl.ds(at, wide)] = value[:, c * wide : (c + 1) * wide]


def expert_kernel(count, expert, *refs):
    parts = refs[:count]
    pos, pos_t, named, router, wg, wu, gw = refs[count : count + 7]
    backs = refs[count + 7 : 2 * count + 7]
    rows_out, dg_out, du_out, gact_out, acc, gate, dgate = refs[2 * count + 7 :]
    n = pl.program_id(0)
    tok = pos.shape[1]
    width = rows_out.shape[1]
    experts = router.shape[0]

    @pl.when(n == 0)
    def _():
        for b, (i, first) in enumerate(blocks_of(parts, tok)):
            at = slice(b * CAP, (b + 1) * CAP)
            part = parts[i][first : first + tok, :]
            hot = onehot(pos, b)
            found = mm(hot.astype(BF16), part, ((1,), (0,))).astype(BF16)
            to_distance(rows_out, at, found, expert[1])
            chosen = named[b] > 0
            logits = jnp.where(chosen, mm(router[...], part, ((1,), (1,))), -1e30)
            e = jnp.where(chosen, jnp.exp(logits - jnp.max(logits, axis=0, keepdims=True)), 0.0)
            gates = e / jnp.sum(e, axis=0, keepdims=True)
            mine = lax.broadcasted_iota(jnp.int32, gates.shape, 0) == expert[0]
            row = jnp.sum(jnp.where(mine, gates, 0.0), axis=0, keepdims=True)
            gate[at, :] = jnp.sum(jnp.where(hot, row, 0.0), axis=1, keepdims=True)
            dgate[at, :] = jnp.zeros((CAP, 1), F32)

    rows = rows_out[...]
    g = mm(rows, wg[...], ((1,), (0,)))
    u = mm(rows, wu[...], ((1,), (0,)))
    sg = 1.0 / (1.0 + jnp.exp(-g))
    silu = g * sg
    act = (silu * u).astype(BF16).astype(F32)
    gw_v = gw[...]
    dgate[...] += jnp.sum(act * gw_v, axis=1, keepdims=True)
    gate_v = gate[...]
    gact_out[...] = (gate_v * act).astype(BF16)
    dact = gate_v * gw_v
    dg = (dact * u * (sg * (1.0 + g * (1.0 - sg)))).astype(BF16)
    du = (dact * silu).astype(BF16)
    dg_out[...] = dg
    du_out[...] = du
    back = mm(dg, wg[...], ((1,), (1,))) + mm(du, wu[...], ((1,), (1,)))

    @pl.when(n == 0)
    def _():
        acc[...] = back

    @pl.when(n > 0)
    def _():
        acc[...] += back

    @pl.when(n == pl.num_programs(0) - 1)
    def _():
        lane = lax.broadcasted_iota(jnp.int32, (CAP, EXTRA), 1)
        for b, (i, first) in enumerate(blocks_of(parts, tok)):
            at = slice(b * CAP, (b + 1) * CAP)
            to = slice(first, first + tok)
            hot = onehot_back(pos_t, b)
            out = backs[i]
            found = mm(hot, acc[at, :].astype(BF16), ((1,), (0,))).astype(BF16)
            to_distance(out, to, found, expert[1])
            d = dgate[at, :]
            hi = d.astype(BF16).astype(F32)
            beside = jnp.where(
                lane == expert[0], hi, jnp.where(lane == experts + expert[0], d - hi, 0.0)
            ).astype(BF16)
            out[to, width:] = mm(hot, beside, ((1,), (0,))).astype(BF16)


def run_expert(parts, pos, pos_t, named, router, weights, gw, expert, ff):
    count, width = len(parts), weights.shape[0]
    slots = pos.shape[0] * CAP
    tile = min(256, ff)
    steps = ff // tile
    whole = lambda x: pl.BlockSpec(x.shape, lambda n, e: (0,) * x.ndim)
    column = pl.BlockSpec((slots, tile), lambda n, e: (0, n))
    backs = [jax.ShapeDtypeStruct((x.shape[0], width + EXTRA), BF16) for x in parts]
    thin = jax.ShapeDtypeStruct((slots, ff), BF16)
    outs = pl.pallas_call(
        functools.partial(expert_kernel, count),
        grid_spec=pltpu.PrefetchScalarGridSpec(
            num_scalar_prefetch=1,
            grid=(steps,),
            in_specs=[whole(x) for x in parts]
            + [
                whole(pos),
                whole(pos_t),
                whole(named),
                whole(router),
                pl.BlockSpec((width, tile), lambda n, e: (0, n)),
                pl.BlockSpec((width, tile), lambda n, e: (0, steps + n)),
                column,
            ],
            out_specs=[whole(x) for x in backs]
            + [pl.BlockSpec((slots, width), lambda n, e: (0, 0)), column, column, column],
            scratch_shapes=[
                pltpu.VMEM((slots, width), F32),
                pltpu.VMEM((slots, 1), F32),
                pltpu.VMEM((slots, 1), F32),
            ],
        ),
        out_shape=backs
        + [jax.ShapeDtypeStruct((slots, width), BF16), thin, thin, thin],
        compiler_params=pltpu.CompilerParams(vmem_limit_bytes=VMEM),
        cost_estimate=COST,
        name="expert",
    )(expert, *parts, pos, pos_t, named, router, weights, weights, gw)
    return outs[:count], outs[count:]


def result_kernel(count, me, gact, wd, pos_t, *outs):
    tok = pos_t.shape[0]
    y = mm(gact[...], wd[...], ((1,), (1,))).astype(BF16)
    for b, (i, at) in enumerate(blocks_of(outs, tok)):
        outs[i][at : at + tok, :] = mm(
            onehot_back(pos_t, b), y[b * CAP : (b + 1) * CAP, :], ((1,), (0,))
        ).astype(BF16)


def result(gact, pos_t, weights, count, me):
    slots, ff = gact.shape
    width = weights.shape[0]
    tile = width // lax.axis_size("dp")
    last = (weights.shape[1] - ff) // ff
    out = jax.ShapeDtypeStruct((pos_t.shape[1] // count * pos_t.shape[0], width), BF16)
    return pl.pallas_call(
        functools.partial(result_kernel, count),
        grid_spec=pltpu.PrefetchScalarGridSpec(
            num_scalar_prefetch=1,
            grid=(width // tile,),
            in_specs=[
                pl.BlockSpec((slots, ff), lambda n, me: (0, 0)),
                pl.BlockSpec((tile, ff), lambda n, me: (n, last)),
                pl.BlockSpec(pos_t.shape, lambda n, me: (0, 0)),
            ],
            out_specs=[pl.BlockSpec((out.shape[0], tile), lambda n, me: (0, me[0] ^ n))] * count,
        ),
        out_shape=[out] * count,
        compiler_params=pltpu.CompilerParams(vmem_limit_bytes=VMEM),
        cost_estimate=COST,
        name="result",
    )(me, gact, weights, pos_t)


def grads_kernel(count, *refs):
    out = refs[-1]
    ff = refs[2].shape[1]
    gate = up = down = 0.0
    for c in range(count):
        rows, gs, dg, du, gact = refs[5 * c : 5 * c + 5]
        gate = gate + mm(rows[...], dg[...], ((0,), (0,)))
        up = up + mm(rows[...], du[...], ((0,), (0,)))
        down = down + mm(gs[...], gact[...], ((0,), (0,)))
    out[0, :, :ff] = gate.astype(BF16)
    out[0, :, ff : 2 * ff] = up.astype(BF16)
    out[0, :, 2 * ff :] = down.astype(BF16)


def grads(chunks, first, blocks, rows):
    ff = chunks[0][2].shape[1]
    specs, ins = [], []
    for chunk in chunks:
        slots = chunk[0].shape[0]
        tall = pl.BlockSpec((slots, rows), lambda i: (0, first + i))
        flat = pl.BlockSpec((slots, ff), lambda i: (0, 0))
        specs += [tall, tall, flat, flat, flat]
        ins += list(chunk)
    slots = sum(chunk[0].shape[0] for chunk in chunks)
    return pl.pallas_call(
        functools.partial(grads_kernel, len(chunks)),
        grid=(blocks,),
        in_specs=specs,
        out_specs=pl.BlockSpec((1, rows, 3 * ff), lambda i: (i, 0, 0)),
        out_shape=jax.ShapeDtypeStruct((blocks, rows, 3 * ff), BF16),
        compiler_params=pltpu.CompilerParams(vmem_limit_bytes=VMEM),
        cost_estimate=COST,
        name="grads",
    )(*ins)


def attn_grads_kernel(me, a, d, *rest):
    k = d.shape[1]
    out = rest[-1]
    out[:, :k] = mm(a[...], d[...], ((0,), (0,))).astype(BF16)
    if len(rest) > 1:
        out[:, k:] = rest[0][...]


def attn_grads(a, d, extra, me, first, stride):
    rows, width = a.shape
    n = lax.axis_size("dp")
    tile = width // n
    count = n // stride
    at = lambda i, me: me[0] ^ (first + stride * i)
    k = d.shape[1] + sum(e.shape[1] for e in extra)
    return pl.pallas_call(
        attn_grads_kernel,
        grid_spec=pltpu.PrefetchScalarGridSpec(
            num_scalar_prefetch=1,
            grid=(count,),
            in_specs=[
                pl.BlockSpec((rows, tile), lambda i, me: (0, at(i, me))),
                pl.BlockSpec(d.shape, lambda i, me: (0, 0)),
            ]
            + [pl.BlockSpec((tile, e.shape[1]), lambda i, me: (at(i, me), 0)) for e in extra],
            out_specs=pl.BlockSpec((tile, k), lambda i, me: (i, 0)),
        ),
        out_shape=jax.ShapeDtypeStruct((count * tile, k), BF16),
        compiler_params=pltpu.CompilerParams(vmem_limit_bytes=VMEM),
        cost_estimate=COST,
        name="attn_grads",
    )(me, a, d, *extra)


def halves(held, rows):
    n = lax.axis_size("dp")
    wide = held.shape[1] // 256 * 128
    out = []
    for left, right, order in (
        (0, wide, bits_of(2, n)),
        (wide, held.shape[1], bits_of(2, n)[::-1]),
    ):
        side = {2 * i: held[i * rows : (i + 1) * rows, left:right] for i in range(n // 2)}
        out.append((side, order))
    return out


def stage(at, sides, step):
    for s, (side, order) in enumerate(sides):
        keys = sorted(r for r in side if r & order[step])
        v = [side[r] for r in keys]
        at["side", s] = flip(jnp.concatenate(v, axis=0) if len(v) > 1 else v[0], order[step])


def unstage(at, sides, step):
    out = []
    for s, (side, order) in enumerate(sides):
        bit = order[step]
        keys = sorted(r for r in side if r & bit)
        rows = side[0].shape[0]
        got = at["side", s]
        kept = {r: v for r, v in side.items() if not r & bit}
        for i, r in enumerate(keys):
            kept[r ^ bit] = add(kept[r ^ bit], got[i * rows : (i + 1) * rows])
        out.append((kept, order))
    return out


def spread(first, n):
    local = len(first)
    have = {(0, e): v for e, v in first.items()}
    for bit in bits_of(1, local):
        for key in sorted(key for key in have if key[1] & bit):
            have[(key[0] ^ bit, key[1] ^ bit)] = flip(have.pop(key), bit)
    for bit in bits_of(local, n):
        for key in sorted(have):
            have[(key[0] ^ bit, 0)] = flip(have[key], bit)
    return jnp.concatenate([have[key] for key in sorted(have)], axis=0)


def gather_back(held, local, n):
    held = dict(held)
    for bit in reversed(bits_of(local, n // 2)):
        for r in sorted(r for r in held if r & bit):
            held[r ^ bit] = add(held[r ^ bit], flip(held.pop(r), bit))
    have = {(r, 0): v for r, v in held.items()}
    for bit in reversed(bits_of(1, local)):
        for key in sorted(key for key in have if key[0] & bit):
            have[(key[0] ^ bit, key[1] ^ bit)] = flip(have.pop(key), bit)
    return {e: v for (_, e), v in have.items()}


def per_row(row):
    return jnp.broadcast_to(row, (row.shape[1], row.shape[1])).T


def turn(v, cos, sin):
    return v * cos + pltpu.roll(v, v.shape[1] // 2, 1) * sin


def softmax_rows(qr, kr, same, scale):
    s = jnp.where(same, mm(qr, kr, ((1,), (1,))) * scale, -1e30)
    e = jnp.exp(s - jnp.max(s, axis=1, keepdims=True))
    return e / jnp.sum(e, axis=1, keepdims=True)


def attend_kernel(scale, qkv, r, gains, cos, sin, seg, qr_out, kr_out, vb_out, o_out):
    cols = o_out.shape[1]
    rq, rk = per_row(r[0, 0:1, :]), per_row(r[0, 1:2, :])
    seg_row = seg[0]
    same = per_row(seg_row) == seg_row
    for h in range(cols // HEAD_DIM):
        at = slice(h * HEAD_DIM, (h + 1) * HEAD_DIM)
        k_at = slice(cols + h * HEAD_DIM, cols + (h + 1) * HEAD_DIM)
        v_at = slice(2 * cols + h * HEAD_DIM, 2 * cols + (h + 1) * HEAD_DIM)
        qr = turn(qkv[:, at] * rq * gains[0:1, at], cos[...], sin[...]).astype(BF16)
        kr = turn(qkv[:, k_at] * rk * gains[1:2, at], cos[...], sin[...]).astype(BF16)
        vb = qkv[:, v_at].astype(BF16)
        p = softmax_rows(qr, kr, same, scale)
        qr_out[:, at] = qr
        kr_out[:, at] = kr
        vb_out[:, at] = vb
        o_out[:, at] = mm(p.astype(BF16), vb, ((1,), (0,))).astype(BF16)


def attend(qkv, r, gains, cos, sin, seg):
    total, cols = qkv.shape[0], qkv.shape[1] // 3
    zs, tok = seg.shape[0], seg.shape[2]
    tall = lambda w: pl.BlockSpec((tok, w), lambda b: (b, 0))
    fixed = lambda x: pl.BlockSpec(x.shape, lambda b: (0, 0))
    thin = jax.ShapeDtypeStruct((total, cols), BF16)
    return pl.pallas_call(
        functools.partial(attend_kernel, HEAD_DIM ** (-0.5)),
        grid=(zs,),
        in_specs=[
            tall(qkv.shape[1]),
            pl.BlockSpec((1, 2, tok), lambda b: (b, 0, 0)),
            fixed(gains),
            tall(HEAD_DIM),
            tall(HEAD_DIM),
            pl.BlockSpec((1, 1, tok), lambda b: (b, 0, 0)),
        ],
        out_specs=[tall(cols)] * 4,
        out_shape=[thin] * 4,
        compiler_params=pltpu.CompilerParams(vmem_limit_bytes=VMEM),
        cost_estimate=COST,
        name="attend",
    )(qkv, r, gains, cos, sin, seg)


def attend_back_kernel(
    scale, dhb, wo, q, k, qr, kr, vb, gains, cos, sin, seg, dq_out, dk_out, dv_out, sums
):
    cols = wo.shape[0]
    seg_row = seg[0]
    same = per_row(seg_row) == seg_row
    do_all = mm(dhb[...], wo[...], ((1,), (1,))).astype(BF16)
    sum_q = sum_k = 0.0
    for h in range(cols // HEAD_DIM):
        at = slice(h * HEAD_DIM, (h + 1) * HEAD_DIM)
        do = do_all[:, at]
        p = softmax_rows(qr[:, at], kr[:, at], same, scale)
        dp = mm(do, vb[:, at], ((1,), (1,)))
        ds = (p * (dp - jnp.sum(p * dp, axis=1, keepdims=True))).astype(BF16)
        dv_out[:, at] = mm(p.astype(BF16), do, ((0,), (0,))).astype(BF16)
        dq = turn(mm(ds, kr[:, at], ((1,), (0,))) * scale, cos[...], -sin[...])
        dk = turn(mm(ds, qr[:, at], ((0,), (0,))) * scale, cos[...], -sin[...])
        dq_out[:, at] = dq
        dk_out[:, at] = dk
        sum_q = sum_q + jnp.sum(q[:, at] * gains[0:1, at] * dq, axis=1, keepdims=True)
        sum_k = sum_k + jnp.sum(k[:, at] * gains[1:2, at] * dk, axis=1, keepdims=True)
    tok = dhb.shape[0]
    sums[0, 0:1, :] = jnp.broadcast_to(sum_q, (tok, tok)).T[0:1, :]
    sums[0, 1:2, :] = jnp.broadcast_to(sum_k, (tok, tok)).T[0:1, :]


def attend_back(dhb, wo, qkv, qr, kr, vb, gains, cos, sin, seg):
    total, cols = qkv.shape[0], wo.shape[0]
    zs, tok = seg.shape[0], seg.shape[2]
    tall = lambda w, at=0: pl.BlockSpec((tok, w), lambda b: (b, at))
    fixed = lambda x: pl.BlockSpec(x.shape, lambda b: (0, 0))
    wide = jax.ShapeDtypeStruct((total, cols), F32)
    return pl.pallas_call(
        functools.partial(attend_back_kernel, HEAD_DIM ** (-0.5)),
        grid=(zs,),
        in_specs=[
            tall(dhb.shape[1]),
            fixed(wo),
            tall(cols, 0),
            tall(cols, 1),
            tall(cols),
            tall(cols),
            tall(cols),
            fixed(gains),
            tall(HEAD_DIM),
            tall(HEAD_DIM),
            pl.BlockSpec((1, 1, tok), lambda b: (b, 0, 0)),
        ],
        out_specs=[tall(cols)] * 3 + [pl.BlockSpec((1, 2, tok), lambda b: (b, 0, 0))],
        out_shape=[
            wide,
            wide,
            jax.ShapeDtypeStruct((total, cols), BF16),
            jax.ShapeDtypeStruct((zs, 2, tok), F32),
        ],
        compiler_params=pltpu.CompilerParams(vmem_limit_bytes=VMEM),
        cost_estimate=COST,
        name="attend_back",
    )(dhb, wo, qkv, qkv, qr, kr, vb, gains, cos, sin, seg)


def join_back_kernel(q, k, dqn, dkn, dv, r, means, gains, out, gain_out):
    cols = dv.shape[1]
    for at, v, d in ((0, q, dqn), (1, k, dkn)):
        rr = per_row(r[0, at : at + 1, :])
        mean = per_row(means[0, at : at + 1, :])
        part = []
        for h in range(cols // HEAD_DIM):
            to = slice(h * HEAD_DIM, (h + 1) * HEAD_DIM)
            vr = v[:, to] * rr
            out[:, at * cols + h * HEAD_DIM : at * cols + (h + 1) * HEAD_DIM] = (
                rr * (gains[at : at + 1, to] * d[:, to]) - vr * (rr * rr) * mean
            ).astype(BF16)
            part.append(jnp.sum(d[:, to] * vr, axis=0, keepdims=True))
        row = jnp.concatenate(part, axis=1)

        @pl.when(pl.program_id(0) == 0)
        def _():
            gain_out[at : at + 1, :] = row

        @pl.when(pl.program_id(0) > 0)
        def _():
            gain_out[at : at + 1, :] += row

    out[:, 2 * cols :] = dv[...]


def join_back(qkv, dqn, dkn, dv, r, means, gains):
    total, cols = dv.shape
    zs, tok = r.shape[0], r.shape[2]
    tall = lambda w, at=0: pl.BlockSpec((tok, w), lambda b: (b, at))
    row = pl.BlockSpec((1, 2, tok), lambda b: (b, 0, 0))
    return pl.pallas_call(
        join_back_kernel,
        grid=(zs,),
        in_specs=[tall(cols, 0), tall(cols, 1), tall(cols), tall(cols), tall(cols), row, row]
        + [pl.BlockSpec(gains.shape, lambda b: (0, 0))],
        out_specs=[tall(3 * cols), pl.BlockSpec((2, cols), lambda b: (0, 0))],
        out_shape=[
            jax.ShapeDtypeStruct((total, 3 * cols), BF16),
            jax.ShapeDtypeStruct((2, cols), F32),
        ],
        compiler_params=pltpu.CompilerParams(vmem_limit_bytes=VMEM),
        cost_estimate=COST,
        name="join_back",
    )(qkv, qkv, dqn, dkn, dv, r, means, gains)


def first_back_kernel(d, w, x, r, da, gain):
    back = mm(d[...], w[...], ((1,), (1,)))
    da[...] = back.astype(BF16)
    row = jnp.sum(back * (x[...].astype(F32) * r[...]), axis=0, keepdims=True)

    @pl.when(pl.program_id(0) == 0)
    def _():
        gain[...] = row

    @pl.when(pl.program_id(0) > 0)
    def _():
        gain[...] += row


def first_back(d, w, x, r, tok):
    total, width = x.shape
    k = d.shape[1]
    return pl.pallas_call(
        first_back_kernel,
        grid=(total // tok,),
        in_specs=[
            pl.BlockSpec((tok, k), lambda b: (b, 0)),
            pl.BlockSpec((width, k), lambda b: (0, 0)),
            pl.BlockSpec((tok, width), lambda b: (b, 0)),
            pl.BlockSpec((tok, 1), lambda b: (b, 0)),
        ],
        out_specs=[
            pl.BlockSpec((tok, width), lambda b: (b, 0)),
            pl.BlockSpec((1, width), lambda b: (0, 0)),
        ],
        out_shape=[
            jax.ShapeDtypeStruct((total, width), BF16),
            jax.ShapeDtypeStruct((1, width), F32),
        ],
        compiler_params=pltpu.CompilerParams(vmem_limit_bytes=VMEM),
        cost_estimate=COST,
        name="first_back",
    )(d, w, x, r)


def inv_rms(v):
    return lax.rsqrt(jnp.mean(v * v, axis=-1, keepdims=True) + EPSILON)


def rms_back(v, r, gain, c):
    gc = gain * c
    return r * gc - v * (r * r * r) * jnp.mean(v * gc, axis=-1, keepdims=True)


def places_and_tables(at, dp, zs, rows):
    dealt = lax.dynamic_slice_in_dim(at["order"], dp * zs * SEQ_DEV, zs * SEQ_DEV)
    lens = jnp.take(at["lengths"], dealt).reshape(zs, SEQ_DEV)
    ends = jnp.cumsum(lens, axis=1)
    places = jnp.arange(rows, dtype=jnp.int32)
    segment = jnp.sum((places[None, :, None] >= ends[:, None, :]).astype(jnp.int32), axis=2)
    starts = ends - lens
    offset = jnp.sum(
        jnp.where(
            segment[:, :, None] == jnp.arange(SEQ_DEV, dtype=jnp.int32), starts[:, None, :], 0
        ),
        axis=2,
    )
    half = HEAD_DIM // 2
    inverse = ROPE_BASE ** (-2.0 * jnp.arange(half, dtype=F32) / HEAD_DIM)
    turned = (places[None] - offset).astype(F32)[..., None] * inverse
    at["cos"] = jnp.tile(jnp.cos(turned), (1, 1, 2)).reshape(zs * rows, HEAD_DIM)
    sin = jnp.sin(turned)
    at["sin"] = jnp.concatenate([-sin, sin], axis=2).reshape(zs * rows, HEAD_DIM)
    at["seg"] = segment.astype(F32)[:, None, :]


def on_device(
    tokens,
    lengths,
    permutation,
    routes,
    norm_gains,
    w_qkv,
    w_out,
    router,
    w_gate_up,
    w_down,
    cotangent,
):
    rows, width = tokens.shape
    zs = lax.axis_size("expert")
    dps = lax.axis_size("dp")
    z = lax.axis_index("expert")
    dp = lax.axis_index("dp")
    local = w_gate_up.shape[1]
    ff = w_down.shape[2]
    experts = router.shape[1]
    own_rows = w_qkv.shape[0]
    e_rows = w_gate_up.shape[0]
    cols = width // zs
    expert = z * local + lax.rem(dp, local)
    own = lax.rem(dp, local)
    top = local // 2
    far_bit = dps // 2
    mid = zs // 2
    laid_out = local == 4 and dps == 8
    me_at = jnp.reshape(dp, (1,)).astype(jnp.int32)
    expert_at = jnp.stack([expert, dp]).astype(jnp.int32)
    at = Flow()

    extra = jnp.concatenate(
        [router, norm_gains, jnp.zeros((own_rows, EXTRA - experts - 4), BF16)], axis=1
    )
    sent = jnp.stack(
        [
            jnp.concatenate(
                [w_qkv[:, i * width + e * cols : i * width + (e + 1) * cols] for i in range(3)]
                + [extra],
                axis=1,
            )
            for e in range(zs)
        ]
    )
    at["mine"] = lax.all_to_all(sent, "expert", split_axis=0, concat_axis=0, tiled=True)
    moved = [(b, (b % dps) * zs + b // dps) for b in range(dps * zs)]

    for e in range(local):
        at["w", 0, e] = jnp.concatenate(
            [pick(w_gate_up, own ^ e, 1), pick(w_down, own ^ e, 1)], axis=1
        )
    at["x0"] = tokens
    at["out"] = w_out
    at.fence("mine", "x0", "out", *at.having("w"))

    at["attn"] = lax.all_gather(
        at["mine"].reshape(zs * own_rows, 3 * cols + EXTRA), "dp", axis=0, tiled=True
    )
    if laid_out:
        at["w", 1, 0] = flip(at["w", 0, 1], 1)
        at["w", 1, 2] = flip(at["w", 0, 3], 1)
    at["lengths"], at["order"], at["routes"], at["cot"] = lengths, permutation, routes, cotangent
    for i in range(1, zs):
        at[f"x{i}"] = hop(at[f"x{i - 1}"])
        if i == 1:
            at.fence("x1", "lengths", "order", "routes", "cot", "out")
            places_and_tables(at, dp, zs, rows)
        elif i == 2:
            at.fence("x2", "cos", "sin", "seg", "routes", "cot")
            at["mask"] = jnp.sum(
                (at["routes"][:, :, None] == jnp.arange(experts, dtype=jnp.int32)).astype(BF16),
                axis=1,
            )
            mask_pad = jnp.concatenate(
                [at["mask"], jnp.zeros((rows, EXTRA - experts), BF16)], axis=1
            )
            at["g0"] = jnp.concatenate([at["cot"], mask_pad], axis=1)
            at["out"] = lax.ppermute(at["out"], ("dp", "expert"), moved)
        else:
            at.fence(f"x{i}")
    xs = [f"x{i}" for i in range(zs)]
    at.fence("attn", "out", "g0", "mask", *xs, *at.having("w"))

    cut = e_rows // 4
    if laid_out:
        at["w", 2, 0] = flip(at["w", 0, 2], 2)
        at["w", 4, 0] = flip(at["w", 0, 0], 4)
        at["wa", 5] = flip(at["w", 1, 0][:cut], 4)
    at["g1"] = hop(at["g0"])
    out_w = lax.all_gather(at["out"], "dp", axis=0, tiled=True)
    attn_w = at["attn"]
    qkv_w = attn_w[:, : 3 * cols]
    router_full = attn_w[:, 3 * cols : 3 * cols + experts]
    gains = attn_w[:, 3 * cols + experts : 3 * cols + experts + 4].astype(F32).T
    router_t = router_full.T
    x_all = by_line([at[key] for key in xs])
    xf = x_all.astype(F32)
    r_attn = inv_rms(xf)
    a_all = (xf * r_attn * gains[0]).astype(BF16)
    at["qkv"] = nn(a_all, qkv_w)
    at.fence("qkv", "g1")
    qkv = at["qkv"]
    q, k = qkv[:, :cols], qkv[:, cols : 2 * cols]
    at["squares"] = lax.psum(
        jnp.stack([jnp.sum(q * q, axis=1), jnp.sum(k * k, axis=1)]), "expert"
    )
    at.fence("squares", "g1")
    at["g2"] = hop(at["g1"])
    by_block = lambda v: v.reshape(2, zs, rows).transpose(1, 0, 2)
    r_qk = by_block(lax.rsqrt(at["squares"] / width + EPSILON))
    gain_qk = lax.dynamic_slice_in_dim(gains[1:3], z * cols, cols, axis=1)
    cos, sin, seg = at["cos"], at["sin"], at["seg"]
    qr, kr, vb, o = attend(qkv, r_qk, gain_qk, cos, sin, seg)
    at["added"] = nn(o, out_w, BF16)
    at.fence("added", "g2", *(w for w in at.having("w") + at.having("wa") if laid_out))
    at["added"] = lax.psum_scatter(at["added"], "expert", scatter_dimension=0, tiled=True)
    for i in range(3, zs):
        at[f"g{i}"] = hop(at[f"g{i - 1}"])
    if laid_out:
        at["w", 3, 0] = flip(at["w", 1, 2], 2)
        at["wb", 5] = flip(at["w", 1, 0][cut:], 4)
        at["wa", 6] = flip(at["w", 2, 0][: 3 * cut], 4)
    first_g = [f"g{i}" for i in range(mid)]
    last_g = [f"g{i}" for i in range(mid, zs)]
    at["far ga"] = flip(jnp.concatenate([at[key] for key in first_g], axis=0), top)
    weight_keys = at.having("w") + at.having("wa") + at.having("wb")
    at.fence("added", "far ga", f"g{zs - 1}", *(w for w in weight_keys if laid_out))
    at["far gb"] = flip(jnp.concatenate([at[key] for key in last_g], axis=0), top)
    if laid_out:
        at["wb", 6] = flip(at["w", 2, 0][3 * cut :], 4)
        at["w", 7, 0] = flip(at["w", 3, 0], 4)
    hid = tokens.astype(F32) + at["added"].astype(F32)
    r_ffn = inv_rms(hid)
    m = (hid * r_ffn * gains[3]).astype(BF16)

    at["m0"] = m
    at["far m0"] = flip(m, top)
    for i in range(1, zs):
        at[f"m{i}"] = hop(at[f"m{i - 1}"])
        at.fence(f"m{i}")
        at[f"far m{i}"] = flip(at[f"m{i}"], top)
    mine_e = (jnp.arange(experts) == expert).astype(F32)
    g_near = [jnp.concatenate([at[key] for key in first_g + last_g], axis=0)]
    near_parts = [x for xs in fan(g_near, top) for x in xs]
    far_parts = [x for xs in fan([at["far ga"], at["far gb"]], top) for x in xs]
    if laid_out:
        keys = [("w", r, 0) for r in range(5)] + [(h, r) for r in (5, 6) for h in ("wa", "wb")]
        weights = jnp.concatenate([at[key] for key in [*keys, ("w", 7, 0)]], axis=0)
    else:
        weights = spread({e: at["w", 0, e] for e in range(local)}, dps)

    def chunk_front(parts):
        masks = jnp.concatenate([x[:, width : width + experts] for x in parts], axis=0)
        masks = masks.astype(F32).reshape(-1, rows, experts)
        on = jnp.sum(masks * mine_e, axis=2)
        pos = jnp.where(on > 0, jnp.cumsum(on, axis=1) - 1.0, -1.0).astype(jnp.int32)
        gs, gw = front(parts, pos, weights, ff, me_at)
        return pos, pos.T, masks.transpose(0, 2, 1), gs, gw

    def chunk_expert(blocks, pieces, fronted):
        pos, pos_t, named, gs, gw = fronted
        parts = [blocks] + fan(pieces, top)[1:]
        flat = [x for xs in parts for x in xs]
        backs, outs = run_expert(flat, pos, pos_t, named, router_t, weights, gw, expert_at, ff)
        back = []
        for xs in parts:
            back.append(backs[: len(xs)])
            backs = backs[len(xs) :]
        return back, (outs[0], gs, outs[1], outs[2], outs[3])

    ms = [at[f"m{i}"] for i in range(zs)]
    near = chunk_front(near_parts)
    near_back, near_outs = chunk_expert(ms, [jnp.concatenate(ms, axis=0)], near)
    far = chunk_front(far_parts)
    far_ms = [f"far m{i}" for i in range(zs)]
    at["near gact"] = near_outs[4]
    at.fence("near gact", *far_ms)
    ms = [at[key] for key in far_ms]
    pieces = [jnp.concatenate(ms[:mid], axis=0), jnp.concatenate(ms[mid:], axis=0)]
    far_back, far_outs = chunk_expert(ms, pieces, far)
    near_outs = (*near_outs[:4], at["near gact"])

    quarter = dps // 4
    near_sum = fold(near_back)
    far_sum = fold(far_back)
    chunk_keys = [("c", n) for n in range(10)]
    for key, v in zip(chunk_keys, (*near_outs, *far_outs), strict=True):
        at[key] = v
    for i, v in enumerate(far_sum):
        at["far", i] = v
    at.fence(*at.having("far"), *chunk_keys)

    def chunk_grads(first):
        c = [at[key] for key in chunk_keys]
        return grads([c[:5], c[5:]], first, quarter, e_rows)

    last = zs - 1
    highs = [("got", 3 * quarter + i) for i in range(quarter)]
    at["there"] = flip(at["far", last], top)
    at["send high"] = chunk_grads(3 * quarter)
    at.fence("there", "send high", *chunk_keys)
    for i in reversed(range(zs)):
        here = near_sum[i].astype(F32) + at["there"].astype(F32)
        if i < last:
            here = here + at["acc"].astype(F32)
        at["acc"] = here.astype(BF16)
        if not i:
            break
        at["acc"] = hop(at["acc"], -1)
        at["there"] = flip(at["far", i - 1], top)
        beside = []
        if i == last:
            for n in range(quarter):
                at["got", 3 * quarter + n] = flip(at["send high"][n], far_bit)
            for n, y in enumerate(result(at["c", 9], far[1], weights, top, me_at)):
                at["y part", n] = y
            beside = at.having("y part")
        if i == last - 1:
            at["send low"] = chunk_grads(2 * quarter)
            at["y far"] = fold([[at[key]] for key in at.having("y part")])[0]
            beside = ["send low", "y far", *highs[: quarter // 2]]
        if i == last - 2:
            at["keep high"] = chunk_grads(quarter)
            beside = ["keep high", *highs[quarter // 2 :]]
        at.fence("acc", "there", *beside, *chunk_keys)
    dm = at["acc"].astype(F32)
    at["y far"] = flip(at["y far"], top)
    at["got", 2 * quarter] = flip(at["send low"][0], far_bit)

    own_mask = at["mask"].astype(F32)
    own_logits = jnp.where(own_mask > 0, nn(m, router_full), -1e30)
    own_e = jnp.where(
        own_mask > 0, jnp.exp(own_logits - jnp.max(own_logits, axis=1, keepdims=True)), 0.0
    )
    gate_own = own_e / jnp.sum(own_e, axis=1, keepdims=True)
    dgates = dm[:, width : width + experts] + dm[:, width + experts : width + 2 * experts]
    dz = (
        gate_own * (dgates - jnp.sum(gate_own * dgates, axis=1, keepdims=True))
    ).astype(BF16)
    dmt = nt(dz, router_full) + dm[:, :width]
    grad_out = cotangent.astype(F32)
    dh = grad_out + rms_back(hid, r_ffn, gains[3], dmt)
    at["dhb"] = lax.all_gather(dh.astype(BF16), "expert", axis=0, tiled=True)
    router_part = tn(m, dz)
    gain_ffn = jnp.sum(dmt * hid * r_ffn, axis=0)
    at["keep low"] = chunk_grads(0)
    at["y near"] = fold([[x] for x in result(at["c", 4], near[1], weights, top, me_at)])[0]
    at["router"], at["gain ffn"] = router_part, gain_ffn
    at.fence(
        "dhb", "y far", "y near", "keep low", "send low", "router", "gain ffn",
        ("got", 2 * quarter),
    )
    dhb = at["dhb"]
    for i in range(1, quarter):
        at["got", 2 * quarter + i] = flip(at["send low"][i], far_bit)
    for i in range(quarter):
        at["tail", quarter + i, 0] = add(at["keep high"][i], at["got", 3 * quarter + i])
    if laid_out:
        at["tail", 0, 2] = flip(at["tail", 2, 0], 2)
    y_own = add(at["y near"], at["y far"])
    at["y"] = lax.psum_scatter(
        by_line([y_own[i * rows : (i + 1) * rows] for i in range(zs)]),
        "expert",
        scatter_dimension=0,
        tiled=True,
    )

    dqn, dkn, dv, sums = attend_back(dhb, out_w, qkv, qr, kr, vb, gain_qk, cos, sin, seg)
    means = lax.psum(sums.transpose(1, 0, 2).reshape(2, zs * rows), "expert") / width
    dqkv, gains_qk = join_back(qkv, dqn, dkn, dv, r_qk, by_block(means), gain_qk)
    at["dqkv"] = dqkv
    lows = [("got", 2 * quarter + i) for i in range(quarter)]
    at.fence("dqkv", "dhb", "y", *lows, *at.having("tail"))
    if laid_out:
        at["tail", 1, 2] = flip(at["tail", 3, 0], 2)

    at["odd"] = attn_grads(a_all, at["dqkv"], [], me_at, 1, 2)
    at.fence("odd", "dqkv", "dhb")
    at["odd"] = flip(at["odd"], 1)
    at["da"], at["gain attn"] = first_back(at["dqkv"], attn_w, x_all, r_attn, rows)
    at.fence("odd", "dqkv", "da", "gain attn")
    at["da"] = lax.psum_scatter(at["da"], "expert", scatter_dimension=0, tiled=True)
    at["held"] = add(attn_grads(a_all, at["dqkv"], [], me_at, 0, 2), at["odd"])
    at.fence("held", "dhb")
    sides = halves(at["held"], zs * own_rows)
    stage(at, sides, 0)
    out_blocks = tn(o, at["dhb"], BF16).reshape(dps, own_rows, width)
    at["out grad"] = jnp.concatenate([pick(out_blocks, dp ^ r, 0) for r in range(dps)], axis=0)
    for i in range(quarter):
        at["tail", i, 0] = add(at["keep low"][i], at["got", 2 * quarter + i])
    for turn_ in range(1, len(bits_of(2, dps))):
        at.fence(*at.having("side"), "out grad", *at.having("tail"))
        sides = unstage(at, sides, turn_ - 1)
        stage(at, sides, turn_)
        if laid_out:
            for e in (0, 2):
                at["tail", 0, e ^ 1] = flip(at["tail", 1, e], 1)
    at.fence(*at.having("side"), "out grad", "gain attn", "da", *at.having("tail"))
    sides = unstage(at, sides, len(bits_of(2, dps)) - 1)
    at["back"] = lax.all_to_all(
        jnp.concatenate([sides[0][0][0], sides[1][0][0]], axis=1).reshape(zs, own_rows, 3 * cols),
        "expert",
        split_axis=0,
        concat_axis=0,
        tiled=True,
    )
    if laid_out:
        blocks = {e: at["tail", 0, e] for e in range(local)}
    else:
        blocks = gather_back({k[1]: at[k] for k in at.having("tail")}, local, dps)
    stacked = jnp.stack([blocks[e] for e in range(local)])
    blocks = [pick(stacked, own ^ e, 0) for e in range(local)]
    at["gu"] = jnp.stack([b[:, : 2 * ff] for b in blocks], axis=1).astype(F32)
    at["dn"] = jnp.stack([b[:, 2 * ff :] for b in blocks], axis=1).astype(F32)
    zero = jnp.zeros((2, width), F32)
    gain_rows = jnp.concatenate(
        [
            at["gain attn"],
            lax.dynamic_update_slice_in_dim(zero, gains_qk, z * cols, 1),
            at["gain ffn"][None],
            jnp.zeros((EXTRA - experts - 4, width), F32),
        ],
        axis=0,
    )
    extra_part = jnp.concatenate([at["router"], gain_rows.T], axis=1).astype(BF16)
    at["extra"] = lax.psum_scatter(extra_part, "dp", scatter_dimension=0, tiled=True)
    at["out grad"] = scatter_dp(at["out grad"], own_rows)
    at.fence("back", "extra", "gu", "dn", "out grad")
    grad_w_out = lax.ppermute(
        at["out grad"], ("dp", "expert"), [(b, a) for a, b in moved]
    ).astype(F32)
    back = at["back"].astype(F32)
    grad_w_qkv = jnp.concatenate(
        [back[e, :, i * cols : (i + 1) * cols] for i in range(3) for e in range(zs)], axis=1
    )
    extra_back = lax.all_to_all(
        at["extra"].reshape(zs, own_rows, EXTRA), "expert", split_axis=0, concat_axis=0, tiled=True
    )
    extra_sum = jnp.sum(extra_back.astype(F32), axis=0)
    grad_router = extra_sum[:, :experts]
    grad_gains = extra_sum[:, experts : experts + 4]
    da = at["da"].astype(F32)

    output = hid + at["y"].astype(F32)
    x_own = tokens.astype(F32)
    grad_tokens = dh + rms_back(x_own, inv_rms(x_own), gains[0], da)
    return (
        output,
        grad_tokens,
        grad_gains,
        grad_w_qkv,
        grad_w_out,
        grad_router,
        at["gu"],
        at["dn"],
    )


def solution(mesh):
    both = P(("dp", "expert"), None)
    experts = P("dp", "expert", None)
    return jax.shard_map(
        on_device,
        mesh=mesh,
        in_specs=(both, P(), P(), both, both, both, both, both, experts, experts, both),
        out_specs=(both, both, both, both, both, both, experts, experts),
        check_vma=False,
    )
```

time: 842 us -> 769 us (0.913)
  waiting for transfers between devices: 309 us -> 220 us
  Pallas kernels: 138 us -> 184 us
  matrix products: 45.8 us -> 12.4 us
  starting transfers between devices: 57.8 us -> 79.6 us
  other arithmetic: 103 us -> 92.9 us
    ppermute x14, waiting for transfers between devices: 115 us -> 45 us  [the longest x12 41.6 us: hop(): return lax.ppermute(v, 'expert', pairs)]
    pallas_call x0 -> x4, Pallas kernels: none -> 40.3 us  [the longest x1 13.9 us: attend_back(): pl.pallas_call(functools.partial(attend_back_kernel, HEAD_DIM ** (-0.5)),...]
    dot_general x8 -> x6, matrix products: 30.4 us -> 12.4 us  [dot(): lax.dot_general(a, b, (dims, ((), ())), preferred_element_type=F32)]
    reshape x6 -> x0, local copies, waits for them, and re-layouts: 13.2 us -> none  [the longest x2 4.02 us: on_device(): do = nt(dhb, out_w, BF16).reshape(split)]
    all_to_all x1 -> x2, waiting for transfers between devices: 12.6 us -> 0.01 us  [the longest x1 0.01 us: on_device(): lax.all_to_all(jnp.concatenate([sides[0][0][0], sides[1][0][0]], axis=1)....]
    dot_general x5 -> x0, matrix products: 12 us -> none  [the longest x1 3.62 us: on_device(): dv = jnp.einsum('bhts,bthd->bshd', pb, do, preferred_element_type=F32)]
    another operation x10 -> x3, other arithmetic: 12.9 us -> 3.51 us  [the longest x1 3.33 us: on_device(): stacked = jnp.stack([blocks[e] for e in range(local)])]
    ppermute x14, starting transfers between devices: 17.9 us -> 27.1 us  [the longest x12 23.2 us: hop(): return lax.ppermute(v, 'expert', pairs)]
  transfers between devices with their start and end apart: 61 -> 72, of which waited for: 25 -> 26; matrix products, arithmetic and copies ran while one was open for 27% -> 25% of each run, Pallas kernels for 17% -> 20%
where the time goes in v3:
time: 769 us; the launch traced here: 755 us
  waiting for transfers between devices  220 us (29%)
  Pallas kernels  184 us (24%)
  local copies, waits for them, and re-layouts  124 us (16%)
  other arithmetic  92.9 us (12%)
  starting transfers between devices  79.6 us (10%)
  between operations  23.6 us (3%)
  blocking collectives  19.9 us (3%)
  matrix products  12.4 us (2%)
    ppermute x48, waiting for transfers between devices, flip(): lax.ppermute(v, 'dp', [(i, i ^ bit) for i in range(lax.axis_size('dp'))])  169 us
    unnamed x195, local copies, waits for them, and re-layouts  57.7 us
    pallas_call x2, Pallas kernels, run_expert(): pl.pallas_call(functools.partial(expert_kernel, count), grid_spec=pltpu.P...  51.8 us
    ppermute x12, waiting for transfers between devices, hop(): return lax.ppermute(v, 'expert', pairs)  41.6 us
    pallas_call x4, Pallas kernels, grads(): pl.pallas_call(functools.partial(grads_kernel, len(chunks)), grid=(blocks...  41.1 us
    ppermute x48, starting transfers between devices, flip(): lax.ppermute(v, 'dp', [(i, i ^ bit) for i in range(lax.axis_size('dp'))])  38.3 us
    convert_element_type x13, other arithmetic, add(): return (a.astype(F32) + b.astype(F32)).astype(BF16)  32.2 us
    ppermute x12, starting transfers between devices, hop(): return lax.ppermute(v, 'expert', pairs)  23.2 us
  transfers between devices with their start and end apart: 72, of which 26 were waited for; matrix products, arithmetic and copies ran while one was open for 25% of the time, Pallas kernels for 20%

profile of v3, /device:TPU:4, one launch (start us, length us, event | category | flops | bytes accessed | tf_op | source)
XLA Modules:
  0.0 755.5 jit_solution(1690199339837154859)
XLA Ops:
  16.3 14.5 %constant_dynamic-slice_fusion.2 = (bf16[256,1,2048]{2,1,0:T(2,128)(2,1)S(1)}, bf16[256,1,2048]{2,1,0:T(2,128)(2,1)S(1)}, bf16[256,1,2048]{2,1,0:T(2,128)(2,1)S(1)}, bf16[256,1,2048]{2,1,0:T(2,128)(2,1)S(1)}) fusion(bf16[256,4,2048]{2,1,0:T(4,128)(2,1)} %param.21, s32[]{:T(128)S(6)} %select_n.126, s32[]{:T(128)S(6)} %select_n.125, s32[]{:T(128)S(6)} %select_n.124, ...), kind=kLoop, calls=%fused_computation.208 | loop fusion | bytes 8388624 | tf_op jit(solution)/shard_map/jit(dynamic_index_in_dim)/dynamic_slice | solution.py:81
  48.1 10.1 %collective-permute-done = bf16[128,2048]{1,0:T(8,128)(2,1)} collective-permute-done((bf16[128,2048]{1,0:T(8,128)(2,1)S(1)}, bf16[128,2048]{1,0:T(8,128)(2,1)}, u32[]{:S(2)}, u32[]{:S(2)}) %collective-permute-start) | collective-permute-done | bytes 524320 | tf_op jit(solution)/shard_map/ppermute | solution.py:52
  123.8 9.0 %psum.14 = f32[2,512]{1,0:T(2,128)S(1)} all-reduce(f32[2,512]{1,0:T(2,128)} %pad_maximum_fusion.23), channel_id=1, replica_groups=mesh['dp'=8,'expert'=4] {'expert'}, use_global_device_ids=true, to_apply=%region_7.8 | all-reduce | flops 1024 | bytes 8192 | tf_op jit(solution)/shard_map/psum | solution.py:832
  147.6 15.7 %collective-permute-done.10 = bf16[64,3072]{1,0:T(8,128)(2,1)S(1)} collective-permute-done((bf16[64,3072]{1,0:T(8,128)(2,1)}, bf16[64,3072]{1,0:T(8,128)(2,1)S(1)}, u32[]{:S(2)}, u32[]{:S(2)}) %collective-permute-start.10) | collective-permute-done | bytes 393248 | tf_op jit(solution)/shard_map/ppermute | solution.py:41
  183.7 40.2 %collective-permute-done.11.refs_0_ = bf16[256,2176]{1,0:T(8,128)(2,1)} collective-permute-done((bf16[256,2176]{1,0:T(8,128)(2,1)}, bf16[256,2176]{1,0:T(8,128)(2,1)}, u32[]{:S(2)}, u32[]{:S(2)}) %collective-permute-start.11) | collective-permute-done | bytes 1114144 | tf_op jit(solution)/shard_map/ppermute | solution.py:41
  286.8 9.0 %front.2 = (bf16[640,2048]{1,0:T(8,128)(2,1)}, f32[640,1024]{1,0:T(8,128)}) custom-call(s32[1]{0:T(128)} %bitcast.34.me, bf16[512,2176]{1,0:T(8,128)(2,1)} %constant_dynamic-update-slice_fusion.refs_0_, bf16[512,2176]{1,0:T(8,128)(2,1)} %collective-permute-done.20.refs_1_, s32[8,128]{1,0:T(8,128)} %copy-done.62, ...), custom_call_target="tpu_custom_call" | custom-call | flops 1000000 | bytes 100000 | tf_op jit(solution)/shard_map/front/pallas_call | solution.py:186
  296.4 25.9 %expert.2 = (bf16[128,2176]{1,0:T(8,128)(2,1)}, bf16[128,2176]{1,0:T(8,128)(2,1)}, bf16[128,2176]{1,0:T(8,128)(2,1)}, bf16[128,2176]{1,0:T(8,128)(2,1)}, bf16[51...) custom-call(s32[2]{0:T(128)} %pad_add_fusion.expert, ...), custom_call_target="tpu_custom_call" | custom-call | flops 1000000 | bytes 100000 | tf_op jit(solution)/shard_map/expert/pallas_call | solution.py:295
  338.5 26.0 %expert.3 = (bf16[128,2176]{1,0:T(8,128)(2,1)}, bf16[128,2176]{1,0:T(8,128)(2,1)}, bf16[128,2176]{1,0:T(8,128)(2,1)}, bf16[128,2176]{1,0:T(8,128)(2,1)}, bf16[25...) custom-call(s32[2]{0:T(128)} %pad_add_fusion.expert, ...), custom_call_target="tpu_custom_call" | custom-call | flops 1000000 | bytes 100000 | tf_op jit(solution)/shard_map/expert/pallas_call | solution.py:295
  373.3 10.2 %grads.4 = bf16[2,256,3072]{2,1,0:T(8,128)(2,1)} custom-call(bf16[640,2048]{1,0:T(8,128)(2,1)} %get-tuple-element.363.refs_0_, bf16[640,2048]{1,0:T(8,128)(2,1)} %get-tuple-element.364.refs_1_, bf16[640,1024]{1,0:T(8,128)(2,1)} %get-tuple-element.365.refs_2_, bf16[640,1024]{1,0:T(8,128)(2,1)} %get-tuple-element.366.refs_3_, ...), custom_call_target="tpu_custom_call" | custom-call | flops 1000000 | bytes 100000 | tf_op jit(solution)/shard_map/grads/pallas_call | solution.py:385
  388.3 11.0 %result.2 = (bf16[512,2048]{1,0:T(8,128)(2,1)}, bf16[512,2048]{1,0:T(8,128)(2,1)}) custom-call(s32[1]{0:T(128)} %bitcast.34.me, bf16[640,1024]{1,0:T(8,128)(2,1)} %get-tuple-element.371.refs_9_.gact, bf16[2048,3072]{1,0:T(8,128)(2,1)} %constant_dynamic-update-slice_fusion.4.refs_3_.refs_9_.refs_10_.refs_5_.refs_11_.wd, s32[128,8]{1,0:T(8,128)} %bitcast.255), custom_call_target="tpu_custom_call" | custom-call | flops 1000000 | bytes 100000 | tf_op jit(solution)/shard_map/result/pallas_call | solution.py:342
  408.2 10.2 %grads.5 = bf16[2,256,3072]{2,1,0:T(8,128)(2,1)} custom-call(bf16[640,2048]{1,0:T(8,128)(2,1)} %get-tuple-element.363.refs_0_, bf16[640,2048]{1,0:T(8,128)(2,1)} %get-tuple-element.364.refs_1_, bf16[640,1024]{1,0:T(8,128)(2,1)} %get-tuple-element.365.refs_2_, bf16[640,1024]{1,0:T(8,128)(2,1)} %get-tuple-element.366.refs_3_, ...), custom_call_target="tpu_custom_call" | custom-call | flops 1000000 | bytes 100000 | tf_op jit(solution)/shard_map/grads/pallas_call | solution.py:385
  424.2 11.0 %collective-permute-done.38 = bf16[128,2176]{1,0:T(8,128)(2,1)S(1)} collective-permute-done((bf16[128,2176]{1,0:T(8,128)(2,1)S(1)}, bf16[128,2176]{1,0:T(8,128)(2,1)S(1)}, u32[]{:S(2)}, u32[]{:S(2)}) %collective-permute-start.38) | collective-permute-done | bytes 557088 | tf_op jit(solution)/shard_map/ppermute | solution.py:52
  445.8 10.3 %grads.6 = bf16[2,256,3072]{2,1,0:T(8,128)(2,1)} custom-call(bf16[640,2048]{1,0:T(8,128)(2,1)} %get-tuple-element.363.refs_0_, bf16[640,2048]{1,0:T(8,128)(2,1)} %get-tuple-element.364.refs_1_, bf16[640,1024]{1,0:T(8,128)(2,1)} %get-tuple-element.365.refs_2_, bf16[640,1024]{1,0:T(8,128)(2,1)} %get-tuple-element.366.refs_3_, ...), custom_call_target="tpu_custom_call" | custom-call | flops 1000000 | bytes 100000 | tf_op jit(solution)/shard_map/grads/pallas_call | solution.py:385
  456.1 18.8 %collective-permute-done.44 = bf16[256,3072]{1,0:T(8,128)(2,1)} collective-permute-done((bf16[256,3072]{1,0:T(8,128)(2,1)}, bf16[256,3072]{1,0:T(8,128)(2,1)}, u32[]{:S(2)}, u32[]{:S(2)}) %collective-permute-start.44) | collective-permute-done | bytes 1572896 | tf_op jit(solution)/shard_map/ppermute | solution.py:41
  480.1 10.8 %result.3 = (bf16[512,2048]{1,0:T(8,128)(2,1)}, bf16[512,2048]{1,0:T(8,128)(2,1)}) custom-call(s32[1]{0:T(128)} %bitcast.34.me, bf16[640,1024]{1,0:T(8,128)(2,1)} %get-tuple-element.360.refs_4_.gact, bf16[2048,3072]{1,0:T(8,128)(2,1)} %constant_dynamic-update-slice_fusion.4.refs_3_.refs_9_.refs_10_.refs_5_.refs_11_.wd, s32[128,8]{1,0:T(8,128)} %bitcast.253), custom_call_target="tpu_custom_call" | custom-call | flops 1000000 | bytes 100000 | tf_op jit(solution)/shard_map/result/pallas_call | solution.py:342
  493.0 10.3 %grads.7 = bf16[2,256,3072]{2,1,0:T(8,128)(2,1)} custom-call(bf16[640,2048]{1,0:T(8,128)(2,1)} %get-tuple-element.363.refs_0_, bf16[640,2048]{1,0:T(8,128)(2,1)} %get-tuple-element.364.refs_1_, bf16[640,1024]{1,0:T(8,128)(2,1)} %get-tuple-element.365.refs_2_, bf16[640,1024]{1,0:T(8,128)(2,1)} %get-tuple-element.366.refs_3_, ...), custom_call_target="tpu_custom_call" | custom-call | flops 1000000 | bytes 100000 | tf_op jit(solution)/shard_map/grads/pallas_call | solution.py:385
  505.9 22.7 %collective-permute-done.47 = bf16[256,3072]{1,0:T(8,128)(2,1)} collective-permute-done((bf16[256,3072]{1,0:T(8,128)(2,1)S(1)}, bf16[256,3072]{1,0:T(8,128)(2,1)}, u32[]{:S(2)}, u32[]{:S(2)}) %collective-permute-start.47) | collective-permute-done | bytes 1572896 | tf_op jit(solution)/shard_map/ppermute | solution.py:41
  528.6 10.6 %collective-permute-done.45 = bf16[512,2048]{1,0:T(8,128)(2,1)} collective-permute-done((bf16[512,2048]{1,0:T(8,128)(2,1)}, bf16[512,2048]{1,0:T(8,128)(2,1)}, u32[]{:S(2)}, u32[]{:S(2)}) %collective-permute-start.45) | collective-permute-done | bytes 2097184 | tf_op jit(solution)/shard_map/ppermute | solution.py:41
  553.7 13.9 %attend_back.1 = (f32[512,512]{1,0:T(8,128)}, f32[512,512]{1,0:T(8,128)}, bf16[512,512]{1,0:T(8,128)(2,1)}, f32[4,2,128]{2,1,0:T(2,128)}) custom-call(bf16[512,2048]{1,0:T(8,128)(2,1)} %all-gather.8.cloned.1.call-done.dhb, bf16[512,2048]{1,0:T(8,128)(2,1)} %all-gather.6.cloned.1.call-done.wo, f32[512,1536]{1,0:T(8,128)} %copy-done.2, f32[512,1536]{1,0:T(8,128)} %copy-done.2, ...), custom_call_target="tpu_custom_call" | custom-call | flops 1000000 | bytes 100000 | tf_op jit(solution)/shard_map/attend_back/pallas_call | solution.py:579
  567.6 10.9 %psum.15 = f32[2,512]{1,0:T(2,128)S(1)} all-reduce(f32[2,512]{1,0:T(2,128)} %bitcast.265), channel_id=1, replica_groups=mesh['dp'=8,'expert'=4] {'expert'}, use_global_device_ids=true, to_apply=%region_19.20 | all-reduce | flops 1024 | bytes 8192 | tf_op jit(solution)/shard_map/psum | solution.py:997
  596.2 12.9 %first_back.1 = (bf16[512,2048]{1,0:T(8,128)(2,1)}, f32[1,2048]{1,0:T(1,128)}) custom-call(bf16[512,1536]{1,0:T(8,128)(2,1)} %get-tuple-element.396.d, bf16[2048,1664]{1,0:T(8,128)(2,1)} %all-gather.4.cloned.1.call-done.w, bf16[512,2048]{1,0:T(8,128)(2,1)} %copy-done.6, f32[512,1]{1,0:T(8,128)} %copy.336.r), custom_call_target="tpu_custom_call" | custom-call | flops 1000000 | bytes 100000 | tf_op jit(solution)/shard_map/first_back/pallas_call | solution.py:672
  632.8 16.2 %collective-permute-done.51 = bf16[512,768]{1,0:T(8,128)(2,1)S(1)} collective-permute-done((bf16[512,768]{1,0:T(8,128)(2,1)S(1)}, bf16[512,768]{1,0:T(8,128)(2,1)S(1)}, u32[]{:S(2)}, u32[]{:S(2)}) %collective-permute-start.51) | collective-permute-done | bytes 786464 | tf_op jit(solution)/shard_map/ppermute | solution.py:41
  697.3 12.5 %collective-permute-done.59 = bf16[128,2048]{1,0:T(8,128)(2,1)S(1)} collective-permute-done((bf16[128,2048]{1,0:T(8,128)(2,1)S(1)}, bf16[128,2048]{1,0:T(8,128)(2,1)S(1)}, u32[]{:S(2)}, u32[]{:S(2)}) %collective-permute-start.59) | collective-permute-done | bytes 524320 | tf_op jit(solution)/shard_map/ppermute | solution.py:41
  728.9 12.3 %copy.343 = f32[256,4,2048]{2,1,0:T(4,128)} copy(f32[256,4,2048]{2,0,1:T(8,128)} %maximum_convert_fusion) | data formatting | bytes 16777216
  (514 shorter events, 377.2 us)
Async XLA Ops:
  16.3 82.0 %all-gather.4.cloned.1.call-start = ((), (), s32[]{:S(2)}) async-start(), calls=%async_computation.7 | async-start | bytes 7667712 | tf_op jit(solution)/shard_map/all_gather | solution.py:784
  44.6 98.7 %all-gather.6.cloned.1.call-start = ((), (), s32[]{:S(2)}) async-start(), calls=%async_computation.8 | async-start | bytes 2359296 | tf_op jit(solution)/shard_map/all_gather | solution.py:818
  47.6 46.7 %collective-permute-start.4 = (bf16[256,3072]{1,0:T(8,128)(2,1)}, bf16[256,3072]{1,0:T(8,128)(2,1)S(1)}, u32[]{:S(2)}, u32[]{:S(2)}) collective-permute-start(bf16[256,3072]{1,0:T(8,128)(2,1)} %pad_maximum_fusion.7), channel_id=1, source_target_pairs={{0,4},{4,0},{8,12},{12,8},{16,20},{20,16},{24,28},{28,24},{1,5},{5... | collective-permute-start | bytes 4718600 | tf_op jit(solution)/shard_map/ppermute | solution.py:41
  47.6 46.7 %collective-permute-start.5 = (bf16[256,3072]{1,0:T(8,128)(2,1)}, bf16[256,3072]{1,0:T(8,128)(2,1)}, u32[]{:S(2)}, u32[]{:S(2)}) collective-permute-start(bf16[256,3072]{1,0:T(8,128)(2,1)} %pad_maximum_fusion.9), channel_id=1, source_target_pairs={{0,4},{4,0},{8,12},{12,8},{16,20},{20,16},{24,28},{28,24},{1,5},{5... | collective-permute-start | bytes 4718600 | tf_op jit(solution)/shard_map/ppermute | solution.py:41
  103.9 120.1 %reduce-scatter.5.cloned.1.call-start = ((), (), s32[]{:S(2)}) async-start(), calls=%async_computation.9 | async-start | bytes 2621440 | tf_op jit(solution)/shard_map/reduce_scatter | solution.py:844
  106.2 57.0 %collective-permute-start.8 = (bf16[256,3072]{1,0:T(8,128)(2,1)}, bf16[256,3072]{1,0:T(8,128)(2,1)}, u32[]{:S(2)}, u32[]{:S(2)}) collective-permute-start(bf16[256,3072]{1,0:T(8,128)(2,1)} %pad_maximum_fusion.8), channel_id=1, source_target_pairs={{0,8},{4,12},{8,0},{12,4},{16,24},{20,28},{24,16},{28,20},{1,9},{5... | collective-permute-start | bytes 4718600 | tf_op jit(solution)/shard_map/ppermute | solution.py:41
  110.2 53.1 %collective-permute-start.9 = (bf16[256,3072]{1,0:T(8,128)(2,1)}, bf16[256,3072]{1,0:T(8,128)(2,1)}, u32[]{:S(2)}, u32[]{:S(2)}) collective-permute-start(bf16[256,3072]{1,0:T(8,128)(2,1)} %pad_maximum_fusion.6), channel_id=1, source_target_pairs={{0,16},{4,20},{8,24},{12,28},{16,0},{20,4},{24,8},{28,12},{1,17},{... | collective-permute-start | bytes 4718600 | tf_op jit(solution)/shard_map/ppermute | solution.py:41
  111.0 52.3 %collective-permute-start.10 = (bf16[64,3072]{1,0:T(8,128)(2,1)}, bf16[64,3072]{1,0:T(8,128)(2,1)S(1)}, u32[]{:S(2)}, u32[]{:S(2)}) collective-permute-start(bf16[64,3072]{1,0:T(8,128)(2,1)} %slice.348), channel_id=1, source_target_pairs={{0,16},{4,20},{8,24},{12,28},{16,0},{20,4},{24,8},{28,12},{1,17},{... | collective-permute-start | bytes 1179656 | tf_op jit(solution)/shard_map/ppermute | solution.py:41
  163.3 375.9 %all-gather.8.cloned.1.call-start = ((), (), s32[]{:S(2)}) async-start(), calls=%async_computation.10 | async-start | bytes 2621440 | tf_op jit(solution)/shard_map/all_gather | solution.py:971
  164.6 59.3 %collective-permute-start.13 = (bf16[256,3072]{1,0:T(8,128)(2,1)}, bf16[256,3072]{1,0:T(8,128)(2,1)}, u32[]{:S(2)}, u32[]{:S(2)}) collective-permute-start(bf16[256,3072]{1,0:T(8,128)(2,1)} %collective-permute-done.5), channel_id=1, source_target_pairs={{0,8},{4,12},{8,0},{12,4},{16,24},{20,28},{24,16},{28,20},{1,9},{5... | collective-permute-start | bytes 4718600 | tf_op jit(solution)/shard_map/ppermute | solution.py:41
  167.3 56.6 %collective-permute-start.11 = (bf16[256,2176]{1,0:T(8,128)(2,1)}, bf16[256,2176]{1,0:T(8,128)(2,1)}, u32[]{:S(2)}, u32[]{:S(2)}) collective-permute-start(bf16[256,2176]{1,0:T(8,128)(2,1)} %pad_maximum_fusion.10), channel_id=1, source_target_pairs={{0,8},{4,12},{8,0},{12,4},{16,24},{20,28},{24,16},{28,20},{1,9},{5... | collective-permute-start | bytes 3342344 | tf_op jit(solution)/shard_map/ppermute | solution.py:41
  171.4 52.5 %collective-permute-start.14 = (bf16[192,3072]{1,0:T(8,128)(2,1)}, bf16[192,3072]{1,0:T(8,128)(2,1)}, u32[]{:S(2)}, u32[]{:S(2)}) collective-permute-start(bf16[192,3072]{1,0:T(8,128)(2,1)} %slice.349), channel_id=1, source_target_pairs={{0,16},{4,20},{8,24},{12,28},{16,0},{20,4},{24,8},{28,12},{1,17},{... | collective-permute-start | bytes 3538952 | tf_op jit(solution)/shard_map/ppermute | solution.py:41
  172.8 51.1 %collective-permute-start.15 = (bf16[192,3072]{1,0:T(8,128)(2,1)}, bf16[192,3072]{1,0:T(8,128)(2,1)}, u32[]{:S(2)}, u32[]{:S(2)}) collective-permute-start(bf16[192,3072]{1,0:T(8,128)(2,1)} %slice.350), channel_id=1, source_target_pairs={{0,16},{4,20},{8,24},{12,28},{16,0},{20,4},{24,8},{28,12},{1,17},{... | collective-permute-start | bytes 3538952 | tf_op jit(solution)/shard_map/ppermute | solution.py:41
  178.4 45.5 %collective-permute-start.12 = (bf16[128,2176]{1,0:T(8,128)(2,1)}, bf16[128,2176]{1,0:T(8,128)(2,1)}, u32[]{:S(2)}, u32[]{:S(2)}) collective-permute-start(bf16[128,2176]{1,0:T(8,128)(2,1)} %collective-permute-done.7), channel_id=1, source_target_pairs={{0,2},{2,3},{3,1},{1,0},{4,6},{6,7},{7,5},{5,4},{8,10},{10,11},{11... | collective-permute-start | bytes 1671176 | tf_op jit(solution)/shard_map/ppermute | solution.py:52
  223.9 54.0 %collective-permute-start.22 = (bf16[256,3072]{1,0:T(8,128)(2,1)}, bf16[256,3072]{1,0:T(8,128)(2,1)}, u32[]{:S(2)}, u32[]{:S(2)}) collective-permute-start(bf16[256,3072]{1,0:T(8,128)(2,1)} %collective-permute-done.13), channel_id=1, source_target_pairs={{0,16},{4,20},{8,24},{12,28},{16,0},{20,4},{24,8},{28,12},{1,17},{... | collective-permute-start | bytes 4718600 | tf_op jit(solution)/shard_map/ppermute | solution.py:41
  230.3 48.7 %collective-permute-start.20 = (bf16[512,2176]{1,0:T(8,128)(2,1)}, bf16[512,2176]{1,0:T(8,128)(2,1)}, u32[]{:S(2)}, u32[]{:S(2)}) collective-permute-start(bf16[512,2176]{1,0:T(8,128)(2,1)} %constant_dynamic-update-slice_fusion.refs_0_), channel_id=1, source_target_pairs={{0,4},{4,0},{8,12},{12,8},{16,20},{20,16},{24,28},{28,24},{1,5},{5... | collective-permute-start | bytes 6684680 | tf_op jit(solution)/shard_map/ppermute | solution.py:41
  276.0 46.2 %collective-permute-start.24 = (bf16[128,2048]{1,0:T(8,128)(2,1)S(1)}, bf16[128,2048]{1,0:T(8,128)(2,1)S(1)}, u32[]{:S(2)}, u32[]{:S(2)}) collective-permute-start(bf16[128,2048]{1,0:T(8,128)(2,1)S(1)} %multiply_convert_fusion.refs_0_), channel_id=1, source_target_pairs={{0,8},{4,12},{8,0},{12,4},{16,24},{20,28},{24,16},{28,20},{1,9},{5... | collective-permute-start | bytes 1572872 | tf_op jit(solution)/shard_map/ppermute | solution.py:41
  277.9 44.4 %collective-permute-start.25 = (bf16[128,2048]{1,0:T(8,128)(2,1)}, bf16[128,2048]{1,0:T(8,128)(2,1)S(1)}, u32[]{:S(2)}, u32[]{:S(2)}) collective-permute-start(bf16[128,2048]{1,0:T(8,128)(2,1)} %collective-permute-done.16.refs_1_), channel_id=1, source_target_pairs={{0,8},{4,12},{8,0},{12,4},{16,24},{20,28},{24,16},{28,20},{1,9},{5... | collective-permute-start | bytes 1572872 | tf_op jit(solution)/shard_map/ppermute | solution.py:41
  405.9 50.2 %collective-permute-start.43 = (bf16[128,2176]{1,0:T(8,128)(2,1)}, bf16[128,2176]{1,0:T(8,128)(2,1)}, u32[]{:S(2)}, u32[]{:S(2)}) collective-permute-start(bf16[128,2176]{1,0:T(8,128)(2,1)} %get-tuple-element.346), channel_id=1, source_target_pairs={{0,8},{4,12},{8,0},{12,4},{16,24},{20,28},{24,16},{28,20},{1,9},{5... | collective-permute-start | bytes 1671176 | tf_op jit(solution)/shard_map/ppermute | solution.py:41
  407.0 67.9 %collective-permute-start.44 = (bf16[256,3072]{1,0:T(8,128)(2,1)}, bf16[256,3072]{1,0:T(8,128)(2,1)}, u32[]{:S(2)}, u32[]{:S(2)}) collective-permute-start(bf16[256,3072]{1,0:T(8,128)(2,1)} %get-tuple-element.519), channel_id=1, source_target_pairs={{0,16},{4,20},{8,24},{12,28},{16,0},{20,4},{24,8},{28,12},{1,17},{... | collective-permute-start | bytes 4718600 | tf_op jit(solution)/shard_map/ppermute | solution.py:41
  480.1 108.7 %reduce-scatter.7.cloned.1.call-start = ((), (), s32[]{:S(2)}) async-start(), calls=%async_computation.11 | async-start | bytes 2621440 | tf_op jit(solution)/shard_map/reduce_scatter | solution.py:989
  490.9 48.4 %collective-permute-start.45 = (bf16[512,2048]{1,0:T(8,128)(2,1)}, bf16[512,2048]{1,0:T(8,128)(2,1)}, u32[]{:S(2)}, u32[]{:S(2)}) collective-permute-start(bf16[512,2048]{1,0:T(8,128)(2,1)} %add_convert_fusion.3), channel_id=1, source_target_pairs={{0,8},{4,12},{8,0},{12,4},{16,24},{20,28},{24,16},{28,20},{1,9},{5... | collective-permute-start | bytes 6291464 | tf_op jit(solution)/shard_map/ppermute | solution.py:41
  543.9 118.9 %reduce-scatter.9.cloned.1.call-start = ((), (), s32[]{:S(2)}) async-start(), calls=%async_computation.12 | async-start | bytes 2621440 | tf_op jit(solution)/shard_map/reduce_scatter | solution.py:1010
  618.8 101.3 %reduce-scatter.11.cloned.1.call-start = ((), (), s32[]{:S(2)}) async-start(), calls=%async_computation.13 | async-start | bytes 589824 | tf_op jit(solution)/shard_map/reduce_scatter | solution.py:1054
  (127 other events, 1866.3 us)
Sparse Core Ops, SparseCore 0:
  44.7 53.5 all-gather.3
  104.0 39.2 all-gather.5
  163.4 54.7 reduce-scatter.4
  480.2 45.3 all-gather.7
  544.0 43.5 reduce-scatter.6
  618.9 43.2 reduce-scatter.8
  679.8 34.5 reduce-scatter.10

commit v4 on v3

--- a/solution.py
+++ b/solution.py
@@ -85,6 +85,66 @@
     return lax.optimization_barrier(values)
 
 
+(
+    ORDER,
+    LENGTHS,
+    COS,
+    SIN,
+    SEG,
+    MINE,
+    W,
+    X,
+    OUT,
+    ATTN,
+    ROUTES,
+    COT,
+    MASK,
+    G,
+    QKV,
+    SQUARES,
+    ADDED,
+    WA,
+    FAR_GA,
+    WB,
+    M,
+    NEAR_GACT,
+    C,
+    FAR,
+    THERE,
+    SEND_HIGH,
+    ACC,
+    Y_PART,
+    NEAR_PART,
+    SEND_LOW,
+    Y_FAR,
+    Y_NEAR,
+    DHB,
+    KEEP_HIGH,
+    KEEP_LOW,
+    ROUTER,
+    GAIN_FFN,
+    TAIL,
+    Y,
+    DQKV,
+    ODD,
+    DA,
+    GAIN_ATTN,
+    HELD,
+    OUT_GRAD,
+    BESIDE,
+    SIDE,
+    BACK,
+    GU,
+    DN,
+    NEAR,
+    DISTANT,
+    PIECE,
+    BACKS,
+    ROWS,
+    HALF,
+) = range(56)
+
+
 class Flow:
     def __init__(self):
         self.of = {}
@@ -133,14 +193,14 @@
     return parts[0]
 
 
-def scatter_dp(part, rows):
-    n = lax.axis_size("dp")
-    held = [part[r * rows : (r + 1) * rows] for r in range(n)]
-    for bit in bits_of(1, n):
-        odd = jnp.concatenate(held[1::2], axis=0) if len(held) > 2 else held[1]
-        got = flip(odd, bit)
-        held = [add(v, got[i * rows : (i + 1) * rows]) for i, v in enumerate(held[::2])]
-    return held[0]
+def scatter_step(at, bit):
+    keys = sorted(key for key in at.having(OUT_GRAD) if key[1] & bit)
+    v = [at.of.pop(key) for key in keys]
+    got = flip(jnp.concatenate(v, axis=0) if len(v) > 1 else v[0], bit)
+    rows = v[0].shape[0]
+    for i, (_, r) in enumerate(keys):
+        to = OUT_GRAD, r ^ bit
+        at[to] = add(at[to], got[i * rows : (i + 1) * rows])
 
 
 def blocks_of(parts, tok):
@@ -159,50 +219,6 @@
 
 def mm(a, b, dims):
     return lax.dot_general(a, b, (dims, ((), ())), preferred_element_type=F32)
-
-
-def front_kernel(count, me, *refs):
-    parts, (pos, wd, rows_out, gw) = refs[:count], refs[count:]
-    tok = pos.shape[1]
-    width = rows_out.shape[1]
-
-    @pl.when(pl.program_id(0) == 0)
-    def _():
-        for b, (i, at) in enumerate(blocks_of(parts, tok)):
-            part = parts[i][at : at + tok, :width]
-            hot = onehot(pos, b).astype(BF16)
-            found = mm(hot, part, ((1,), (0,))).astype(BF16)
-            to_distance(rows_out, slice(b * CAP, (b + 1) * CAP), found, me[0])
-
-    gw[...] = mm(rows_out[...], wd[...], ((1,), (0,)))
-
-
-def front(parts, pos, weights, ff, me):
-    count, width = len(parts), weights.shape[0]
-    slots = pos.shape[0] * CAP
-    tile = min(256, ff)
-    first = (weights.shape[1] - ff) // tile
-    whole = lambda x: pl.BlockSpec(x.shape, lambda n, me: (0, 0))
-    return pl.pallas_call(
-        functools.partial(front_kernel, count),
-        grid_spec=pltpu.PrefetchScalarGridSpec(
-            num_scalar_prefetch=1,
-            grid=(ff // tile,),
-            in_specs=[whole(x) for x in parts]
-            + [whole(pos), pl.BlockSpec((width, tile), lambda n, me: (0, first + n))],
-            out_specs=[
-                pl.BlockSpec((slots, width), lambda n, me: (0, 0)),
-                pl.BlockSpec((slots, tile), lambda n, me: (0, n)),
-            ],
-        ),
-        out_shape=[
-            jax.ShapeDtypeStruct((slots, width), BF16),
-            jax.ShapeDtypeStruct((slots, ff), F32),
-        ],
-        compiler_params=pltpu.CompilerParams(vmem_limit_bytes=VMEM),
-        cost_estimate=COST,
-        name="front",
-    )(me, *parts, pos, weights)
 
 
 def to_distance(ref, rows, value, me):
@@ -213,44 +229,88 @@
         ref[rows, pl.ds(at, wide)] = value[:, c * wide : (c + 1) * wide]
 
 
-def expert_kernel(count, expert, *refs):
-    parts = refs[:count]
-    pos, pos_t, named, router, wg, wu, gw = refs[count : count + 7]
-    backs = refs[count + 7 : 2 * count + 7]
-    rows_out, dg_out, du_out, gact_out, acc, gate, dgate = refs[2 * count + 7 :]
-    n = pl.program_id(0)
+def gather_kernel(count, g_count, expert, *refs):
+    parts, refs = refs[:count], refs[count:]
+    g_parts, refs = refs[:g_count], refs[g_count:]
+    pos, named, router, rows_out, gs_out, gate = refs
     tok = pos.shape[1]
     width = rows_out.shape[1]
-    experts = router.shape[0]
-
-    @pl.when(n == 0)
-    def _():
-        for b, (i, first) in enumerate(blocks_of(parts, tok)):
-            at = slice(b * CAP, (b + 1) * CAP)
-            part = parts[i][first : first + tok, :]
-            hot = onehot(pos, b)
-            found = mm(hot.astype(BF16), part, ((1,), (0,))).astype(BF16)
-            to_distance(rows_out, at, found, expert[1])
-            chosen = named[b] > 0
-            logits = jnp.where(chosen, mm(router[...], part, ((1,), (1,))), -1e30)
-            e = jnp.where(chosen, jnp.exp(logits - jnp.max(logits, axis=0, keepdims=True)), 0.0)
-            gates = e / jnp.sum(e, axis=0, keepdims=True)
-            mine = lax.broadcasted_iota(jnp.int32, gates.shape, 0) == expert[0]
-            row = jnp.sum(jnp.where(mine, gates, 0.0), axis=0, keepdims=True)
-            gate[at, :] = jnp.sum(jnp.where(hot, row, 0.0), axis=1, keepdims=True)
-            dgate[at, :] = jnp.zeros((CAP, 1), F32)
-
-    rows = rows_out[...]
+    for b, (i, first) in enumerate(blocks_of(parts, tok)):
+        at = slice(b * CAP, (b + 1) * CAP)
+        part = parts[i][first : first + tok, :]
+        hot = onehot(pos, b)
+        found = mm(hot.astype(BF16), part, ((1,), (0,))).astype(BF16)
+        to_distance(rows_out, at, found, expert[1])
+        chosen = named[b] > 0
+        logits = jnp.where(chosen, mm(router[...], part, ((1,), (1,))), -1e30)
+        e = jnp.where(chosen, jnp.exp(logits - jnp.max(logits, axis=0, keepdims=True)), 0.0)
+        gates = e / jnp.sum(e, axis=0, keepdims=True)
+        mine = lax.broadcasted_iota(jnp.int32, gates.shape, 0) == expert[0]
+        row = jnp.sum(jnp.where(mine, gates, 0.0), axis=0, keepdims=True)
+        gate[at, :] = jnp.sum(jnp.where(hot, row, 0.0), axis=1, keepdims=True)
+    for b, (i, first) in enumerate(blocks_of(g_parts, tok)):
+        part = g_parts[i][first : first + tok, :width]
+        found = mm(onehot(pos, b).astype(BF16), part, ((1,), (0,))).astype(BF16)
+        to_distance(gs_out, slice(b * CAP, (b + 1) * CAP), found, expert[1])
+
+
+def gather(parts, g_parts, pos, named, router, expert):
+    slots, width = pos.shape[0] * CAP, parts[0].shape[1]
+    ins = [*parts, *g_parts, pos, named, router]
+    whole = lambda x: pl.BlockSpec(x.shape, lambda n, e: (0,) * len(x.shape))
+    outs = [
+        jax.ShapeDtypeStruct((slots, width), BF16),
+        jax.ShapeDtypeStruct((slots, width), BF16),
+        jax.ShapeDtypeStruct((slots, 1), F32),
+    ]
+    return pl.pallas_call(
+        functools.partial(gather_kernel, len(parts), len(g_parts)),
+        grid_spec=pltpu.PrefetchScalarGridSpec(
+            num_scalar_prefetch=1,
+            grid=(1,),
+            in_specs=[whole(x) for x in ins],
+            out_specs=[whole(x) for x in outs],
+        ),
+        out_shape=outs,
+        compiler_params=pltpu.CompilerParams(vmem_limit_bytes=VMEM),
+        cost_estimate=COST,
+        name="gather",
+    )(expert, *ins)
+
+
+def spans(pieces):
+    out, at = [], 0
+    for p in pieces:
+        out.append(slice(at, at + p.shape[0]))
+        at += p.shape[0]
+    return out
+
+
+def expert_kernel(count, pieces, expert, *refs):
+    rows_in, gs_in, gate, pos_t = refs[:4]
+    parts = [refs[4 + i * pieces : 4 + (i + 1) * pieces] for i in range(3)]
+    refs = refs[4 + 3 * pieces :]
+    backs, refs = refs[:count], refs[count:]
+    dg_out, du_out, gact_out, acc, dgate, wg, wu, wd = refs
+    n = pl.program_id(0)
+    tok = pos_t.shape[0]
+    width = rows_in.shape[1]
+    for at, a, b, c in zip(spans(parts[0]), *parts, strict=True):
+        wg[at, :] = a[...]
+        wu[at, :] = b[...]
+        wd[at, :] = c[...]
+
+    rows = rows_in[...]
     g = mm(rows, wg[...], ((1,), (0,)))
     u = mm(rows, wu[...], ((1,), (0,)))
+    gw = mm(gs_in[...], wd[...], ((1,), (0,)))
     sg = 1.0 / (1.0 + jnp.exp(-g))
     silu = g * sg
     act = (silu * u).astype(BF16).astype(F32)
-    gw_v = gw[...]
-    dgate[...] += jnp.sum(act * gw_v, axis=1, keepdims=True)
+    part = jnp.sum(act * gw, axis=1, keepdims=True)
     gate_v = gate[...]
     gact_out[...] = (gate_v * act).astype(BF16)
-    dact = gate_v * gw_v
+    dact = gate_v * gw
     dg = (dact * u * (sg * (1.0 + g * (1.0 - sg)))).astype(BF16)
     du = (dact * silu).astype(BF16)
     dg_out[...] = dg
@@ -260,15 +320,17 @@
     @pl.when(n == 0)
     def _():
         acc[...] = back
+        dgate[...] = part
 
     @pl.when(n > 0)
     def _():
         acc[...] += back
+        dgate[...] += part
 
     @pl.when(n == pl.num_programs(0) - 1)
     def _():
         lane = lax.broadcasted_iota(jnp.int32, (CAP, EXTRA), 1)
-        for b, (i, first) in enumerate(blocks_of(parts, tok)):
+        for b, (i, first) in enumerate(blocks_of(backs, tok)):
             at = slice(b * CAP, (b + 1) * CAP)
             to = slice(first, first + tok)
             hot = onehot_back(pos_t, b)
@@ -278,84 +340,87 @@
             d = dgate[at, :]
             hi = d.astype(BF16).astype(F32)
             beside = jnp.where(
-                lane == expert[0], hi, jnp.where(lane == experts + expert[0], d - hi, 0.0)
+                lane == expert[0], hi, jnp.where(lane == expert[2] + expert[0], d - hi, 0.0)
             ).astype(BF16)
             out[to, width:] = mm(hot, beside, ((1,), (0,))).astype(BF16)
 
 
-def run_expert(parts, pos, pos_t, named, router, weights, gw, expert, ff):
-    count, width = len(parts), weights.shape[0]
-    slots = pos.shape[0] * CAP
-    tile = min(256, ff)
+def run_expert(rows, gs, gate, pos_t, pieces, expert, heights, ff):
+    slots, width = rows.shape
+    tile = min(512, ff)
     steps = ff // tile
-    whole = lambda x: pl.BlockSpec(x.shape, lambda n, e: (0,) * x.ndim)
+    whole = lambda x: pl.BlockSpec(x.shape, lambda n, e: (0,) * len(x.shape))
     column = pl.BlockSpec((slots, tile), lambda n, e: (0, n))
-    backs = [jax.ShapeDtypeStruct((x.shape[0], width + EXTRA), BF16) for x in parts]
+    backs = [jax.ShapeDtypeStruct((h, width + EXTRA), BF16) for h in heights]
     thin = jax.ShapeDtypeStruct((slots, ff), BF16)
     outs = pl.pallas_call(
-        functools.partial(expert_kernel, count),
+        functools.partial(expert_kernel, len(heights), len(pieces)),
         grid_spec=pltpu.PrefetchScalarGridSpec(
             num_scalar_prefetch=1,
             grid=(steps,),
-            in_specs=[whole(x) for x in parts]
-            + [
-                whole(pos),
-                whole(pos_t),
-                whole(named),
-                whole(router),
-                pl.BlockSpec((width, tile), lambda n, e: (0, n)),
-                pl.BlockSpec((width, tile), lambda n, e: (0, steps + n)),
-                column,
-            ],
-            out_specs=[whole(x) for x in backs]
-            + [pl.BlockSpec((slots, width), lambda n, e: (0, 0)), column, column, column],
-            scratch_shapes=[
-                pltpu.VMEM((slots, width), F32),
-                pltpu.VMEM((slots, 1), F32),
-                pltpu.VMEM((slots, 1), F32),
-            ],
+            in_specs=[whole(x) for x in (rows, gs, gate, pos_t)]
+            + [pl.BlockSpec((p.shape[0], tile), lambda n, e: (0, n)) for p in pieces]
+            + [pl.BlockSpec((p.shape[0], tile), lambda n, e: (0, steps + n)) for p in pieces]
+            + [pl.BlockSpec((p.shape[0], tile), lambda n, e: (0, 2 * steps + n)) for p in pieces],
+            out_specs=[whole(x) for x in backs] + [column, column, column],
+            scratch_shapes=[pltpu.VMEM((slots, width), F32), pltpu.VMEM((slots, 1), F32)]
+            + [pltpu.VMEM((width, tile), BF16)] * 3,
         ),
-        out_shape=backs
-        + [jax.ShapeDtypeStruct((slots, width), BF16), thin, thin, thin],
+        out_shape=backs + [thin, thin, thin],
         compiler_params=pltpu.CompilerParams(vmem_limit_bytes=VMEM),
         cost_estimate=COST,
         name="expert",
-    )(expert, *parts, pos, pos_t, named, router, weights, weights, gw)
-    return outs[:count], outs[count:]
-
-
-def result_kernel(count, me, gact, wd, pos_t, *outs):
+    )(expert, rows, gs, gate, pos_t, *pieces, *pieces, *pieces)
+    return outs[: len(heights)], outs[len(heights) :]
+
+
+def result_kernel(count, pieces, wide, me, gact, pos_t, *refs):
+    parts, outs, wd = refs[:pieces], refs[pieces : pieces + count], refs[-1]
     tok = pos_t.shape[0]
-    y = mm(gact[...], wd[...], ((1,), (1,))).astype(BF16)
+    n = pl.program_id(0)
+    blocks = wd.shape[0] // wide // pl.num_programs(0)
+
+    @pl.when(n == 0)
+    def _():
+        for at, w in zip(spans(parts), parts, strict=True):
+            wd[at, :] = w[...]
+
+    step = blocks * wide
+    here = wd[pl.ds(pl.multiple_of(n * step, step), step), :]
+    y = mm(gact[...], here, ((1,), (1,))).astype(BF16)
     for b, (i, at) in enumerate(blocks_of(outs, tok)):
-        outs[i][at : at + tok, :] = mm(
-            onehot_back(pos_t, b), y[b * CAP : (b + 1) * CAP, :], ((1,), (0,))
-        ).astype(BF16)
-
-
-def result(gact, pos_t, weights, count, me):
+        part = y[b * CAP : (b + 1) * CAP, :]
+        part = mm(onehot_back(pos_t, b), part, ((1,), (0,))).astype(BF16)
+        for k in range(blocks):
+            to = pl.multiple_of((me[0] ^ (blocks * n + k)) * wide, wide)
+            outs[i][at : at + tok, pl.ds(to, wide)] = part[:, k * wide : (k + 1) * wide]
+
+
+def result(gact, pos_t, pieces, count, me):
     slots, ff = gact.shape
-    width = weights.shape[0]
-    tile = width // lax.axis_size("dp")
-    last = (weights.shape[1] - ff) // ff
+    width = sum(p.shape[0] for p in pieces)
+    wide = width // lax.axis_size("dp")
+    tile = max(wide, min(512, width))
+    last = (pieces[0].shape[1] - ff) // ff
     out = jax.ShapeDtypeStruct((pos_t.shape[1] // count * pos_t.shape[0], width), BF16)
     return pl.pallas_call(
-        functools.partial(result_kernel, count),
+        functools.partial(result_kernel, count, len(pieces), wide),
         grid_spec=pltpu.PrefetchScalarGridSpec(
             num_scalar_prefetch=1,
             grid=(width // tile,),
             in_specs=[
                 pl.BlockSpec((slots, ff), lambda n, me: (0, 0)),
-                pl.BlockSpec((tile, ff), lambda n, me: (n, last)),
                 pl.BlockSpec(pos_t.shape, lambda n, me: (0, 0)),
-            ],
-            out_specs=[pl.BlockSpec((out.shape[0], tile), lambda n, me: (0, me[0] ^ n))] * count,
+            ]
+            + [pl.BlockSpec((p.shape[0], ff), lambda n, me: (0, last)) for p in pieces],
+            out_specs=[pl.BlockSpec(out.shape, lambda n, me: (0, 0))] * count,
+            scratch_shapes=[pltpu.VMEM((width, ff), BF16)],
         ),
         out_shape=[out] * count,
         compiler_params=pltpu.CompilerParams(vmem_limit_bytes=VMEM),
         cost_estimate=COST,
         name="result",
-    )(me, gact, weights, pos_t)
+    )(me, gact, pos_t, *pieces)
 
 
 def grads_kernel(count, *refs):
@@ -445,7 +510,7 @@
     for s, (side, order) in enumerate(sides):
         keys = sorted(r for r in side if r & order[step])
         v = [side[r] for r in keys]
-        at["side", s] = flip(jnp.concatenate(v, axis=0) if len(v) > 1 else v[0], order[step])
+        at[SIDE, s] = flip(jnp.concatenate(v, axis=0) if len(v) > 1 else v[0], order[step])
 
 
 def unstage(at, sides, step):
@@ -454,7 +519,7 @@
         bit = order[step]
         keys = sorted(r for r in side if r & bit)
         rows = side[0].shape[0]
-        got = at["side", s]
+        got = at[SIDE, s]
         kept = {r: v for r, v in side.items() if not r & bit}
         for i, r in enumerate(keys):
             kept[r ^ bit] = add(kept[r ^ bit], got[i * rows : (i + 1) * rows])
@@ -471,7 +536,7 @@
     for bit in bits_of(local, n):
         for key in sorted(have):
             have[(key[0] ^ bit, 0)] = flip(have[key], bit)
-    return jnp.concatenate([have[key] for key in sorted(have)], axis=0)
+    return [have[key] for key in sorted(have)]
 
 
 def gather_back(held, local, n):
@@ -692,6 +757,42 @@
     )(d, w, x, r)
 
 
+def form_kernel(count, own, *refs):
+    ins, (gate_up, down) = refs[:count], refs[count:]
+    wide = gate_up.shape[2]
+    for o in range(count):
+
+        @pl.when(own[0] == o)
+        def _():
+            for e in range(count):
+                gate_up[:, e, :] = ins[o ^ e][:, :wide].astype(F32)
+                down[:, e, :] = ins[o ^ e][:, wide:].astype(F32)
+
+
+def form(blocks, own):
+    rows, k = blocks[0].shape
+    count, ff, tile = len(blocks), k // 3, 32
+    return pl.pallas_call(
+        functools.partial(form_kernel, count),
+        grid_spec=pltpu.PrefetchScalarGridSpec(
+            num_scalar_prefetch=1,
+            grid=(rows // tile,),
+            in_specs=[pl.BlockSpec((tile, k), lambda i, o: (i, 0))] * count,
+            out_specs=[
+                pl.BlockSpec((tile, count, 2 * ff), lambda i, o: (i, 0, 0)),
+                pl.BlockSpec((tile, count, ff), lambda i, o: (i, 0, 0)),
+            ],
+        ),
+        out_shape=[
+            jax.ShapeDtypeStruct((rows, count, 2 * ff), F32),
+            jax.ShapeDtypeStruct((rows, count, ff), F32),
+        ],
+        compiler_params=pltpu.CompilerParams(vmem_limit_bytes=VMEM),
+        cost_estimate=COST,
+        name="form",
+    )(own, *blocks)
+
+
 def inv_rms(v):
     return lax.rsqrt(jnp.mean(v * v, axis=-1, keepdims=True) + EPSILON)
 
@@ -702,8 +803,8 @@
 
 
 def places_and_tables(at, dp, zs, rows):
-    dealt = lax.dynamic_slice_in_dim(at["order"], dp * zs * SEQ_DEV, zs * SEQ_DEV)
-    lens = jnp.take(at["lengths"], dealt).reshape(zs, SEQ_DEV)
+    dealt = lax.dynamic_slice_in_dim(at[ORDER], dp * zs * SEQ_DEV, zs * SEQ_DEV)
+    lens = jnp.take(at[LENGTHS], dealt).reshape(zs, SEQ_DEV)
     ends = jnp.cumsum(lens, axis=1)
     places = jnp.arange(rows, dtype=jnp.int32)
     segment = jnp.sum((places[None, :, None] >= ends[:, None, :]).astype(jnp.int32), axis=2)
@@ -717,10 +818,10 @@
     half = HEAD_DIM // 2
     inverse = ROPE_BASE ** (-2.0 * jnp.arange(half, dtype=F32) / HEAD_DIM)
     turned = (places[None] - offset).astype(F32)[..., None] * inverse
-    at["cos"] = jnp.tile(jnp.cos(turned), (1, 1, 2)).reshape(zs * rows, HEAD_DIM)
+    at[COS] = jnp.tile(jnp.cos(turned), (1, 1, 2)).reshape(zs * rows, HEAD_DIM)
     sin = jnp.sin(turned)
-    at["sin"] = jnp.concatenate([-sin, sin], axis=2).reshape(zs * rows, HEAD_DIM)
-    at["seg"] = segment.astype(F32)[:, None, :]
+    at[SIN] = jnp.concatenate([-sin, sin], axis=2).reshape(zs * rows, HEAD_DIM)
+    at[SEG] = segment.astype(F32)[:, None, :]
 
 
 def on_device(
@@ -754,7 +855,7 @@
     mid = zs // 2
     laid_out = local == 4 and dps == 8
     me_at = jnp.reshape(dp, (1,)).astype(jnp.int32)
-    expert_at = jnp.stack([expert, dp]).astype(jnp.int32)
+    expert_at = jnp.stack([expert, dp, jnp.int32(experts)]).astype(jnp.int32)
     at = Flow()
 
     extra = jnp.concatenate(
@@ -770,53 +871,52 @@
             for e in range(zs)
         ]
     )
-    at["mine"] = lax.all_to_all(sent, "expert", split_axis=0, concat_axis=0, tiled=True)
+    at[MINE] = lax.all_to_all(sent, "expert", split_axis=0, concat_axis=0, tiled=True)
     moved = [(b, (b % dps) * zs + b // dps) for b in range(dps * zs)]
 
     for e in range(local):
-        at["w", 0, e] = jnp.concatenate(
+        at[W, 0, e] = jnp.concatenate(
             [pick(w_gate_up, own ^ e, 1), pick(w_down, own ^ e, 1)], axis=1
         )
-    at["x0"] = tokens
-    at["out"] = w_out
-    at.fence("mine", "x0", "out", *at.having("w"))
-
-    at["attn"] = lax.all_gather(
-        at["mine"].reshape(zs * own_rows, 3 * cols + EXTRA), "dp", axis=0, tiled=True
+    at[X, 0] = tokens
+    at[OUT] = w_out
+    at.fence(MINE, (X, 0), OUT, *at.having(W))
+
+    at[ATTN] = lax.all_gather(
+        at[MINE].reshape(zs * own_rows, 3 * cols + EXTRA), "dp", axis=0, tiled=True
     )
     if laid_out:
-        at["w", 1, 0] = flip(at["w", 0, 1], 1)
-        at["w", 1, 2] = flip(at["w", 0, 3], 1)
-    at["lengths"], at["order"], at["routes"], at["cot"] = lengths, permutation, routes, cotangent
+        at[W, 1, 0] = flip(at[W, 0, 1], 1)
+        at[W, 1, 2] = flip(at[W, 0, 3], 1)
+    at[LENGTHS], at[ORDER], at[ROUTES], at[COT] = lengths, permutation, routes, cotangent
     for i in range(1, zs):
-        at[f"x{i}"] = hop(at[f"x{i - 1}"])
+        at[X, i] = hop(at[X, i - 1])
         if i == 1:
-            at.fence("x1", "lengths", "order", "routes", "cot", "out")
+            at.fence((X, 1), LENGTHS, ORDER, ROUTES, COT, OUT)
             places_and_tables(at, dp, zs, rows)
         elif i == 2:
-            at.fence("x2", "cos", "sin", "seg", "routes", "cot")
-            at["mask"] = jnp.sum(
-                (at["routes"][:, :, None] == jnp.arange(experts, dtype=jnp.int32)).astype(BF16),
+            at.fence((X, 2), COS, SIN, SEG, ROUTES, COT)
+            at[MASK] = jnp.sum(
+                (at[ROUTES][:, :, None] == jnp.arange(experts, dtype=jnp.int32)).astype(BF16),
                 axis=1,
             )
             mask_pad = jnp.concatenate(
-                [at["mask"], jnp.zeros((rows, EXTRA - experts), BF16)], axis=1
+                [at[MASK], jnp.zeros((rows, EXTRA - experts), BF16)], axis=1
             )
-            at["g0"] = jnp.concatenate([at["cot"], mask_pad], axis=1)
-            at["out"] = lax.ppermute(at["out"], ("dp", "expert"), moved)
+            at[G, 0] = jnp.concatenate([at[COT], mask_pad], axis=1)
+            at[OUT] = lax.ppermute(at[OUT], ("dp", "expert"), moved)
         else:
-            at.fence(f"x{i}")
-    xs = [f"x{i}" for i in range(zs)]
-    at.fence("attn", "out", "g0", "mask", *xs, *at.having("w"))
+            at.fence((X, i))
+    xs = [(X, i) for i in range(zs)]
+    at.fence(ATTN, OUT, (G, 0), MASK, *xs, *at.having(W))
 
     cut = e_rows // 4
     if laid_out:
-        at["w", 2, 0] = flip(at["w", 0, 2], 2)
-        at["w", 4, 0] = flip(at["w", 0, 0], 4)
-        at["wa", 5] = flip(at["w", 1, 0][:cut], 4)
-    at["g1"] = hop(at["g0"])
-    out_w = lax.all_gather(at["out"], "dp", axis=0, tiled=True)
-    attn_w = at["attn"]
+        at[W, 2, 0] = flip(at[W, 0, 2], 2)
+        at[W, 4, 0] = flip(at[W, 0, 0], 4)
+    at[G, 1] = hop(at[G, 0])
+    out_w = lax.all_gather(at[OUT], "dp", axis=0, tiled=True)
+    attn_w = at[ATTN]
     qkv_w = attn_w[:, : 3 * cols]
     router_full = attn_w[:, 3 * cols : 3 * cols + experts]
     gains = attn_w[:, 3 * cols + experts : 3 * cols + experts + 4].astype(F32).T
@@ -825,137 +925,178 @@
     xf = x_all.astype(F32)
     r_attn = inv_rms(xf)
     a_all = (xf * r_attn * gains[0]).astype(BF16)
-    at["qkv"] = nn(a_all, qkv_w)
-    at.fence("qkv", "g1")
-    qkv = at["qkv"]
+    at[QKV] = nn(a_all, qkv_w)
+    at.fence(QKV, (G, 1))
+    qkv = at[QKV]
     q, k = qkv[:, :cols], qkv[:, cols : 2 * cols]
-    at["squares"] = lax.psum(
+    at[SQUARES] = lax.psum(
         jnp.stack([jnp.sum(q * q, axis=1), jnp.sum(k * k, axis=1)]), "expert"
     )
-    at.fence("squares", "g1")
-    at["g2"] = hop(at["g1"])
+    at.fence(SQUARES, (G, 1))
+    at[G, 2] = hop(at[G, 1])
     by_block = lambda v: v.reshape(2, zs, rows).transpose(1, 0, 2)
-    r_qk = by_block(lax.rsqrt(at["squares"] / width + EPSILON))
+    r_qk = by_block(lax.rsqrt(at[SQUARES] / width + EPSILON))
     gain_qk = lax.dynamic_slice_in_dim(gains[1:3], z * cols, cols, axis=1)
-    cos, sin, seg = at["cos"], at["sin"], at["seg"]
+    cos, sin, seg = at[COS], at[SIN], at[SEG]
     qr, kr, vb, o = attend(qkv, r_qk, gain_qk, cos, sin, seg)
-    at["added"] = nn(o, out_w, BF16)
-    at.fence("added", "g2", *(w for w in at.having("w") + at.having("wa") if laid_out))
-    at["added"] = lax.psum_scatter(at["added"], "expert", scatter_dimension=0, tiled=True)
+    at[ADDED] = nn(o, out_w, BF16)
+    at.fence(ADDED, (G, 2), *(w for w in at.having(W) if laid_out))
+    at[ADDED] = lax.psum_scatter(at[ADDED], "expert", scatter_dimension=0, tiled=True)
     for i in range(3, zs):
-        at[f"g{i}"] = hop(at[f"g{i - 1}"])
+        at[G, i] = hop(at[G, i - 1])
     if laid_out:
-        at["w", 3, 0] = flip(at["w", 1, 2], 2)
-        at["wb", 5] = flip(at["w", 1, 0][cut:], 4)
-        at["wa", 6] = flip(at["w", 2, 0][: 3 * cut], 4)
-    first_g = [f"g{i}" for i in range(mid)]
-    last_g = [f"g{i}" for i in range(mid, zs)]
-    at["far ga"] = flip(jnp.concatenate([at[key] for key in first_g], axis=0), top)
-    weight_keys = at.having("w") + at.having("wa") + at.having("wb")
-    at.fence("added", "far ga", f"g{zs - 1}", *(w for w in weight_keys if laid_out))
-    at["far gb"] = flip(jnp.concatenate([at[key] for key in last_g], axis=0), top)
-    if laid_out:
-        at["wb", 6] = flip(at["w", 2, 0][3 * cut :], 4)
-        at["w", 7, 0] = flip(at["w", 3, 0], 4)
-    hid = tokens.astype(F32) + at["added"].astype(F32)
+        at[W, 3, 0] = flip(at[W, 1, 2], 2)
+        at[W, 5, 0] = flip(at[W, 1, 0], 4)
+        at[WA, 6] = flip(at[W, 2, 0][: 2 * cut], 4)
+    first_g = [(G, i) for i in range(mid)]
+    last_g = [(G, i) for i in range(mid, zs)]
+    at[FAR_GA] = flip(jnp.concatenate([at[key] for key in first_g], axis=0), top)
+    weight_keys = at.having(W) + at.having(WA)
+    at.fence(ADDED, FAR_GA, (G, zs - 1), *(w for w in weight_keys if laid_out))
+    later = {1: lambda: flip(at[W, 2, 0][2 * cut :], 4)}
+    later[2] = lambda: flip(at[W, 3, 0][: 2 * cut], 4)
+    later[3] = lambda: flip(at[W, 3, 0][2 * cut :], 4)
+    hid = tokens.astype(F32) + at[ADDED].astype(F32)
     r_ffn = inv_rms(hid)
     m = (hid * r_ffn * gains[3]).astype(BF16)
 
-    at["m0"] = m
-    at["far m0"] = flip(m, top)
-    for i in range(1, zs):
-        at[f"m{i}"] = hop(at[f"m{i - 1}"])
-        at.fence(f"m{i}")
-        at[f"far m{i}"] = flip(at[f"m{i}"], top)
+    at[M, 0] = m
     mine_e = (jnp.arange(experts) == expert).astype(F32)
-    g_near = [jnp.concatenate([at[key] for key in first_g + last_g], axis=0)]
-    near_parts = [x for xs in fan(g_near, top) for x in xs]
-    far_parts = [x for xs in fan([at["far ga"], at["far gb"]], top) for x in xs]
-    if laid_out:
-        keys = [("w", r, 0) for r in range(5)] + [(h, r) for r in (5, 6) for h in ("wa", "wb")]
-        weights = jnp.concatenate([at[key] for key in [*keys, ("w", 7, 0)]], axis=0)
-    else:
-        weights = spread({e: at["w", 0, e] for e in range(local)}, dps)
-
-    def chunk_front(parts):
+
+    def chunk_places(kind, parts):
         masks = jnp.concatenate([x[:, width : width + experts] for x in parts], axis=0)
         masks = masks.astype(F32).reshape(-1, rows, experts)
         on = jnp.sum(masks * mine_e, axis=2)
         pos = jnp.where(on > 0, jnp.cumsum(on, axis=1) - 1.0, -1.0).astype(jnp.int32)
-        gs, gw = front(parts, pos, weights, ff, me_at)
-        return pos, pos.T, masks.transpose(0, 2, 1), gs, gw
-
-    def chunk_expert(blocks, pieces, fronted):
-        pos, pos_t, named, gs, gw = fronted
+        at[kind, 0], at[kind, 1], at[kind, 2] = pos, pos.T, masks.transpose(0, 2, 1)
+
+    waiting = [(G, key) for key in last_g] + [(M, (M, i)) for i in range(zs)]
+    for i in range(1, zs):
+        at[M, i] = hop(at[M, i - 1])
+        kind, key = waiting.pop(0)
+        at[FAR, *key] = flip(at[key], top)
+        beside = [(FAR, *key)]
+        if laid_out:
+            at[WB, i] = later[i]()
+            beside.append((WB, i))
+        if i == 2:
+            g_near = [jnp.concatenate([at[key] for key in first_g + last_g], axis=0)]
+            near_parts = [x for xs in fan(g_near, top) for x in xs]
+            chunk_places(NEAR, near_parts)
+        if i == zs - 1:
+            beside += at.having(NEAR)
+        at.fence((M, i), *beside)
+    key = waiting.pop(0)[1]
+    at[FAR, *key] = flip(at[key], top)
+    g_far = [at[FAR_GA], *[at[FAR, *k] for k in last_g]]
+    far_parts = [x for xs in fan(g_far, top) for x in xs]
+    chunk_places(DISTANT, far_parts)
+
+    def chunk_gather(kind, blocks, pieces, g_parts):
         parts = [blocks] + fan(pieces, top)[1:]
         flat = [x for xs in parts for x in xs]
-        backs, outs = run_expert(flat, pos, pos_t, named, router_t, weights, gw, expert_at, ff)
+        got = gather(flat, g_parts, at[kind, 0], at[kind, 2], router_t, expert_at)
+        return parts, got
+
+    def chunk_expert(kind, parts, got):
+        heights = [x.shape[0] for xs in parts for x in xs]
+        backs, outs = run_expert(*got, at[kind, 1], weights, expert_at, heights, ff)
         back = []
         for xs in parts:
             back.append(backs[: len(xs)])
             backs = backs[len(xs) :]
-        return back, (outs[0], gs, outs[1], outs[2], outs[3])
-
-    ms = [at[f"m{i}"] for i in range(zs)]
-    near = chunk_front(near_parts)
-    near_back, near_outs = chunk_expert(ms, [jnp.concatenate(ms, axis=0)], near)
-    far = chunk_front(far_parts)
-    far_ms = [f"far m{i}" for i in range(zs)]
-    at["near gact"] = near_outs[4]
-    at.fence("near gact", *far_ms)
+        return back, (got[0], got[1], *outs)
+
+    ms = [at[M, i] for i in range(zs)]
+    near_parts, near_rows = chunk_gather(NEAR, ms, [jnp.concatenate(ms, axis=0)], near_parts)
+    for i, v in enumerate(near_rows):
+        at[ROWS, i] = v
+    at.fence(*at.having(ROWS), *at.having(DISTANT), (FAR, *key))
+    while waiting:
+        key = waiting.pop(0)[1]
+        at[FAR, *key] = flip(at[key], top)
+    if laid_out:
+        keys = [(W, r, 0) for r in range(6)] + [(WA, 6), (WB, 1), (WB, 2), (WB, 3)]
+        weights = [at[key] for key in keys]
+    else:
+        weights = spread({e: at[W, 0, e] for e in range(local)}, dps)
+    near_back, near_outs = chunk_expert(NEAR, near_parts, [at[ROWS, i] for i in range(3)])
+    far_ms = [(FAR, M, i) for i in range(zs)]
+    at[NEAR_GACT] = near_outs[4]
+    at.fence(NEAR_GACT, *far_ms)
     ms = [at[key] for key in far_ms]
     pieces = [jnp.concatenate(ms[:mid], axis=0), jnp.concatenate(ms[mid:], axis=0)]
-    far_back, far_outs = chunk_expert(ms, pieces, far)
-    near_outs = (*near_outs[:4], at["near gact"])
+    far_parts, far_rows = chunk_gather(DISTANT, ms, pieces, far_parts)
+    far_back, far_outs = chunk_expert(DISTANT, far_parts, far_rows)
+    near_outs = (*near_outs[:4], at[NEAR_GACT])
 
     quarter = dps // 4
     near_sum = fold(near_back)
     far_sum = fold(far_back)
-    chunk_keys = [("c", n) for n in range(10)]
+    chunk_keys = [(C, n) for n in range(10)]
     for key, v in zip(chunk_keys, (*near_outs, *far_outs), strict=True):
         at[key] = v
     for i, v in enumerate(far_sum):
-        at["far", i] = v
-    at.fence(*at.having("far"), *chunk_keys)
+        at[BACKS, i] = v
+    at.fence(*at.having(BACKS), *chunk_keys)
 
     def chunk_grads(first):
         c = [at[key] for key in chunk_keys]
         return grads([c[:5], c[5:]], first, quarter, e_rows)
 
     last = zs - 1
-    highs = [("got", 3 * quarter + i) for i in range(quarter)]
-    at["there"] = flip(at["far", last], top)
-    at["send high"] = chunk_grads(3 * quarter)
-    at.fence("there", "send high", *chunk_keys)
+
+    unit = e_rows // 16
+
+    def send_part(key, row, start, stop):
+        at[PIECE, key, row, start] = flip(at[key][row][start * unit : stop * unit], far_bit)
+
+    def got_row(key, row):
+        if not laid_out:
+            return flip(at[key][row], far_bit)
+        parts = sorted(k for k in at.having(PIECE) if k[1:3] == (key, row))
+        return jnp.concatenate([at[k] for k in parts], axis=0)
+
+    at[THERE] = flip(at[BACKS, last], top)
+    at[SEND_HIGH] = chunk_grads(3 * quarter)
+    at.fence(THERE, SEND_HIGH, *chunk_keys)
     for i in reversed(range(zs)):
-        here = near_sum[i].astype(F32) + at["there"].astype(F32)
+        here = near_sum[i].astype(F32) + at[THERE].astype(F32)
         if i < last:
-            here = here + at["acc"].astype(F32)
-        at["acc"] = here.astype(BF16)
+            here = here + at[ACC].astype(F32)
+        at[ACC] = here.astype(BF16)
         if not i:
             break
-        at["acc"] = hop(at["acc"], -1)
-        at["there"] = flip(at["far", i - 1], top)
+        at[ACC] = hop(at[ACC], -1)
+        at[THERE] = flip(at[BACKS, i - 1], top)
         beside = []
         if i == last:
-            for n in range(quarter):
-                at["got", 3 * quarter + n] = flip(at["send high"][n], far_bit)
-            for n, y in enumerate(result(at["c", 9], far[1], weights, top, me_at)):
-                at["y part", n] = y
-            beside = at.having("y part")
+            if laid_out:
+                send_part(SEND_HIGH, 0, 0, 8)
+            for n, y in enumerate(result(at[C, 9], at[DISTANT, 1], weights, top, me_at)):
+                at[Y_PART, n] = y
+            beside = [*at.having(Y_PART), *at.having(PIECE)]
         if i == last - 1:
-            at["send low"] = chunk_grads(2 * quarter)
-            at["y far"] = fold([[at[key]] for key in at.having("y part")])[0]
-            beside = ["send low", "y far", *highs[: quarter // 2]]
+            for n, y in enumerate(result(at[C, 4], at[NEAR, 1], weights, top, me_at)):
+                at[NEAR_PART, n] = y
+            if laid_out:
+                send_part(SEND_HIGH, 0, 8, 16)
+            beside = [*at.having(NEAR_PART), *at.having(PIECE)]
         if i == last - 2:
-            at["keep high"] = chunk_grads(quarter)
-            beside = ["keep high", *highs[quarter // 2 :]]
-        at.fence("acc", "there", *beside, *chunk_keys)
-    dm = at["acc"].astype(F32)
-    at["y far"] = flip(at["y far"], top)
-    at["got", 2 * quarter] = flip(at["send low"][0], far_bit)
-
-    own_mask = at["mask"].astype(F32)
+            if laid_out:
+                send_part(SEND_HIGH, 1, 0, 8)
+            at[SEND_LOW] = chunk_grads(2 * quarter)
+            at[Y_FAR] = fold([[at[key]] for key in at.having(Y_PART)])[0]
+            at[Y_NEAR] = fold([[at[key]] for key in at.having(NEAR_PART)])[0]
+            beside = [SEND_LOW, Y_FAR, Y_NEAR, *at.having(PIECE)]
+        at.fence(ACC, THERE, *beside, *chunk_keys)
+    dm = at[ACC].astype(F32)
+    at[Y_FAR] = flip(at[Y_FAR], top)
+    if laid_out:
+        send_part(SEND_HIGH, 1, 8, 16)
+        send_part(SEND_LOW, 0, 0, 8)
+
+    own_mask = at[MASK].astype(F32)
     own_logits = jnp.where(own_mask > 0, nn(m, router_full), -1e30)
     own_e = jnp.where(
         own_mask > 0, jnp.exp(own_logits - jnp.max(own_logits, axis=1, keepdims=True)), 0.0
@@ -968,25 +1109,26 @@
     dmt = nt(dz, router_full) + dm[:, :width]
     grad_out = cotangent.astype(F32)
     dh = grad_out + rms_back(hid, r_ffn, gains[3], dmt)
-    at["dhb"] = lax.all_gather(dh.astype(BF16), "expert", axis=0, tiled=True)
+    at[DHB] = lax.all_gather(dh.astype(BF16), "expert", axis=0, tiled=True)
     router_part = tn(m, dz)
     gain_ffn = jnp.sum(dmt * hid * r_ffn, axis=0)
-    at["keep low"] = chunk_grads(0)
-    at["y near"] = fold([[x] for x in result(at["c", 4], near[1], weights, top, me_at)])[0]
-    at["router"], at["gain ffn"] = router_part, gain_ffn
+    at[KEEP_HIGH] = chunk_grads(quarter)
+    at[KEEP_LOW] = chunk_grads(0)
+    at[ROUTER], at[GAIN_FFN] = router_part, gain_ffn
     at.fence(
-        "dhb", "y far", "y near", "keep low", "send low", "router", "gain ffn",
-        ("got", 2 * quarter),
+        DHB, Y_FAR, Y_NEAR, KEEP_LOW, KEEP_HIGH, SEND_LOW, ROUTER, GAIN_FFN, *at.having(PIECE)
     )
-    dhb = at["dhb"]
-    for i in range(1, quarter):
-        at["got", 2 * quarter + i] = flip(at["send low"][i], far_bit)
+    dhb = at[DHB]
+    if laid_out:
+        send_part(SEND_LOW, 0, 8, 16)
+        send_part(SEND_LOW, 1, 0, 10)
     for i in range(quarter):
-        at["tail", quarter + i, 0] = add(at["keep high"][i], at["got", 3 * quarter + i])
+        at[TAIL, quarter + i, 0] = add(at[KEEP_HIGH][i], got_row(SEND_HIGH, i))
     if laid_out:
-        at["tail", 0, 2] = flip(at["tail", 2, 0], 2)
-    y_own = add(at["y near"], at["y far"])
-    at["y"] = lax.psum_scatter(
+        at[TAIL, 0, 2] = flip(at[TAIL, 2, 0], 2)
+        at[HALF, 0] = flip(at[TAIL, 3, 0][: 4 * unit], 2)
+    y_own = add(at[Y_NEAR], at[Y_FAR])
+    at[Y] = lax.psum_scatter(
         by_line([y_own[i * rows : (i + 1) * rows] for i in range(zs)]),
         "expert",
         scatter_dimension=0,
@@ -994,82 +1136,91 @@
     )
 
     dqn, dkn, dv, sums = attend_back(dhb, out_w, qkv, qr, kr, vb, gain_qk, cos, sin, seg)
-    means = lax.psum(sums.transpose(1, 0, 2).reshape(2, zs * rows), "expert") / width
-    dqkv, gains_qk = join_back(qkv, dqn, dkn, dv, r_qk, by_block(means), gain_qk)
-    at["dqkv"] = dqkv
-    lows = [("got", 2 * quarter + i) for i in range(quarter)]
-    at.fence("dqkv", "dhb", "y", *lows, *at.having("tail"))
+    means = lax.psum(sums.reshape(-1, rows), "expert").reshape(zs, 2, rows) / width
+    dqkv, gains_qk = join_back(qkv, dqn, dkn, dv, r_qk, means, gain_qk)
+    at[DQKV] = dqkv
+    at.fence(DQKV, DHB, Y, SEND_LOW, *at.having(PIECE), *at.having(TAIL), *at.having(HALF))
     if laid_out:
-        at["tail", 1, 2] = flip(at["tail", 3, 0], 2)
-
-    at["odd"] = attn_grads(a_all, at["dqkv"], [], me_at, 1, 2)
-    at.fence("odd", "dqkv", "dhb")
-    at["odd"] = flip(at["odd"], 1)
-    at["da"], at["gain attn"] = first_back(at["dqkv"], attn_w, x_all, r_attn, rows)
-    at.fence("odd", "dqkv", "da", "gain attn")
-    at["da"] = lax.psum_scatter(at["da"], "expert", scatter_dimension=0, tiled=True)
-    at["held"] = add(attn_grads(a_all, at["dqkv"], [], me_at, 0, 2), at["odd"])
-    at.fence("held", "dhb")
-    sides = halves(at["held"], zs * own_rows)
+        send_part(SEND_LOW, 1, 10, 16)
+        at[HALF, 4] = flip(at[TAIL, 3, 0][4 * unit : 11 * unit], 2)
+
+    at[ODD] = attn_grads(a_all, at[DQKV], [], me_at, 1, 2)
+    at.fence(ODD, DQKV)
+    at[ODD] = flip(at[ODD], 1)
+    at[DA], at[GAIN_ATTN] = first_back(at[DQKV], attn_w, x_all, r_attn, rows)
+    at.fence(ODD, DQKV, DA, GAIN_ATTN, *at.having(HALF), *at.having(PIECE), *at.having(TAIL))
+    if laid_out:
+        at[HALF, 11] = flip(at[TAIL, 3, 0][11 * unit :], 2)
+    at[DA] = lax.psum_scatter(at[DA], "expert", scatter_dimension=0, tiled=True)
+    at[HELD] = add(attn_grads(a_all, at[DQKV], [], me_at, 0, 2), at[ODD])
+    at.fence(HELD, DHB, GAIN_ATTN, *at.having(HALF))
+    sides = halves(at[HELD], zs * own_rows)
     stage(at, sides, 0)
-    out_blocks = tn(o, at["dhb"], BF16).reshape(dps, own_rows, width)
-    at["out grad"] = jnp.concatenate([pick(out_blocks, dp ^ r, 0) for r in range(dps)], axis=0)
-    for i in range(quarter):
-        at["tail", i, 0] = add(at["keep low"][i], at["got", 2 * quarter + i])
+    out_blocks = tn(o, at[DHB], BF16).reshape(dps, own_rows, width)
+    for r in range(dps):
+        at[OUT_GRAD, r] = pick(out_blocks, dp ^ r, 0)
+    zero = jnp.zeros((2, width), F32)
+    gain_rows = jnp.concatenate(
+        [
+            at[GAIN_ATTN],
+            lax.dynamic_update_slice_in_dim(zero, gains_qk, z * cols, 1),
+            at[GAIN_FFN][None],
+            jnp.zeros((EXTRA - experts - 4, width), F32),
+        ],
+        axis=0,
+    )
+    at[BESIDE] = jnp.concatenate([at[ROUTER], gain_rows.T], axis=1).astype(BF16)
     for turn_ in range(1, len(bits_of(2, dps))):
-        at.fence(*at.having("side"), "out grad", *at.having("tail"))
+        at.fence(*at.having(SIDE), BESIDE, DA, *at.having(OUT_GRAD))
         sides = unstage(at, sides, turn_ - 1)
         stage(at, sides, turn_)
-        if laid_out:
-            for e in (0, 2):
-                at["tail", 0, e ^ 1] = flip(at["tail", 1, e], 1)
-    at.fence(*at.having("side"), "out grad", "gain attn", "da", *at.having("tail"))
+        if turn_ == 1 and laid_out:
+            scatter_step(at, 1)
+    at[BESIDE] = lax.psum_scatter(at[BESIDE], "dp", scatter_dimension=0, tiled=True)
+    at.fence(*at.having(SIDE), *at.having(OUT_GRAD))
     sides = unstage(at, sides, len(bits_of(2, dps)) - 1)
-    at["back"] = lax.all_to_all(
-        jnp.concatenate([sides[0][0][0], sides[1][0][0]], axis=1).reshape(zs, own_rows, 3 * cols),
+    at[BACK] = jnp.concatenate([sides[0][0][0], sides[1][0][0]], axis=1)
+    at.fence(BACK, KEEP_LOW, *at.having(OUT_GRAD), *at.having(TAIL), *at.having(HALF))
+    for i in range(quarter):
+        at[TAIL, i, 0] = add(at[KEEP_LOW][i], got_row(SEND_LOW, i))
+    if laid_out:
+        at[TAIL, 1, 2] = jnp.concatenate([at[HALF, 0], at[HALF, 4], at[HALF, 11]], axis=0)
+        for e in (0, 2):
+            at[TAIL, 0, e ^ 1] = flip(at[TAIL, 1, e], 1)
+    at[BACK] = lax.all_to_all(
+        at[BACK].reshape(zs, own_rows, 3 * cols),
         "expert",
         split_axis=0,
         concat_axis=0,
         tiled=True,
     )
     if laid_out:
-        blocks = {e: at["tail", 0, e] for e in range(local)}
+        blocks = {e: at[TAIL, 0, e] for e in range(local)}
     else:
-        blocks = gather_back({k[1]: at[k] for k in at.having("tail")}, local, dps)
-    stacked = jnp.stack([blocks[e] for e in range(local)])
-    blocks = [pick(stacked, own ^ e, 0) for e in range(local)]
-    at["gu"] = jnp.stack([b[:, : 2 * ff] for b in blocks], axis=1).astype(F32)
-    at["dn"] = jnp.stack([b[:, 2 * ff :] for b in blocks], axis=1).astype(F32)
-    zero = jnp.zeros((2, width), F32)
-    gain_rows = jnp.concatenate(
-        [
-            at["gain attn"],
-            lax.dynamic_update_slice_in_dim(zero, gains_qk, z * cols, 1),
-            at["gain ffn"][None],
-            jnp.zeros((EXTRA - experts - 4, width), F32),
-        ],
-        axis=0,
-    )
-    extra_part = jnp.concatenate([at["router"], gain_rows.T], axis=1).astype(BF16)
-    at["extra"] = lax.psum_scatter(extra_part, "dp", scatter_dimension=0, tiled=True)
-    at["out grad"] = scatter_dp(at["out grad"], own_rows)
-    at.fence("back", "extra", "gu", "dn", "out grad")
+        blocks = gather_back({k[1]: at[k] for k in at.having(TAIL)}, local, dps)
+    at[GU], at[DN] = form([blocks[e] for e in range(local)], jnp.reshape(own, (1,)))
+    for bit in bits_of(2 if laid_out else 1, dps):
+        scatter_step(at, bit)
+    at.fence(BACK, GU, DN, BESIDE, *at.having(OUT_GRAD))
     grad_w_out = lax.ppermute(
-        at["out grad"], ("dp", "expert"), [(b, a) for a, b in moved]
+        at[OUT_GRAD, 0], ("dp", "expert"), [(b, a) for a, b in moved]
     ).astype(F32)
-    back = at["back"].astype(F32)
+    back = at[BACK].astype(F32)
     grad_w_qkv = jnp.concatenate(
         [back[e, :, i * cols : (i + 1) * cols] for i in range(3) for e in range(zs)], axis=1
     )
-    extra_back = lax.all_to_all(
-        at["extra"].reshape(zs, own_rows, EXTRA), "expert", split_axis=0, concat_axis=0, tiled=True
-    )
-    extra_sum = jnp.sum(extra_back.astype(F32), axis=0)
+    line = ring(zs)
+    place = jnp.asarray([line.index(i) for i in range(zs)], jnp.int32)[z]
+    blocks = at[BESIDE].reshape(zs, own_rows, EXTRA)
+    extra_sum = pick(blocks, z, 0).astype(F32)
+    for i in range(1, zs):
+        to = jnp.asarray(line, jnp.int32)[lax.rem(place + i, zs)]
+        extra_sum = extra_sum + hop(pick(blocks, to, 0), i).astype(F32)
     grad_router = extra_sum[:, :experts]
     grad_gains = extra_sum[:, experts : experts + 4]
-    da = at["da"].astype(F32)
-
-    output = hid + at["y"].astype(F32)
+    da = at[DA].astype(F32)
+
+    output = hid + at[Y].astype(F32)
     x_own = tokens.astype(F32)
     grad_tokens = dh + rms_back(x_own, inv_rms(x_own), gains[0], da)
     return (
@@ -1079,8 +1230,8 @@
         grad_w_qkv,
         grad_w_out,
         grad_router,
-        at["gu"],
-        at["dn"],
+        at[GU],
+        at[DN],
     )
 
 

time: 769 us -> 735 us (0.956)
  local copies, waits for them, and re-layouts: 124 us -> 81 us
    unnamed x195 -> x204, local copies, waits for them, and re-layouts: 57.7 us -> 15.5 us
    ppermute x2, waiting for transfers between devices: 3.33 us -> 15.6 us  [the longest x1 12.8 us: on_device(): lax.ppermute(at[OUT_GRAD, 0], ('dp', 'expert'), [(b, a) for a, b in moved])]
    ppermute x12 -> x15, waiting for transfers between devices: 41.6 us -> 29.8 us  [hop(): return lax.ppermute(v, 'expert', pairs)]
    ppermute x48 -> x56, waiting for transfers between devices: 169 us -> 160 us  [flip(): lax.ppermute(v, 'dp', [(i, i ^ bit) for i in range(lax.axis_size('dp'))])]
    slice x17 -> x27, local copies, waits for them, and re-layouts: 12.3 us -> 21.4 us  [the longest x16 9.01 us: chunk_places(): x[:, width:width + experts]]
    pallas_call x6 -> x7, Pallas kernels: 91.4 us -> 96.4 us  [the longest x2 49.7 us: run_expert(): pl.pallas_call(functools.partial(expert_kernel, len(heights), len(pieces)...]
    convert_element_type x12 -> x10, other arithmetic: 16.4 us -> 12.1 us  [the longest x3 5.6 us: on_device(): at[ACC] = here.astype(BF16)]
    ppermute x48 -> x56, starting transfers between devices: 38.3 us -> 41.9 us  [flip(): lax.ppermute(v, 'dp', [(i, i ^ bit) for i in range(lax.axis_size('dp'))])]
  transfers between devices with their start and end apart: 72 -> 82, of which waited for: 26 -> 39; matrix products, arithmetic and copies ran while one was open for 25% -> 20% of each run, Pallas kernels for 20% -> 21%
where the time goes in v4:
time: 735 us; the launch traced here: 724 us
  waiting for transfers between devices  217 us (30%)
  Pallas kernels  190 us (26%)
  other arithmetic  89.6 us (12%)
  local copies, waits for them, and re-layouts  81 us (11%)
  starting transfers between devices  80.4 us (11%)
  between operations  31 us (4%)
  blocking collectives  19.9 us (3%)
  matrix products  15.6 us (2%)
    ppermute x56, waiting for transfers between devices, flip(): lax.ppermute(v, 'dp', [(i, i ^ bit) for i in range(lax.axis_size('dp'))])  160 us
    pallas_call x2, Pallas kernels, run_expert(): pl.pallas_call(functools.partial(expert_kernel, len(heights), len(pieces)...  49.7 us
    ppermute x56, starting transfers between devices, flip(): lax.ppermute(v, 'dp', [(i, i ^ bit) for i in range(lax.axis_size('dp'))])  41.9 us
    pallas_call x4, Pallas kernels, grads(): pl.pallas_call(functools.partial(grads_kernel, len(chunks)), grid=(blocks...  41.6 us
    ppermute x15, waiting for transfers between devices, hop(): return lax.ppermute(v, 'expert', pairs)  29.8 us
    convert_element_type x13, other arithmetic, add(): return (a.astype(F32) + b.astype(F32)).astype(BF16)  29.5 us
    ppermute x15, starting transfers between devices, hop(): return lax.ppermute(v, 'expert', pairs)  25.9 us
    pallas_call x2, Pallas kernels, result(): pl.pallas_call(functools.partial(result_kernel, count, len(pieces), wide)...  19.7 us
  transfers between devices with their start and end apart: 82, of which 39 were waited for; matrix products, arithmetic and copies ran while one was open for 20% of the time, Pallas kernels for 21%

profile of v4, /device:TPU:4, one launch (start us, length us, event | category | flops | bytes accessed | tf_op | source)
XLA Modules:
  0.0 724.0 jit_solution(16915240841218231162)
XLA Ops:
  20.7 8.7 %constant_dynamic-slice_fusion.2 = (bf16[256,1,2048]{2,1,0:T(2,128)(2,1)S(1)}, bf16[256,1,2048]{2,1,0:T(2,128)(2,1)S(1)}, bf16[256,1,2048]{2,1,0:T(2,128)(2,1)S(1)}, bf16[256,1,2048]{2,1,0:T(2,128)(2,1)S(1)}) fusion(bf16[256,4,2048]{2,1,0:T(4,128)(2,1)S(1)} %copy-done.13, s32[]{:T(128)S(6)} %select_n.142, s32[]{:T(128)S(6)} %select_n.141, ...), kind=kLoop, calls=%fused_computation.199 | loop fusion | bytes 8388624 | tf_op jit(solution)/shard_map/jit(dynamic_index_in_dim)/dynamic_slice | solution.py:81
  41.4 10.7 %collective-permute-done = bf16[128,2048]{1,0:T(8,128)(2,1)} collective-permute-done((bf16[128,2048]{1,0:T(8,128)(2,1)}, bf16[128,2048]{1,0:T(8,128)(2,1)}, u32[]{:S(2)}, u32[]{:S(2)}) %collective-permute-start) | collective-permute-done | bytes 524320 | tf_op jit(solution)/shard_map/ppermute | solution.py:52
  119.1 9.9 %psum.14 = f32[2,512]{1,0:T(2,128)S(1)} all-reduce(f32[2,512]{1,0:T(2,128)S(1)} %pad_maximum_fusion.21), channel_id=1, replica_groups=mesh['dp'=8,'expert'=4] {'expert'}, use_global_device_ids=true, to_apply=%region_7.8 | all-reduce | flops 1024 | bytes 8192 | tf_op jit(solution)/shard_map/psum | solution.py:932
  129.7 8.7 %attend.1 = (bf16[512,512]{1,0:T(8,128)(2,1)}, bf16[512,512]{1,0:T(8,128)(2,1)}, bf16[512,512]{1,0:T(8,128)(2,1)}, bf16[512,512]{1,0:T(8,128)(2,1)}) custom-call(f32[512,1536]{1,0:T(8,128)} %copy-done.5, f32[4,2,128]{2,1,0:T(2,128)} %rsqrt_bitcast_fusion.r, f32[2,512]{1,0:T(2,128)} %copy.252.gains, f32[512,128]{1,0:T(8,128)} %copy.253.cos, ...), custom_call_target="tpu_custom_call" | custom-call | flops 1000000 | bytes 100000 | tf_op jit(solution)/shard_map/attend/pallas_call | solution.py:593
  159.5 50.3 %collective-permute-done.10.refs_6_ = bf16[256,2176]{1,0:T(8,128)(2,1)} collective-permute-done((bf16[256,2176]{1,0:T(8,128)(2,1)S(1)}, bf16[256,2176]{1,0:T(8,128)(2,1)}, u32[]{:S(2)}, u32[]{:S(2)}) %collective-permute-start.10) | collective-permute-done | bytes 1114144 | tf_op jit(solution)/shard_map/ppermute | solution.py:41
  223.3 8.3 %collective-permute-done.15.refs_1_ = bf16[128,2048]{1,0:T(8,128)(2,1)} collective-permute-done((bf16[128,2048]{1,0:T(8,128)(2,1)S(1)}, bf16[128,2048]{1,0:T(8,128)(2,1)}, u32[]{:S(2)}, u32[]{:S(2)}) %collective-permute-start.15) | collective-permute-done | bytes 524320 | tf_op jit(solution)/shard_map/ppermute | solution.py:52
  288.8 8.5 %gather.9 = (bf16[640,2048]{1,0:T(8,128)(2,1)}, bf16[640,2048]{1,0:T(8,128)(2,1)}, f32[640,1]{1,0:T(8,128)}) custom-call(s32[3]{0:T(128)} %pad_add_fusion.expert, bf16[128,2048]{1,0:T(8,128)(2,1)} %copy-done.14, bf16[128,2048]{1,0:T(8,128)(2,1)} %collective-permute-done.15.refs_1_, bf16[128,2048]{1,0:T(8,128)(2,1)} %copy-done.41, ...), custom_call_target="tpu_custom_call" | custom-call | flops 1000000 | bytes 100000 | tf_op jit(solution)/shard_map/gather/pallas_call | solution.py:266
  298.7 24.7 %expert.2 = (bf16[128,2176]{1,0:T(8,128)(2,1)}, bf16[128,2176]{1,0:T(8,128)(2,1)}, bf16[128,2176]{1,0:T(8,128)(2,1)}, bf16[128,2176]{1,0:T(8,128)(2,1)}, bf16[51...) custom-call(s32[3]{0:T(128)} %pad_add_fusion.expert, ...), custom_call_target="tpu_custom_call" | custom-call | flops 1000000 | bytes 100000 | tf_op jit(solution)/shard_map/expert/pallas_call | solution.py:356
  328.1 8.4 %gather.10 = (bf16[640,2048]{1,0:T(8,128)(2,1)}, bf16[640,2048]{1,0:T(8,128)(2,1)}, f32[640,1]{1,0:T(8,128)}) custom-call(s32[3]{0:T(128)} %pad_add_fusion.expert, bf16[128,2048]{1,0:T(8,128)(2,1)} %copy-done.37, bf16[128,2048]{1,0:T(8,128)(2,1)} %copy-done.38, bf16[128,2048]{1,0:T(8,128)(2,1)} %copy-done.39, bf16[128,2048]{1,0:T(8,128)(2,1)} %copy-done.40, ...), custom_call_target="tpu_custom_call" | custom-call | flops 1000000 | bytes 100000 | tf_op jit(solution)/shard_map/gather/pallas_call | solution.py:266
  336.6 25.0 %expert.3 = (bf16[128,2176]{1,0:T(8,128)(2,1)}, bf16[128,2176]{1,0:T(8,128)(2,1)}, bf16[128,2176]{1,0:T(8,128)(2,1)}, bf16[128,2176]{1,0:T(8,128)(2,1)}, bf16[25...) custom-call(s32[3]{0:T(128)} %pad_add_fusion.expert, ...), custom_call_target="tpu_custom_call" | custom-call | flops 1000000 | bytes 100000 | tf_op jit(solution)/shard_map/expert/pallas_call | solution.py:356
  368.6 10.2 %grads.4 = bf16[2,256,3072]{2,1,0:T(8,128)(2,1)} custom-call(bf16[640,2048]{1,0:T(8,128)(2,1)} %get-tuple-element.441.refs_0_, bf16[640,2048]{1,0:T(8,128)(2,1)} %get-tuple-element.442.refs_1_, bf16[640,1024]{1,0:T(8,128)(2,1)} %get-tuple-element.443.refs_2_, bf16[640,1024]{1,0:T(8,128)(2,1)} %get-tuple-element.444.refs_3_, ...), custom_call_target="tpu_custom_call" | custom-call | flops 1000000 | bytes 100000 | tf_op jit(solution)/shard_map/grads/pallas_call | solution.py:450
  389.6 10.0 %result.2 = (bf16[512,2048]{1,0:T(8,128)(2,1)}, bf16[512,2048]{1,0:T(8,128)(2,1)}) custom-call(s32[1]{0:T(128)} %bitcast.34.me, bf16[640,1024]{1,0:T(8,128)(2,1)} %get-tuple-element.450.refs_9_.gact, s32[128,8]{1,0:T(8,128)} %bitcast.227, bf16[256,3072]{1,0:T(8,128)(2,1)} %copy-done.2, bf16[256,3072]{1,0:T(8,128)(2,1)} %copy-done.6, ...), custom_call_target="tpu_custom_call" | custom-call | flops 1000000 | bytes 100000 | tf_op jit(solution)/shard_map/result/pallas_call | solution.py:406
  408.1 9.8 %result.3 = (bf16[512,2048]{1,0:T(8,128)(2,1)}, bf16[512,2048]{1,0:T(8,128)(2,1)}) custom-call(s32[1]{0:T(128)} %bitcast.34.me, bf16[640,1024]{1,0:T(8,128)(2,1)} %get-tuple-element.445.refs_4_.gact, s32[128,8]{1,0:T(8,128)} %bitcast.225, bf16[256,3072]{1,0:T(8,128)(2,1)} %copy-done.2, bf16[256,3072]{1,0:T(8,128)(2,1)} %copy-done.6, ...), custom_call_target="tpu_custom_call" | custom-call | flops 1000000 | bytes 100000 | tf_op jit(solution)/shard_map/result/pallas_call | solution.py:406
  430.2 10.4 %grads.5 = bf16[2,256,3072]{2,1,0:T(8,128)(2,1)} custom-call(bf16[640,2048]{1,0:T(8,128)(2,1)} %get-tuple-element.441.refs_0_, bf16[640,2048]{1,0:T(8,128)(2,1)} %get-tuple-element.442.refs_1_, bf16[640,1024]{1,0:T(8,128)(2,1)} %get-tuple-element.443.refs_2_, bf16[640,1024]{1,0:T(8,128)(2,1)} %get-tuple-element.444.refs_3_, ...), custom_call_target="tpu_custom_call" | custom-call | flops 1000000 | bytes 100000 | tf_op jit(solution)/shard_map/grads/pallas_call | solution.py:450
  459.1 10.7 %grads.6 = bf16[2,256,3072]{2,1,0:T(8,128)(2,1)} custom-call(bf16[640,2048]{1,0:T(8,128)(2,1)} %get-tuple-element.441.refs_0_, bf16[640,2048]{1,0:T(8,128)(2,1)} %get-tuple-element.442.refs_1_, bf16[640,1024]{1,0:T(8,128)(2,1)} %get-tuple-element.443.refs_2_, bf16[640,1024]{1,0:T(8,128)(2,1)} %get-tuple-element.444.refs_3_, ...), custom_call_target="tpu_custom_call" | custom-call | flops 1000000 | bytes 100000 | tf_op jit(solution)/shard_map/grads/pallas_call | solution.py:450
  469.8 10.3 %grads.7 = bf16[2,256,3072]{2,1,0:T(8,128)(2,1)} custom-call(bf16[640,2048]{1,0:T(8,128)(2,1)} %get-tuple-element.441.refs_0_, bf16[640,2048]{1,0:T(8,128)(2,1)} %get-tuple-element.442.refs_1_, bf16[640,1024]{1,0:T(8,128)(2,1)} %get-tuple-element.443.refs_2_, bf16[640,1024]{1,0:T(8,128)(2,1)} %get-tuple-element.444.refs_3_, ...), custom_call_target="tpu_custom_call" | custom-call | flops 1000000 | bytes 100000 | tf_op jit(solution)/shard_map/grads/pallas_call | solution.py:450
  481.9 9.9 %collective-permute-done.51 = bf16[128,3072]{1,0:T(8,128)(2,1)} collective-permute-done((bf16[128,3072]{1,0:T(8,128)(2,1)S(1)}, bf16[128,3072]{1,0:T(8,128)(2,1)}, u32[]{:S(2)}, u32[]{:S(2)}) %collective-permute-start.51) | collective-permute-done | bytes 786464 | tf_op jit(solution)/shard_map/ppermute | solution.py:41
  491.8 11.1 %collective-permute-done.49 = bf16[512,2048]{1,0:T(8,128)(2,1)} collective-permute-done((bf16[512,2048]{1,0:T(8,128)(2,1)}, bf16[512,2048]{1,0:T(8,128)(2,1)}, u32[]{:S(2)}, u32[]{:S(2)}) %collective-permute-start.49) | collective-permute-done | bytes 2097184 | tf_op jit(solution)/shard_map/ppermute | solution.py:41
  518.6 14.0 %attend_back.1 = (f32[512,512]{1,0:T(8,128)}, f32[512,512]{1,0:T(8,128)}, bf16[512,512]{1,0:T(8,128)(2,1)}, f32[4,2,128]{2,1,0:T(2,128)}) custom-call(bf16[512,2048]{1,0:T(8,128)(2,1)} %all-gather.8.cloned.1.call-done.dhb, bf16[512,2048]{1,0:T(8,128)(2,1)} %all-gather.6.cloned.1.call-done.wo, f32[512,1536]{1,0:T(8,128)} %copy-done.5, f32[512,1536]{1,0:T(8,128)} %copy-done.5, ...), custom_call_target="tpu_custom_call" | custom-call | flops 1000000 | bytes 100000 | tf_op jit(solution)/shard_map/attend_back/pallas_call | solution.py:644
  532.6 10.0 %psum.15 = f32[8,128]{1,0:T(8,128)S(1)} all-reduce(f32[8,128]{1,0:T(8,128)} %bitcast.247), channel_id=1, replica_groups=mesh['dp'=8,'expert'=4] {'expert'}, use_global_device_ids=true, to_apply=%region_19.20 | all-reduce | flops 1024 | bytes 8192 | tf_op jit(solution)/shard_map/psum | solution.py:1139
  567.4 12.8 %first_back.1 = (bf16[512,2048]{1,0:T(8,128)(2,1)}, f32[1,2048]{1,0:T(1,128)}) custom-call(bf16[512,1536]{1,0:T(8,128)(2,1)} %get-tuple-element.486.d, bf16[2048,1664]{1,0:T(8,128)(2,1)} %all-gather.4.cloned.1.call-done.w, bf16[512,2048]{1,0:T(8,128)(2,1)} %copy-done.12, f32[512,1]{1,0:T(8,128)} %copy.279.r), custom_call_target="tpu_custom_call" | custom-call | flops 1000000 | bytes 100000 | tf_op jit(solution)/shard_map/first_back/pallas_call | solution.py:737
  612.3 8.0 %collective-permute-done.60 = bf16[512,768]{1,0:T(8,128)(2,1)} collective-permute-done((bf16[512,768]{1,0:T(8,128)(2,1)}, bf16[512,768]{1,0:T(8,128)(2,1)}, u32[]{:S(2)}, u32[]{:S(2)}) %collective-permute-start.60) | collective-permute-done | bytes 786464 | tf_op jit(solution)/shard_map/ppermute | solution.py:41
  680.4 10.1 %form.1 = (f32[256,4,2048]{2,1,0:T(4,128)}, f32[256,4,1024]{2,1,0:T(4,128)}) custom-call(s32[1]{0:T(128)} %bitcast.75.own, bf16[256,3072]{1,0:T(8,128)(2,1)} %get-tuple-element.600.refs_0_, bf16[256,3072]{1,0:T(8,128)(2,1)} %collective-permute-done.65.refs_1_, bf16[256,3072]{1,0:T(8,128)(2,1)} %collective-permute-done.54.refs_2_, ...), custom_call_target="tpu_custom_call" | custom-call | flops 1000000 | bytes 100000 | tf_op jit(solution)/shard_map/form/pallas_call | solution.py:775
  703.3 12.8 %collective-permute-done.72 = bf16[64,2048]{1,0:T(8,128)(2,1)S(1)} collective-permute-done((bf16[64,2048]{1,0:T(8,128)(2,1)S(1)}, bf16[64,2048]{1,0:T(8,128)(2,1)S(1)}, u32[]{:S(2)}, u32[]{:S(2)}) %collective-permute-start.72) | collective-permute-done | bytes 262176 | tf_op jit(solution)/shard_map/ppermute | solution.py:1205
  (547 shorter events, 379.8 us)
Async XLA Ops:
  16.3 75.2 %all-gather.4.cloned.1.call-start = ((), (), s32[]{:S(2)}) async-start(), calls=%async_computation.6 | async-start | bytes 7667712 | tf_op jit(solution)/shard_map/all_gather | solution.py:885
  38.8 99.6 %all-gather.6.cloned.1.call-start = ((), (), s32[]{:S(2)}) async-start(), calls=%async_computation.7 | async-start | bytes 2359296 | tf_op jit(solution)/shard_map/all_gather | solution.py:918
  40.9 46.1 %collective-permute-start.4 = (bf16[256,3072]{1,0:T(8,128)(2,1)}, bf16[256,3072]{1,0:T(8,128)(2,1)S(1)}, u32[]{:S(2)}, u32[]{:S(2)}) collective-permute-start(bf16[256,3072]{1,0:T(8,128)(2,1)} %pad_maximum_fusion.6), channel_id=1, source_target_pairs={{0,4},{4,0},{8,12},{12,8},{16,20},{20,16},{24,28},{28,24},{1,5},{5... | collective-permute-start | bytes 4718600 | tf_op jit(solution)/shard_map/ppermute | solution.py:41
  40.9 46.1 %collective-permute-start.5 = (bf16[256,3072]{1,0:T(8,128)(2,1)}, bf16[256,3072]{1,0:T(8,128)(2,1)}, u32[]{:S(2)}, u32[]{:S(2)}) collective-permute-start(bf16[256,3072]{1,0:T(8,128)(2,1)} %pad_maximum_fusion.8), channel_id=1, source_target_pairs={{0,4},{4,0},{8,12},{12,8},{16,20},{20,16},{24,28},{28,24},{1,5},{5... | collective-permute-start | bytes 4718600 | tf_op jit(solution)/shard_map/ppermute | solution.py:41
  97.1 114.2 %reduce-scatter.5.cloned.1.call-start = ((), (), s32[]{:S(2)}) async-start(), calls=%async_computation.8 | async-start | bytes 2621440 | tf_op jit(solution)/shard_map/reduce_scatter | solution.py:944
  101.7 47.1 %collective-permute-start.8 = (bf16[256,3072]{1,0:T(8,128)(2,1)}, bf16[256,3072]{1,0:T(8,128)(2,1)S(1)}, u32[]{:S(2)}, u32[]{:S(2)}) collective-permute-start(bf16[256,3072]{1,0:T(8,128)(2,1)} %pad_maximum_fusion.7), channel_id=1, source_target_pairs={{0,8},{4,12},{8,0},{12,4},{16,24},{20,28},{24,16},{28,20},{1,9},{5... | collective-permute-start | bytes 4718600 | tf_op jit(solution)/shard_map/ppermute | solution.py:41
  105.7 44.5 %collective-permute-start.9 = (bf16[256,3072]{1,0:T(8,128)(2,1)S(1)}, bf16[256,3072]{1,0:T(8,128)(2,1)}, u32[]{:S(2)}, u32[]{:S(2)}) collective-permute-start(bf16[256,3072]{1,0:T(8,128)(2,1)S(1)} %pad_maximum_fusion.5.refs_4_.refs_14_.refs_24_.refs_0_), channel_id=1, source_target_pairs={{0,16},{4,20},{8,24},{12,28},{16,0},{20,4},{24,8},{28,12},{1,17},{... | collective-permute-start | bytes 4718600 | tf_op jit(solution)/shard_map/ppermute | solution.py:41
  150.2 352.7 %all-gather.8.cloned.1.call-start = ((), (), s32[]{:S(2)}) async-start(), calls=%async_computation.9 | async-start | bytes 2621440 | tf_op jit(solution)/shard_map/all_gather | solution.py:1112
  150.3 60.2 %collective-permute-start.12 = (bf16[256,3072]{1,0:T(8,128)(2,1)}, bf16[256,3072]{1,0:T(8,128)(2,1)S(1)}, u32[]{:S(2)}, u32[]{:S(2)}) collective-permute-start(bf16[256,3072]{1,0:T(8,128)(2,1)} %collective-permute-done.5), channel_id=1, source_target_pairs={{0,8},{4,12},{8,0},{12,4},{16,24},{20,28},{24,16},{28,20},{1,9},{5... | collective-permute-start | bytes 4718600 | tf_op jit(solution)/shard_map/ppermute | solution.py:41
  150.7 60.6 %collective-permute-start.13 = (bf16[256,3072]{1,0:T(8,128)(2,1)}, bf16[256,3072]{1,0:T(8,128)(2,1)}, u32[]{:S(2)}, u32[]{:S(2)}) collective-permute-start(bf16[256,3072]{1,0:T(8,128)(2,1)} %copy-done.6), channel_id=1, source_target_pairs={{0,16},{4,20},{8,24},{12,28},{16,0},{20,4},{24,8},{28,12},{1,17},{... | collective-permute-start | bytes 4718600 | tf_op jit(solution)/shard_map/ppermute | solution.py:41
  152.2 57.6 %collective-permute-start.10 = (bf16[256,2176]{1,0:T(8,128)(2,1)S(1)}, bf16[256,2176]{1,0:T(8,128)(2,1)}, u32[]{:S(2)}, u32[]{:S(2)}) collective-permute-start(bf16[256,2176]{1,0:T(8,128)(2,1)S(1)} %pad_maximum_fusion.10), channel_id=1, source_target_pairs={{0,8},{4,12},{8,0},{12,4},{16,24},{20,28},{24,16},{28,20},{1,9},{5... | collective-permute-start | bytes 3342344 | tf_op jit(solution)/shard_map/ppermute | solution.py:41
  154.1 56.4 %collective-permute-start.14 = (bf16[128,3072]{1,0:T(8,128)(2,1)S(1)}, bf16[128,3072]{1,0:T(8,128)(2,1)S(1)}, u32[]{:S(2)}, u32[]{:S(2)}) collective-permute-start(bf16[128,3072]{1,0:T(8,128)(2,1)S(1)} %slice.367), channel_id=1, source_target_pairs={{0,16},{4,20},{8,24},{12,28},{16,0},{20,4},{24,8},{28,12},{1,17},{... | collective-permute-start | bytes 2359304 | tf_op jit(solution)/shard_map/ppermute | solution.py:41
  155.9 54.5 %collective-permute-start.11 = (bf16[128,2176]{1,0:T(8,128)(2,1)}, bf16[128,2176]{1,0:T(8,128)(2,1)}, u32[]{:S(2)}, u32[]{:S(2)}) collective-permute-start(bf16[128,2176]{1,0:T(8,128)(2,1)} %collective-permute-done.7), channel_id=1, source_target_pairs={{0,2},{2,3},{3,1},{1,0},{4,6},{6,7},{7,5},{5,4},{8,10},{10,11},{11... | collective-permute-start | bytes 1671176 | tf_op jit(solution)/shard_map/ppermute | solution.py:52
  215.8 48.5 %collective-permute-start.24 = (bf16[512,2176]{1,0:T(8,128)(2,1)}, bf16[512,2176]{1,0:T(8,128)(2,1)}, u32[]{:S(2)}, u32[]{:S(2)}) collective-permute-start(bf16[512,2176]{1,0:T(8,128)(2,1)} %constant_dynamic-update-slice_fusion.refs_5_), channel_id=1, source_target_pairs={{0,4},{4,0},{8,12},{12,8},{16,20},{20,16},{24,28},{28,24},{1,5},{5... | collective-permute-start | bytes 6684680 | tf_op jit(solution)/shard_map/ppermute | solution.py:41
  285.0 38.5 %collective-permute-start.31 = (bf16[128,2048]{1,0:T(8,128)(2,1)}, bf16[128,2048]{1,0:T(8,128)(2,1)S(1)}, u32[]{:S(2)}, u32[]{:S(2)}) collective-permute-start(bf16[128,2048]{1,0:T(8,128)(2,1)} %copy-done.41), channel_id=1, source_target_pairs={{0,8},{4,12},{8,0},{12,4},{16,24},{20,28},{24,16},{28,20},{1,9},{5... | collective-permute-start | bytes 1572872 | tf_op jit(solution)/shard_map/ppermute | solution.py:41
  285.8 37.7 %collective-permute-start.32 = (bf16[128,2048]{1,0:T(8,128)(2,1)}, bf16[128,2048]{1,0:T(8,128)(2,1)S(1)}, u32[]{:S(2)}, u32[]{:S(2)}) collective-permute-start(bf16[128,2048]{1,0:T(8,128)(2,1)} %collective-permute-done.21.refs_3_), channel_id=1, source_target_pairs={{0,8},{4,12},{8,0},{12,4},{16,24},{20,28},{24,16},{28,20},{1,9},{5... | collective-permute-start | bytes 1572872 | tf_op jit(solution)/shard_map/ppermute | solution.py:41
  455.0 100.9 %reduce-scatter.7.cloned.1.call-start = ((), (), s32[]{:S(2)}) async-start(), calls=%async_computation.10 | async-start | bytes 2621440 | tf_op jit(solution)/shard_map/reduce_scatter | solution.py:1131
  455.1 47.9 %collective-permute-start.49 = (bf16[512,2048]{1,0:T(8,128)(2,1)}, bf16[512,2048]{1,0:T(8,128)(2,1)}, u32[]{:S(2)}, u32[]{:S(2)}) collective-permute-start(bf16[512,2048]{1,0:T(8,128)(2,1)} %add_convert_fusion.3), channel_id=1, source_target_pairs={{0,8},{4,12},{8,0},{12,4},{16,24},{20,28},{24,16},{28,20},{1,9},{5... | collective-permute-start | bytes 6291464 | tf_op jit(solution)/shard_map/ppermute | solution.py:41
  507.5 117.3 %reduce-scatter.9.cloned.1.call-start = ((), (), s32[]{:S(2)}) async-start(), calls=%async_computation.11 | async-start | bytes 2621440 | tf_op jit(solution)/shard_map/reduce_scatter | solution.py:1154
  511.8 44.0 %collective-permute-start.54 = (bf16[256,3072]{1,0:T(8,128)(2,1)}, bf16[256,3072]{1,0:T(8,128)(2,1)}, u32[]{:S(2)}, u32[]{:S(2)}) collective-permute-start(bf16[256,3072]{1,0:T(8,128)(2,1)} %get-tuple-element.608), channel_id=1, source_target_pairs={{0,8},{4,12},{8,0},{12,4},{16,24},{20,28},{24,16},{28,20},{1,9},{5... | collective-permute-start | bytes 4718600 | tf_op jit(solution)/shard_map/ppermute | solution.py:41
  513.4 42.4 %collective-permute-start.53 = (bf16[160,3072]{1,0:T(8,128)(2,1)}, bf16[160,3072]{1,0:T(8,128)(2,1)}, u32[]{:S(2)}, u32[]{:S(2)}) collective-permute-start(bf16[160,3072]{1,0:T(8,128)(2,1)} %slice_bitcast_fusion), channel_id=1, source_target_pairs={{0,16},{4,20},{8,24},{12,28},{16,0},{20,4},{24,8},{28,12},{1,17},{... | collective-permute-start | bytes 2949128 | tf_op jit(solution)/shard_map/ppermute | solution.py:41
  516.0 39.8 %collective-permute-start.52 = (bf16[128,3072]{1,0:T(8,128)(2,1)}, bf16[128,3072]{1,0:T(8,128)(2,1)}, u32[]{:S(2)}, u32[]{:S(2)}) collective-permute-start(bf16[128,3072]{1,0:T(8,128)(2,1)} %slice_bitcast_fusion.1), channel_id=1, source_target_pairs={{0,16},{4,20},{8,24},{12,28},{16,0},{20,4},{24,8},{28,12},{1,17},{... | collective-permute-start | bytes 2359304 | tf_op jit(solution)/shard_map/ppermute | solution.py:41
  517.2 38.7 %collective-permute-start.55 = (bf16[64,3072]{1,0:T(8,128)(2,1)}, bf16[64,3072]{1,0:T(8,128)(2,1)S(1)}, u32[]{:S(2)}, u32[]{:S(2)}) collective-permute-start(bf16[64,3072]{1,0:T(8,128)(2,1)} %slice.478), channel_id=1, source_target_pairs={{0,8},{4,12},{8,0},{12,4},{16,24},{20,28},{24,16},{28,20},{1,9},{5... | collective-permute-start | bytes 1179656 | tf_op jit(solution)/shard_map/ppermute | solution.py:41
  581.6 111.0 %reduce-scatter.11.cloned.1.call-start = ((), (), s32[]{:S(2)}) async-start(), calls=%async_computation.12 | async-start | bytes 589824 | tf_op jit(solution)/shard_map/reduce_scatter | solution.py:1179
  (148 other events, 2139.3 us)
Sparse Core Ops, SparseCore 0:
  38.9 52.6 all-gather.3
  97.2 39.2 all-gather.5
  150.3 52.9 reduce-scatter.4
  455.1 45.5 all-gather.7
  507.6 43.4 reduce-scatter.6
  581.7 42.9 reduce-scatter.8
  660.0 32.6 reduce-scatter.10

commit v5 on v4

--- a/solution.py
+++ b/solution.py
@@ -142,7 +142,8 @@
     BACKS,
     ROWS,
     HALF,
-) = range(56)
+    SMALL,
+) = range(57)
 
 
 class Flow:
@@ -193,14 +194,13 @@
     return parts[0]
 
 
-def scatter_step(at, bit):
-    keys = sorted(key for key in at.having(OUT_GRAD) if key[1] & bit)
+def scatter_step(at, kind, bit):
+    keys = sorted(key for key in at.having(kind) if key[1] & bit)
     v = [at.of.pop(key) for key in keys]
     got = flip(jnp.concatenate(v, axis=0) if len(v) > 1 else v[0], bit)
     rows = v[0].shape[0]
     for i, (_, r) in enumerate(keys):
-        to = OUT_GRAD, r ^ bit
-        at[to] = add(at[to], got[i * rows : (i + 1) * rows])
+        at[kind, r ^ bit] = add(at[kind, r ^ bit], got[i * rows : (i + 1) * rows])
 
 
 def blocks_of(parts, tok):
@@ -229,12 +229,9 @@
         ref[rows, pl.ds(at, wide)] = value[:, c * wide : (c + 1) * wide]
 
 
-def gather_kernel(count, g_count, expert, *refs):
-    parts, refs = refs[:count], refs[count:]
-    g_parts, refs = refs[:g_count], refs[g_count:]
-    pos, named, router, rows_out, gs_out, gate = refs
+def gather_kernel(count, expert, *refs):
+    parts, (pos, named, router, rows_out, gate) = refs[:count], refs[count:]
     tok = pos.shape[1]
-    width = rows_out.shape[1]
     for b, (i, first) in enumerate(blocks_of(parts, tok)):
         at = slice(b * CAP, (b + 1) * CAP)
         part = parts[i][first : first + tok, :]
@@ -248,23 +245,23 @@
         mine = lax.broadcasted_iota(jnp.int32, gates.shape, 0) == expert[0]
         row = jnp.sum(jnp.where(mine, gates, 0.0), axis=0, keepdims=True)
         gate[at, :] = jnp.sum(jnp.where(hot, row, 0.0), axis=1, keepdims=True)
-    for b, (i, first) in enumerate(blocks_of(g_parts, tok)):
-        part = g_parts[i][first : first + tok, :width]
+
+
+def gather_cot_kernel(count, expert, *refs):
+    parts, (pos, rows_out) = refs[:count], refs[count:]
+    tok = pos.shape[1]
+    width = rows_out.shape[1]
+    for b, (i, first) in enumerate(blocks_of(parts, tok)):
+        part = parts[i][first : first + tok, :width]
         found = mm(onehot(pos, b).astype(BF16), part, ((1,), (0,))).astype(BF16)
-        to_distance(gs_out, slice(b * CAP, (b + 1) * CAP), found, expert[1])
-
-
-def gather(parts, g_parts, pos, named, router, expert):
-    slots, width = pos.shape[0] * CAP, parts[0].shape[1]
-    ins = [*parts, *g_parts, pos, named, router]
+        to_distance(rows_out, slice(b * CAP, (b + 1) * CAP), found, expert[1])
+
+
+def pick_rows(kernel, name, parts, others, outs, expert):
+    ins = [*parts, *others]
     whole = lambda x: pl.BlockSpec(x.shape, lambda n, e: (0,) * len(x.shape))
-    outs = [
-        jax.ShapeDtypeStruct((slots, width), BF16),
-        jax.ShapeDtypeStruct((slots, width), BF16),
-        jax.ShapeDtypeStruct((slots, 1), F32),
-    ]
     return pl.pallas_call(
-        functools.partial(gather_kernel, len(parts), len(g_parts)),
+        functools.partial(kernel, len(parts)),
         grid_spec=pltpu.PrefetchScalarGridSpec(
             num_scalar_prefetch=1,
             grid=(1,),
@@ -274,7 +271,7 @@
         out_shape=outs,
         compiler_params=pltpu.CompilerParams(vmem_limit_bytes=VMEM),
         cost_estimate=COST,
-        name="gather",
+        name=name,
     )(expert, *ins)
 
 
@@ -423,40 +420,65 @@
     )(me, gact, pos_t, *pieces)
 
 
-def grads_kernel(count, *refs):
-    out = refs[-1]
-    ff = refs[2].shape[1]
-    gate = up = down = 0.0
-    for c in range(count):
-        rows, gs, dg, du, gact = refs[5 * c : 5 * c + 5]
-        gate = gate + mm(rows[...], dg[...], ((0,), (0,)))
-        up = up + mm(rows[...], du[...], ((0,), (0,)))
-        down = down + mm(gs[...], gact[...], ((0,), (0,)))
-    out[0, :, :ff] = gate.astype(BF16)
-    out[0, :, ff : 2 * ff] = up.astype(BF16)
-    out[0, :, 2 * ff :] = down.astype(BF16)
-
-
-def grads(chunks, first, blocks, rows):
+def grads_kernel(count, rows, cuts, *refs):
+    ins, outs = refs[: 5 * count], list(refs[5 * count :])
+    ff = ins[2].shape[1]
+    for b, cut in enumerate(cuts):
+        at = slice(b * rows, (b + 1) * rows)
+        gate = up = down = 0.0
+        for c in range(count):
+            tall, gs, dg, du, gact = ins[5 * c : 5 * c + 5]
+            gate = gate + mm(tall[:, at], dg[...], ((0,), (0,)))
+            up = up + mm(tall[:, at], du[...], ((0,), (0,)))
+            down = down + mm(gs[:, at], gact[...], ((0,), (0,)))
+        for start, stop in zip(cut[:-1], cut[1:], strict=True):
+            out = outs.pop(0)
+            out[:, :ff] = gate[start:stop].astype(BF16)
+            out[:, ff : 2 * ff] = up[start:stop].astype(BF16)
+            out[:, 2 * ff :] = down[start:stop].astype(BF16)
+
+
+def grads(chunks, first, rows, cuts):
     ff = chunks[0][2].shape[1]
+    blocks = len(cuts)
     specs, ins = [], []
     for chunk in chunks:
         slots = chunk[0].shape[0]
-        tall = pl.BlockSpec((slots, rows), lambda i: (0, first + i))
+        tall = pl.BlockSpec((slots, blocks * rows), lambda i: (0, first // blocks))
         flat = pl.BlockSpec((slots, ff), lambda i: (0, 0))
         specs += [tall, tall, flat, flat, flat]
         ins += list(chunk)
-    slots = sum(chunk[0].shape[0] for chunk in chunks)
+    heights = [b - a for cut in cuts for a, b in zip(cut[:-1], cut[1:], strict=True)]
     return pl.pallas_call(
-        functools.partial(grads_kernel, len(chunks)),
-        grid=(blocks,),
+        functools.partial(grads_kernel, len(chunks), rows, cuts),
+        grid=(1,),
         in_specs=specs,
-        out_specs=pl.BlockSpec((1, rows, 3 * ff), lambda i: (i, 0, 0)),
-        out_shape=jax.ShapeDtypeStruct((blocks, rows, 3 * ff), BF16),
+        out_specs=[pl.BlockSpec((h, 3 * ff), lambda i: (0, 0)) for h in heights],
+        out_shape=[jax.ShapeDtypeStruct((h, 3 * ff), BF16) for h in heights],
         compiler_params=pltpu.CompilerParams(vmem_limit_bytes=VMEM),
         cost_estimate=COST,
         name="grads",
     )(*ins)
+
+
+def add_pieces_kernel(keep, *refs):
+    pieces, out = refs[:-1], refs[-1]
+    for at, p in zip(spans(pieces), pieces, strict=True):
+        out[at, :] = (keep[at, :].astype(F32) + p[...].astype(F32)).astype(BF16)
+
+
+def add_pieces(keep, pieces):
+    whole = lambda x: pl.BlockSpec(x.shape, lambda i: (0, 0))
+    return pl.pallas_call(
+        add_pieces_kernel,
+        grid=(1,),
+        in_specs=[whole(x) for x in (keep, *pieces)],
+        out_specs=whole(keep),
+        out_shape=jax.ShapeDtypeStruct(keep.shape, BF16),
+        compiler_params=pltpu.CompilerParams(vmem_limit_bytes=VMEM),
+        cost_estimate=COST,
+        name="add_pieces",
+    )(keep, *pieces)
 
 
 def attn_grads_kernel(me, a, d, *rest):
@@ -758,7 +780,7 @@
 
 
 def form_kernel(count, own, *refs):
-    ins, (gate_up, down) = refs[:count], refs[count:]
+    ins, (gate_up, down) = refs[:count], refs[-2:]
     wide = gate_up.shape[2]
     for o in range(count):
 
@@ -769,28 +791,35 @@
                 down[:, e, :] = ins[o ^ e][:, wide:].astype(F32)
 
 
-def form(blocks, own):
-    rows, k = blocks[0].shape
+def form(blocks, own, rows, start, stop, before=()):
+    k = blocks[0][0].shape[1]
     count, ff, tile = len(blocks), k // 3, 32
+
+    def spec(at):
+        return pl.BlockSpec((tile, k), lambda i, o: (i + (start - at) // tile, 0))
+
+    shapes = [
+        jax.ShapeDtypeStruct((rows, count, 2 * ff), F32),
+        jax.ShapeDtypeStruct((rows, count, ff), F32),
+    ]
+    outs = [
+        pl.BlockSpec((tile, *s.shape[1:]), lambda i, o: (i + start // tile, 0, 0)) for s in shapes
+    ]
     return pl.pallas_call(
         functools.partial(form_kernel, count),
         grid_spec=pltpu.PrefetchScalarGridSpec(
             num_scalar_prefetch=1,
-            grid=(rows // tile,),
-            in_specs=[pl.BlockSpec((tile, k), lambda i, o: (i, 0))] * count,
-            out_specs=[
-                pl.BlockSpec((tile, count, 2 * ff), lambda i, o: (i, 0, 0)),
-                pl.BlockSpec((tile, count, ff), lambda i, o: (i, 0, 0)),
-            ],
+            grid=((stop - start) // tile,),
+            in_specs=[spec(at) for _, at in blocks]
+            + [pl.BlockSpec(memory_space=pl.ANY)] * len(before),
+            out_specs=outs,
         ),
-        out_shape=[
-            jax.ShapeDtypeStruct((rows, count, 2 * ff), F32),
-            jax.ShapeDtypeStruct((rows, count, ff), F32),
-        ],
+        out_shape=shapes,
+        input_output_aliases={1 + count + n: n for n in range(len(before))},
         compiler_params=pltpu.CompilerParams(vmem_limit_bytes=VMEM),
         cost_estimate=COST,
         name="form",
-    )(own, *blocks)
+    )(own, *[v for v, _ in blocks], *before)
 
 
 def inv_rms(v):
@@ -947,15 +976,13 @@
     if laid_out:
         at[W, 3, 0] = flip(at[W, 1, 2], 2)
         at[W, 5, 0] = flip(at[W, 1, 0], 4)
-        at[WA, 6] = flip(at[W, 2, 0][: 2 * cut], 4)
+        at[WA, 6] = flip(at[W, 2, 0][: 11 * cut // 4], 4)
     first_g = [(G, i) for i in range(mid)]
     last_g = [(G, i) for i in range(mid, zs)]
     at[FAR_GA] = flip(jnp.concatenate([at[key] for key in first_g], axis=0), top)
     weight_keys = at.having(W) + at.having(WA)
     at.fence(ADDED, FAR_GA, (G, zs - 1), *(w for w in weight_keys if laid_out))
-    later = {1: lambda: flip(at[W, 2, 0][2 * cut :], 4)}
-    later[2] = lambda: flip(at[W, 3, 0][: 2 * cut], 4)
-    later[3] = lambda: flip(at[W, 3, 0][2 * cut :], 4)
+    marks = (0, 3 * cut // 4, 9 * cut // 4, e_rows)
     hid = tokens.astype(F32) + at[ADDED].astype(F32)
     r_ffn = inv_rms(hid)
     m = (hid * r_ffn * gains[3]).astype(BF16)
@@ -969,65 +996,81 @@
         on = jnp.sum(masks * mine_e, axis=2)
         pos = jnp.where(on > 0, jnp.cumsum(on, axis=1) - 1.0, -1.0).astype(jnp.int32)
         at[kind, 0], at[kind, 1], at[kind, 2] = pos, pos.T, masks.transpose(0, 2, 1)
+        out = jax.ShapeDtypeStruct((pos.shape[0] * CAP, width), BF16)
+        (at[kind, 3],) = pick_rows(gather_cot_kernel, "gather_cot", parts, [pos], [out], expert_at)
 
     waiting = [(G, key) for key in last_g] + [(M, (M, i)) for i in range(zs)]
+    near_cores = [fan([m], top)[1:]]
     for i in range(1, zs):
         at[M, i] = hop(at[M, i - 1])
         kind, key = waiting.pop(0)
         at[FAR, *key] = flip(at[key], top)
         beside = [(FAR, *key)]
         if laid_out:
-            at[WB, i] = later[i]()
+            at[WB, i] = flip(at[W, 3, 0][marks[i - 1] : marks[i]], 4)
             beside.append((WB, i))
+            if i == 1:
+                at[WA, 7] = flip(at[W, 2, 0][11 * cut // 4 :], 4)
+                beside.append((WA, 7))
+        if i == 1:
+            g_near = [jnp.concatenate([at[key] for key in first_g + last_g], axis=0)]
+            chunk_places(NEAR, [x for xs in fan(g_near, top) for x in xs])
         if i == 2:
-            g_near = [jnp.concatenate([at[key] for key in first_g + last_g], axis=0)]
-            near_parts = [x for xs in fan(g_near, top) for x in xs]
-            chunk_places(NEAR, near_parts)
+            beside += at.having(NEAR)
         if i == zs - 1:
-            beside += at.having(NEAR)
+            g_far = [at[FAR_GA], *[at[FAR, *k] for k in last_g]]
+            chunk_places(DISTANT, [x for xs in fan(g_far, top) for x in xs])
+            beside += at.having(DISTANT)
         at.fence((M, i), *beside)
+        near_cores.append(fan([at[M, i]], top)[1:])
     key = waiting.pop(0)[1]
     at[FAR, *key] = flip(at[key], top)
-    g_far = [at[FAR_GA], *[at[FAR, *k] for k in last_g]]
-    far_parts = [x for xs in fan(g_far, top) for x in xs]
-    chunk_places(DISTANT, far_parts)
-
-    def chunk_gather(kind, blocks, pieces, g_parts):
-        parts = [blocks] + fan(pieces, top)[1:]
-        flat = [x for xs in parts for x in xs]
-        got = gather(flat, g_parts, at[kind, 0], at[kind, 2], router_t, expert_at)
-        return parts, got
-
-    def chunk_expert(kind, parts, got):
-        heights = [x.shape[0] for xs in parts for x in xs]
+
+    def chunk_gather(kind, blocks, cores):
+        flat = [*blocks, *(x[0] for d in range(top - 1) for x in (c[d] for c in cores))]
+        slots = at[kind, 0].shape[0] * CAP
+        outs = [
+            jax.ShapeDtypeStruct((slots, width), BF16),
+            jax.ShapeDtypeStruct((slots, 1), F32),
+        ]
+        others = [at[kind, 0], at[kind, 2], router_t]
+        picked, gate = pick_rows(gather_kernel, "gather", flat, others, outs, expert_at)
+        return picked, at[kind, 3], gate
+
+    def chunk_expert(kind, groups, got):
+        heights = [h for group in groups for h in group]
         backs, outs = run_expert(*got, at[kind, 1], weights, expert_at, heights, ff)
         back = []
-        for xs in parts:
-            back.append(backs[: len(xs)])
-            backs = backs[len(xs) :]
+        for group in groups:
+            back.append(backs[: len(group)])
+            backs = backs[len(group) :]
         return back, (got[0], got[1], *outs)
 
     ms = [at[M, i] for i in range(zs)]
-    near_parts, near_rows = chunk_gather(NEAR, ms, [jnp.concatenate(ms, axis=0)], near_parts)
+    near_rows = chunk_gather(NEAR, ms, near_cores)
     for i, v in enumerate(near_rows):
         at[ROWS, i] = v
-    at.fence(*at.having(ROWS), *at.having(DISTANT), (FAR, *key))
+    at.fence(*at.having(ROWS), (FAR, *key))
     while waiting:
         key = waiting.pop(0)[1]
         at[FAR, *key] = flip(at[key], top)
     if laid_out:
-        keys = [(W, r, 0) for r in range(6)] + [(WA, 6), (WB, 1), (WB, 2), (WB, 3)]
+        keys = [(W, r, 0) for r in range(6)] + [(WA, 6), (WA, 7), (WB, 1), (WB, 2), (WB, 3)]
         weights = [at[key] for key in keys]
     else:
         weights = spread({e: at[W, 0, e] for e in range(local)}, dps)
-    near_back, near_outs = chunk_expert(NEAR, near_parts, [at[ROWS, i] for i in range(3)])
+    own_heights = [rows] * zs
+    near_back, near_outs = chunk_expert(
+        NEAR, [own_heights] + [[zs * rows]] * (top - 1), [at[ROWS, i] for i in range(3)]
+    )
     far_ms = [(FAR, M, i) for i in range(zs)]
     at[NEAR_GACT] = near_outs[4]
     at.fence(NEAR_GACT, *far_ms)
     ms = [at[key] for key in far_ms]
-    pieces = [jnp.concatenate(ms[:mid], axis=0), jnp.concatenate(ms[mid:], axis=0)]
-    far_parts, far_rows = chunk_gather(DISTANT, ms, pieces, far_parts)
-    far_back, far_outs = chunk_expert(DISTANT, far_parts, far_rows)
+    far_rows = chunk_gather(DISTANT, ms, [fan([v], top)[1:] for v in ms])
+    far_back, far_outs = chunk_expert(
+        DISTANT, [own_heights] + [[mid * rows, (zs - mid) * rows]] * (top - 1), far_rows
+    )
     near_outs = (*near_outs[:4], at[NEAR_GACT])
 
     quarter = dps // 4
@@ -1040,26 +1083,32 @@
         at[BACKS, i] = v
     at.fence(*at.having(BACKS), *chunk_keys)
 
-    def chunk_grads(first):
+    halves_cut = [(0, e_rows // 2, e_rows) if laid_out else (0, e_rows)] * quarter
+
+    def chunk_grads(kind, first, cuts):
         c = [at[key] for key in chunk_keys]
-        return grads([c[:5], c[5:]], first, quarter, e_rows)
-
+        made = list(grads([c[:5], c[5:]], first, e_rows, cuts))
+        for row, cut in enumerate(cuts):
+            for start in cut[:-1]:
+                at[kind, row, start] = made.pop(0)
+
+    def send_part(key, row, start):
+        at[PIECE, key, row, start] = flip(at[key, row, start], far_bit)
+
+    def sum_row(keep, key, row):
+        starts = sorted(k[2] for k in at.having(key) if k[1] == row)
+        if not laid_out:
+            send_part(key, row, 0)
+        return add_pieces(at[keep, row, 0], [at[PIECE, key, row, start] for start in starts])
+
+    whole_cut = [(0, e_rows)] * quarter
     last = zs - 1
 
-    unit = e_rows // 16
-
-    def send_part(key, row, start, stop):
-        at[PIECE, key, row, start] = flip(at[key][row][start * unit : stop * unit], far_bit)
-
-    def got_row(key, row):
-        if not laid_out:
-            return flip(at[key][row], far_bit)
-        parts = sorted(k for k in at.having(PIECE) if k[1:3] == (key, row))
-        return jnp.concatenate([at[k] for k in parts], axis=0)
-
     at[THERE] = flip(at[BACKS, last], top)
-    at[SEND_HIGH] = chunk_grads(3 * quarter)
-    at.fence(THERE, SEND_HIGH, *chunk_keys)
+    chunk_grads(SEND_HIGH, 3 * quarter, halves_cut)
+    at.fence(THERE, *at.having(SEND_HIGH), *chunk_keys)
+    half = e_rows // 2
+    early = 3 * e_rows // 8
     for i in reversed(range(zs)):
         here = near_sum[i].astype(F32) + at[THERE].astype(F32)
         if i < last:
@@ -1072,7 +1121,7 @@
         beside = []
         if i == last:
             if laid_out:
-                send_part(SEND_HIGH, 0, 0, 8)
+                send_part(SEND_HIGH, 0, 0)
             for n, y in enumerate(result(at[C, 9], at[DISTANT, 1], weights, top, me_at)):
                 at[Y_PART, n] = y
             beside = [*at.having(Y_PART), *at.having(PIECE)]
@@ -1080,21 +1129,24 @@
             for n, y in enumerate(result(at[C, 4], at[NEAR, 1], weights, top, me_at)):
                 at[NEAR_PART, n] = y
             if laid_out:
-                send_part(SEND_HIGH, 0, 8, 16)
+                send_part(SEND_HIGH, 0, half)
             beside = [*at.having(NEAR_PART), *at.having(PIECE)]
         if i == last - 2:
             if laid_out:
-                send_part(SEND_HIGH, 1, 0, 8)
-            at[SEND_LOW] = chunk_grads(2 * quarter)
+                send_part(SEND_HIGH, 1, 0)
+            low_cut = halves_cut
+            if laid_out:
+                low_cut = [halves_cut[0], (0, e_rows - early, e_rows)]
+            chunk_grads(SEND_LOW, 2 * quarter, low_cut)
             at[Y_FAR] = fold([[at[key]] for key in at.having(Y_PART)])[0]
             at[Y_NEAR] = fold([[at[key]] for key in at.having(NEAR_PART)])[0]
-            beside = [SEND_LOW, Y_FAR, Y_NEAR, *at.having(PIECE)]
+            beside = [Y_FAR, Y_NEAR, *at.having(SEND_LOW), *at.having(PIECE)]
         at.fence(ACC, THERE, *beside, *chunk_keys)
     dm = at[ACC].astype(F32)
     at[Y_FAR] = flip(at[Y_FAR], top)
     if laid_out:
-        send_part(SEND_HIGH, 1, 8, 16)
-        send_part(SEND_LOW, 0, 0, 8)
+        send_part(SEND_HIGH, 1, half)
+        send_part(SEND_LOW, 0, 0)
 
     own_mask = at[MASK].astype(F32)
     own_logits = jnp.where(own_mask > 0, nn(m, router_full), -1e30)
@@ -1112,21 +1164,21 @@
     at[DHB] = lax.all_gather(dh.astype(BF16), "expert", axis=0, tiled=True)
     router_part = tn(m, dz)
     gain_ffn = jnp.sum(dmt * hid * r_ffn, axis=0)
-    at[KEEP_HIGH] = chunk_grads(quarter)
-    at[KEEP_LOW] = chunk_grads(0)
+    chunk_grads(KEEP_HIGH, quarter, whole_cut)
+    if laid_out:
+        at[TAIL, quarter, 0] = sum_row(KEEP_HIGH, SEND_HIGH, 0)
+    chunk_grads(KEEP_LOW, 0, whole_cut)
     at[ROUTER], at[GAIN_FFN] = router_part, gain_ffn
-    at.fence(
-        DHB, Y_FAR, Y_NEAR, KEEP_LOW, KEEP_HIGH, SEND_LOW, ROUTER, GAIN_FFN, *at.having(PIECE)
-    )
+    tails = at.having(TAIL)
+    keeps = at.having(KEEP_LOW) + at.having(KEEP_HIGH) + at.having(SEND_LOW)
+    at.fence(DHB, Y_FAR, Y_NEAR, ROUTER, GAIN_FFN, *keeps, *at.having(PIECE), *tails)
     dhb = at[DHB]
     if laid_out:
-        send_part(SEND_LOW, 0, 8, 16)
-        send_part(SEND_LOW, 1, 0, 10)
-    for i in range(quarter):
-        at[TAIL, quarter + i, 0] = add(at[KEEP_HIGH][i], got_row(SEND_HIGH, i))
-    if laid_out:
         at[TAIL, 0, 2] = flip(at[TAIL, 2, 0], 2)
-        at[HALF, 0] = flip(at[TAIL, 3, 0][: 4 * unit], 2)
+        send_part(SEND_LOW, 0, half)
+        send_part(SEND_LOW, 1, 0)
+    for i in range(1 if laid_out else 0, quarter):
+        at[TAIL, quarter + i, 0] = sum_row(KEEP_HIGH, SEND_HIGH, i)
     y_own = add(at[Y_NEAR], at[Y_FAR])
     at[Y] = lax.psum_scatter(
         by_line([y_own[i * rows : (i + 1) * rows] for i in range(zs)]),
@@ -1137,28 +1189,24 @@
 
     dqn, dkn, dv, sums = attend_back(dhb, out_w, qkv, qr, kr, vb, gain_qk, cos, sin, seg)
     means = lax.psum(sums.reshape(-1, rows), "expert").reshape(zs, 2, rows) / width
+    at[OUT_GRAD] = tn(o, dhb, BF16)
     dqkv, gains_qk = join_back(qkv, dqn, dkn, dv, r_qk, means, gain_qk)
     at[DQKV] = dqkv
-    at.fence(DQKV, DHB, Y, SEND_LOW, *at.having(PIECE), *at.having(TAIL), *at.having(HALF))
+    at.fence(DQKV, OUT_GRAD, Y, *at.having(PIECE), *at.having(TAIL))
+    at[OUT_GRAD] = lax.psum_scatter(at[OUT_GRAD], "dp", scatter_dimension=0, tiled=True)
+
+    at[ODD] = attn_grads(a_all, at[DQKV], [], me_at, 1, 2)
+    at.fence(ODD, DQKV, *at.having(TAIL), *at.having(SEND_LOW))
+    at[ODD] = flip(at[ODD], 1)
     if laid_out:
-        send_part(SEND_LOW, 1, 10, 16)
-        at[HALF, 4] = flip(at[TAIL, 3, 0][4 * unit : 11 * unit], 2)
-
-    at[ODD] = attn_grads(a_all, at[DQKV], [], me_at, 1, 2)
-    at.fence(ODD, DQKV)
-    at[ODD] = flip(at[ODD], 1)
-    at[DA], at[GAIN_ATTN] = first_back(at[DQKV], attn_w, x_all, r_attn, rows)
-    at.fence(ODD, DQKV, DA, GAIN_ATTN, *at.having(HALF), *at.having(PIECE), *at.having(TAIL))
-    if laid_out:
-        at[HALF, 11] = flip(at[TAIL, 3, 0][11 * unit :], 2)
-    at[DA] = lax.psum_scatter(at[DA], "expert", scatter_dimension=0, tiled=True)
-    at[HELD] = add(attn_grads(a_all, at[DQKV], [], me_at, 0, 2), at[ODD])
-    at.fence(HELD, DHB, GAIN_ATTN, *at.having(HALF))
+        at[HALF, 0] = flip(at[TAIL, 3, 0][:early], 2)
+        send_part(SEND_LOW, 1, e_rows - early)
+    even = attn_grads(a_all, at[DQKV], [], me_at, 0, 2)
+    at[HELD] = add(even, at[ODD])
+    at.fence(HELD, DQKV, *at.having(HALF), *at.having(PIECE))
     sides = halves(at[HELD], zs * own_rows)
     stage(at, sides, 0)
-    out_blocks = tn(o, at[DHB], BF16).reshape(dps, own_rows, width)
-    for r in range(dps):
-        at[OUT_GRAD, r] = pick(out_blocks, dp ^ r, 0)
+    at[DA], at[GAIN_ATTN] = first_back(at[DQKV], attn_w, x_all, r_attn, rows)
     zero = jnp.zeros((2, width), F32)
     gain_rows = jnp.concatenate(
         [
@@ -1171,22 +1219,21 @@
     )
     at[BESIDE] = jnp.concatenate([at[ROUTER], gain_rows.T], axis=1).astype(BF16)
     for turn_ in range(1, len(bits_of(2, dps))):
-        at.fence(*at.having(SIDE), BESIDE, DA, *at.having(OUT_GRAD))
+        at.fence(*at.having(SIDE), BESIDE, DA, OUT_GRAD, *at.having(KEEP_LOW), *at.having(PIECE))
+        if turn_ == 1:
+            at[DA] = lax.psum_scatter(at[DA], "expert", scatter_dimension=0, tiled=True)
+            stacked = at[BESIDE].reshape(dps, e_rows, EXTRA)
+            for r in range(dps):
+                at[SMALL, r] = pick(stacked, dp ^ r, 0)
+            scatter_step(at, SMALL, 1)
+            for i in range(quarter):
+                at[TAIL, i, 0] = sum_row(KEEP_LOW, SEND_LOW, i)
         sides = unstage(at, sides, turn_ - 1)
         stage(at, sides, turn_)
-        if turn_ == 1 and laid_out:
-            scatter_step(at, 1)
-    at[BESIDE] = lax.psum_scatter(at[BESIDE], "dp", scatter_dimension=0, tiled=True)
-    at.fence(*at.having(SIDE), *at.having(OUT_GRAD))
+    at.fence(*at.having(SIDE), *at.having(SMALL), *at.having(TAIL))
     sides = unstage(at, sides, len(bits_of(2, dps)) - 1)
     at[BACK] = jnp.concatenate([sides[0][0][0], sides[1][0][0]], axis=1)
-    at.fence(BACK, KEEP_LOW, *at.having(OUT_GRAD), *at.having(TAIL), *at.having(HALF))
-    for i in range(quarter):
-        at[TAIL, i, 0] = add(at[KEEP_LOW][i], got_row(SEND_LOW, i))
-    if laid_out:
-        at[TAIL, 1, 2] = jnp.concatenate([at[HALF, 0], at[HALF, 4], at[HALF, 11]], axis=0)
-        for e in (0, 2):
-            at[TAIL, 0, e ^ 1] = flip(at[TAIL, 1, e], 1)
+    at.fence(BACK, OUT_GRAD, *at.having(SMALL), *at.having(HALF), *at.having(TAIL))
     at[BACK] = lax.all_to_all(
         at[BACK].reshape(zs, own_rows, 3 * cols),
         "expert",
@@ -1194,24 +1241,32 @@
         concat_axis=0,
         tiled=True,
     )
+    at[OUT_GRAD] = lax.ppermute(
+        at[OUT_GRAD], ("dp", "expert"), [(b, a) for a, b in moved]
+    )
+    for bit in bits_of(2, dps):
+        scatter_step(at, SMALL, bit)
+    own_at = jnp.reshape(own, (1,))
     if laid_out:
-        blocks = {e: at[TAIL, 0, e] for e in range(local)}
+        at[HALF, early] = flip(at[TAIL, 3, 0][early:], 2)
+        at[TAIL, 0, 1] = flip(at[TAIL, 1, 0], 1)
+        blocks = [(at[TAIL, 0, e], 0) for e in range(local - 1)]
+        at[HALF, 0], at[HALF, early] = flip(at[HALF, 0], 1), flip(at[HALF, early], 1)
+        first = form([*blocks, (at[HALF, 0], 0)], own_at, e_rows, 0, early)
+        blocks += [(at[HALF, early], early)]
+        at[GU], at[DN] = form(blocks, own_at, e_rows, early, e_rows, first)
     else:
-        blocks = gather_back({k[1]: at[k] for k in at.having(TAIL)}, local, dps)
-    at[GU], at[DN] = form([blocks[e] for e in range(local)], jnp.reshape(own, (1,)))
-    for bit in bits_of(2 if laid_out else 1, dps):
-        scatter_step(at, bit)
-    at.fence(BACK, GU, DN, BESIDE, *at.having(OUT_GRAD))
-    grad_w_out = lax.ppermute(
-        at[OUT_GRAD, 0], ("dp", "expert"), [(b, a) for a, b in moved]
-    ).astype(F32)
+        rest = gather_back({k[1]: at[k] for k in at.having(TAIL)}, local, dps)
+        at[GU], at[DN] = form([(rest[e], 0) for e in range(local)], own_at, e_rows, 0, e_rows)
+    at.fence(BACK, OUT_GRAD, DA, GU, DN, *at.having(SMALL))
+    grad_w_out = at[OUT_GRAD].astype(F32)
     back = at[BACK].astype(F32)
     grad_w_qkv = jnp.concatenate(
         [back[e, :, i * cols : (i + 1) * cols] for i in range(3) for e in range(zs)], axis=1
     )
     line = ring(zs)
     place = jnp.asarray([line.index(i) for i in range(zs)], jnp.int32)[z]
-    blocks = at[BESIDE].reshape(zs, own_rows, EXTRA)
+    blocks = at[SMALL, 0].reshape(zs, own_rows, EXTRA)
     extra_sum = pick(blocks, z, 0).astype(F32)
     for i in range(1, zs):
         to = jnp.asarray(line, jnp.int32)[lax.rem(place + i, zs)]

time: 735 us -> 703 us (0.956)
  waiting for transfers between devices: 217 us -> 180 us
  Pallas kernels: 190 us -> 211 us
  other arithmetic: 89.6 us -> 73.1 us
    pallas_call x6 -> x12, Pallas kernels: 58.5 us -> 78 us  [the longest x4 41.3 us: grads(): pl.pallas_call(functools.partial(grads_kernel, len(chunks), rows, cuts),...]
    ppermute x56 -> x62, waiting for transfers between devices: 160 us -> 145 us  [flip(): lax.ppermute(v, 'dp', [(i, i ^ bit) for i in range(lax.axis_size('dp'))])]
    ppermute x1, waiting for transfers between devices: 12.8 us -> 0.01 us  [on_device(): lax.ppermute(at[OUT_GRAD], ('dp', 'expert'), [(b, a) for a, b in moved])]
    ppermute x15, waiting for transfers between devices: 29.8 us -> 20.3 us  [hop(): return lax.ppermute(v, 'expert', pairs)]
    slice x11 -> x7, local copies, waits for them, and re-layouts: 12.4 us -> 4.52 us  [the longest x3 2.47 us: on_device(): at[WB, i] = flip(at[W, 3, 0][marks[i - 1]:marks[i]], 4)]
    convert_element_type x13 -> x11, other arithmetic: 29.5 us -> 22.4 us  [add(): return (a.astype(F32) + b.astype(F32)).astype(BF16)]
    unnamed x204 -> x200, local copies, waits for them, and re-layouts: 15.5 us -> 19.5 us
    ppermute x56 -> x62, starting transfers between devices: 41.9 us -> 42.8 us  [flip(): lax.ppermute(v, 'dp', [(i, i ^ bit) for i in range(lax.axis_size('dp'))])]
  transfers between devices with their start and end apart: 82 -> 88, of which waited for: 39 -> 36; matrix products, arithmetic and copies ran while one was open for 20% -> 18% of each run, Pallas kernels for 21% -> 25%
where the time goes in v5:
time: 703 us; the launch traced here: 691 us
  Pallas kernels  211 us (30%)
  waiting for transfers between devices  180 us (26%)
  starting transfers between devices  85.4 us (12%)
  local copies, waits for them, and re-layouts  74.1 us (11%)
  other arithmetic  73.1 us (10%)
  between operations  31.4 us (4%)
  blocking collectives  20.8 us (3%)
  matrix products  15.6 us (2%)
    ppermute x62, waiting for transfers between devices, flip(): lax.ppermute(v, 'dp', [(i, i ^ bit) for i in range(lax.axis_size('dp'))])  145 us
    pallas_call x2, Pallas kernels, run_expert(): pl.pallas_call(functools.partial(expert_kernel, len(heights), len(pieces)...  50.4 us
    ppermute x62, starting transfers between devices, flip(): lax.ppermute(v, 'dp', [(i, i ^ bit) for i in range(lax.axis_size('dp'))])  42.8 us
    pallas_call x4, Pallas kernels, grads(): pl.pallas_call(functools.partial(grads_kernel, len(chunks), rows, cuts),...  41.3 us
    ppermute x15, starting transfers between devices, hop(): return lax.ppermute(v, 'expert', pairs)  28.1 us
    pallas_call x4, Pallas kernels, pick_rows(): pl.pallas_call(functools.partial(kernel, len(parts)), grid_spec=pltpu.Pre...  23.1 us
    convert_element_type x11, other arithmetic, add(): return (a.astype(F32) + b.astype(F32)).astype(BF16)  22.4 us
    ppermute x15, waiting for transfers between devices, hop(): return lax.ppermute(v, 'expert', pairs)  20.3 us
  transfers between devices with their start and end apart: 88, of which 36 were waited for; matrix products, arithmetic and copies ran while one was open for 18% of the time, Pallas kernels for 25%

profile of v5, /device:TPU:4, one launch (start us, length us, event | category | flops | bytes accessed | tf_op | source)
XLA Modules:
  0.0 691.3 jit_solution(14789759269535641394)
XLA Ops:
  20.7 8.7 %constant_dynamic-slice_fusion.2 = (bf16[256,1,2048]{2,1,0:T(2,128)(2,1)S(1)}, bf16[256,1,2048]{2,1,0:T(2,128)(2,1)S(1)}, bf16[256,1,2048]{2,1,0:T(2,128)(2,1)S(1)}, bf16[256,1,2048]{2,1,0:T(2,128)(2,1)S(1)}) fusion(bf16[256,4,2048]{2,1,0:T(4,128)(2,1)S(1)} %copy-done.14, s32[]{:T(128)S(6)} %select_n.142, s32[]{:T(128)S(6)} %select_n.141, ...), kind=kLoop, calls=%fused_computation.179 | loop fusion | bytes 8388624 | tf_op jit(solution)/shard_map/jit(dynamic_index_in_dim)/dynamic_slice | solution.py:81
  41.4 10.7 %collective-permute-done = bf16[128,2048]{1,0:T(8,128)(2,1)} collective-permute-done((bf16[128,2048]{1,0:T(8,128)(2,1)}, bf16[128,2048]{1,0:T(8,128)(2,1)}, u32[]{:S(2)}, u32[]{:S(2)}) %collective-permute-start) | collective-permute-done | bytes 524320 | tf_op jit(solution)/shard_map/ppermute | solution.py:52
  60.5 6.4 collective-permute-done.2
  118.0 9.8 %psum.14 = f32[2,512]{1,0:T(2,128)S(1)} all-reduce(f32[2,512]{1,0:T(2,128)S(1)} %pad_maximum_fusion.17), channel_id=1, replica_groups=mesh['dp'=8,'expert'=4] {'expert'}, use_global_device_ids=true, to_apply=%region_7.8 | all-reduce | flops 1024 | bytes 8192 | tf_op jit(solution)/shard_map/psum | solution.py:961
  128.4 8.7 %attend.1 = (bf16[512,512]{1,0:T(8,128)(2,1)}, bf16[512,512]{1,0:T(8,128)(2,1)}, bf16[512,512]{1,0:T(8,128)(2,1)}, bf16[512,512]{1,0:T(8,128)(2,1)}) custom-call(f32[512,1536]{1,0:T(8,128)} %copy-done.5, f32[4,2,128]{2,1,0:T(2,128)} %rsqrt_bitcast_fusion.r, f32[2,512]{1,0:T(2,128)} %copy.217.gains, f32[512,128]{1,0:T(8,128)} %copy.218.cos, ...), custom_call_target="tpu_custom_call" | custom-call | flops 1000000 | bytes 100000 | tf_op jit(solution)/shard_map/attend/pallas_call | solution.py:615
  141.5 6.1 collective-permute-done.8.refs_6_.refs_17_.refs_28_.refs_2_
  158.4 50.0 %collective-permute-done.10.refs_0_ = bf16[256,2176]{1,0:T(8,128)(2,1)S(1)} collective-permute-done((bf16[256,2176]{1,0:T(8,128)(2,1)S(1)}, bf16[256,2176]{1,0:T(8,128)(2,1)S(1)}, u32[]{:S(2)}, u32[]{:S(2)}) %collective-permute-start.10) | collective-permute-done | bytes 1114144 | tf_op jit(solution)/shard_map/ppermute | solution.py:41
  279.9 6.2 gather.9
  289.0 25.0 %expert.2 = (bf16[128,2176]{1,0:T(8,128)(2,1)}, bf16[128,2176]{1,0:T(8,128)(2,1)}, bf16[128,2176]{1,0:T(8,128)(2,1)}, bf16[128,2176]{1,0:T(8,128)(2,1)}, bf16[51...) custom-call(s32[3]{0:T(128)} %pad_add_fusion.expert, ...), custom_call_target="tpu_custom_call" | custom-call | flops 1000000 | bytes 100000 | tf_op jit(solution)/shard_map/expert/pallas_call | solution.py:353
  318.4 6.3 gather.10
  324.7 25.4 %expert.3 = (bf16[128,2176]{1,0:T(8,128)(2,1)}, bf16[128,2176]{1,0:T(8,128)(2,1)}, bf16[128,2176]{1,0:T(8,128)(2,1)}, bf16[128,2176]{1,0:T(8,128)(2,1)}, bf16[25...) custom-call(s32[3]{0:T(128)} %pad_add_fusion.expert, ...), custom_call_target="tpu_custom_call" | custom-call | flops 1000000 | bytes 100000 | tf_op jit(solution)/shard_map/expert/pallas_call | solution.py:353
  357.9 10.3 %grads.4 = (bf16[128,3072]{1,0:T(8,128)(2,1)}, bf16[128,3072]{1,0:T(8,128)(2,1)}, bf16[128,3072]{1,0:T(8,128)(2,1)}, bf16[128,3072]{1,0:T(8,128)(2,1)}) custom-call(bf16[640,2048]{1,0:T(8,128)(2,1)} %get-tuple-element.470.refs_0_, bf16[640,2048]{1,0:T(8,128)(2,1)} %gather_cot.2.refs_1_, bf16[640,1024]{1,0:T(8,128)(2,1)} %get-tuple-element.472.refs_2_, ...), custom_call_target="tpu_custom_call" | custom-call | flops 1000000 | bytes 100000 | tf_op jit(solution)/shard_map/grads/pallas_call | solution.py:452
  375.3 9.6 %result.2 = (bf16[512,2048]{1,0:T(8,128)(2,1)}, bf16[512,2048]{1,0:T(8,128)(2,1)}) custom-call(s32[1]{0:T(128)} %bitcast.34.me, bf16[640,1024]{1,0:T(8,128)(2,1)} %get-tuple-element.479.refs_9_.gact, s32[128,8]{1,0:T(8,128)} %bitcast.204, bf16[256,3072]{1,0:T(8,128)(2,1)} %copy-done.2, bf16[256,3072]{1,0:T(8,128)(2,1)} %copy-done.6, ...), custom_call_target="tpu_custom_call" | custom-call | flops 1000000 | bytes 100000 | tf_op jit(solution)/shard_map/result/pallas_call | solution.py:403
  393.2 9.5 %result.3 = (bf16[512,2048]{1,0:T(8,128)(2,1)}, bf16[512,2048]{1,0:T(8,128)(2,1)}) custom-call(s32[1]{0:T(128)} %bitcast.34.me, bf16[640,1024]{1,0:T(8,128)(2,1)} %get-tuple-element.474.refs_4_.gact, s32[128,8]{1,0:T(8,128)} %bitcast.202, bf16[256,3072]{1,0:T(8,128)(2,1)} %copy-done.2, bf16[256,3072]{1,0:T(8,128)(2,1)} %copy-done.6, ...), custom_call_target="tpu_custom_call" | custom-call | flops 1000000 | bytes 100000 | tf_op jit(solution)/shard_map/result/pallas_call | solution.py:403
  415.8 10.3 %grads.5 = (bf16[128,3072]{1,0:T(8,128)(2,1)}, bf16[128,3072]{1,0:T(8,128)(2,1)}, bf16[160,3072]{1,0:T(8,128)(2,1)}, bf16[96,3072]{1,0:T(8,128)(2,1)}) custom-call(bf16[640,2048]{1,0:T(8,128)(2,1)} %get-tuple-element.470.refs_0_, bf16[640,2048]{1,0:T(8,128)(2,1)} %gather_cot.2.refs_1_, bf16[640,1024]{1,0:T(8,128)(2,1)} %get-tuple-element.472.refs_2_, ...), custom_call_target="tpu_custom_call" | custom-call | flops 1000000 | bytes 100000 | tf_op jit(solution)/shard_map/grads/pallas_call | solution.py:452
  444.4 10.4 %grads.6 = (bf16[256,3072]{1,0:T(8,128)(2,1)}, bf16[256,3072]{1,0:T(8,128)(2,1)}) custom-call(bf16[640,2048]{1,0:T(8,128)(2,1)} %get-tuple-element.470.refs_0_, bf16[640,2048]{1,0:T(8,128)(2,1)} %gather_cot.2.refs_1_, bf16[640,1024]{1,0:T(8,128)(2,1)} %get-tuple-element.472.refs_2_, bf16[640,1024]{1,0:T(8,128)(2,1)} %get-tuple-element.473.refs_3_, ...), custom_call_target="tpu_custom_call" | custom-call | flops 1000000 | bytes 100000 | tf_op jit(solution)/shard_map/grads/pallas_call | solution.py:452
  454.9 10.3 %grads.7 = (bf16[256,3072]{1,0:T(8,128)(2,1)}, bf16[256,3072]{1,0:T(8,128)(2,1)}) custom-call(bf16[640,2048]{1,0:T(8,128)(2,1)} %get-tuple-element.470.refs_0_, bf16[640,2048]{1,0:T(8,128)(2,1)} %gather_cot.2.refs_1_, bf16[640,1024]{1,0:T(8,128)(2,1)} %get-tuple-element.472.refs_2_, bf16[640,1024]{1,0:T(8,128)(2,1)} %get-tuple-element.473.refs_3_, ...), custom_call_target="tpu_custom_call" | custom-call | flops 1000000 | bytes 100000 | tf_op jit(solution)/shard_map/grads/pallas_call | solution.py:452
  469.8 8.3 %collective-permute-done.57.refs_0_ = bf16[128,3072]{1,0:T(8,128)(2,1)} collective-permute-done((bf16[128,3072]{1,0:T(8,128)(2,1)}, bf16[128,3072]{1,0:T(8,128)(2,1)}, u32[]{:S(2)}, u32[]{:S(2)}) %collective-permute-start.57) | collective-permute-done | bytes 786464 | tf_op jit(solution)/shard_map/ppermute | solution.py:41
  478.2 10.9 %collective-permute-done.55 = bf16[512,2048]{1,0:T(8,128)(2,1)} collective-permute-done((bf16[512,2048]{1,0:T(8,128)(2,1)}, bf16[512,2048]{1,0:T(8,128)(2,1)}, u32[]{:S(2)}, u32[]{:S(2)}) %collective-permute-start.55) | collective-permute-done | bytes 2097184 | tf_op jit(solution)/shard_map/ppermute | solution.py:41
  501.4 13.9 %attend_back.1 = (f32[512,512]{1,0:T(8,128)}, f32[512,512]{1,0:T(8,128)}, bf16[512,512]{1,0:T(8,128)(2,1)}, f32[4,2,128]{2,1,0:T(2,128)}) custom-call(bf16[512,2048]{1,0:T(8,128)(2,1)} %all-gather.8.cloned.1.call-done.dhb, bf16[512,2048]{1,0:T(8,128)(2,1)} %all-gather.6.cloned.1.call-done.wo, f32[512,1536]{1,0:T(8,128)} %copy-done.5, f32[512,1536]{1,0:T(8,128)} %copy-done.5, ...), custom_call_target="tpu_custom_call" | custom-call | flops 1000000 | bytes 100000 | tf_op jit(solution)/shard_map/attend_back/pallas_call | solution.py:666
  515.3 11.0 %psum.15 = f32[8,128]{1,0:T(8,128)S(1)} all-reduce(f32[8,128]{1,0:T(8,128)} %bitcast.224), channel_id=1, replica_groups=mesh['dp'=8,'expert'=4] {'expert'}, use_global_device_ids=true, to_apply=%region_19.20 | all-reduce | flops 1024 | bytes 8192 | tf_op jit(solution)/shard_map/psum | solution.py:1191
  569.0 12.8 %first_back.1 = (bf16[512,2048]{1,0:T(8,128)(2,1)}, f32[1,2048]{1,0:T(1,128)}) custom-call(bf16[512,1536]{1,0:T(8,128)(2,1)} %get-tuple-element.524.d, bf16[2048,1664]{1,0:T(8,128)(2,1)} %all-gather.4.cloned.1.call-done.w, bf16[512,2048]{1,0:T(8,128)(2,1)} %copy-done.12, f32[512,1]{1,0:T(8,128)} %copy.246.r), custom_call_target="tpu_custom_call" | custom-call | flops 1000000 | bytes 100000 | tf_op jit(solution)/shard_map/first_back/pallas_call | solution.py:759
  615.9 17.1 %collective-permute-done.71 = bf16[160,3072]{1,0:T(8,128)(2,1)} collective-permute-done((bf16[160,3072]{1,0:T(8,128)(2,1)S(1)}, bf16[160,3072]{1,0:T(8,128)(2,1)}, u32[]{:S(2)}, u32[]{:S(2)}) %collective-permute-start.71) | collective-permute-done | bytes 983072 | tf_op jit(solution)/shard_map/ppermute | solution.py:41
  661.6 7.2 %form.3 = (f32[256,4,2048]{2,1,0:T(4,128)}, f32[256,4,1024]{2,1,0:T(4,128)}) custom-call(s32[1]{0:T(128)} %bitcast.65.own, bf16[256,3072]{1,0:T(8,128)(2,1)} %add_pieces.6.refs_0_, bf16[256,3072]{1,0:T(8,128)(2,1)} %copy-done.22, bf16[256,3072]{1,0:T(8,128)(2,1)} %copy-done.21, ...), custom_call_target="tpu_custom_call", output_to_operand_aliasing={{0}: (5, {}), {1}: (6, {})} | custom-call | flops 1000000 | bytes 100000 | tf_op jit(solution)/shard_map/form/pallas_call | solution.py:808
  (555 shorter events, 354.9 us)
Async XLA Ops:
  16.3 75.2 %all-gather.4.cloned.1.call-start = ((), (), s32[]{:S(2)}) async-start(), calls=%async_computation.6 | async-start | bytes 7667712 | tf_op jit(solution)/shard_map/all_gather | solution.py:914
  38.8 98.4 %all-gather.6.cloned.1.call-start = ((), (), s32[]{:S(2)}) async-start(), calls=%async_computation.7 | async-start | bytes 2359296 | tf_op jit(solution)/shard_map/all_gather | solution.py:947
  40.9 46.2 %collective-permute-start.4 = (bf16[256,3072]{1,0:T(8,128)(2,1)}, bf16[256,3072]{1,0:T(8,128)(2,1)S(1)}, u32[]{:S(2)}, u32[]{:S(2)}) collective-permute-start(bf16[256,3072]{1,0:T(8,128)(2,1)} %pad_maximum_fusion.5), channel_id=1, source_target_pairs={{0,4},{4,0},{8,12},{12,8},{16,20},{20,16},{24,28},{28,24},{1,5},{5... | collective-permute-start | bytes 4718600 | tf_op jit(solution)/shard_map/ppermute | solution.py:41
  40.9 46.2 %collective-permute-start.5 = (bf16[256,3072]{1,0:T(8,128)(2,1)}, bf16[256,3072]{1,0:T(8,128)(2,1)}, u32[]{:S(2)}, u32[]{:S(2)}) collective-permute-start(bf16[256,3072]{1,0:T(8,128)(2,1)} %pad_maximum_fusion.7), channel_id=1, source_target_pairs={{0,4},{4,0},{8,12},{12,8},{16,20},{20,16},{24,28},{28,24},{1,5},{5... | collective-permute-start | bytes 4718600 | tf_op jit(solution)/shard_map/ppermute | solution.py:41
  97.1 112.7 %reduce-scatter.5.cloned.1.call-start = ((), (), s32[]{:S(2)}) async-start(), calls=%async_computation.8 | async-start | bytes 2621440 | tf_op jit(solution)/shard_map/reduce_scatter | solution.py:973
  100.5 47.1 %collective-permute-start.8 = (bf16[256,3072]{1,0:T(8,128)(2,1)}, bf16[256,3072]{1,0:T(8,128)(2,1)S(1)}, u32[]{:S(2)}, u32[]{:S(2)}) collective-permute-start(bf16[256,3072]{1,0:T(8,128)(2,1)} %pad_maximum_fusion.6), channel_id=1, source_target_pairs={{0,8},{4,12},{8,0},{12,4},{16,24},{20,28},{24,16},{28,20},{1,9},{5... | collective-permute-start | bytes 4718600 | tf_op jit(solution)/shard_map/ppermute | solution.py:41
  104.5 44.5 %collective-permute-start.9 = (bf16[256,3072]{1,0:T(8,128)(2,1)S(1)}, bf16[256,3072]{1,0:T(8,128)(2,1)}, u32[]{:S(2)}, u32[]{:S(2)}) collective-permute-start(bf16[256,3072]{1,0:T(8,128)(2,1)S(1)} %pad_maximum_fusion.4.refs_4_.refs_15_.refs_26_.refs_0_), channel_id=1, source_target_pairs={{0,16},{4,20},{8,24},{12,28},{16,0},{20,4},{24,8},{28,12},{1,17},{... | collective-permute-start | bytes 4718600 | tf_op jit(solution)/shard_map/ppermute | solution.py:41
  149.0 340.0 %all-gather.8.cloned.1.call-start = ((), (), s32[]{:S(2)}) async-start(), calls=%async_computation.9 | async-start | bytes 2621440 | tf_op jit(solution)/shard_map/all_gather | solution.py:1164
  149.1 59.3 %collective-permute-start.12 = (bf16[256,3072]{1,0:T(8,128)(2,1)}, bf16[256,3072]{1,0:T(8,128)(2,1)S(1)}, u32[]{:S(2)}, u32[]{:S(2)}) collective-permute-start(bf16[256,3072]{1,0:T(8,128)(2,1)} %collective-permute-done.5), channel_id=1, source_target_pairs={{0,8},{4,12},{8,0},{12,4},{16,24},{20,28},{24,16},{28,20},{1,9},{5... | collective-permute-start | bytes 4718600 | tf_op jit(solution)/shard_map/ppermute | solution.py:41
  149.5 60.3 %collective-permute-start.13 = (bf16[256,3072]{1,0:T(8,128)(2,1)}, bf16[256,3072]{1,0:T(8,128)(2,1)}, u32[]{:S(2)}, u32[]{:S(2)}) collective-permute-start(bf16[256,3072]{1,0:T(8,128)(2,1)} %copy-done.6), channel_id=1, source_target_pairs={{0,16},{4,20},{8,24},{12,28},{16,0},{20,4},{24,8},{28,12},{1,17},{... | collective-permute-start | bytes 4718600 | tf_op jit(solution)/shard_map/ppermute | solution.py:41
  151.0 57.3 %collective-permute-start.10 = (bf16[256,2176]{1,0:T(8,128)(2,1)S(1)}, bf16[256,2176]{1,0:T(8,128)(2,1)S(1)}, u32[]{:S(2)}, u32[]{:S(2)}) collective-permute-start(bf16[256,2176]{1,0:T(8,128)(2,1)S(1)} %pad_maximum_fusion.8), channel_id=1, source_target_pairs={{0,8},{4,12},{8,0},{12,4},{16,24},{20,28},{24,16},{28,20},{1,9},{5... | collective-permute-start | bytes 3342344 | tf_op jit(solution)/shard_map/ppermute | solution.py:41
  152.9 55.4 %collective-permute-start.14 = (bf16[176,3072]{1,0:T(8,128)(2,1)S(1)}, bf16[176,3072]{1,0:T(8,128)(2,1)S(1)}, u32[]{:S(2)}, u32[]{:S(2)}) collective-permute-start(bf16[176,3072]{1,0:T(8,128)(2,1)S(1)} %slice.291), channel_id=1, source_target_pairs={{0,16},{4,20},{8,24},{12,28},{16,0},{20,4},{24,8},{28,12},{1,17},{... | collective-permute-start | bytes 3244040 | tf_op jit(solution)/shard_map/ppermute | solution.py:41
  154.8 53.6 %collective-permute-start.11 = (bf16[128,2176]{1,0:T(8,128)(2,1)}, bf16[128,2176]{1,0:T(8,128)(2,1)S(1)}, u32[]{:S(2)}, u32[]{:S(2)}) collective-permute-start(bf16[128,2176]{1,0:T(8,128)(2,1)} %collective-permute-done.7), channel_id=1, source_target_pairs={{0,2},{2,3},{3,1},{1,0},{4,6},{6,7},{7,5},{5,4},{8,10},{10,11},{11... | collective-permute-start | bytes 1671176 | tf_op jit(solution)/shard_map/ppermute | solution.py:52
  275.3 38.7 %collective-permute-start.35 = (bf16[128,2048]{1,0:T(8,128)(2,1)}, bf16[128,2048]{1,0:T(8,128)(2,1)S(1)}, u32[]{:S(2)}, u32[]{:S(2)}) collective-permute-start(bf16[128,2048]{1,0:T(8,128)(2,1)} %collective-permute-done.19.refs_2_), channel_id=1, source_target_pairs={{0,8},{4,12},{8,0},{12,4},{16,24},{20,28},{24,16},{28,20},{1,9},{5... | collective-permute-start | bytes 1572872 | tf_op jit(solution)/shard_map/ppermute | solution.py:41
  276.1 37.9 %collective-permute-start.36 = (bf16[128,2048]{1,0:T(8,128)(2,1)}, bf16[128,2048]{1,0:T(8,128)(2,1)S(1)}, u32[]{:S(2)}, u32[]{:S(2)}) collective-permute-start(bf16[128,2048]{1,0:T(8,128)(2,1)} %collective-permute-done.23.refs_3_), channel_id=1, source_target_pairs={{0,8},{4,12},{8,0},{12,4},{16,24},{20,28},{24,16},{28,20},{1,9},{5... | collective-permute-start | bytes 1572872 | tf_op jit(solution)/shard_map/ppermute | solution.py:41
  440.9 96.4 %reduce-scatter.7.cloned.1.call-start = ((), (), s32[]{:S(2)}) async-start(), calls=%async_computation.10 | async-start | bytes 2621440 | tf_op jit(solution)/shard_map/reduce_scatter | solution.py:1183
  441.2 47.9 %collective-permute-start.55 = (bf16[512,2048]{1,0:T(8,128)(2,1)}, bf16[512,2048]{1,0:T(8,128)(2,1)}, u32[]{:S(2)}, u32[]{:S(2)}) collective-permute-start(bf16[512,2048]{1,0:T(8,128)(2,1)} %add_convert_fusion.3), channel_id=1, source_target_pairs={{0,8},{4,12},{8,0},{12,4},{16,24},{20,28},{24,16},{28,20},{1,9},{5... | collective-permute-start | bytes 6291464 | tf_op jit(solution)/shard_map/ppermute | solution.py:41
  493.6 97.0 %reduce-scatter.9.cloned.1.call-start = ((), (), s32[]{:S(2)}) async-start(), calls=%async_computation.11 | async-start | bytes 2359296 | tf_op jit(solution)/shard_map/reduce_scatter | solution.py:1196
  495.0 40.1 %collective-permute-start.60 = (bf16[256,3072]{1,0:T(8,128)(2,1)S(1)}, bf16[256,3072]{1,0:T(8,128)(2,1)S(1)}, u32[]{:S(2)}, u32[]{:S(2)}) collective-permute-start(bf16[256,3072]{1,0:T(8,128)(2,1)S(1)} %copy-done.39), channel_id=1, source_target_pairs={{0,8},{4,12},{8,0},{12,4},{16,24},{20,28},{24,16},{28,20},{1,9},{5... | collective-permute-start | bytes 4718600 | tf_op jit(solution)/shard_map/ppermute | solution.py:41
  495.8 39.3 %collective-permute-start.59 = (bf16[160,3072]{1,0:T(8,128)(2,1)}, bf16[160,3072]{1,0:T(8,128)(2,1)}, u32[]{:S(2)}, u32[]{:S(2)}) collective-permute-start(bf16[160,3072]{1,0:T(8,128)(2,1)} %get-tuple-element.507), channel_id=1, source_target_pairs={{0,16},{4,20},{8,24},{12,28},{16,0},{20,4},{24,8},{28,12},{1,17},{... | collective-permute-start | bytes 2949128 | tf_op jit(solution)/shard_map/ppermute | solution.py:41
  496.9 38.1 %collective-permute-start.58 = (bf16[128,3072]{1,0:T(8,128)(2,1)}, bf16[128,3072]{1,0:T(8,128)(2,1)}, u32[]{:S(2)}, u32[]{:S(2)}) collective-permute-start(bf16[128,3072]{1,0:T(8,128)(2,1)} %get-tuple-element.506), channel_id=1, source_target_pairs={{0,16},{4,20},{8,24},{12,28},{16,0},{20,4},{24,8},{28,12},{1,17},{... | collective-permute-start | bytes 2359304 | tf_op jit(solution)/shard_map/ppermute | solution.py:41
  542.9 126.0 %reduce-scatter.11.cloned.1.call-start = ((), (), s32[]{:S(2)}) async-start(), calls=%async_computation.12 | async-start | bytes 2621440 | tf_op jit(solution)/shard_map/reduce_scatter | solution.py:1224
  611.3 42.9 %collective-permute-start.70 = (bf16[256,3072]{1,0:T(8,128)(2,1)}, bf16[256,3072]{1,0:T(8,128)(2,1)S(1)}, u32[]{:S(2)}, u32[]{:S(2)}) collective-permute-start(bf16[256,3072]{1,0:T(8,128)(2,1)} %add_pieces.7), channel_id=1, source_target_pairs={{0,4},{4,0},{8,12},{12,8},{16,20},{20,16},{24,28},{28,24},{1,5},{5... | collective-permute-start | bytes 4718600 | tf_op jit(solution)/shard_map/ppermute | solution.py:41
  611.3 57.5 %all-to-all-start.1 = ((bf16[4,64,1536]{2,1,0:T(8,128)(2,1)}), bf16[4,64,1536]{2,1,0:T(8,128)(2,1)S(1)}, u32[]{:S(2)}, u32[]{:S(2)}) async-start(bf16[4,64,1536]{2,1,0:T(8,128)(2,1)} %bitcast.64), calls=%async_computation.4 | async-start | bytes 1572864 | tf_op jit(solution)/shard_map/all_to_all | solution.py:1237
  (152 other events, 2073.7 us)
Sparse Core Ops, SparseCore 0:
  38.9 52.6 all-gather.3
  97.2 39.3 all-gather.5
  149.1 52.8 reduce-scatter.4
  441.0 45.6 all-gather.7
  493.7 43.5 reduce-scatter.6
  543.0 47.6 reduce-scatter.8
  593.1 56.3 reduce-scatter.10

commit v6 on v5

--- a/solution.py
+++ b/solution.py
@@ -56,17 +56,24 @@
     return [v] + [hop(v, i) for i in range(1, lax.axis_size("expert"))]
 
 
-def places_in_ring():
-    n = lax.axis_size("expert")
-    at = [ring(n).index(i) for i in range(n)]
-    at = jnp.asarray(at, jnp.int32)
-    return lax.rem(at[lax.axis_index("expert")] - at + n, n)
+def place_in_ring(i, n):
+    half = i // 2
+    return jnp.where(i % 2 == 0, half, n - 1 - half) if not isinstance(i, int) else (
+        half if i % 2 == 0 else n - 1 - half
+    )
+
+
+def at_place(p, n):
+    return jnp.where(p < (n + 1) // 2, 2 * p, 2 * (n - 1 - p) + 1)
 
 
 def by_line(blocks):
-    where = places_in_ring()
+    n = len(blocks)
+    mine = place_in_ring(lax.axis_index("expert"), n)
     stacked = jnp.stack(blocks)
-    return jnp.concatenate([pick(stacked, where[i], 0) for i in range(len(blocks))], axis=0)
+    return jnp.concatenate(
+        [pick(stacked, lax.rem(mine - place_in_ring(i, n) + n, n), 0) for i in range(n)], axis=0
+    )
 
 
 def bits_of(low, high):
@@ -194,13 +201,25 @@
     return parts[0]
 
 
-def scatter_step(at, kind, bit):
-    keys = sorted(key for key in at.having(kind) if key[1] & bit)
-    v = [at.of.pop(key) for key in keys]
-    got = flip(jnp.concatenate(v, axis=0) if len(v) > 1 else v[0], bit)
-    rows = v[0].shape[0]
-    for i, (_, r) in enumerate(keys):
-        at[kind, r ^ bit] = add(at[kind, r ^ bit], got[i * rows : (i + 1) * rows])
+class Halving:
+    def __init__(self, at, kind, value):
+        self.at, self.kind, self.dp = at, kind, lax.axis_index("dp")
+        n = lax.axis_size("dp")
+        self.left = bits_of(1, n)[::-1]
+        shape = (2,) * len(self.left) + (value.shape[0] // n, value.shape[1])
+        at[kind, 0] = value.reshape(shape)
+
+    def begin(self, bit):
+        at, axis = self.at, self.left.index(bit)
+        mine = lax.rem(self.dp // bit, 2)
+        v = at[self.kind, 0]
+        at[self.kind, 1] = flip(pick(v, 1 - mine, axis), bit)
+        at[self.kind, 0] = pick(v, mine, axis)
+        self.left.remove(bit)
+
+    def end(self):
+        at = self.at
+        at[self.kind, 0] = add(at[self.kind, 0], at.of.pop((self.kind, 1)))
 
 
 def blocks_of(parts, tok):
@@ -822,6 +841,37 @@
     )(own, *[v for v, _ in blocks], *before)
 
 
+def extra_kernel(zat, router, attn, qk, ffn, out, rows):
+    experts, cols = router.shape[0], qk.shape[1]
+    rows[...] = jnp.zeros_like(rows)
+    rows[:experts, :] = router[...]
+    rows[experts : experts + 1, :] = attn[...]
+    at = pl.ds(pl.multiple_of(zat[0] * cols, cols), cols)
+    rows[experts + 1 : experts + 3, at] = qk[...]
+    rows[experts + 3 : experts + 4, :] = ffn[...]
+    out[...] = rows[...].T.astype(BF16)
+
+
+def extra_columns(router, attn, qk, ffn, zat):
+    width = attn.shape[1]
+    whole = lambda x: pl.BlockSpec(x.shape, lambda i, z: (0, 0))
+    out = jax.ShapeDtypeStruct((width, EXTRA), BF16)
+    return pl.pallas_call(
+        extra_kernel,
+        grid_spec=pltpu.PrefetchScalarGridSpec(
+            num_scalar_prefetch=1,
+            grid=(1,),
+            in_specs=[whole(x) for x in (router, attn, qk, ffn)],
+            out_specs=whole(out),
+            scratch_shapes=[pltpu.VMEM((EXTRA, width), F32)],
+        ),
+        out_shape=out,
+        compiler_params=pltpu.CompilerParams(vmem_limit_bytes=VMEM),
+        cost_estimate=COST,
+        name="extra_columns",
+    )(zat, router, attn, qk, ffn)
+
+
 def inv_rms(v):
     return lax.rsqrt(jnp.mean(v * v, axis=-1, keepdims=True) + EPSILON)
 
@@ -1108,7 +1158,7 @@
     chunk_grads(SEND_HIGH, 3 * quarter, halves_cut)
     at.fence(THERE, *at.having(SEND_HIGH), *chunk_keys)
     half = e_rows // 2
-    early = 3 * e_rows // 8
+    early, most = 3 * e_rows // 8, 3 * e_rows // 4
     for i in reversed(range(zs)):
         here = near_sum[i].astype(F32) + at[THERE].astype(F32)
         if i < last:
@@ -1139,9 +1189,9 @@
                 low_cut = [halves_cut[0], (0, e_rows - early, e_rows)]
             chunk_grads(SEND_LOW, 2 * quarter, low_cut)
             at[Y_FAR] = fold([[at[key]] for key in at.having(Y_PART)])[0]
-            at[Y_NEAR] = fold([[at[key]] for key in at.having(NEAR_PART)])[0]
-            beside = [Y_FAR, Y_NEAR, *at.having(SEND_LOW), *at.having(PIECE)]
+            beside = [Y_FAR, *at.having(SEND_LOW), *at.having(PIECE)]
         at.fence(ACC, THERE, *beside, *chunk_keys)
+    at.fence(ACC, *at.having(NEAR_PART))
     dm = at[ACC].astype(F32)
     at[Y_FAR] = flip(at[Y_FAR], top)
     if laid_out:
@@ -1162,8 +1212,9 @@
     grad_out = cotangent.astype(F32)
     dh = grad_out + rms_back(hid, r_ffn, gains[3], dmt)
     at[DHB] = lax.all_gather(dh.astype(BF16), "expert", axis=0, tiled=True)
-    router_part = tn(m, dz)
+    router_part = tn(dz, m)
     gain_ffn = jnp.sum(dmt * hid * r_ffn, axis=0)
+    at[Y_NEAR] = fold([[at[key]] for key in at.having(NEAR_PART)])[0]
     chunk_grads(KEEP_HIGH, quarter, whole_cut)
     if laid_out:
         at[TAIL, quarter, 0] = sum_row(KEEP_HIGH, SEND_HIGH, 0)
@@ -1189,43 +1240,44 @@
 
     dqn, dkn, dv, sums = attend_back(dhb, out_w, qkv, qr, kr, vb, gain_qk, cos, sin, seg)
     means = lax.psum(sums.reshape(-1, rows), "expert").reshape(zs, 2, rows) / width
-    at[OUT_GRAD] = tn(o, dhb, BF16)
+    out_sum = Halving(at, OUT_GRAD, tn(o, dhb, BF16))
     dqkv, gains_qk = join_back(qkv, dqn, dkn, dv, r_qk, means, gain_qk)
     at[DQKV] = dqkv
-    at.fence(DQKV, OUT_GRAD, Y, *at.having(PIECE), *at.having(TAIL))
-    at[OUT_GRAD] = lax.psum_scatter(at[OUT_GRAD], "dp", scatter_dimension=0, tiled=True)
+    at.fence(DQKV, Y, *at.having(OUT_GRAD), *at.having(PIECE), *at.having(TAIL))
+    out_sum.begin(1)
 
     at[ODD] = attn_grads(a_all, at[DQKV], [], me_at, 1, 2)
-    at.fence(ODD, DQKV, *at.having(TAIL), *at.having(SEND_LOW))
+    at.fence(ODD, DQKV, *at.having(OUT_GRAD), *at.having(TAIL), *at.having(SEND_LOW))
+    out_sum.end()
+    out_sum.begin(far_bit)
     at[ODD] = flip(at[ODD], 1)
     if laid_out:
-        at[HALF, 0] = flip(at[TAIL, 3, 0][:early], 2)
+        at[HALF, 0] = flip(at[TAIL, 3, 0][:most], 2)
         send_part(SEND_LOW, 1, e_rows - early)
+    at[DA], at[GAIN_ATTN] = first_back(at[DQKV], attn_w, x_all, r_attn, rows)
     even = attn_grads(a_all, at[DQKV], [], me_at, 0, 2)
     at[HELD] = add(even, at[ODD])
-    at.fence(HELD, DQKV, *at.having(HALF), *at.having(PIECE))
+    at.fence(HELD, DQKV, DA, GAIN_ATTN, *at.having(OUT_GRAD), *at.having(HALF), *at.having(PIECE))
+    at[DA] = lax.psum_scatter(at[DA], "expert", scatter_dimension=0, tiled=True)
     sides = halves(at[HELD], zs * own_rows)
     stage(at, sides, 0)
-    at[DA], at[GAIN_ATTN] = first_back(at[DQKV], attn_w, x_all, r_attn, rows)
-    zero = jnp.zeros((2, width), F32)
-    gain_rows = jnp.concatenate(
-        [
-            at[GAIN_ATTN],
-            lax.dynamic_update_slice_in_dim(zero, gains_qk, z * cols, 1),
-            at[GAIN_FFN][None],
-            jnp.zeros((EXTRA - experts - 4, width), F32),
-        ],
-        axis=0,
-    )
-    at[BESIDE] = jnp.concatenate([at[ROUTER], gain_rows.T], axis=1).astype(BF16)
+    out_sum.end()
+    out_sum.begin(2)
+    at[BESIDE] = extra_columns(
+        at[ROUTER], at[GAIN_ATTN], gains_qk, at[GAIN_FFN][None], jnp.reshape(z, (1,))
+    )
     for turn_ in range(1, len(bits_of(2, dps))):
-        at.fence(*at.having(SIDE), BESIDE, DA, OUT_GRAD, *at.having(KEEP_LOW), *at.having(PIECE))
+        at.fence(*at.having(SIDE), BESIDE, *at.having(OUT_GRAD), *at.having(KEEP_LOW), *at.having(PIECE))
+        out_sum.end()
+        if laid_out:
+            at[OUT_GRAD, 0] = lax.ppermute(
+                at[OUT_GRAD, 0], ("dp", "expert"), [(b, a) for a, b in moved]
+            )
+        if turn_ < len(bits_of(2, dps)) - 1:
+            out_sum.begin(2 << turn_)
         if turn_ == 1:
-            at[DA] = lax.psum_scatter(at[DA], "expert", scatter_dimension=0, tiled=True)
-            stacked = at[BESIDE].reshape(dps, e_rows, EXTRA)
-            for r in range(dps):
-                at[SMALL, r] = pick(stacked, dp ^ r, 0)
-            scatter_step(at, SMALL, 1)
+            small_sum = Halving(at, SMALL, at[BESIDE])
+            small_sum.begin(1)
             for i in range(quarter):
                 at[TAIL, i, 0] = sum_row(KEEP_LOW, SEND_LOW, i)
         sides = unstage(at, sides, turn_ - 1)
@@ -1233,7 +1285,12 @@
     at.fence(*at.having(SIDE), *at.having(SMALL), *at.having(TAIL))
     sides = unstage(at, sides, len(bits_of(2, dps)) - 1)
     at[BACK] = jnp.concatenate([sides[0][0][0], sides[1][0][0]], axis=1)
-    at.fence(BACK, OUT_GRAD, *at.having(SMALL), *at.having(HALF), *at.having(TAIL))
+    at.fence(BACK, DA, *at.having(OUT_GRAD), *at.having(SMALL), *at.having(HALF), *at.having(TAIL))
+    small_sum.end()
+    if not laid_out:
+        at[OUT_GRAD, 0] = lax.ppermute(
+            at[OUT_GRAD, 0], ("dp", "expert"), [(b, a) for a, b in moved]
+        )
     at[BACK] = lax.all_to_all(
         at[BACK].reshape(zs, own_rows, 3 * cols),
         "expert",
@@ -1241,35 +1298,36 @@
         concat_axis=0,
         tiled=True,
     )
-    at[OUT_GRAD] = lax.ppermute(
-        at[OUT_GRAD], ("dp", "expert"), [(b, a) for a, b in moved]
-    )
-    for bit in bits_of(2, dps):
-        scatter_step(at, SMALL, bit)
     own_at = jnp.reshape(own, (1,))
+    bits = bits_of(2, dps)
+    small_sum.begin(bits[0])
     if laid_out:
-        at[HALF, early] = flip(at[TAIL, 3, 0][early:], 2)
+        at[HALF, most] = flip(at[TAIL, 3, 0][most:], 2)
         at[TAIL, 0, 1] = flip(at[TAIL, 1, 0], 1)
         blocks = [(at[TAIL, 0, e], 0) for e in range(local - 1)]
-        at[HALF, 0], at[HALF, early] = flip(at[HALF, 0], 1), flip(at[HALF, early], 1)
-        first = form([*blocks, (at[HALF, 0], 0)], own_at, e_rows, 0, early)
-        blocks += [(at[HALF, early], early)]
-        at[GU], at[DN] = form(blocks, own_at, e_rows, early, e_rows, first)
+        at[HALF, 0] = flip(at[HALF, 0], 1)
+        at[GU], at[DN] = form([*blocks, (at[HALF, 0], 0)], own_at, e_rows, 0, most)
+        at.fence(GU, DN, *at.having(SMALL))
+        blocks += [(flip(at[HALF, most], 1), most)]
+        at[GU], at[DN] = form(blocks, own_at, e_rows, most, e_rows, (at[GU], at[DN]))
     else:
         rest = gather_back({k[1]: at[k] for k in at.having(TAIL)}, local, dps)
         at[GU], at[DN] = form([(rest[e], 0) for e in range(local)], own_at, e_rows, 0, e_rows)
-    at.fence(BACK, OUT_GRAD, DA, GU, DN, *at.having(SMALL))
-    grad_w_out = at[OUT_GRAD].astype(F32)
+    small_sum.end()
+    for bit in bits[1:]:
+        small_sum.begin(bit)
+        small_sum.end()
+    at.fence(BACK, GU, DN, *at.having(OUT_GRAD), *at.having(SMALL))
+    grad_w_out = at[OUT_GRAD, 0].astype(F32)
     back = at[BACK].astype(F32)
     grad_w_qkv = jnp.concatenate(
         [back[e, :, i * cols : (i + 1) * cols] for i in range(3) for e in range(zs)], axis=1
     )
-    line = ring(zs)
-    place = jnp.asarray([line.index(i) for i in range(zs)], jnp.int32)[z]
+    place = place_in_ring(z, zs)
     blocks = at[SMALL, 0].reshape(zs, own_rows, EXTRA)
     extra_sum = pick(blocks, z, 0).astype(F32)
     for i in range(1, zs):
-        to = jnp.asarray(line, jnp.int32)[lax.rem(place + i, zs)]
+        to = at_place(lax.rem(place + i, zs), zs)
         extra_sum = extra_sum + hop(pick(blocks, to, 0), i).astype(F32)
     grad_router = extra_sum[:, :experts]
     grad_gains = extra_sum[:, experts : experts + 4]

time: 703 us -> 690 us (0.982)
  waiting for transfers between devices: 180 us -> 197 us
  between operations: 31.4 us -> 16 us
  other arithmetic: 73.1 us -> 60.7 us
  local copies, waits for them, and re-layouts: 74.1 us -> 66.3 us
    ppermute x1, waiting for transfers between devices: 0.01 us -> 14.4 us  [on_device(): lax.ppermute(at[OUT_GRAD, 0], ('dp', 'expert'), [(b, a) for a, b in moved])]
    ppermute x15, waiting for transfers between devices: 20.3 us -> 28.3 us  [hop(): return lax.ppermute(v, 'expert', pairs)]
    convert_element_type x11 -> x14, other arithmetic: 22.4 us -> 16.4 us  [add(): return (a.astype(F32) + b.astype(F32)).astype(BF16)]
    unnamed x200 -> x174, local copies, waits for them, and re-layouts: 19.5 us -> 17 us
    ppermute x62 -> x65, starting transfers between devices: 42.8 us -> 44.5 us  [flip(): lax.ppermute(v, 'dp', [(i, i ^ bit) for i in range(lax.axis_size('dp'))])]
    ppermute x62 -> x65, waiting for transfers between devices: 145 us -> 144 us  [flip(): lax.ppermute(v, 'dp', [(i, i ^ bit) for i in range(lax.axis_size('dp'))])]
  transfers between devices with their start and end apart: 88 -> 90, of which waited for: 36 -> 34; matrix products, arithmetic and copies ran while one was open for 18% -> 16% of each run, Pallas kernels for 25% -> 27%
where the time goes in v6:
time: 690 us; the launch traced here: 677 us
  Pallas kernels  213 us (31%)
  waiting for transfers between devices  197 us (29%)
  starting transfers between devices  87.4 us (13%)
  local copies, waits for them, and re-layouts  66.3 us (10%)
  other arithmetic  60.7 us (9%)
  blocking collectives  20.1 us (3%)
  matrix products  16.5 us (2%)
  between operations  16 us (2%)
    ppermute x65, waiting for transfers between devices, flip(): lax.ppermute(v, 'dp', [(i, i ^ bit) for i in range(lax.axis_size('dp'))])  144 us
    pallas_call x2, Pallas kernels, run_expert(): pl.pallas_call(functools.partial(expert_kernel, len(heights), len(pieces)...  50.2 us
    ppermute x65, starting transfers between devices, flip(): lax.ppermute(v, 'dp', [(i, i ^ bit) for i in range(lax.axis_size('dp'))])  44.5 us
    pallas_call x4, Pallas kernels, grads(): pl.pallas_call(functools.partial(grads_kernel, len(chunks), rows, cuts),...  41.8 us
    ppermute x15, starting transfers between devices, hop(): return lax.ppermute(v, 'expert', pairs)  28.6 us
    ppermute x15, waiting for transfers between devices, hop(): return lax.ppermute(v, 'expert', pairs)  28.3 us
    pallas_call x4, Pallas kernels, pick_rows(): pl.pallas_call(functools.partial(kernel, len(parts)), grid_spec=pltpu.Pre...  23.1 us
    pallas_call x2, Pallas kernels, result(): pl.pallas_call(functools.partial(result_kernel, count, len(pieces), wide)...  19.2 us
  transfers between devices with their start and end apart: 90, of which 34 were waited for; matrix products, arithmetic and copies ran while one was open for 16% of the time, Pallas kernels for 27%

profile of v6, /device:TPU:4, one launch (start us, length us, event | category | flops | bytes accessed | tf_op | source)
XLA Modules:
  0.0 677.0 jit_solution(11726138217052687834)
XLA Ops:
  20.7 8.7 %constant_dynamic-slice_fusion.2 = (bf16[256,1,2048]{2,1,0:T(2,128)(2,1)S(1)}, bf16[256,1,2048]{2,1,0:T(2,128)(2,1)S(1)}, bf16[256,1,2048]{2,1,0:T(2,128)(2,1)S(1)}, bf16[256,1,2048]{2,1,0:T(2,128)(2,1)S(1)}) fusion(bf16[256,4,2048]{2,1,0:T(4,128)(2,1)S(1)} %copy-done.14, s32[]{:T(128)S(6)} %select_n.167, s32[]{:T(128)S(6)} %select_n.166, ...), kind=kLoop, calls=%fused_computation.176 | loop fusion | bytes 8388624 | tf_op jit(solution)/shard_map/jit(dynamic_index_in_dim)/dynamic_slice | solution.py:88
  41.4 10.7 %collective-permute-done = bf16[128,2048]{1,0:T(8,128)(2,1)} collective-permute-done((bf16[128,2048]{1,0:T(8,128)(2,1)}, bf16[128,2048]{1,0:T(8,128)(2,1)}, u32[]{:S(2)}, u32[]{:S(2)}) %collective-permute-start) | collective-permute-done | bytes 524320 | tf_op jit(solution)/shard_map/ppermute | solution.py:52
  60.2 6.4 collective-permute-done.2
  74.8 7.1 %collective-permute-done.3 = bf16[128,2048]{1,0:T(8,128)(2,1)} collective-permute-done((bf16[128,2048]{1,0:T(8,128)(2,1)}, bf16[128,2048]{1,0:T(8,128)(2,1)}, u32[]{:S(2)}, u32[]{:S(2)}) %collective-permute-start.3) | collective-permute-done | bytes 524320 | tf_op jit(solution)/shard_map/ppermute | solution.py:52
  117.9 9.8 %psum.14 = f32[2,512]{1,0:T(2,128)S(1)} all-reduce(f32[2,512]{1,0:T(2,128)S(1)} %pad_maximum_fusion.14), channel_id=1, replica_groups=mesh['dp'=8,'expert'=4] {'expert'}, use_global_device_ids=true, to_apply=%region_7.8 | all-reduce | flops 1024 | bytes 8192 | tf_op jit(solution)/shard_map/psum | solution.py:1011
  128.4 8.7 %attend.1 = (bf16[512,512]{1,0:T(8,128)(2,1)}, bf16[512,512]{1,0:T(8,128)(2,1)}, bf16[512,512]{1,0:T(8,128)(2,1)}, bf16[512,512]{1,0:T(8,128)(2,1)}) custom-call(f32[512,1536]{1,0:T(8,128)} %copy-done.5, f32[4,2,128]{2,1,0:T(2,128)} %rsqrt_bitcast_fusion.r, f32[2,512]{1,0:T(2,128)} %copy.201.gains, f32[512,128]{1,0:T(8,128)} %copy.202.cos, ...), custom_call_target="tpu_custom_call" | custom-call | flops 1000000 | bytes 100000 | tf_op jit(solution)/shard_map/attend/pallas_call | solution.py:634
  158.3 50.0 %collective-permute-done.10.refs_0_ = bf16[256,2176]{1,0:T(8,128)(2,1)S(1)} collective-permute-done((bf16[256,2176]{1,0:T(8,128)(2,1)S(1)}, bf16[256,2176]{1,0:T(8,128)(2,1)S(1)}, u32[]{:S(2)}, u32[]{:S(2)}) %collective-permute-start.10) | collective-permute-done | bytes 1114144 | tf_op jit(solution)/shard_map/ppermute | solution.py:41
  289.2 24.9 %expert.2 = (bf16[128,2176]{1,0:T(8,128)(2,1)}, bf16[128,2176]{1,0:T(8,128)(2,1)}, bf16[128,2176]{1,0:T(8,128)(2,1)}, bf16[128,2176]{1,0:T(8,128)(2,1)}, bf16[51...) custom-call(s32[3]{0:T(128)} %pad_add_fusion.expert, ...), custom_call_target="tpu_custom_call" | custom-call | flops 1000000 | bytes 100000 | tf_op jit(solution)/shard_map/expert/pallas_call | solution.py:372
  324.8 25.4 %expert.3 = (bf16[128,2176]{1,0:T(8,128)(2,1)}, bf16[128,2176]{1,0:T(8,128)(2,1)}, bf16[128,2176]{1,0:T(8,128)(2,1)}, bf16[128,2176]{1,0:T(8,128)(2,1)}, bf16[25...) custom-call(s32[3]{0:T(128)} %pad_add_fusion.expert, ...), custom_call_target="tpu_custom_call" | custom-call | flops 1000000 | bytes 100000 | tf_op jit(solution)/shard_map/expert/pallas_call | solution.py:372
  359.4 10.2 %grads.4 = (bf16[128,3072]{1,0:T(8,128)(2,1)}, bf16[128,3072]{1,0:T(8,128)(2,1)}, bf16[128,3072]{1,0:T(8,128)(2,1)}, bf16[128,3072]{1,0:T(8,128)(2,1)}) custom-call(bf16[640,2048]{1,0:T(8,128)(2,1)} %get-tuple-element.479.refs_0_, bf16[640,2048]{1,0:T(8,128)(2,1)} %gather_cot.2.refs_1_, bf16[640,1024]{1,0:T(8,128)(2,1)} %get-tuple-element.481.refs_2_, ...), custom_call_target="tpu_custom_call" | custom-call | flops 1000000 | bytes 100000 | tf_op jit(solution)/shard_map/grads/pallas_call | solution.py:471
  377.8 9.7 %result.2 = (bf16[512,2048]{1,0:T(8,128)(2,1)}, bf16[512,2048]{1,0:T(8,128)(2,1)}) custom-call(s32[1]{0:T(128)} %bitcast.29.me, bf16[640,1024]{1,0:T(8,128)(2,1)} %get-tuple-element.488.refs_9_.gact, s32[128,8]{1,0:T(8,128)} %bitcast.201, bf16[256,3072]{1,0:T(8,128)(2,1)} %copy-done.2, bf16[256,3072]{1,0:T(8,128)(2,1)} %copy-done.6, ...), custom_call_target="tpu_custom_call" | custom-call | flops 1000000 | bytes 100000 | tf_op jit(solution)/shard_map/result/pallas_call | solution.py:422
  399.8 9.6 %result.3 = (bf16[512,2048]{1,0:T(8,128)(2,1)}, bf16[512,2048]{1,0:T(8,128)(2,1)}) custom-call(s32[1]{0:T(128)} %bitcast.29.me, bf16[640,1024]{1,0:T(8,128)(2,1)} %get-tuple-element.483.refs_4_.gact, s32[128,8]{1,0:T(8,128)} %bitcast.199, bf16[256,3072]{1,0:T(8,128)(2,1)} %copy-done.2, bf16[256,3072]{1,0:T(8,128)(2,1)} %copy-done.6, ...), custom_call_target="tpu_custom_call" | custom-call | flops 1000000 | bytes 100000 | tf_op jit(solution)/shard_map/result/pallas_call | solution.py:422
  414.9 10.5 %grads.5 = (bf16[128,3072]{1,0:T(8,128)(2,1)}, bf16[128,3072]{1,0:T(8,128)(2,1)}, bf16[160,3072]{1,0:T(8,128)(2,1)}, bf16[96,3072]{1,0:T(8,128)(2,1)}) custom-call(bf16[640,2048]{1,0:T(8,128)(2,1)} %get-tuple-element.479.refs_0_, bf16[640,2048]{1,0:T(8,128)(2,1)} %gather_cot.2.refs_1_, bf16[640,1024]{1,0:T(8,128)(2,1)} %get-tuple-element.481.refs_2_, ...), custom_call_target="tpu_custom_call" | custom-call | flops 1000000 | bytes 100000 | tf_op jit(solution)/shard_map/grads/pallas_call | solution.py:471
  441.5 10.7 %grads.6 = (bf16[256,3072]{1,0:T(8,128)(2,1)}, bf16[256,3072]{1,0:T(8,128)(2,1)}) custom-call(bf16[640,2048]{1,0:T(8,128)(2,1)} %get-tuple-element.479.refs_0_, bf16[640,2048]{1,0:T(8,128)(2,1)} %gather_cot.2.refs_1_, bf16[640,1024]{1,0:T(8,128)(2,1)} %get-tuple-element.481.refs_2_, bf16[640,1024]{1,0:T(8,128)(2,1)} %get-tuple-element.482.refs_3_, ...), custom_call_target="tpu_custom_call" | custom-call | flops 1000000 | bytes 100000 | tf_op jit(solution)/shard_map/grads/pallas_call | solution.py:471
  452.3 10.3 %grads.7 = (bf16[256,3072]{1,0:T(8,128)(2,1)}, bf16[256,3072]{1,0:T(8,128)(2,1)}) custom-call(bf16[640,2048]{1,0:T(8,128)(2,1)} %get-tuple-element.479.refs_0_, bf16[640,2048]{1,0:T(8,128)(2,1)} %gather_cot.2.refs_1_, bf16[640,1024]{1,0:T(8,128)(2,1)} %get-tuple-element.481.refs_2_, bf16[640,1024]{1,0:T(8,128)(2,1)} %get-tuple-element.482.refs_3_, ...), custom_call_target="tpu_custom_call" | custom-call | flops 1000000 | bytes 100000 | tf_op jit(solution)/shard_map/grads/pallas_call | solution.py:471
  469.0 7.2 %collective-permute-done.57.refs_0_ = bf16[128,3072]{1,0:T(8,128)(2,1)S(1)} collective-permute-done((bf16[128,3072]{1,0:T(8,128)(2,1)}, bf16[128,3072]{1,0:T(8,128)(2,1)S(1)}, u32[]{:S(2)}, u32[]{:S(2)}) %collective-permute-start.57) | collective-permute-done | bytes 786464 | tf_op jit(solution)/shard_map/ppermute | solution.py:41
  476.2 10.4 %collective-permute-done.54 = bf16[512,2048]{1,0:T(8,128)(2,1)} collective-permute-done((bf16[512,2048]{1,0:T(8,128)(2,1)}, bf16[512,2048]{1,0:T(8,128)(2,1)}, u32[]{:S(2)}, u32[]{:S(2)}) %collective-permute-start.54) | collective-permute-done | bytes 2097184 | tf_op jit(solution)/shard_map/ppermute | solution.py:41
  499.3 13.9 %attend_back.1 = (f32[512,512]{1,0:T(8,128)}, f32[512,512]{1,0:T(8,128)}, bf16[512,512]{1,0:T(8,128)(2,1)}, f32[4,2,128]{2,1,0:T(2,128)}) custom-call(bf16[512,2048]{1,0:T(8,128)(2,1)} %all-gather.8.cloned.1.call-done.dhb, bf16[512,2048]{1,0:T(8,128)(2,1)} %all-gather.6.cloned.1.call-done.wo, f32[512,1536]{1,0:T(8,128)} %copy-done.5, f32[512,1536]{1,0:T(8,128)} %copy-done.5, ...), custom_call_target="tpu_custom_call" | custom-call | flops 1000000 | bytes 100000 | tf_op jit(solution)/shard_map/attend_back/pallas_call | solution.py:685
  513.2 10.3 %psum.15 = f32[8,128]{1,0:T(8,128)S(1)} all-reduce(f32[8,128]{1,0:T(8,128)} %bitcast.222), channel_id=1, replica_groups=mesh['dp'=8,'expert'=4] {'expert'}, use_global_device_ids=true, to_apply=%region_19.20 | all-reduce | flops 1024 | bytes 8192 | tf_op jit(solution)/shard_map/psum | solution.py:1242
  554.3 12.9 %first_back.1 = (bf16[512,2048]{1,0:T(8,128)(2,1)}, f32[1,2048]{1,0:T(1,128)}) custom-call(bf16[512,1536]{1,0:T(8,128)(2,1)} %get-tuple-element.525.d, bf16[2048,1664]{1,0:T(8,128)(2,1)} %all-gather.4.cloned.1.call-done.w, bf16[512,2048]{1,0:T(8,128)(2,1)} %copy-done.12, f32[512,1]{1,0:T(8,128)} %copy.230.r), custom_call_target="tpu_custom_call" | custom-call | flops 1000000 | bytes 100000 | tf_op jit(solution)/shard_map/first_back/pallas_call | solution.py:778
  580.1 17.7 %collective-permute-done.68 = bf16[64,2048]{1,0:T(8,128)(2,1)S(1)} collective-permute-done((bf16[64,2048]{1,0:T(8,128)(2,1)S(1)}, bf16[64,2048]{1,0:T(8,128)(2,1)S(1)}, u32[]{:S(2)}, u32[]{:S(2)}) %collective-permute-start.68) | collective-permute-done | bytes 262176 | tf_op jit(solution)/shard_map/ppermute | solution.py:41
  611.5 14.4 %collective-permute-done.72 = bf16[64,2048]{1,0:T(8,128)(2,1)} collective-permute-done((bf16[64,2048]{1,0:T(8,128)(2,1)S(1)}, bf16[64,2048]{1,0:T(8,128)(2,1)}, u32[]{:S(2)}, u32[]{:S(2)}) %collective-permute-start.72) | collective-permute-done | bytes 262176 | tf_op jit(solution)/shard_map/ppermute | solution.py:1273
  635.8 7.5 %collective-permute-done.74 = bf16[64,3072]{1,0:T(8,128)(2,1)S(1)} collective-permute-done((bf16[64,3072]{1,0:T(8,128)(2,1)S(1)}, bf16[64,3072]{1,0:T(8,128)(2,1)S(1)}, u32[]{:S(2)}, u32[]{:S(2)}) %collective-permute-start.74) | collective-permute-done | bytes 393248 | tf_op jit(solution)/shard_map/ppermute | solution.py:41
  644.5 8.1 %form.2 = (f32[256,4,2048]{2,1,0:T(4,128)}, f32[256,4,1024]{2,1,0:T(4,128)}) custom-call(s32[1]{0:T(128)} %bitcast.62.own, bf16[256,3072]{1,0:T(8,128)(2,1)} %add_pieces.6.refs_0_, bf16[256,3072]{1,0:T(8,128)(2,1)} %copy-done.22, bf16[256,3072]{1,0:T(8,128)(2,1)} %copy-done.21, bf16[192,3072]{1,0:T(8,128)(2,1)} %collective-permute-done.76.refs_3_), custom_call_target="tpu_custom_call" | custom-call | flops 1000000 | bytes 100000 | tf_op jit(solution)/shard_map/form/pallas_call | solution.py:827
  (525 shorter events, 346.1 us)
Async XLA Ops:
  16.3 75.2 %all-gather.4.cloned.1.call-start = ((), (), s32[]{:S(2)}) async-start(), calls=%async_computation.5 | async-start | bytes 7667712 | tf_op jit(solution)/shard_map/all_gather | solution.py:964
  38.8 98.4 %all-gather.6.cloned.1.call-start = ((), (), s32[]{:S(2)}) async-start(), calls=%async_computation.6 | async-start | bytes 2359296 | tf_op jit(solution)/shard_map/all_gather | solution.py:997
  40.9 45.4 %collective-permute-start.4 = (bf16[256,3072]{1,0:T(8,128)(2,1)}, bf16[256,3072]{1,0:T(8,128)(2,1)S(1)}, u32[]{:S(2)}, u32[]{:S(2)}) collective-permute-start(bf16[256,3072]{1,0:T(8,128)(2,1)} %pad_maximum_fusion.5), channel_id=1, source_target_pairs={{0,4},{4,0},{8,12},{12,8},{16,20},{20,16},{24,28},{28,24},{1,5},{5... | collective-permute-start | bytes 4718600 | tf_op jit(solution)/shard_map/ppermute | solution.py:41
  40.9 45.4 %collective-permute-start.5 = (bf16[256,3072]{1,0:T(8,128)(2,1)}, bf16[256,3072]{1,0:T(8,128)(2,1)}, u32[]{:S(2)}, u32[]{:S(2)}) collective-permute-start(bf16[256,3072]{1,0:T(8,128)(2,1)} %pad_maximum_fusion.7), channel_id=1, source_target_pairs={{0,4},{4,0},{8,12},{12,8},{16,20},{20,16},{24,28},{28,24},{1,5},{5... | collective-permute-start | bytes 4718600 | tf_op jit(solution)/shard_map/ppermute | solution.py:41
  97.1 112.7 %reduce-scatter.4.cloned.1.call-start = ((), (), s32[]{:S(2)}) async-start(), calls=%async_computation.7 | async-start | bytes 2621440 | tf_op jit(solution)/shard_map/reduce_scatter | solution.py:1023
  100.5 47.1 %collective-permute-start.8 = (bf16[256,3072]{1,0:T(8,128)(2,1)}, bf16[256,3072]{1,0:T(8,128)(2,1)S(1)}, u32[]{:S(2)}, u32[]{:S(2)}) collective-permute-start(bf16[256,3072]{1,0:T(8,128)(2,1)} %pad_maximum_fusion.6), channel_id=1, source_target_pairs={{0,8},{4,12},{8,0},{12,4},{16,24},{20,28},{24,16},{28,20},{1,9},{5... | collective-permute-start | bytes 4718600 | tf_op jit(solution)/shard_map/ppermute | solution.py:41
  104.5 44.5 %collective-permute-start.9 = (bf16[256,3072]{1,0:T(8,128)(2,1)S(1)}, bf16[256,3072]{1,0:T(8,128)(2,1)}, u32[]{:S(2)}, u32[]{:S(2)}) collective-permute-start(bf16[256,3072]{1,0:T(8,128)(2,1)S(1)} %pad_maximum_fusion.4.refs_4_.refs_15_.refs_26_.refs_0_), channel_id=1, source_target_pairs={{0,16},{4,20},{8,24},{12,28},{16,0},{20,4},{24,8},{28,12},{1,17},{... | collective-permute-start | bytes 4718600 | tf_op jit(solution)/shard_map/ppermute | solution.py:41
  149.0 337.6 %all-gather.8.cloned.1.call-start = ((), (), s32[]{:S(2)}) async-start(), calls=%async_computation.8 | async-start | bytes 2621440 | tf_op jit(solution)/shard_map/all_gather | solution.py:1214
  149.1 59.3 %collective-permute-start.12 = (bf16[256,3072]{1,0:T(8,128)(2,1)}, bf16[256,3072]{1,0:T(8,128)(2,1)S(1)}, u32[]{:S(2)}, u32[]{:S(2)}) collective-permute-start(bf16[256,3072]{1,0:T(8,128)(2,1)} %collective-permute-done.5), channel_id=1, source_target_pairs={{0,8},{4,12},{8,0},{12,4},{16,24},{20,28},{24,16},{28,20},{1,9},{5... | collective-permute-start | bytes 4718600 | tf_op jit(solution)/shard_map/ppermute | solution.py:41
  149.5 60.3 %collective-permute-start.13 = (bf16[256,3072]{1,0:T(8,128)(2,1)}, bf16[256,3072]{1,0:T(8,128)(2,1)}, u32[]{:S(2)}, u32[]{:S(2)}) collective-permute-start(bf16[256,3072]{1,0:T(8,128)(2,1)} %copy-done.6), channel_id=1, source_target_pairs={{0,16},{4,20},{8,24},{12,28},{16,0},{20,4},{24,8},{28,12},{1,17},{... | collective-permute-start | bytes 4718600 | tf_op jit(solution)/shard_map/ppermute | solution.py:41
  151.0 57.3 %collective-permute-start.10 = (bf16[256,2176]{1,0:T(8,128)(2,1)S(1)}, bf16[256,2176]{1,0:T(8,128)(2,1)S(1)}, u32[]{:S(2)}, u32[]{:S(2)}) collective-permute-start(bf16[256,2176]{1,0:T(8,128)(2,1)S(1)} %pad_maximum_fusion.8), channel_id=1, source_target_pairs={{0,8},{4,12},{8,0},{12,4},{16,24},{20,28},{24,16},{28,20},{1,9},{5... | collective-permute-start | bytes 3342344 | tf_op jit(solution)/shard_map/ppermute | solution.py:41
  152.9 55.4 %collective-permute-start.14 = (bf16[176,3072]{1,0:T(8,128)(2,1)S(1)}, bf16[176,3072]{1,0:T(8,128)(2,1)S(1)}, u32[]{:S(2)}, u32[]{:S(2)}) collective-permute-start(bf16[176,3072]{1,0:T(8,128)(2,1)S(1)} %slice.245), channel_id=1, source_target_pairs={{0,16},{4,20},{8,24},{12,28},{16,0},{20,4},{24,8},{28,12},{1,17},{... | collective-permute-start | bytes 3244040 | tf_op jit(solution)/shard_map/ppermute | solution.py:41
  154.7 53.6 %collective-permute-start.11 = (bf16[128,2176]{1,0:T(8,128)(2,1)}, bf16[128,2176]{1,0:T(8,128)(2,1)S(1)}, u32[]{:S(2)}, u32[]{:S(2)}) collective-permute-start(bf16[128,2176]{1,0:T(8,128)(2,1)} %collective-permute-done.7), channel_id=1, source_target_pairs={{0,2},{2,3},{3,1},{1,0},{4,6},{6,7},{7,5},{5,4},{8,10},{10,11},{11... | collective-permute-start | bytes 1671176 | tf_op jit(solution)/shard_map/ppermute | solution.py:52
  275.4 38.6 %collective-permute-start.35 = (bf16[128,2048]{1,0:T(8,128)(2,1)}, bf16[128,2048]{1,0:T(8,128)(2,1)S(1)}, u32[]{:S(2)}, u32[]{:S(2)}) collective-permute-start(bf16[128,2048]{1,0:T(8,128)(2,1)} %collective-permute-done.19.refs_2_), channel_id=1, source_target_pairs={{0,8},{4,12},{8,0},{12,4},{16,24},{20,28},{24,16},{28,20},{1,9},{5... | collective-permute-start | bytes 1572872 | tf_op jit(solution)/shard_map/ppermute | solution.py:41
  276.3 37.8 %collective-permute-start.36 = (bf16[128,2048]{1,0:T(8,128)(2,1)}, bf16[128,2048]{1,0:T(8,128)(2,1)S(1)}, u32[]{:S(2)}, u32[]{:S(2)}) collective-permute-start(bf16[128,2048]{1,0:T(8,128)(2,1)} %collective-permute-done.23.refs_3_), channel_id=1, source_target_pairs={{0,8},{4,12},{8,0},{12,4},{16,24},{20,28},{24,16},{28,20},{1,9},{5... | collective-permute-start | bytes 1572872 | tf_op jit(solution)/shard_map/ppermute | solution.py:41
  377.0 33.7 %collective-permute-start.49 = (bf16[128,3072]{1,0:T(8,128)(2,1)}, bf16[128,3072]{1,0:T(8,128)(2,1)S(1)}, u32[]{:S(2)}, u32[]{:S(2)}) collective-permute-start(bf16[128,3072]{1,0:T(8,128)(2,1)} %get-tuple-element.439), channel_id=1, source_target_pairs={{0,16},{4,20},{8,24},{12,28},{16,0},{20,4},{24,8},{28,12},{1,17},{... | collective-permute-start | bytes 2359304 | tf_op jit(solution)/shard_map/ppermute | solution.py:41
  437.9 96.1 %reduce-scatter.6.cloned.1.call-start = ((), (), s32[]{:S(2)}) async-start(), calls=%async_computation.9 | async-start | bytes 2621440 | tf_op jit(solution)/shard_map/reduce_scatter | solution.py:1234
  438.2 48.4 %collective-permute-start.54 = (bf16[512,2048]{1,0:T(8,128)(2,1)}, bf16[512,2048]{1,0:T(8,128)(2,1)}, u32[]{:S(2)}, u32[]{:S(2)}) collective-permute-start(bf16[512,2048]{1,0:T(8,128)(2,1)} %add_convert_fusion.3), channel_id=1, source_target_pairs={{0,8},{4,12},{8,0},{12,4},{16,24},{20,28},{24,16},{28,20},{1,9},{5... | collective-permute-start | bytes 6291464 | tf_op jit(solution)/shard_map/ppermute | solution.py:41
  440.4 35.8 %collective-permute-start.57 = (bf16[128,3072]{1,0:T(8,128)(2,1)}, bf16[128,3072]{1,0:T(8,128)(2,1)S(1)}, u32[]{:S(2)}, u32[]{:S(2)}) collective-permute-start(bf16[128,3072]{1,0:T(8,128)(2,1)} %get-tuple-element.493), channel_id=1, source_target_pairs={{0,16},{4,20},{8,24},{12,28},{16,0},{20,4},{24,8},{28,12},{1,17},{... | collective-permute-start | bytes 2359304 | tf_op jit(solution)/shard_map/ppermute | solution.py:41
  491.2 134.8 %reduce-scatter.8.cloned.1.call-start = ((), (), s32[]{:S(2)}) async-start(), calls=%async_computation.10 | async-start | bytes 2621440 | tf_op jit(solution)/shard_map/reduce_scatter | solution.py:1261
  492.5 41.4 %collective-permute-start.60 = (bf16[256,3072]{1,0:T(8,128)(2,1)S(1)}, bf16[256,3072]{1,0:T(8,128)(2,1)S(1)}, u32[]{:S(2)}, u32[]{:S(2)}) collective-permute-start(bf16[256,3072]{1,0:T(8,128)(2,1)S(1)} %copy-done.39), channel_id=1, source_target_pairs={{0,8},{4,12},{8,0},{12,4},{16,24},{20,28},{24,16},{28,20},{1,9},{5... | collective-permute-start | bytes 4718600 | tf_op jit(solution)/shard_map/ppermute | solution.py:41
  493.8 40.2 %collective-permute-start.59 = (bf16[160,3072]{1,0:T(8,128)(2,1)}, bf16[160,3072]{1,0:T(8,128)(2,1)}, u32[]{:S(2)}, u32[]{:S(2)}) collective-permute-start(bf16[160,3072]{1,0:T(8,128)(2,1)} %get-tuple-element.516), channel_id=1, source_target_pairs={{0,16},{4,20},{8,24},{12,28},{16,0},{20,4},{24,8},{28,12},{1,17},{... | collective-permute-start | bytes 2949128 | tf_op jit(solution)/shard_map/ppermute | solution.py:41
  494.7 39.3 %collective-permute-start.58 = (bf16[128,3072]{1,0:T(8,128)(2,1)}, bf16[128,3072]{1,0:T(8,128)(2,1)}, u32[]{:S(2)}, u32[]{:S(2)}) collective-permute-start(bf16[128,3072]{1,0:T(8,128)(2,1)} %get-tuple-element.515), channel_id=1, source_target_pairs={{0,16},{4,20},{8,24},{12,28},{16,0},{20,4},{24,8},{28,12},{1,17},{... | collective-permute-start | bytes 2359304 | tf_op jit(solution)/shard_map/ppermute | solution.py:41
  626.5 33.5 %all-to-all-start.1 = ((bf16[4,64,1536]{2,1,0:T(8,128)(2,1)}), bf16[4,64,1536]{2,1,0:T(8,128)(2,1)S(1)}, u32[]{:S(2)}, u32[]{:S(2)}) async-start(bf16[4,64,1536]{2,1,0:T(8,128)(2,1)} %bitcast.61), calls=%async_computation.4 | async-start | bytes 1572864 | tf_op jit(solution)/shard_map/all_to_all | solution.py:1294
  (141 other events, 1958.8 us)
Sparse Core Ops, SparseCore 0:
  38.9 52.6 all-gather.3
  97.2 39.2 all-gather.5
  149.1 52.8 reduce-scatter.3
  438.0 44.2 all-gather.7
  491.3 42.5 reduce-scatter.5
  573.6 47.7 reduce-scatter.7

commit v7 on v6

--- a/solution.py
+++ b/solution.py
@@ -1217,7 +1217,8 @@
     at[Y_NEAR] = fold([[at[key]] for key in at.having(NEAR_PART)])[0]
     chunk_grads(KEEP_HIGH, quarter, whole_cut)
     if laid_out:
-        at[TAIL, quarter, 0] = sum_row(KEEP_HIGH, SEND_HIGH, 0)
+        for i in range(quarter):
+            at[TAIL, quarter + i, 0] = sum_row(KEEP_HIGH, SEND_HIGH, i)
     chunk_grads(KEEP_LOW, 0, whole_cut)
     at[ROUTER], at[GAIN_FFN] = router_part, gain_ffn
     tails = at.having(TAIL)
@@ -1228,8 +1229,9 @@
         at[TAIL, 0, 2] = flip(at[TAIL, 2, 0], 2)
         send_part(SEND_LOW, 0, half)
         send_part(SEND_LOW, 1, 0)
-    for i in range(1 if laid_out else 0, quarter):
-        at[TAIL, quarter + i, 0] = sum_row(KEEP_HIGH, SEND_HIGH, i)
+    if not laid_out:
+        for i in range(quarter):
+            at[TAIL, quarter + i, 0] = sum_row(KEEP_HIGH, SEND_HIGH, i)
     y_own = add(at[Y_NEAR], at[Y_FAR])
     at[Y] = lax.psum_scatter(
         by_line([y_own[i * rows : (i + 1) * rows] for i in range(zs)]),
@@ -1285,7 +1287,7 @@
     at.fence(*at.having(SIDE), *at.having(SMALL), *at.having(TAIL))
     sides = unstage(at, sides, len(bits_of(2, dps)) - 1)
     at[BACK] = jnp.concatenate([sides[0][0][0], sides[1][0][0]], axis=1)
-    at.fence(BACK, DA, *at.having(OUT_GRAD), *at.having(SMALL), *at.having(HALF), *at.having(TAIL))
+    at.fence(BACK, *at.having(OUT_GRAD), *at.having(SMALL), *at.having(HALF), *at.having(TAIL))
     small_sum.end()
     if not laid_out:
         at[OUT_GRAD, 0] = lax.ppermute(
@@ -1307,7 +1309,7 @@
         blocks = [(at[TAIL, 0, e], 0) for e in range(local - 1)]
         at[HALF, 0] = flip(at[HALF, 0], 1)
         at[GU], at[DN] = form([*blocks, (at[HALF, 0], 0)], own_at, e_rows, 0, most)
-        at.fence(GU, DN, *at.having(SMALL))
+        at.fence(GU, DN, DA, *at.having(SMALL))
         blocks += [(flip(at[HALF, most], 1), most)]
         at[GU], at[DN] = form(blocks, own_at, e_rows, most, e_rows, (at[GU], at[DN]))
     else:

time: 690 us -> 686 us (level)
    unnamed x174 -> x176, local copies, waits for them, and re-layouts: 17 us -> 17.3 us
  transfers between devices with their start and end apart: 90 -> 90, of which waited for: 34 -> 34; matrix products, arithmetic and copies ran while one was open for 16% -> 17% of each run, Pallas kernels for 27% -> 27%
where the time goes in v7:
time: 686 us; the launch traced here: 673 us
  Pallas kernels  213 us (31%)
  waiting for transfers between devices  193 us (28%)
  starting transfers between devices  85.2 us (12%)
  local copies, waits for them, and re-layouts  67.2 us (10%)
  other arithmetic  62.5 us (9%)
  blocking collectives  19.9 us (3%)
  matrix products  16.5 us (2%)
  between operations  15.9 us (2%)
    ppermute x65, waiting for transfers between devices, flip(): lax.ppermute(v, 'dp', [(i, i ^ bit) for i in range(lax.axis_size('dp'))])  140 us
    pallas_call x2, Pallas kernels, run_expert(): pl.pallas_call(functools.partial(expert_kernel, len(heights), len(pieces)...  50.3 us
    ppermute x65, starting transfers between devices, flip(): lax.ppermute(v, 'dp', [(i, i ^ bit) for i in range(lax.axis_size('dp'))])  44.5 us
    pallas_call x4, Pallas kernels, grads(): pl.pallas_call(functools.partial(grads_kernel, len(chunks), rows, cuts),...  41.8 us
    ppermute x15, waiting for transfers between devices, hop(): return lax.ppermute(v, 'expert', pairs)  28.7 us
    ppermute x15, starting transfers between devices, hop(): return lax.ppermute(v, 'expert', pairs)  26.4 us
    pallas_call x4, Pallas kernels, pick_rows(): pl.pallas_call(functools.partial(kernel, len(parts)), grid_spec=pltpu.Pre...  23.1 us
    pallas_call x2, Pallas kernels, result(): pl.pallas_call(functools.partial(result_kernel, count, len(pieces), wide)...  19 us
  transfers between devices with their start and end apart: 90, of which 34 were waited for; matrix products, arithmetic and copies ran while one was open for 17% of the time, Pallas kernels for 27%

profile of v7, /device:TPU:4, one launch (start us, length us, event | category | flops | bytes accessed | tf_op | source)
XLA Modules:
  0.0 673.3 jit_solution(3173361542050874716)
XLA Ops:
  20.7 8.7 %constant_dynamic-slice_fusion.2 = (bf16[256,1,2048]{2,1,0:T(2,128)(2,1)S(1)}, bf16[256,1,2048]{2,1,0:T(2,128)(2,1)S(1)}, bf16[256,1,2048]{2,1,0:T(2,128)(2,1)S(1)}, bf16[256,1,2048]{2,1,0:T(2,128)(2,1)S(1)}) fusion(bf16[256,4,2048]{2,1,0:T(4,128)(2,1)S(1)} %copy-done.14, s32[]{:T(128)S(6)} %select_n.167, s32[]{:T(128)S(6)} %select_n.166, ...), kind=kLoop, calls=%fused_computation.176 | loop fusion | bytes 8388624 | tf_op jit(solution)/shard_map/jit(dynamic_index_in_dim)/dynamic_slice | solution.py:88
  41.4 10.7 %collective-permute-done = bf16[128,2048]{1,0:T(8,128)(2,1)} collective-permute-done((bf16[128,2048]{1,0:T(8,128)(2,1)}, bf16[128,2048]{1,0:T(8,128)(2,1)}, u32[]{:S(2)}, u32[]{:S(2)}) %collective-permute-start) | collective-permute-done | bytes 524320 | tf_op jit(solution)/shard_map/ppermute | solution.py:52
  60.1 6.4 collective-permute-done.2
  74.8 7.1 %collective-permute-done.3 = bf16[128,2048]{1,0:T(8,128)(2,1)} collective-permute-done((bf16[128,2048]{1,0:T(8,128)(2,1)}, bf16[128,2048]{1,0:T(8,128)(2,1)}, u32[]{:S(2)}, u32[]{:S(2)}) %collective-permute-start.3) | collective-permute-done | bytes 524320 | tf_op jit(solution)/shard_map/ppermute | solution.py:52
  117.9 9.8 %psum.14 = f32[2,512]{1,0:T(2,128)S(1)} all-reduce(f32[2,512]{1,0:T(2,128)S(1)} %pad_maximum_fusion.14), channel_id=1, replica_groups=mesh['dp'=8,'expert'=4] {'expert'}, use_global_device_ids=true, to_apply=%region_7.8 | all-reduce | flops 1024 | bytes 8192 | tf_op jit(solution)/shard_map/psum | solution.py:1011
  128.4 8.7 %attend.1 = (bf16[512,512]{1,0:T(8,128)(2,1)}, bf16[512,512]{1,0:T(8,128)(2,1)}, bf16[512,512]{1,0:T(8,128)(2,1)}, bf16[512,512]{1,0:T(8,128)(2,1)}) custom-call(f32[512,1536]{1,0:T(8,128)} %copy-done.5, f32[4,2,128]{2,1,0:T(2,128)} %rsqrt_bitcast_fusion.r, f32[2,512]{1,0:T(2,128)} %copy.201.gains, f32[512,128]{1,0:T(8,128)} %copy.202.cos, ...), custom_call_target="tpu_custom_call" | custom-call | flops 1000000 | bytes 100000 | tf_op jit(solution)/shard_map/attend/pallas_call | solution.py:634
  158.3 50.0 %collective-permute-done.10.refs_0_ = bf16[256,2176]{1,0:T(8,128)(2,1)S(1)} collective-permute-done((bf16[256,2176]{1,0:T(8,128)(2,1)S(1)}, bf16[256,2176]{1,0:T(8,128)(2,1)S(1)}, u32[]{:S(2)}, u32[]{:S(2)}) %collective-permute-start.10) | collective-permute-done | bytes 1114144 | tf_op jit(solution)/shard_map/ppermute | solution.py:41
  280.1 6.3 gather.9
  289.2 24.9 %expert.2 = (bf16[128,2176]{1,0:T(8,128)(2,1)}, bf16[128,2176]{1,0:T(8,128)(2,1)}, bf16[128,2176]{1,0:T(8,128)(2,1)}, bf16[128,2176]{1,0:T(8,128)(2,1)}, bf16[51...) custom-call(s32[3]{0:T(128)} %pad_add_fusion.expert, ...), custom_call_target="tpu_custom_call" | custom-call | flops 1000000 | bytes 100000 | tf_op jit(solution)/shard_map/expert/pallas_call | solution.py:372
  318.5 6.3 gather.10
  324.8 25.4 %expert.3 = (bf16[128,2176]{1,0:T(8,128)(2,1)}, bf16[128,2176]{1,0:T(8,128)(2,1)}, bf16[128,2176]{1,0:T(8,128)(2,1)}, bf16[128,2176]{1,0:T(8,128)(2,1)}, bf16[25...) custom-call(s32[3]{0:T(128)} %pad_add_fusion.expert, ...), custom_call_target="tpu_custom_call" | custom-call | flops 1000000 | bytes 100000 | tf_op jit(solution)/shard_map/expert/pallas_call | solution.py:372
  359.5 10.2 %grads.4 = (bf16[128,3072]{1,0:T(8,128)(2,1)}, bf16[128,3072]{1,0:T(8,128)(2,1)}, bf16[128,3072]{1,0:T(8,128)(2,1)}, bf16[128,3072]{1,0:T(8,128)(2,1)}) custom-call(bf16[640,2048]{1,0:T(8,128)(2,1)} %get-tuple-element.477.refs_0_, bf16[640,2048]{1,0:T(8,128)(2,1)} %gather_cot.2.refs_1_, bf16[640,1024]{1,0:T(8,128)(2,1)} %get-tuple-element.479.refs_2_, ...), custom_call_target="tpu_custom_call" | custom-call | flops 1000000 | bytes 100000 | tf_op jit(solution)/shard_map/grads/pallas_call | solution.py:471
  377.9 9.5 %result.2 = (bf16[512,2048]{1,0:T(8,128)(2,1)}, bf16[512,2048]{1,0:T(8,128)(2,1)}) custom-call(s32[1]{0:T(128)} %bitcast.29.me, bf16[640,1024]{1,0:T(8,128)(2,1)} %get-tuple-element.486.refs_9_.gact, s32[128,8]{1,0:T(8,128)} %bitcast.201, bf16[256,3072]{1,0:T(8,128)(2,1)} %copy-done.2, bf16[256,3072]{1,0:T(8,128)(2,1)} %copy-done.6, ...), custom_call_target="tpu_custom_call" | custom-call | flops 1000000 | bytes 100000 | tf_op jit(solution)/shard_map/result/pallas_call | solution.py:422
  399.9 9.5 %result.3 = (bf16[512,2048]{1,0:T(8,128)(2,1)}, bf16[512,2048]{1,0:T(8,128)(2,1)}) custom-call(s32[1]{0:T(128)} %bitcast.29.me, bf16[640,1024]{1,0:T(8,128)(2,1)} %get-tuple-element.481.refs_4_.gact, s32[128,8]{1,0:T(8,128)} %bitcast.199, bf16[256,3072]{1,0:T(8,128)(2,1)} %copy-done.2, bf16[256,3072]{1,0:T(8,128)(2,1)} %copy-done.6, ...), custom_call_target="tpu_custom_call" | custom-call | flops 1000000 | bytes 100000 | tf_op jit(solution)/shard_map/result/pallas_call | solution.py:422
  415.0 10.5 %grads.5 = (bf16[128,3072]{1,0:T(8,128)(2,1)}, bf16[128,3072]{1,0:T(8,128)(2,1)}, bf16[160,3072]{1,0:T(8,128)(2,1)}, bf16[96,3072]{1,0:T(8,128)(2,1)}) custom-call(bf16[640,2048]{1,0:T(8,128)(2,1)} %get-tuple-element.477.refs_0_, bf16[640,2048]{1,0:T(8,128)(2,1)} %gather_cot.2.refs_1_, bf16[640,1024]{1,0:T(8,128)(2,1)} %get-tuple-element.479.refs_2_, ...), custom_call_target="tpu_custom_call" | custom-call | flops 1000000 | bytes 100000 | tf_op jit(solution)/shard_map/grads/pallas_call | solution.py:471
  441.6 10.7 %grads.6 = (bf16[256,3072]{1,0:T(8,128)(2,1)}, bf16[256,3072]{1,0:T(8,128)(2,1)}) custom-call(bf16[640,2048]{1,0:T(8,128)(2,1)} %get-tuple-element.477.refs_0_, bf16[640,2048]{1,0:T(8,128)(2,1)} %gather_cot.2.refs_1_, bf16[640,1024]{1,0:T(8,128)(2,1)} %get-tuple-element.479.refs_2_, bf16[640,1024]{1,0:T(8,128)(2,1)} %get-tuple-element.480.refs_3_, ...), custom_call_target="tpu_custom_call" | custom-call | flops 1000000 | bytes 100000 | tf_op jit(solution)/shard_map/grads/pallas_call | solution.py:471
  452.3 10.4 %grads.7 = (bf16[256,3072]{1,0:T(8,128)(2,1)}, bf16[256,3072]{1,0:T(8,128)(2,1)}) custom-call(bf16[640,2048]{1,0:T(8,128)(2,1)} %get-tuple-element.477.refs_0_, bf16[640,2048]{1,0:T(8,128)(2,1)} %gather_cot.2.refs_1_, bf16[640,1024]{1,0:T(8,128)(2,1)} %get-tuple-element.479.refs_2_, bf16[640,1024]{1,0:T(8,128)(2,1)} %get-tuple-element.480.refs_3_, ...), custom_call_target="tpu_custom_call" | custom-call | flops 1000000 | bytes 100000 | tf_op jit(solution)/shard_map/grads/pallas_call | solution.py:471
  476.2 10.4 %collective-permute-done.54 = bf16[512,2048]{1,0:T(8,128)(2,1)} collective-permute-done((bf16[512,2048]{1,0:T(8,128)(2,1)}, bf16[512,2048]{1,0:T(8,128)(2,1)}, u32[]{:S(2)}, u32[]{:S(2)}) %collective-permute-start.54) | collective-permute-done | bytes 2097184 | tf_op jit(solution)/shard_map/ppermute | solution.py:41
  495.8 14.0 %attend_back.1 = (f32[512,512]{1,0:T(8,128)}, f32[512,512]{1,0:T(8,128)}, bf16[512,512]{1,0:T(8,128)(2,1)}, f32[4,2,128]{2,1,0:T(2,128)}) custom-call(bf16[512,2048]{1,0:T(8,128)(2,1)} %all-gather.8.cloned.1.call-done.dhb, bf16[512,2048]{1,0:T(8,128)(2,1)} %all-gather.6.cloned.1.call-done.wo, f32[512,1536]{1,0:T(8,128)} %copy-done.5, f32[512,1536]{1,0:T(8,128)} %copy-done.5, ...), custom_call_target="tpu_custom_call" | custom-call | flops 1000000 | bytes 100000 | tf_op jit(solution)/shard_map/attend_back/pallas_call | solution.py:685
  509.8 10.1 %psum.15 = f32[8,128]{1,0:T(8,128)S(1)} all-reduce(f32[8,128]{1,0:T(8,128)} %bitcast.222), channel_id=1, replica_groups=mesh['dp'=8,'expert'=4] {'expert'}, use_global_device_ids=true, to_apply=%region_19.20 | all-reduce | flops 1024 | bytes 8192 | tf_op jit(solution)/shard_map/psum | solution.py:1244
  554.4 12.9 %first_back.1 = (bf16[512,2048]{1,0:T(8,128)(2,1)}, f32[1,2048]{1,0:T(1,128)}) custom-call(bf16[512,1536]{1,0:T(8,128)(2,1)} %get-tuple-element.521.d, bf16[2048,1664]{1,0:T(8,128)(2,1)} %all-gather.4.cloned.1.call-done.w, bf16[512,2048]{1,0:T(8,128)(2,1)} %copy-done.12, f32[512,1]{1,0:T(8,128)} %copy.230.r), custom_call_target="tpu_custom_call" | custom-call | flops 1000000 | bytes 100000 | tf_op jit(solution)/shard_map/first_back/pallas_call | solution.py:778
  580.1 17.7 %collective-permute-done.68 = bf16[64,2048]{1,0:T(8,128)(2,1)S(1)} collective-permute-done((bf16[64,2048]{1,0:T(8,128)(2,1)S(1)}, bf16[64,2048]{1,0:T(8,128)(2,1)S(1)}, u32[]{:S(2)}, u32[]{:S(2)}) %collective-permute-start.68) | collective-permute-done | bytes 262176 | tf_op jit(solution)/shard_map/ppermute | solution.py:41
  611.5 14.4 %collective-permute-done.72 = bf16[64,2048]{1,0:T(8,128)(2,1)} collective-permute-done((bf16[64,2048]{1,0:T(8,128)(2,1)S(1)}, bf16[64,2048]{1,0:T(8,128)(2,1)}, u32[]{:S(2)}, u32[]{:S(2)}) %collective-permute-start.72) | collective-permute-done | bytes 262176 | tf_op jit(solution)/shard_map/ppermute | solution.py:1275
  640.8 8.0 %form.2 = (f32[256,4,2048]{2,1,0:T(4,128)}, f32[256,4,1024]{2,1,0:T(4,128)}) custom-call(s32[1]{0:T(128)} %bitcast.49.own, bf16[256,3072]{1,0:T(8,128)(2,1)} %add_pieces.6.refs_0_, bf16[256,3072]{1,0:T(8,128)(2,1)} %copy-done.22, bf16[256,3072]{1,0:T(8,128)(2,1)} %copy-done.21, bf16[192,3072]{1,0:T(8,128)(2,1)} %collective-permute-done.74.refs_3_), custom_call_target="tpu_custom_call" | custom-call | flops 1000000 | bytes 100000 | tf_op jit(solution)/shard_map/form/pallas_call | solution.py:827
  (527 shorter events, 344.8 us)
Async XLA Ops:
  16.3 75.2 %all-gather.4.cloned.1.call-start = ((), (), s32[]{:S(2)}) async-start(), calls=%async_computation.5 | async-start | bytes 7667712 | tf_op jit(solution)/shard_map/all_gather | solution.py:964
  38.8 98.3 %all-gather.6.cloned.1.call-start = ((), (), s32[]{:S(2)}) async-start(), calls=%async_computation.6 | async-start | bytes 2359296 | tf_op jit(solution)/shard_map/all_gather | solution.py:997
  40.9 45.4 %collective-permute-start.4 = (bf16[256,3072]{1,0:T(8,128)(2,1)}, bf16[256,3072]{1,0:T(8,128)(2,1)S(1)}, u32[]{:S(2)}, u32[]{:S(2)}) collective-permute-start(bf16[256,3072]{1,0:T(8,128)(2,1)} %pad_maximum_fusion.5), channel_id=1, source_target_pairs={{0,4},{4,0},{8,12},{12,8},{16,20},{20,16},{24,28},{28,24},{1,5},{5... | collective-permute-start | bytes 4718600 | tf_op jit(solution)/shard_map/ppermute | solution.py:41
  40.9 45.4 %collective-permute-start.5 = (bf16[256,3072]{1,0:T(8,128)(2,1)}, bf16[256,3072]{1,0:T(8,128)(2,1)}, u32[]{:S(2)}, u32[]{:S(2)}) collective-permute-start(bf16[256,3072]{1,0:T(8,128)(2,1)} %pad_maximum_fusion.7), channel_id=1, source_target_pairs={{0,4},{4,0},{8,12},{12,8},{16,20},{20,16},{24,28},{28,24},{1,5},{5... | collective-permute-start | bytes 4718600 | tf_op jit(solution)/shard_map/ppermute | solution.py:41
  97.1 112.8 %reduce-scatter.4.cloned.1.call-start = ((), (), s32[]{:S(2)}) async-start(), calls=%async_computation.7 | async-start | bytes 2621440 | tf_op jit(solution)/shard_map/reduce_scatter | solution.py:1023
  100.5 47.1 %collective-permute-start.8 = (bf16[256,3072]{1,0:T(8,128)(2,1)}, bf16[256,3072]{1,0:T(8,128)(2,1)S(1)}, u32[]{:S(2)}, u32[]{:S(2)}) collective-permute-start(bf16[256,3072]{1,0:T(8,128)(2,1)} %pad_maximum_fusion.6), channel_id=1, source_target_pairs={{0,8},{4,12},{8,0},{12,4},{16,24},{20,28},{24,16},{28,20},{1,9},{5... | collective-permute-start | bytes 4718600 | tf_op jit(solution)/shard_map/ppermute | solution.py:41
  104.4 44.5 %collective-permute-start.9 = (bf16[256,3072]{1,0:T(8,128)(2,1)S(1)}, bf16[256,3072]{1,0:T(8,128)(2,1)}, u32[]{:S(2)}, u32[]{:S(2)}) collective-permute-start(bf16[256,3072]{1,0:T(8,128)(2,1)S(1)} %pad_maximum_fusion.4.refs_4_.refs_15_.refs_26_.refs_0_), channel_id=1, source_target_pairs={{0,16},{4,20},{8,24},{12,28},{16,0},{20,4},{24,8},{28,12},{1,17},{... | collective-permute-start | bytes 4718600 | tf_op jit(solution)/shard_map/ppermute | solution.py:41
  149.0 337.6 %all-gather.8.cloned.1.call-start = ((), (), s32[]{:S(2)}) async-start(), calls=%async_computation.8 | async-start | bytes 2621440 | tf_op jit(solution)/shard_map/all_gather | solution.py:1214
  149.0 59.3 %collective-permute-start.12 = (bf16[256,3072]{1,0:T(8,128)(2,1)}, bf16[256,3072]{1,0:T(8,128)(2,1)S(1)}, u32[]{:S(2)}, u32[]{:S(2)}) collective-permute-start(bf16[256,3072]{1,0:T(8,128)(2,1)} %collective-permute-done.5), channel_id=1, source_target_pairs={{0,8},{4,12},{8,0},{12,4},{16,24},{20,28},{24,16},{28,20},{1,9},{5... | collective-permute-start | bytes 4718600 | tf_op jit(solution)/shard_map/ppermute | solution.py:41
  149.5 60.4 %collective-permute-start.13 = (bf16[256,3072]{1,0:T(8,128)(2,1)}, bf16[256,3072]{1,0:T(8,128)(2,1)}, u32[]{:S(2)}, u32[]{:S(2)}) collective-permute-start(bf16[256,3072]{1,0:T(8,128)(2,1)} %copy-done.6), channel_id=1, source_target_pairs={{0,16},{4,20},{8,24},{12,28},{16,0},{20,4},{24,8},{28,12},{1,17},{... | collective-permute-start | bytes 4718600 | tf_op jit(solution)/shard_map/ppermute | solution.py:41
  151.0 57.3 %collective-permute-start.10 = (bf16[256,2176]{1,0:T(8,128)(2,1)S(1)}, bf16[256,2176]{1,0:T(8,128)(2,1)S(1)}, u32[]{:S(2)}, u32[]{:S(2)}) collective-permute-start(bf16[256,2176]{1,0:T(8,128)(2,1)S(1)} %pad_maximum_fusion.8), channel_id=1, source_target_pairs={{0,8},{4,12},{8,0},{12,4},{16,24},{20,28},{24,16},{28,20},{1,9},{5... | collective-permute-start | bytes 3342344 | tf_op jit(solution)/shard_map/ppermute | solution.py:41
  152.9 55.4 %collective-permute-start.14 = (bf16[176,3072]{1,0:T(8,128)(2,1)S(1)}, bf16[176,3072]{1,0:T(8,128)(2,1)S(1)}, u32[]{:S(2)}, u32[]{:S(2)}) collective-permute-start(bf16[176,3072]{1,0:T(8,128)(2,1)S(1)} %slice.245), channel_id=1, source_target_pairs={{0,16},{4,20},{8,24},{12,28},{16,0},{20,4},{24,8},{28,12},{1,17},{... | collective-permute-start | bytes 3244040 | tf_op jit(solution)/shard_map/ppermute | solution.py:41
  154.7 53.6 %collective-permute-start.11 = (bf16[128,2176]{1,0:T(8,128)(2,1)}, bf16[128,2176]{1,0:T(8,128)(2,1)S(1)}, u32[]{:S(2)}, u32[]{:S(2)}) collective-permute-start(bf16[128,2176]{1,0:T(8,128)(2,1)} %collective-permute-done.7), channel_id=1, source_target_pairs={{0,2},{2,3},{3,1},{1,0},{4,6},{6,7},{7,5},{5,4},{8,10},{10,11},{11... | collective-permute-start | bytes 1671176 | tf_op jit(solution)/shard_map/ppermute | solution.py:52
  275.5 38.6 %collective-permute-start.35 = (bf16[128,2048]{1,0:T(8,128)(2,1)}, bf16[128,2048]{1,0:T(8,128)(2,1)S(1)}, u32[]{:S(2)}, u32[]{:S(2)}) collective-permute-start(bf16[128,2048]{1,0:T(8,128)(2,1)} %collective-permute-done.19.refs_2_), channel_id=1, source_target_pairs={{0,8},{4,12},{8,0},{12,4},{16,24},{20,28},{24,16},{28,20},{1,9},{5... | collective-permute-start | bytes 1572872 | tf_op jit(solution)/shard_map/ppermute | solution.py:41
  276.3 37.8 %collective-permute-start.36 = (bf16[128,2048]{1,0:T(8,128)(2,1)}, bf16[128,2048]{1,0:T(8,128)(2,1)S(1)}, u32[]{:S(2)}, u32[]{:S(2)}) collective-permute-start(bf16[128,2048]{1,0:T(8,128)(2,1)} %collective-permute-done.23.refs_3_), channel_id=1, source_target_pairs={{0,8},{4,12},{8,0},{12,4},{16,24},{20,28},{24,16},{28,20},{1,9},{5... | collective-permute-start | bytes 1572872 | tf_op jit(solution)/shard_map/ppermute | solution.py:41
  377.0 33.6 %collective-permute-start.49 = (bf16[128,3072]{1,0:T(8,128)(2,1)}, bf16[128,3072]{1,0:T(8,128)(2,1)S(1)}, u32[]{:S(2)}, u32[]{:S(2)}) collective-permute-start(bf16[128,3072]{1,0:T(8,128)(2,1)} %get-tuple-element.437), channel_id=1, source_target_pairs={{0,16},{4,20},{8,24},{12,28},{16,0},{20,4},{24,8},{28,12},{1,17},{... | collective-permute-start | bytes 2359304 | tf_op jit(solution)/shard_map/ppermute | solution.py:41
  438.0 96.1 %reduce-scatter.6.cloned.1.call-start = ((), (), s32[]{:S(2)}) async-start(), calls=%async_computation.9 | async-start | bytes 2621440 | tf_op jit(solution)/shard_map/reduce_scatter | solution.py:1236
  438.2 34.3 %collective-permute-start.55 = (bf16[512,2048]{1,0:T(8,128)(2,1)}, bf16[512,2048]{1,0:T(8,128)(2,1)S(1)}, u32[]{:S(2)}, u32[]{:S(2)}) collective-permute-start(bf16[512,2048]{1,0:T(8,128)(2,1)} %get-tuple-element.476), channel_id=1, source_target_pairs={{0,4},{4,0},{8,12},{12,8},{16,20},{20,16},{24,28},{28,24},{1,5},{5... | collective-permute-start | bytes 6291464 | tf_op jit(solution)/shard_map/ppermute | solution.py:41
  438.3 48.4 %collective-permute-start.54 = (bf16[512,2048]{1,0:T(8,128)(2,1)}, bf16[512,2048]{1,0:T(8,128)(2,1)}, u32[]{:S(2)}, u32[]{:S(2)}) collective-permute-start(bf16[512,2048]{1,0:T(8,128)(2,1)} %add_convert_fusion.3), channel_id=1, source_target_pairs={{0,8},{4,12},{8,0},{12,4},{16,24},{20,28},{24,16},{28,20},{1,9},{5... | collective-permute-start | bytes 6291464 | tf_op jit(solution)/shard_map/ppermute | solution.py:41
  440.5 35.8 %collective-permute-start.57 = (bf16[128,3072]{1,0:T(8,128)(2,1)}, bf16[128,3072]{1,0:T(8,128)(2,1)S(1)}, u32[]{:S(2)}, u32[]{:S(2)}) collective-permute-start(bf16[128,3072]{1,0:T(8,128)(2,1)} %get-tuple-element.491), channel_id=1, source_target_pairs={{0,16},{4,20},{8,24},{12,28},{16,0},{20,4},{24,8},{28,12},{1,17},{... | collective-permute-start | bytes 2359304 | tf_op jit(solution)/shard_map/ppermute | solution.py:41
  491.2 157.7 %reduce-scatter.8.cloned.1.call-start = ((), (), s32[]{:S(2)}) async-start(), calls=%async_computation.10 | async-start | bytes 2621440 | tf_op jit(solution)/shard_map/reduce_scatter | solution.py:1263
  492.6 41.4 %collective-permute-start.60 = (bf16[256,3072]{1,0:T(8,128)(2,1)S(1)}, bf16[256,3072]{1,0:T(8,128)(2,1)S(1)}, u32[]{:S(2)}, u32[]{:S(2)}) collective-permute-start(bf16[256,3072]{1,0:T(8,128)(2,1)S(1)} %copy-done.38), channel_id=1, source_target_pairs={{0,8},{4,12},{8,0},{12,4},{16,24},{20,28},{24,16},{28,20},{1,9},{5... | collective-permute-start | bytes 4718600 | tf_op jit(solution)/shard_map/ppermute | solution.py:41
  493.8 40.2 %collective-permute-start.59 = (bf16[160,3072]{1,0:T(8,128)(2,1)}, bf16[160,3072]{1,0:T(8,128)(2,1)}, u32[]{:S(2)}, u32[]{:S(2)}) collective-permute-start(bf16[160,3072]{1,0:T(8,128)(2,1)} %get-tuple-element.512), channel_id=1, source_target_pairs={{0,16},{4,20},{8,24},{12,28},{16,0},{20,4},{24,8},{28,12},{1,17},{... | collective-permute-start | bytes 2949128 | tf_op jit(solution)/shard_map/ppermute | solution.py:41
  494.7 39.3 %collective-permute-start.58 = (bf16[128,3072]{1,0:T(8,128)(2,1)}, bf16[128,3072]{1,0:T(8,128)(2,1)}, u32[]{:S(2)}, u32[]{:S(2)}) collective-permute-start(bf16[128,3072]{1,0:T(8,128)(2,1)} %get-tuple-element.511), channel_id=1, source_target_pairs={{0,16},{4,20},{8,24},{12,28},{16,0},{20,4},{24,8},{28,12},{1,17},{... | collective-permute-start | bytes 2359304 | tf_op jit(solution)/shard_map/ppermute | solution.py:41
  (142 other events, 1965.1 us)
Sparse Core Ops, SparseCore 0:
  38.9 52.6 all-gather.3
  97.2 39.2 all-gather.5
  149.1 52.8 reduce-scatter.3
  438.1 44.1 all-gather.7
  491.3 42.4 reduce-scatter.5
  573.6 47.7 reduce-scatter.7

commit v8 on v7

--- a/solution.py
+++ b/solution.py
@@ -1158,7 +1158,7 @@
     chunk_grads(SEND_HIGH, 3 * quarter, halves_cut)
     at.fence(THERE, *at.having(SEND_HIGH), *chunk_keys)
     half = e_rows // 2
-    early, most = 3 * e_rows // 8, 3 * e_rows // 4
+    early, most = 3 * e_rows // 8, 7 * e_rows // 8
     for i in reversed(range(zs)):
         here = near_sum[i].astype(F32) + at[THERE].astype(F32)
         if i < last:

time: 686 us -> 688 us (level)
  transfers between devices with their start and end apart: 90 -> 90, of which waited for: 34 -> 35; matrix products, arithmetic and copies ran while one was open for 17% -> 17% of each run, Pallas kernels for 27% -> 27%
where the time goes in v8:
time: 688 us; the launch traced here: 676 us
  Pallas kernels  213 us (31%)
  waiting for transfers between devices  195 us (28%)
  starting transfers between devices  85.4 us (12%)
  local copies, waits for them, and re-layouts  67.2 us (10%)
  other arithmetic  62.5 us (9%)
  blocking collectives  19.9 us (3%)
  matrix products  16.5 us (2%)
  between operations  15.9 us (2%)
    ppermute x65, waiting for transfers between devices, flip(): lax.ppermute(v, 'dp', [(i, i ^ bit) for i in range(lax.axis_size('dp'))])  141 us
    pallas_call x2, Pallas kernels, run_expert(): pl.pallas_call(functools.partial(expert_kernel, len(heights), len(pieces)...  50.3 us
    ppermute x65, starting transfers between devices, flip(): lax.ppermute(v, 'dp', [(i, i ^ bit) for i in range(lax.axis_size('dp'))])  44.1 us
    pallas_call x4, Pallas kernels, grads(): pl.pallas_call(functools.partial(grads_kernel, len(chunks), rows, cuts),...  41.8 us
    ppermute x15, waiting for transfers between devices, hop(): return lax.ppermute(v, 'expert', pairs)  28.7 us
    ppermute x15, starting transfers between devices, hop(): return lax.ppermute(v, 'expert', pairs)  27.1 us
    pallas_call x4, Pallas kernels, pick_rows(): pl.pallas_call(functools.partial(kernel, len(parts)), grid_spec=pltpu.Pre...  23.1 us
    pallas_call x2, Pallas kernels, result(): pl.pallas_call(functools.partial(result_kernel, count, len(pieces), wide)...  19 us
  transfers between devices with their start and end apart: 90, of which 35 were waited for; matrix products, arithmetic and copies ran while one was open for 17% of the time, Pallas kernels for 27%

profile of v8, /device:TPU:4, one launch (start us, length us, event | category | flops | bytes accessed | tf_op | source)
XLA Modules:
  0.0 675.7 jit_solution(12342447971718154267)
XLA Ops:
  20.7 8.7 %constant_dynamic-slice_fusion.2 = (bf16[256,1,2048]{2,1,0:T(2,128)(2,1)S(1)}, bf16[256,1,2048]{2,1,0:T(2,128)(2,1)S(1)}, bf16[256,1,2048]{2,1,0:T(2,128)(2,1)S(1)}, bf16[256,1,2048]{2,1,0:T(2,128)(2,1)S(1)}) fusion(bf16[256,4,2048]{2,1,0:T(4,128)(2,1)S(1)} %copy-done.14, s32[]{:T(128)S(6)} %select_n.167, s32[]{:T(128)S(6)} %select_n.166, ...), kind=kLoop, calls=%fused_computation.176 | loop fusion | bytes 8388624 | tf_op jit(solution)/shard_map/jit(dynamic_index_in_dim)/dynamic_slice | solution.py:88
  41.4 10.7 %collective-permute-done = bf16[128,2048]{1,0:T(8,128)(2,1)} collective-permute-done((bf16[128,2048]{1,0:T(8,128)(2,1)}, bf16[128,2048]{1,0:T(8,128)(2,1)}, u32[]{:S(2)}, u32[]{:S(2)}) %collective-permute-start) | collective-permute-done | bytes 524320 | tf_op jit(solution)/shard_map/ppermute | solution.py:52
  60.1 6.4 collective-permute-done.2
  74.8 7.1 %collective-permute-done.3 = bf16[128,2048]{1,0:T(8,128)(2,1)} collective-permute-done((bf16[128,2048]{1,0:T(8,128)(2,1)}, bf16[128,2048]{1,0:T(8,128)(2,1)}, u32[]{:S(2)}, u32[]{:S(2)}) %collective-permute-start.3) | collective-permute-done | bytes 524320 | tf_op jit(solution)/shard_map/ppermute | solution.py:52
  117.9 9.8 %psum.14 = f32[2,512]{1,0:T(2,128)S(1)} all-reduce(f32[2,512]{1,0:T(2,128)S(1)} %pad_maximum_fusion.14), channel_id=1, replica_groups=mesh['dp'=8,'expert'=4] {'expert'}, use_global_device_ids=true, to_apply=%region_7.8 | all-reduce | flops 1024 | bytes 8192 | tf_op jit(solution)/shard_map/psum | solution.py:1011
  128.4 8.7 %attend.1 = (bf16[512,512]{1,0:T(8,128)(2,1)}, bf16[512,512]{1,0:T(8,128)(2,1)}, bf16[512,512]{1,0:T(8,128)(2,1)}, bf16[512,512]{1,0:T(8,128)(2,1)}) custom-call(f32[512,1536]{1,0:T(8,128)} %copy-done.5, f32[4,2,128]{2,1,0:T(2,128)} %rsqrt_bitcast_fusion.r, f32[2,512]{1,0:T(2,128)} %copy.201.gains, f32[512,128]{1,0:T(8,128)} %copy.202.cos, ...), custom_call_target="tpu_custom_call" | custom-call | flops 1000000 | bytes 100000 | tf_op jit(solution)/shard_map/attend/pallas_call | solution.py:634
  158.3 50.0 %collective-permute-done.10.refs_0_ = bf16[256,2176]{1,0:T(8,128)(2,1)S(1)} collective-permute-done((bf16[256,2176]{1,0:T(8,128)(2,1)S(1)}, bf16[256,2176]{1,0:T(8,128)(2,1)S(1)}, u32[]{:S(2)}, u32[]{:S(2)}) %collective-permute-start.10) | collective-permute-done | bytes 1114144 | tf_op jit(solution)/shard_map/ppermute | solution.py:41
  280.1 6.3 gather.9
  289.2 24.9 %expert.2 = (bf16[128,2176]{1,0:T(8,128)(2,1)}, bf16[128,2176]{1,0:T(8,128)(2,1)}, bf16[128,2176]{1,0:T(8,128)(2,1)}, bf16[128,2176]{1,0:T(8,128)(2,1)}, bf16[51...) custom-call(s32[3]{0:T(128)} %pad_add_fusion.expert, ...), custom_call_target="tpu_custom_call" | custom-call | flops 1000000 | bytes 100000 | tf_op jit(solution)/shard_map/expert/pallas_call | solution.py:372
  318.5 6.3 gather.10
  324.8 25.4 %expert.3 = (bf16[128,2176]{1,0:T(8,128)(2,1)}, bf16[128,2176]{1,0:T(8,128)(2,1)}, bf16[128,2176]{1,0:T(8,128)(2,1)}, bf16[128,2176]{1,0:T(8,128)(2,1)}, bf16[25...) custom-call(s32[3]{0:T(128)} %pad_add_fusion.expert, ...), custom_call_target="tpu_custom_call" | custom-call | flops 1000000 | bytes 100000 | tf_op jit(solution)/shard_map/expert/pallas_call | solution.py:372
  359.5 10.2 %grads.4 = (bf16[128,3072]{1,0:T(8,128)(2,1)}, bf16[128,3072]{1,0:T(8,128)(2,1)}, bf16[128,3072]{1,0:T(8,128)(2,1)}, bf16[128,3072]{1,0:T(8,128)(2,1)}) custom-call(bf16[640,2048]{1,0:T(8,128)(2,1)} %get-tuple-element.477.refs_0_, bf16[640,2048]{1,0:T(8,128)(2,1)} %gather_cot.2.refs_1_, bf16[640,1024]{1,0:T(8,128)(2,1)} %get-tuple-element.479.refs_2_, ...), custom_call_target="tpu_custom_call" | custom-call | flops 1000000 | bytes 100000 | tf_op jit(solution)/shard_map/grads/pallas_call | solution.py:471
  377.9 9.5 %result.2 = (bf16[512,2048]{1,0:T(8,128)(2,1)}, bf16[512,2048]{1,0:T(8,128)(2,1)}) custom-call(s32[1]{0:T(128)} %bitcast.29.me, bf16[640,1024]{1,0:T(8,128)(2,1)} %get-tuple-element.486.refs_9_.gact, s32[128,8]{1,0:T(8,128)} %bitcast.201, bf16[256,3072]{1,0:T(8,128)(2,1)} %copy-done.2, bf16[256,3072]{1,0:T(8,128)(2,1)} %copy-done.6, ...), custom_call_target="tpu_custom_call" | custom-call | flops 1000000 | bytes 100000 | tf_op jit(solution)/shard_map/result/pallas_call | solution.py:422
  399.9 9.5 %result.3 = (bf16[512,2048]{1,0:T(8,128)(2,1)}, bf16[512,2048]{1,0:T(8,128)(2,1)}) custom-call(s32[1]{0:T(128)} %bitcast.29.me, bf16[640,1024]{1,0:T(8,128)(2,1)} %get-tuple-element.481.refs_4_.gact, s32[128,8]{1,0:T(8,128)} %bitcast.199, bf16[256,3072]{1,0:T(8,128)(2,1)} %copy-done.2, bf16[256,3072]{1,0:T(8,128)(2,1)} %copy-done.6, ...), custom_call_target="tpu_custom_call" | custom-call | flops 1000000 | bytes 100000 | tf_op jit(solution)/shard_map/result/pallas_call | solution.py:422
  415.0 10.5 %grads.5 = (bf16[128,3072]{1,0:T(8,128)(2,1)}, bf16[128,3072]{1,0:T(8,128)(2,1)}, bf16[160,3072]{1,0:T(8,128)(2,1)}, bf16[96,3072]{1,0:T(8,128)(2,1)}) custom-call(bf16[640,2048]{1,0:T(8,128)(2,1)} %get-tuple-element.477.refs_0_, bf16[640,2048]{1,0:T(8,128)(2,1)} %gather_cot.2.refs_1_, bf16[640,1024]{1,0:T(8,128)(2,1)} %get-tuple-element.479.refs_2_, ...), custom_call_target="tpu_custom_call" | custom-call | flops 1000000 | bytes 100000 | tf_op jit(solution)/shard_map/grads/pallas_call | solution.py:471
  441.6 10.7 %grads.6 = (bf16[256,3072]{1,0:T(8,128)(2,1)}, bf16[256,3072]{1,0:T(8,128)(2,1)}) custom-call(bf16[640,2048]{1,0:T(8,128)(2,1)} %get-tuple-element.477.refs_0_, bf16[640,2048]{1,0:T(8,128)(2,1)} %gather_cot.2.refs_1_, bf16[640,1024]{1,0:T(8,128)(2,1)} %get-tuple-element.479.refs_2_, bf16[640,1024]{1,0:T(8,128)(2,1)} %get-tuple-element.480.refs_3_, ...), custom_call_target="tpu_custom_call" | custom-call | flops 1000000 | bytes 100000 | tf_op jit(solution)/shard_map/grads/pallas_call | solution.py:471
  452.3 10.4 %grads.7 = (bf16[256,3072]{1,0:T(8,128)(2,1)}, bf16[256,3072]{1,0:T(8,128)(2,1)}) custom-call(bf16[640,2048]{1,0:T(8,128)(2,1)} %get-tuple-element.477.refs_0_, bf16[640,2048]{1,0:T(8,128)(2,1)} %gather_cot.2.refs_1_, bf16[640,1024]{1,0:T(8,128)(2,1)} %get-tuple-element.479.refs_2_, bf16[640,1024]{1,0:T(8,128)(2,1)} %get-tuple-element.480.refs_3_, ...), custom_call_target="tpu_custom_call" | custom-call | flops 1000000 | bytes 100000 | tf_op jit(solution)/shard_map/grads/pallas_call | solution.py:471
  476.2 10.4 %collective-permute-done.54 = bf16[512,2048]{1,0:T(8,128)(2,1)} collective-permute-done((bf16[512,2048]{1,0:T(8,128)(2,1)}, bf16[512,2048]{1,0:T(8,128)(2,1)}, u32[]{:S(2)}, u32[]{:S(2)}) %collective-permute-start.54) | collective-permute-done | bytes 2097184 | tf_op jit(solution)/shard_map/ppermute | solution.py:41
  495.8 14.0 %attend_back.1 = (f32[512,512]{1,0:T(8,128)}, f32[512,512]{1,0:T(8,128)}, bf16[512,512]{1,0:T(8,128)(2,1)}, f32[4,2,128]{2,1,0:T(2,128)}) custom-call(bf16[512,2048]{1,0:T(8,128)(2,1)} %all-gather.8.cloned.1.call-done.dhb, bf16[512,2048]{1,0:T(8,128)(2,1)} %all-gather.6.cloned.1.call-done.wo, f32[512,1536]{1,0:T(8,128)} %copy-done.5, f32[512,1536]{1,0:T(8,128)} %copy-done.5, ...), custom_call_target="tpu_custom_call" | custom-call | flops 1000000 | bytes 100000 | tf_op jit(solution)/shard_map/attend_back/pallas_call | solution.py:685
  509.8 10.1 %psum.15 = f32[8,128]{1,0:T(8,128)S(1)} all-reduce(f32[8,128]{1,0:T(8,128)} %bitcast.222), channel_id=1, replica_groups=mesh['dp'=8,'expert'=4] {'expert'}, use_global_device_ids=true, to_apply=%region_19.20 | all-reduce | flops 1024 | bytes 8192 | tf_op jit(solution)/shard_map/psum | solution.py:1244
  554.4 12.9 %first_back.1 = (bf16[512,2048]{1,0:T(8,128)(2,1)}, f32[1,2048]{1,0:T(1,128)}) custom-call(bf16[512,1536]{1,0:T(8,128)(2,1)} %get-tuple-element.521.d, bf16[2048,1664]{1,0:T(8,128)(2,1)} %all-gather.4.cloned.1.call-done.w, bf16[512,2048]{1,0:T(8,128)(2,1)} %copy-done.12, f32[512,1]{1,0:T(8,128)} %copy.230.r), custom_call_target="tpu_custom_call" | custom-call | flops 1000000 | bytes 100000 | tf_op jit(solution)/shard_map/first_back/pallas_call | solution.py:778
  582.4 18.0 %collective-permute-done.68 = bf16[64,2048]{1,0:T(8,128)(2,1)S(1)} collective-permute-done((bf16[64,2048]{1,0:T(8,128)(2,1)S(1)}, bf16[64,2048]{1,0:T(8,128)(2,1)S(1)}, u32[]{:S(2)}, u32[]{:S(2)}) %collective-permute-start.68) | collective-permute-done | bytes 262176 | tf_op jit(solution)/shard_map/ppermute | solution.py:41
  613.6 14.7 %collective-permute-done.72 = bf16[64,2048]{1,0:T(8,128)(2,1)} collective-permute-done((bf16[64,2048]{1,0:T(8,128)(2,1)S(1)}, bf16[64,2048]{1,0:T(8,128)(2,1)}, u32[]{:S(2)}, u32[]{:S(2)}) %collective-permute-start.72) | collective-permute-done | bytes 262176 | tf_op jit(solution)/shard_map/ppermute | solution.py:1275
  641.8 9.4 %form.2 = (f32[256,4,2048]{2,1,0:T(4,128)}, f32[256,4,1024]{2,1,0:T(4,128)}) custom-call(s32[1]{0:T(128)} %bitcast.49.own, bf16[256,3072]{1,0:T(8,128)(2,1)} %add_pieces.6.refs_0_, bf16[256,3072]{1,0:T(8,128)(2,1)} %copy-done.22, bf16[256,3072]{1,0:T(8,128)(2,1)} %copy-done.21, bf16[224,3072]{1,0:T(8,128)(2,1)} %collective-permute-done.74.refs_3_), custom_call_target="tpu_custom_call" | custom-call | flops 1000000 | bytes 100000 | tf_op jit(solution)/shard_map/form/pallas_call | solution.py:827
  (527 shorter events, 345.3 us)
Async XLA Ops:
  16.3 75.2 %all-gather.4.cloned.1.call-start = ((), (), s32[]{:S(2)}) async-start(), calls=%async_computation.5 | async-start | bytes 7667712 | tf_op jit(solution)/shard_map/all_gather | solution.py:964
  38.8 98.3 %all-gather.6.cloned.1.call-start = ((), (), s32[]{:S(2)}) async-start(), calls=%async_computation.6 | async-start | bytes 2359296 | tf_op jit(solution)/shard_map/all_gather | solution.py:997
  40.9 45.4 %collective-permute-start.4 = (bf16[256,3072]{1,0:T(8,128)(2,1)}, bf16[256,3072]{1,0:T(8,128)(2,1)S(1)}, u32[]{:S(2)}, u32[]{:S(2)}) collective-permute-start(bf16[256,3072]{1,0:T(8,128)(2,1)} %pad_maximum_fusion.5), channel_id=1, source_target_pairs={{0,4},{4,0},{8,12},{12,8},{16,20},{20,16},{24,28},{28,24},{1,5},{5... | collective-permute-start | bytes 4718600 | tf_op jit(solution)/shard_map/ppermute | solution.py:41
  40.9 45.4 %collective-permute-start.5 = (bf16[256,3072]{1,0:T(8,128)(2,1)}, bf16[256,3072]{1,0:T(8,128)(2,1)}, u32[]{:S(2)}, u32[]{:S(2)}) collective-permute-start(bf16[256,3072]{1,0:T(8,128)(2,1)} %pad_maximum_fusion.7), channel_id=1, source_target_pairs={{0,4},{4,0},{8,12},{12,8},{16,20},{20,16},{24,28},{28,24},{1,5},{5... | collective-permute-start | bytes 4718600 | tf_op jit(solution)/shard_map/ppermute | solution.py:41
  97.1 112.8 %reduce-scatter.4.cloned.1.call-start = ((), (), s32[]{:S(2)}) async-start(), calls=%async_computation.7 | async-start | bytes 2621440 | tf_op jit(solution)/shard_map/reduce_scatter | solution.py:1023
  100.5 47.1 %collective-permute-start.8 = (bf16[256,3072]{1,0:T(8,128)(2,1)}, bf16[256,3072]{1,0:T(8,128)(2,1)S(1)}, u32[]{:S(2)}, u32[]{:S(2)}) collective-permute-start(bf16[256,3072]{1,0:T(8,128)(2,1)} %pad_maximum_fusion.6), channel_id=1, source_target_pairs={{0,8},{4,12},{8,0},{12,4},{16,24},{20,28},{24,16},{28,20},{1,9},{5... | collective-permute-start | bytes 4718600 | tf_op jit(solution)/shard_map/ppermute | solution.py:41
  104.4 44.5 %collective-permute-start.9 = (bf16[256,3072]{1,0:T(8,128)(2,1)S(1)}, bf16[256,3072]{1,0:T(8,128)(2,1)}, u32[]{:S(2)}, u32[]{:S(2)}) collective-permute-start(bf16[256,3072]{1,0:T(8,128)(2,1)S(1)} %pad_maximum_fusion.4.refs_4_.refs_15_.refs_26_.refs_0_), channel_id=1, source_target_pairs={{0,16},{4,20},{8,24},{12,28},{16,0},{20,4},{24,8},{28,12},{1,17},{... | collective-permute-start | bytes 4718600 | tf_op jit(solution)/shard_map/ppermute | solution.py:41
  149.0 337.6 %all-gather.8.cloned.1.call-start = ((), (), s32[]{:S(2)}) async-start(), calls=%async_computation.8 | async-start | bytes 2621440 | tf_op jit(solution)/shard_map/all_gather | solution.py:1214
  149.0 59.3 %collective-permute-start.12 = (bf16[256,3072]{1,0:T(8,128)(2,1)}, bf16[256,3072]{1,0:T(8,128)(2,1)S(1)}, u32[]{:S(2)}, u32[]{:S(2)}) collective-permute-start(bf16[256,3072]{1,0:T(8,128)(2,1)} %collective-permute-done.5), channel_id=1, source_target_pairs={{0,8},{4,12},{8,0},{12,4},{16,24},{20,28},{24,16},{28,20},{1,9},{5... | collective-permute-start | bytes 4718600 | tf_op jit(solution)/shard_map/ppermute | solution.py:41
  149.5 60.4 %collective-permute-start.13 = (bf16[256,3072]{1,0:T(8,128)(2,1)}, bf16[256,3072]{1,0:T(8,128)(2,1)}, u32[]{:S(2)}, u32[]{:S(2)}) collective-permute-start(bf16[256,3072]{1,0:T(8,128)(2,1)} %copy-done.6), channel_id=1, source_target_pairs={{0,16},{4,20},{8,24},{12,28},{16,0},{20,4},{24,8},{28,12},{1,17},{... | collective-permute-start | bytes 4718600 | tf_op jit(solution)/shard_map/ppermute | solution.py:41
  151.0 57.3 %collective-permute-start.10 = (bf16[256,2176]{1,0:T(8,128)(2,1)S(1)}, bf16[256,2176]{1,0:T(8,128)(2,1)S(1)}, u32[]{:S(2)}, u32[]{:S(2)}) collective-permute-start(bf16[256,2176]{1,0:T(8,128)(2,1)S(1)} %pad_maximum_fusion.8), channel_id=1, source_target_pairs={{0,8},{4,12},{8,0},{12,4},{16,24},{20,28},{24,16},{28,20},{1,9},{5... | collective-permute-start | bytes 3342344 | tf_op jit(solution)/shard_map/ppermute | solution.py:41
  152.9 55.4 %collective-permute-start.14 = (bf16[176,3072]{1,0:T(8,128)(2,1)S(1)}, bf16[176,3072]{1,0:T(8,128)(2,1)S(1)}, u32[]{:S(2)}, u32[]{:S(2)}) collective-permute-start(bf16[176,3072]{1,0:T(8,128)(2,1)S(1)} %slice.245), channel_id=1, source_target_pairs={{0,16},{4,20},{8,24},{12,28},{16,0},{20,4},{24,8},{28,12},{1,17},{... | collective-permute-start | bytes 3244040 | tf_op jit(solution)/shard_map/ppermute | solution.py:41
  154.7 53.6 %collective-permute-start.11 = (bf16[128,2176]{1,0:T(8,128)(2,1)}, bf16[128,2176]{1,0:T(8,128)(2,1)S(1)}, u32[]{:S(2)}, u32[]{:S(2)}) collective-permute-start(bf16[128,2176]{1,0:T(8,128)(2,1)} %collective-permute-done.7), channel_id=1, source_target_pairs={{0,2},{2,3},{3,1},{1,0},{4,6},{6,7},{7,5},{5,4},{8,10},{10,11},{11... | collective-permute-start | bytes 1671176 | tf_op jit(solution)/shard_map/ppermute | solution.py:52
  275.5 38.6 %collective-permute-start.35 = (bf16[128,2048]{1,0:T(8,128)(2,1)}, bf16[128,2048]{1,0:T(8,128)(2,1)S(1)}, u32[]{:S(2)}, u32[]{:S(2)}) collective-permute-start(bf16[128,2048]{1,0:T(8,128)(2,1)} %collective-permute-done.19.refs_2_), channel_id=1, source_target_pairs={{0,8},{4,12},{8,0},{12,4},{16,24},{20,28},{24,16},{28,20},{1,9},{5... | collective-permute-start | bytes 1572872 | tf_op jit(solution)/shard_map/ppermute | solution.py:41
  276.3 37.8 %collective-permute-start.36 = (bf16[128,2048]{1,0:T(8,128)(2,1)}, bf16[128,2048]{1,0:T(8,128)(2,1)S(1)}, u32[]{:S(2)}, u32[]{:S(2)}) collective-permute-start(bf16[128,2048]{1,0:T(8,128)(2,1)} %collective-permute-done.23.refs_3_), channel_id=1, source_target_pairs={{0,8},{4,12},{8,0},{12,4},{16,24},{20,28},{24,16},{28,20},{1,9},{5... | collective-permute-start | bytes 1572872 | tf_op jit(solution)/shard_map/ppermute | solution.py:41
  377.0 33.6 %collective-permute-start.49 = (bf16[128,3072]{1,0:T(8,128)(2,1)}, bf16[128,3072]{1,0:T(8,128)(2,1)S(1)}, u32[]{:S(2)}, u32[]{:S(2)}) collective-permute-start(bf16[128,3072]{1,0:T(8,128)(2,1)} %get-tuple-element.437), channel_id=1, source_target_pairs={{0,16},{4,20},{8,24},{12,28},{16,0},{20,4},{24,8},{28,12},{1,17},{... | collective-permute-start | bytes 2359304 | tf_op jit(solution)/shard_map/ppermute | solution.py:41
  438.0 96.1 %reduce-scatter.6.cloned.1.call-start = ((), (), s32[]{:S(2)}) async-start(), calls=%async_computation.9 | async-start | bytes 2621440 | tf_op jit(solution)/shard_map/reduce_scatter | solution.py:1236
  438.2 34.3 %collective-permute-start.55 = (bf16[512,2048]{1,0:T(8,128)(2,1)}, bf16[512,2048]{1,0:T(8,128)(2,1)S(1)}, u32[]{:S(2)}, u32[]{:S(2)}) collective-permute-start(bf16[512,2048]{1,0:T(8,128)(2,1)} %get-tuple-element.476), channel_id=1, source_target_pairs={{0,4},{4,0},{8,12},{12,8},{16,20},{20,16},{24,28},{28,24},{1,5},{5... | collective-permute-start | bytes 6291464 | tf_op jit(solution)/shard_map/ppermute | solution.py:41
  438.3 48.4 %collective-permute-start.54 = (bf16[512,2048]{1,0:T(8,128)(2,1)}, bf16[512,2048]{1,0:T(8,128)(2,1)}, u32[]{:S(2)}, u32[]{:S(2)}) collective-permute-start(bf16[512,2048]{1,0:T(8,128)(2,1)} %add_convert_fusion.3), channel_id=1, source_target_pairs={{0,8},{4,12},{8,0},{12,4},{16,24},{20,28},{24,16},{28,20},{1,9},{5... | collective-permute-start | bytes 6291464 | tf_op jit(solution)/shard_map/ppermute | solution.py:41
  440.5 35.8 %collective-permute-start.57 = (bf16[128,3072]{1,0:T(8,128)(2,1)}, bf16[128,3072]{1,0:T(8,128)(2,1)S(1)}, u32[]{:S(2)}, u32[]{:S(2)}) collective-permute-start(bf16[128,3072]{1,0:T(8,128)(2,1)} %get-tuple-element.491), channel_id=1, source_target_pairs={{0,16},{4,20},{8,24},{12,28},{16,0},{20,4},{24,8},{28,12},{1,17},{... | collective-permute-start | bytes 2359304 | tf_op jit(solution)/shard_map/ppermute | solution.py:41
  491.2 160.0 %reduce-scatter.8.cloned.1.call-start = ((), (), s32[]{:S(2)}) async-start(), calls=%async_computation.10 | async-start | bytes 2621440 | tf_op jit(solution)/shard_map/reduce_scatter | solution.py:1263
  492.6 41.4 %collective-permute-start.60 = (bf16[256,3072]{1,0:T(8,128)(2,1)S(1)}, bf16[256,3072]{1,0:T(8,128)(2,1)S(1)}, u32[]{:S(2)}, u32[]{:S(2)}) collective-permute-start(bf16[256,3072]{1,0:T(8,128)(2,1)S(1)} %copy-done.38), channel_id=1, source_target_pairs={{0,8},{4,12},{8,0},{12,4},{16,24},{20,28},{24,16},{28,20},{1,9},{5... | collective-permute-start | bytes 4718600 | tf_op jit(solution)/shard_map/ppermute | solution.py:41
  493.8 40.2 %collective-permute-start.59 = (bf16[160,3072]{1,0:T(8,128)(2,1)}, bf16[160,3072]{1,0:T(8,128)(2,1)}, u32[]{:S(2)}, u32[]{:S(2)}) collective-permute-start(bf16[160,3072]{1,0:T(8,128)(2,1)} %get-tuple-element.512), channel_id=1, source_target_pairs={{0,16},{4,20},{8,24},{12,28},{16,0},{20,4},{24,8},{28,12},{1,17},{... | collective-permute-start | bytes 2949128 | tf_op jit(solution)/shard_map/ppermute | solution.py:41
  494.7 39.3 %collective-permute-start.58 = (bf16[128,3072]{1,0:T(8,128)(2,1)}, bf16[128,3072]{1,0:T(8,128)(2,1)}, u32[]{:S(2)}, u32[]{:S(2)}) collective-permute-start(bf16[128,3072]{1,0:T(8,128)(2,1)} %get-tuple-element.511), channel_id=1, source_target_pairs={{0,16},{4,20},{8,24},{12,28},{16,0},{20,4},{24,8},{28,12},{1,17},{... | collective-permute-start | bytes 2359304 | tf_op jit(solution)/shard_map/ppermute | solution.py:41
  (142 other events, 1970.5 us)
Sparse Core Ops, SparseCore 0:
  38.9 52.6 all-gather.3
  97.2 39.2 all-gather.5
  149.1 52.8 reduce-scatter.3
  438.1 44.1 all-gather.7
  491.3 42.4 reduce-scatter.5
  575.9 47.8 reduce-scatter.7
